TPU v7x, 32 devices: a whole 2x2x4 slice. The times are simulated.
32 devices in a mesh: reader: 4 (over y, x), blk: 8 (over z, core).
Axes of the slice: x: 2, y: 2, z: 4, core: 2. Of those that a mesh axis runs over, the one named last changes fastest.
Arguments:
- features: bfloat16 [4096, 512], P(('reader', 'blk')), may hold values from -40 to 40
- cotangent: bfloat16 [4096, 512], P(('reader', 'blk')), may hold values from -6 to 6
- w_query: bfloat16 [512, 512], replicated, may hold values from -0.25 to 0.25
- w_key: bfloat16 [512, 512], replicated, may hold values from -0.25 to 0.25
- w_value: bfloat16 [512, 512], replicated, may hold values from -0.25 to 0.25
- tile_coords: int32 [4, 8, 8, 3], P('reader', 'blk'), may hold values from 0 to 239, as said below
- tile_count: int32 [4, 8], P('reader', 'blk'), may hold values from 1 to 8, as said below
- mask_table: int32 [240, 128, 4], replicated, may hold values from -2147483648 to 2147483647, as said below
Outputs:
- attn_out: bfloat16 [4096, 512], P(('reader', 'blk'))
- grad_features: bfloat16 [4096, 512], P(('reader', 'blk'))
Inputs may be any that keep to these rules, and one draw needn't show every extreme that they name: `tile_coords`: for every r and b the 8 slots name distinct (qb, kb) pairs with qb < 8, kb < 4, p < 240; the first 1 slots are the tiles in which the nodes of segment r * 8 + b meet themselves. `tile_count`: some pair (r, b) uses all 8 slots, and some pair uses the fewest. `mask_table`: each word packs 32 edge bits as a signed int32; each bit is set with probability 1/32.
All inputs are finite; a program needn't handle non-finite values.
Results may differ from a plain program's by a relative error of at most 0.01265.
The roundings to bfloat16 on the way count: a program that leaves them out, or rounds other values in their place, can miss the bound.
Values may be sent and summed in bfloat16 or wider, within the bound.
No kernel may reach another device: no remote copies, remote signals or barrier semaphores. Data moves between devices by JAX's collectives and lax.ppermute only.
A program may use at most 128 MiB of HBM per device.

v0:
```python
import jax
import jax.numpy as jnp
from jax import lax
from jax.sharding import PartitionSpec as P

HEADS = 8


NEG_FILL = -1e30


def unpack(mask_words):
    shifts = jnp.arange(32, dtype=jnp.int32)
    mask_bits = jnp.right_shift(mask_words[..., None], shifts) & 1
    return mask_bits.reshape(mask_words.shape[:-1] + (mask_words.shape[-1] * 32,)) > 0


def project(rows, weight):
    return jnp.dot(rows, weight, preferred_element_type=jnp.float32).astype(jnp.bfloat16)


def local(features, cotangent, w_query, w_key, w_value, tile_coords, tile_count, mask_table):
    rows_own, model_width = features.shape
    block_size = mask_table.shape[1]
    head_dim = model_width // HEADS
    scale = float(head_dim) ** (-0.5)
    seg_count = rows_own // block_size
    query_count = lax.axis_size("blk") * seg_count
    key_count = lax.axis_size("reader") * seg_count
    blk_index = lax.axis_index("blk")
    reader_index = lax.axis_index("reader")
    queries = project(features, w_query)
    query_rows, grad_rows = (
        lax.all_gather(queries, "blk", axis=0, tiled=True),
        lax.all_gather(cotangent, "blk", axis=0, tiled=True),
    )
    key_rows, value_rows = (
        lax.all_gather(project(features, w_key), "reader", axis=0, tiled=True),
        lax.all_gather(project(features, w_value), "reader", axis=0, tiled=True),
    )
    query_tiles = query_rows.reshape(query_count, block_size, HEADS, head_dim)
    grad_tiles = grad_rows.reshape(query_count, block_size, HEADS, head_dim)
    key_tiles = key_rows.reshape(key_count, block_size, HEADS, head_dim)
    value_tiles = value_rows.reshape(key_count, block_size, HEADS, head_dim)
    coords = tile_coords.reshape(-1, 3)
    tile_total = tile_count.reshape(-1)[0]
    batch_size = 8
    turns = (tile_total + batch_size - 1) // batch_size
    diagonal_cells = jnp.eye(block_size, dtype=bool)

    def tile_scores(turn_index):
        picked = lax.dynamic_slice_in_dim(coords, turn_index * batch_size, batch_size, 0)
        query_blk = picked[:, 0]
        key_blk = picked[:, 1]
        usable = turn_index * batch_size + jnp.arange(batch_size, dtype=jnp.int32) < tile_total
        on_diag = (
            (query_blk // seg_count == blk_index)
            & (key_blk // seg_count == reader_index)
            & (query_blk % seg_count == key_blk % seg_count)
        )
        allowed = (
            unpack(mask_table[picked[:, 2]]) | on_diag[:, None, None] & diagonal_cells
        ) & usable[:, None, None]
        scores = (
            jnp.einsum(
                "gqhd,gkhd->ghqk",
                query_tiles[query_blk],
                key_tiles[key_blk],
                preferred_element_type=jnp.float32,
            )
            * scale
        )
        return (query_blk, key_blk, allowed[:, None], scores)

    def max_turn(turn_index, local_max):
        query_blk, key_blk, allowed, scores = tile_scores(turn_index)
        tile_max = jnp.max(jnp.where(allowed, scores, NEG_FILL), axis=-1)
        return local_max.at[query_blk].max(tile_max)

    local_max = lax.fori_loop(
        0, turns, max_turn, jnp.full((query_count, HEADS, block_size), NEG_FILL, jnp.float32)
    )
    row_max = lax.pmax(local_max, "blk")

    def sum_turn(turn_index, state_now):
        totals, weighted = state_now
        query_blk, key_blk, allowed, scores = tile_scores(turn_index)
        expo = jnp.exp(jnp.where(allowed, scores - row_max[query_blk][..., None], NEG_FILL))
        totals = totals.at[query_blk].add(jnp.sum(expo, axis=-1))
        products = jnp.einsum(
            "ghqk,gkhd->gqhd",
            expo.astype(jnp.bfloat16),
            value_tiles[key_blk],
            preferred_element_type=jnp.float32,
        )
        return (totals, weighted.at[query_blk].add(products))

    start_sums = (
        jnp.zeros((query_count, HEADS, block_size), jnp.float32),
        jnp.zeros((query_count, block_size, HEADS, head_dim), jnp.float32),
    )
    totals, weighted = lax.fori_loop(0, turns, sum_turn, start_sums)
    weighted_all, totals_all = lax.psum((weighted, totals), "blk")
    outputs = weighted_all / totals_all.transpose(0, 2, 1)[..., None]
    delta_all = jnp.sum(grad_tiles.astype(jnp.float32) * outputs, axis=-1).transpose(0, 2, 1)
    outputs_own = lax.dynamic_slice_in_dim(
        outputs.reshape(query_count * block_size, model_width), blk_index * rows_own, rows_own, 0
    )
    attn_out = outputs_own.astype(jnp.bfloat16)

    def grad_turn(turn_index, state_now):
        grad_query, grad_key, grad_value = state_now
        query_blk, key_blk, allowed, scores = tile_scores(turn_index)
        probs = (
            jnp.exp(jnp.where(allowed, scores - row_max[query_blk][..., None], NEG_FILL))
            / totals_all[query_blk][..., None]
        )
        d_rows = grad_tiles[query_blk]
        grad_value = grad_value.at[key_blk].add(
            jnp.einsum(
                "ghqk,gqhd->gkhd",
                probs.astype(jnp.bfloat16),
                d_rows,
                preferred_element_type=jnp.float32,
            )
        )
        d_probs = jnp.einsum(
            "gqhd,gkhd->ghqk", d_rows, value_tiles[key_blk], preferred_element_type=jnp.float32
        )
        d_scores = (probs * (d_probs - delta_all[query_blk][..., None]) * scale).astype(
            jnp.bfloat16
        )
        grad_query = grad_query.at[query_blk].add(
            jnp.einsum(
                "ghqk,gkhd->gqhd", d_scores, key_tiles[key_blk], preferred_element_type=jnp.float32
            )
        )
        grad_key = grad_key.at[key_blk].add(
            jnp.einsum(
                "ghqk,gqhd->gkhd",
                d_scores,
                query_tiles[query_blk],
                preferred_element_type=jnp.float32,
            )
        )
        return (grad_query, grad_key, grad_value)

    start_grads = (
        jnp.zeros((query_count, block_size, HEADS, head_dim), jnp.float32),
        jnp.zeros((key_count, block_size, HEADS, head_dim), jnp.float32),
        jnp.zeros((key_count, block_size, HEADS, head_dim), jnp.float32),
    )
    grad_query, grad_key, grad_value = lax.fori_loop(0, turns, grad_turn, start_grads)
    query_own = lax.psum_scatter(
        grad_query.reshape(query_count * block_size, model_width),
        "blk",
        scatter_dimension=0,
        tiled=True,
    )
    key_own, value_own = (
        lax.psum_scatter(
            grad_key.reshape(key_count * block_size, model_width),
            "reader",
            scatter_dimension=0,
            tiled=True,
        ),
        lax.psum_scatter(
            grad_value.reshape(key_count * block_size, model_width),
            "reader",
            scatter_dimension=0,
            tiled=True,
        ),
    )
    grad_total = jnp.dot(
        query_own.astype(jnp.bfloat16), w_query.T, preferred_element_type=jnp.float32
    )
    grad_total = grad_total + jnp.dot(
        key_own.astype(jnp.bfloat16), w_key.T, preferred_element_type=jnp.float32
    )
    grad_total = grad_total + jnp.dot(
        value_own.astype(jnp.bfloat16), w_value.T, preferred_element_type=jnp.float32
    )
    return (attn_out, grad_total.astype(jnp.bfloat16))


def solution(mesh):
    return jax.shard_map(
        local,
        mesh=mesh,
        in_specs=(
            P(("reader", "blk"), None),
            P(("reader", "blk"), None),
            P(),
            P(),
            P(),
            P("reader", "blk", None, None),
            P("reader", "blk"),
            P(),
        ),
        out_specs=(P(("reader", "blk"), None), P(("reader", "blk"), None)),
        check_vma=False,
    )
```

profile of v0, /device:TPU:0, one launch (start us, length us, event | category | flops | bytes accessed | tf_op | source)
XLA Modules:
  0.0 344.8 jit_solution(14710176868207415808)
XLA Ops:
  7.2 1.0 copy-done
  8.2 1.8 convolution_convert_fusion.2
  10.1 0.7 all-gather.5.cloned.1.call-update
  11.5 0.7 copy.131
  12.2 1.3 convolution_convert_fusion.1
  13.5 1.3 convolution_convert_fusion
  14.9 11.5 %all_gather.14 = bf16[512,512]{1,0:T(8,128)(2,1)S(1)} all-gather(bf16[128,512]{1,0:T(8,128)(2,1)S(1)} %convolution_convert_fusion), channel_id=1, replica_groups=mesh['reader'=4,'blk'=8] {'reader'}, dimensions={0}, use_global_device_ids=true | all-gather | bytes 655360 | tf_op jit(solution)/shard_map/all_gather | solution.py:39
  26.4 10.6 %all_gather.13 = bf16[512,512]{1,0:T(8,128)(2,1)S(1)} all-gather(bf16[128,512]{1,0:T(8,128)(2,1)S(1)} %convolution_convert_fusion.1), channel_id=1, replica_groups=mesh['reader'=4,'blk'=8] {'reader'}, dimensions={0}, use_global_device_ids=true | all-gather | bytes 655360 | tf_op jit(solution)/shard_map/all_gather | solution.py:38
  38.1 1.6 gather_fusion.13
  39.8 3.9 %reshape.603 = bf16[8,128,8,64]{3,2,1,0:T(8,128)(2,1)} reshape(bf16[1024,512]{1,0:T(8,128)(2,1)} %all-gather.3.cloned.1.call-done) | data formatting | bytes 2097152 | tf_op jit(solution)/shard_map/reshape | solution.py:41
  43.7 11.6 %while.51 = (s32[]{:T(128)}, f32[8,8,128]{2,1,0:T(8,128)S(1)}, s32[]{:T(128)}, s32[8,3]{0,1:T(4,128)S(1)}, s32[8,128,4]{1,2,0:T(4,128)S(1)}, /*index=5*/s32[]{:T...) while((s32[]{:T(128)}, f32[8,8,128]{2,1,0:T(8,128)S(1)}, ...), condition=%wide.region_3.4_spmd.clone, body=%wide.region_0.3_spmd.clone.sunk | while | flops 138168416 | bytes 6744593 | solution.py:80
  44.8 2.1 gather_fusion
  46.9 3.7 %gather_fusion.1 = bf16[8,128,8,64]{3,2,1,0:T(8,128)(2,1)} fusion(bf16[8,128,8,64]{3,2,1,0:T(8,128)(2,1)} %get-tuple-element.1613, s32[1024]{0:T(1024)S(1)} %get-tuple-element.1540), kind=kCustom, calls=%fused_computation.clone.clone.1 | custom fusion | bytes 2097184 | tf_op jit(solution)/shard_map/while/body/gather | solution.py:67
  50.7 3.8 %select_reduce_fusion.2 = f32[8,8,128]{2,1,0:T(8,128)S(1)} fusion(bf16[8,128,8,64]{3,2,1,0:T(8,128)(2,1)} %gather_fusion, bf16[8,128,8,64]{3,2,1,0:T(8,128)(2,1)} %gather_fusion.1, pred[8,128,128]{1,2,0:T(8,128)(4,1)S(1)} %fusion.100), kind=kOutput, calls=%fused_computation.23.clone.1 | convolution fusion | flops 137355264 | bytes 2260992 | tf_op jit(solution)/shard_map/while/body/gqhd,gkhd->ghqk/dot_general | solution.py:65
  54.5 0.8 scatter_fusion
  55.3 26.0 %pmax.7 = f32[8,8,128]{2,1,0:T(8,128)S(1)} all-reduce(f32[8,8,128]{2,1,0:T(8,128)S(1)} %get-tuple-element.1007), channel_id=1, replica_groups=mesh['reader'=4,'blk'=8] {'blk'}, use_global_device_ids=true, to_apply=%region_4.5 | all-reduce | flops 8192 | bytes 65536 | tf_op jit(solution)/shard_map/pmax | solution.py:83
  81.3 1.6 broadcast.1168.clone
  83.0 22.0 %while.52 = (s32[]{:T(128)}, f32[8,8,128]{2,1,0:T(8,128)S(1)}, f32[8,128,8,64]{1,3,2,0:T(8,128)}, s32[]{:T(128)}, s32[8,3]{0,1:T(4,128)S(1)}, /*index=5*/s32[8,1...) while((s32[]{:T(128)}, f32[8,8,128]{2,1,0:T(8,128)S(1)}, ...), condition=%wide.region_9.10_spmd.clone, body=%wide.region_5.9_spmd.clone.sunk | while | flops 278153312 | bytes 31124132 | solution.py:102
  84.7 3.7 %gather_fusion.4 = bf16[8,128,8,64]{3,2,1,0:T(8,128)(2,1)} fusion(bf16[8,128,8,64]{3,2,1,0:T(8,128)(2,1)} %get-tuple-element.1656, s32[1024]{0:T(1024)S(1)} %get-tuple-element.1556), kind=kCustom, calls=%fused_computation.2.clone.clone.1 | custom fusion | bytes 2097184 | tf_op jit(solution)/shard_map/while/body/gather | solution.py:67
  88.4 2.1 gather_fusion.5
  90.5 2.2 gather_fusion.3
  92.7 4.2 %fusion.105 = (f32[8,8,128]{2,1,0:T(8,128)S(1)}, f32[8,8,128,128]{2,3,1,0:T(8,128)S(1)}) fusion(f32[8,8,128]{2,1,0:T(8,128)S(1)} %gather_fusion.2, pred[8,128,128]{1,2,0:T(8,128)(4,1)S(1)} %fusion.104, bf16[8,128,8,64]{3,2,1,0:T(8,128)(2,1)} %gather_fusion.3, bf16[8,128,8,64]{3,2,1,0:T(8,128)(2,1)} %gather_fusion.4), kind=kOutput, calls=%fused_computation.42.clone.1 | convolution fusion | flops 138403840 | bytes 6488064 | tf_op jit(solution)/shard_map/while/body/gqhd,gkhd->ghqk/dot_general | solution.py:65
  96.9 2.3 fusion.106
  99.2 0.8 scatter_fusion.1
  100.0 5.0 %scatter_fusion.2 = f32[8,128,8,64]{1,3,2,0:T(8,128)} fusion(f32[8,128,8,64]{1,3,2,0:T(8,128)} %get-tuple-element.1634, s32[8]{0:T(128)S(1)} %get-tuple-element.1554, f32[8,128,8,64]{1,3,2,0:T(8,128)} %fusion.106), kind=kCustom, calls=%fused_computation.16.clone.clone.1 | custom fusion | flops 524288 | bytes 6291488 | tf_op jit(solution)/shard_map/while/body/scatter-add | solution.py:96
  105.0 4.1 %copy.82 = f32[8,128,8,64]{1,0,3,2:T(8,128)} copy(f32[8,128,8,64]{1,3,2,0:T(8,128)} %get-tuple-element.1008) | data formatting | bytes 4194304 | tf_op jit(solution)/shard_map/while | solution.py:102
  109.2 2.3 copy.84
  111.5 2.6 copy.100
  114.1 3.9 %copy.87 = bf16[8,128,8,64]{3,2,1,0:T(8,128)(2,1)} copy(bf16[8,128,8,64]{1,0,3,2:T(8,128)(2,1)} %bitcast.157) | data formatting | bytes 2097152
  117.9 26.5 %psum.15 = f32[8,8,128]{2,1,0:T(8,128)S(1)} all-reduce(f32[8,8,128]{2,1,0:T(8,128)S(1)} %get-tuple-element.1009), channel_id=1, replica_groups=mesh['reader'=4,'blk'=8] {'blk'}, use_global_device_ids=true, to_apply=%region_11.12 | all-reduce | flops 8192 | bytes 65536 | tf_op jit(solution)/shard_map/psum | solution.py:103
  144.4 27.1 %all-reduce.2.cloned.1.call-done = f32[8,128,8,64]{1,0,3,2:T(8,128)} async-done(((f32[8,128,8,64]{1,0,3,2:T(8,128)}), f32[8,128,8,64]{1,0,3,2:T(8,128)}) %all-reduce.2.cloned.1.call-update) | async-done | bytes 2097168 | tf_op jit(solution)/shard_map/psum | solution.py:103
  171.5 3.2 multiply_reduce_fusion
  174.8 1.1 broadcast.1171.clone
  175.9 1.1 broadcast.1171
  177.0 1.6 broadcast.1168
  178.6 57.4 %while.53 = (s32[]{:T(128)}, f32[8,128,8,64]{1,3,2,0:T(8,128)}, f32[4,128,8,64]{1,3,2,0:T(8,128)}, f32[4,128,8,64]{1,3,2,0:T(8,128)}, s32[]{:T(128)}, /*index=5*...) while((s32[]{:T(128)}, f32[8,128,8,64]{1,3,2,0:T(8,128)}, ...), condition=%wide.region_17.18_spmd.clone, body=%wide.region_13.17_spmd.clone.sunk | while | flops 682903680 | bytes 75328352 | solution.py:153
  181.7 2.1 gather_fusion.11
  183.8 2.2 gather_fusion.6
  186.0 3.0 copy.148
  189.0 3.8 %gather_fusion.10 = bf16[8,128,8,64]{3,2,1,0:T(8,128)(2,1)} fusion(bf16[8,128,8,64]{3,2,1,0:T(8,128)(2,1)} %get-tuple-element.1714, s32[1024]{0:T(1024)S(1)} %get-tuple-element.1580), kind=kCustom, calls=%fused_computation.10.clone.clone.1 | custom fusion | bytes 2097184 | tf_op jit(solution)/shard_map/while/body/gather | solution.py:118
  192.8 3.0 copy.151
  195.8 3.8 %gather_fusion.7 = bf16[8,128,8,64]{3,2,1,0:T(8,128)(2,1)} fusion(bf16[8,128,8,64]{3,2,1,0:T(8,128)(2,1)} %get-tuple-element.1711, s32[1024]{0:T(1024)S(1)} %get-tuple-element.1580), kind=kCustom, calls=%fused_computation.7.clone.clone.1 | custom fusion | bytes 2097184 | tf_op jit(solution)/shard_map/while/body/gather | solution.py:67
  199.6 3.0 copy.149
  202.6 4.7 %exponential_divide_fusion.2 = f32[8,8,128,128]{3,2,1,0:T(8,128)S(1)} fusion(bf16[8,128,8,64]{1,3,2,0:T(8,128)(2,1)} %copy.149, bf16[8,128,8,64]{1,3,2,0:T(8,128)(2,1)} %copy.148, f32[8,8,128]{2,1,0:T(8,128)S(1)} %gather_fusion.8, f32[8,8,128]{2,1,0:T(8,128)S(1)} %gather_fusion.9, pred[8,128,128]{2,1,0:T(8,128)(4,1)S(1)} %copy.150), kind=kOutput, calls=%fused_computation.70.clone.1 | convolution fusion | flops 138412032 | bytes 6488064 | tf_op jit(solution)/shard_map/while/body/gqhd,gkhd->ghqk/dot_general | solution.py:65
  207.3 3.3 multiply_convert_fusion.2
  210.6 2.1 fusion.119
  212.6 4.8 %scatter_fusion.5 = f32[4,128,8,64]{1,3,2,0:T(8,128)} fusion(f32[4,128,8,64]{1,3,2,0:T(8,128)} %get-tuple-element.1684, s32[8]{0:T(128)S(1)} %get-tuple-element.1578, f32[8,128,8,64]{1,3,2,0:T(8,128)} %fusion.119), kind=kCustom, calls=%fused_computation.19.clone.clone.1 | custom fusion | flops 524288 | bytes 6291488 | tf_op jit(solution)/shard_map/while/body/scatter-add | solution.py:119
  217.4 4.0 %convolution_bitcast_fusion.5 = f32[8,128,8,64]{1,3,2,0:T(8,128)} fusion(bf16[8,128,8,64]{1,3,2,0:T(8,128)(2,1)} %copy.149, bf16[8,8,128,128]{3,2,1,0:T(8,128)(2,1)} %multiply_convert_fusion.2), kind=kOutput, calls=%fused_computation.75.clone.1 | convolution fusion | flops 134217728 | bytes 5242880 | tf_op jit(solution)/shard_map/while/body/ghqk,gqhd->gkhd/dot_general | solution.py:139
  221.4 4.8 %scatter_fusion.4 = f32[4,128,8,64]{1,3,2,0:T(8,128)} fusion(f32[4,128,8,64]{1,3,2,0:T(8,128)} %get-tuple-element.1683, s32[8]{0:T(128)S(1)} %get-tuple-element.1578, f32[8,128,8,64]{1,3,2,0:T(8,128)} %convolution_bitcast_fusion.5), kind=kCustom, calls=%fused_computation.18.clone.clone.1 | custom fusion | flops 524288 | bytes 6291488 | tf_op jit(solution)/shard_map/while/body/scatter-add | solution.py:138
  226.2 4.8 %convolution_bitcast_fusion.4 = f32[8,128,8,64]{1,3,2,0:T(8,128)} fusion(bf16[8,128,8,64]{1,3,2,0:T(8,128)(2,1)} %copy.148, bf16[8,8,128,128]{3,2,1,0:T(8,128)(2,1)} %multiply_convert_fusion.2), kind=kOutput, calls=%fused_computation.76.clone.1 | convolution fusion | flops 134217728 | bytes 5242880 | tf_op jit(solution)/shard_map/while/body/ghqk,gkhd->gqhd/dot_general | solution.py:134
  231.0 4.9 %scatter_fusion.3 = f32[8,128,8,64]{1,3,2,0:T(8,128)} fusion(f32[8,128,8,64]{1,3,2,0:T(8,128)} %get-tuple-element.1682, s32[8]{0:T(128)S(1)} %get-tuple-element.1577, f32[8,128,8,64]{1,3,2,0:T(8,128)} %convolution_bitcast_fusion.4), kind=kCustom, calls=%fused_computation.17.clone.clone.1 | custom fusion | flops 524288 | bytes 6291488 | tf_op jit(solution)/shard_map/while/body/scatter-add | solution.py:133
  236.0 2.8 copy.90
  238.8 1.8 copy.127
  240.9 0.9 copy-done.5
  242.5 1.1 copy.130
  244.1 0.7 copy.92
  244.8 1.1 copy.129
  246.7 0.8 copy.93
  247.5 28.7 %reduce-scatter.4.cloned.1.call-done = f32[128,512]{0,1:T(8,128)} async-done(((f32[1024,512]{0,1:T(8,128)}), f32[128,512]{0,1:T(8,128)}) %reduce-scatter.4.cloned.1.call-update) | async-done | bytes 262160 | tf_op jit(solution)/shard_map/reduce_scatter | solution.py:154
  276.2 1.3 fusion.54
  277.5 27.8 %reduce-scatter.6.cloned.1.call-done = f32[128,512]{0,1:T(8,128)} async-done(((f32[512,512]{0,1:T(8,128)}), f32[128,512]{0,1:T(8,128)}) %reduce-scatter.6.cloned.1.call-update) | async-done | bytes 262160 | tf_op jit(solution)/shard_map/reduce_scatter | solution.py:161
  305.3 1.3 convolution_add_fusion.1
  306.6 29.5 %reduce-scatter.8.cloned.1.call-done = f32[128,512]{0,1:T(8,128)} async-done(((f32[512,512]{0,1:T(8,128)}), f32[128,512]{0,1:T(8,128)}) %reduce-scatter.8.cloned.1.call-update) | async-done | bytes 262160 | tf_op jit(solution)/shard_map/reduce_scatter | solution.py:167
  336.1 1.9 fusion.51
  (69 shorter events, 9.4 us)
Async XLA Ops:
  7.2 1.0 copy-start
  7.2 32.6 %all-gather.3.cloned.1.call-start = ((), (), s32[]{:S(2)}) async-start(), calls=%async_computation.3 | async-start | bytes 1179648 | tf_op jit(solution)/shard_map/all_gather | solution.py:34
  10.0 99.2 %all-gather.5.cloned.1.call-start = ((), (), s32[]{:S(2)}) async-start(), calls=%async_computation.5 | async-start | bytes 1179648 | tf_op jit(solution)/shard_map/all_gather | solution.py:35
  10.8 160.7 %all-reduce.2.cloned.1.call-start = ((), (), s32[]{:S(2)}) async-start(), calls=%async_computation.4 | async-start | bytes 4194304 | tf_op jit(solution)/shard_map/psum | solution.py:103
  92.7 4.2 %copy-start.3 = (bf16[8,128,8,64]{3,2,1,0:T(8,128)(2,1)S(1)}, bf16[8,128,8,64]{3,2,1,0:T(8,128)(2,1)}, u32[]{:S(2)}) copy-start(bf16[8,128,8,64]{3,2,1,0:T(8,128)(2,1)} %gather_fusion.5) | copy-start | bytes 3145732 | tf_op jit(solution)/shard_map/while
  109.1 167.1 %reduce-scatter.4.cloned.1.call-start = ((), (), s32[]{:S(2)}) async-start(), calls=%async_computation.6 | async-start | bytes 2359296 | tf_op jit(solution)/shard_map/reduce_scatter | solution.py:154
  202.6 4.7 %copy-start.1 = (bf16[8,128,8,64]{1,3,2,0:T(8,128)(2,1)S(1)}, bf16[8,128,8,64]{1,3,2,0:T(8,128)(2,1)}, u32[]{:S(2)}) copy-start(bf16[8,128,8,64]{1,3,2,0:T(8,128)(2,1)} %copy.151) | copy-start | bytes 3145732 | tf_op jit(solution)/shard_map/while
  202.6 4.7 %copy-start.2 = (bf16[8,128,8,64]{3,2,1,0:T(8,128)(2,1)S(1)}, bf16[8,128,8,64]{3,2,1,0:T(8,128)(2,1)}, u32[]{:S(2)}) copy-start(bf16[8,128,8,64]{3,2,1,0:T(8,128)(2,1)} %gather_fusion.11) | copy-start | bytes 3145732 | tf_op jit(solution)/shard_map/while
  240.6 1.2 copy-start.5
  240.6 64.7 %reduce-scatter.6.cloned.1.call-start = ((), (), s32[]{:S(2)}) async-start(), calls=%async_computation.7 | async-start | bytes 1310720 | tf_op jit(solution)/shard_map/reduce_scatter | solution.py:161
  242.5 1.6 copy-start.4
  243.6 92.5 %reduce-scatter.8.cloned.1.call-start = ((), (), s32[]{:S(2)}) async-start(), calls=%async_computation.8 | async-start | bytes 1310720 | tf_op jit(solution)/shard_map/reduce_scatter | solution.py:167
  244.8 1.6 copy-start.6
  245.8 59.5 %copy-start.7 = (bf16[512,512]{1,0:T(8,128)(2,1)S(1)}, bf16[512,512]{1,0:T(8,128)(2,1)}, u32[]{:S(2)}) copy-start(bf16[512,512]{1,0:T(8,128)(2,1)} %param.17) | copy-start | bytes 1572868
  246.4 89.7 %copy-start.8 = (bf16[512,512]{1,0:T(8,128)(2,1)S(1)}, bf16[512,512]{1,0:T(8,128)(2,1)}, u32[]{:S(2)}) copy-start(bf16[512,512]{1,0:T(8,128)(2,1)} %param.18) | copy-start | bytes 1572868
Sparse Core Ops, SparseCore 0:
  10.2 24.7 all-gather.2
  36.6 21.7 all-gather.4
  109.2 62.2 all-reduce.1
  240.7 35.4 reduce-scatter.3
  279.0 26.3 reduce-scatter.5
  308.3 27.7 reduce-scatter.7
where the time goes:
time: 346 us; the launch traced here: 345 us
  waiting for transfers between devices  114 us (33%)
  local copies, waits for them, and re-layouts  75.2 us (22%)
  blocking collectives  74.7 us (22%)
  matrix products  38.1 us (11%)
  other arithmetic  27.3 us (8%)
  between operations  14.9 us (4%)
    reduce_scatter x1, waiting for transfers between devices, local(): lax.psum_scatter(grad_value.reshape(key_count * block_size, model_width),...  29.5 us
    reduce_scatter x1, waiting for transfers between devices, local(): lax.psum_scatter(grad_query.reshape(query_count * block_size, model_width...  28.7 us
    reduce_scatter x1, waiting for transfers between devices, local(): lax.psum_scatter(grad_key.reshape(key_count * block_size, model_width), '...  27.8 us
    psum x1, waiting for transfers between devices, local(): weighted_all, totals_all = lax.psum((weighted, totals), 'blk')  27.1 us
    psum x1, blocking collectives, local(): weighted_all, totals_all = lax.psum((weighted, totals), 'blk')  26.5 us
    pmax x1, blocking collectives, local(): row_max = lax.pmax(local_max, 'blk')  26 us
    unnamed x21, local copies, waits for them, and re-layouts  15 us
    gather x4, local copies, waits for them, and re-layouts, tile_scores(): query_tiles[query_blk]  14.3 us
  transfers between devices with their start and end apart: 6, of which 4 were waited for; matrix products, arithmetic and copies ran while one was open for 19% of the time, Pallas kernels for 0%

commit v1 on v0

v1 whole, which is shorter than its diff:
```python
import functools

import jax
import jax.numpy as jnp
from jax import lax
from jax.experimental import pallas as pl
from jax.experimental.pallas import tpu as pltpu
from jax.sharding import PartitionSpec as P

HEADS = 8
NEG_FILL = -1e30
NT = (((1,), (1,)), ((), ()))
NN = (((1,), (0,)), ((), ()))
EXTRA = 16
VMEM_LIMIT = 48 * 1024 * 1024


def dot(a, b, dims=NN):
    return lax.dot_general(a, b, dims, preferred_element_type=jnp.float32)


def pair_stack(rows):
    lane = lax.broadcasted_iota(jnp.int32, rows.shape, 1)
    half = rows.shape[1] // 2
    zero = jnp.zeros_like(rows)
    return jnp.concatenate([jnp.where(lane < half, rows, zero), jnp.where(lane >= half, rows, zero)], 0)


def tile_bias(mask_ref, pattern, diag):
    words = mask_ref[pattern]
    count, size = words.shape
    keys = lax.broadcasted_iota(jnp.int32, (size, size), 0)
    queries = lax.broadcasted_iota(jnp.int32, (size, size), 1)
    spread = jnp.concatenate(
        [jnp.broadcast_to(words[g : g + 1], (size // count, size)) for g in range(count)], 0
    )
    bits = jnp.right_shift(spread, keys & 31) & 1
    same = keys - queries == jnp.where(diag, 0, 2 * size)
    return jnp.where((bits == 1) | same, 0.0, NEG_FILL)


def list_tiles(coords_ref, counts_ref, list_ref, first, step, lists, cap, column, own):
    def one_list(index, found):
        owner = first + step * index

        def one_slot(slot, found):
            base = (owner * cap + slot) * 3
            other = coords_ref[base + 1 - column]
            list_ref[found * 2] = other * lists + index if column == 0 else index * step + other
            list_ref[found * 2 + 1] = coords_ref[base + 2]
            return found + jnp.where(coords_ref[base + column] == own, 1, 0)

        return lax.fori_loop(0, counts_ref[owner], one_slot, found)

    return lax.fori_loop(0, lists, one_list, 0)


def stream_tiles(total, list_ref, sources, buffers, sems, body):
    def copies(index):
        block = list_ref[index * 2]
        slot = lax.rem(index, 2)
        return [
            pltpu.make_async_copy(
                src.at[block, pl.ds(0, buf.shape[1])], buf.at[slot], sems.at[slot, which]
            )
            for which, (src, buf) in enumerate(zip(sources, buffers))
        ]

    @pl.when(total > 0)
    def _():
        for copy in copies(0):
            copy.start()

    def step(index, carry):
        @pl.when(index + 1 < total)
        def _():
            for copy in copies(index + 1):
                copy.start()

        for copy in copies(index):
            copy.wait()
        body(lax.rem(index, 2), list_ref[index * 2], list_ref[index * 2 + 1])
        return carry

    lax.fori_loop(0, total, step, 0)


def forward_kernel(
    sizes, coords_ref, counts_ref, own_ref, cot_ref, wq_ref, wk_ref, wvt_ref, mask_ref, all_ref,
    out_ref, stats_ref, list_ref, buf_ref, bias_ref, max_ref, sum_ref, acc_ref, sems,
):
    readers, blks, cap = sizes
    reader, blk = lax.axis_index("reader"), lax.axis_index("blk")
    me = reader * blks + blk
    total = list_tiles(coords_ref, counts_ref, list_ref, reader * blks, 1, blks, cap, 0, blk)
    block, width = own_ref.shape
    head = width // HEADS
    queries = dot(own_ref[...], wq_ref[...]).astype(jnp.bfloat16) * jnp.bfloat16(head**-0.5)
    stacks = [pair_stack(queries[:, 2 * head * p : 2 * head * (p + 1)]) for p in range(HEADS // 2)]
    max_ref[...] = jnp.full(max_ref.shape, NEG_FILL, jnp.float32)
    sum_ref[...] = jnp.zeros(sum_ref.shape, jnp.float32)
    acc_ref[...] = jnp.zeros(acc_ref.shape, jnp.float32)

    def tile(slot, other, pattern):
        rows = buf_ref[slot]
        keys = dot(rows, wk_ref[...]).astype(jnp.bfloat16)
        values = dot(wvt_ref[...], rows, NT).astype(jnp.bfloat16)
        bias_ref[...] = tile_bias(mask_ref, pattern, other == me)
        for p in range(HEADS // 2):
            scores = dot(keys[:, 2 * head * p : 2 * head * (p + 1)], stacks[p], NT)
            for e in range(2):
                h = 2 * p + e
                s = scores[:, block * e : block * (e + 1)] + bias_ref[...]
                old = max_ref[h : h + 1]
                new = jnp.maximum(old, jnp.max(s, axis=0, keepdims=True))
                fade = jnp.exp(old - new)
                expo = jnp.exp(s - new)
                max_ref[h : h + 1] = new
                sum_ref[h : h + 1] = sum_ref[h : h + 1] * fade + jnp.sum(expo, axis=0, keepdims=True)
                at = slice(head * h, head * (h + 1))
                acc_ref[at] = acc_ref[at] * fade + dot(values[at], expo.astype(jnp.bfloat16))

    stream_tiles(total, list_ref, [all_ref], [buf_ref], sems, tile)
    inverse = 1.0 / sum_ref[...]
    cot = cot_ref[...].astype(jnp.float32).T
    stats_ref[0:HEADS] = max_ref[...]
    stats_ref[HEADS : 2 * HEADS] = inverse
    for h in range(HEADS):
        at = slice(head * h, head * (h + 1))
        outputs = acc_ref[at] * inverse[h : h + 1]
        acc_ref[at] = outputs
        stats_ref[2 * HEADS + h : 2 * HEADS + h + 1] = jnp.sum(outputs * cot[at], axis=0, keepdims=True)
    out_ref[...] = acc_ref[...].T.astype(out_ref.dtype)


def tile_grads(scores, d_probs, bias, stats, block, p):
    probs, d_scores = [], []
    for e in range(2):
        h = 2 * p + e
        at = slice(block * e, block * (e + 1))
        prob = jnp.exp(scores[:, at] + bias - stats[h : h + 1]) * stats[HEADS + h : HEADS + h + 1]
        probs.append(prob.astype(jnp.bfloat16))
        d_scores.append((prob * (d_probs[:, at] - stats[2 * HEADS + h : 2 * HEADS + h + 1])).astype(jnp.bfloat16))
    return probs, d_scores


def query_grad_kernel(
    sizes, coords_ref, counts_ref, own_ref, cot_ref, wq_ref, wk_ref, wkt_ref, wv_ref, mask_ref, stats_ref, all_ref,
    out_ref, list_ref, buf_ref, bias_ref, acc_ref, sems,
):
    readers, blks, cap = sizes
    reader, blk = lax.axis_index("reader"), lax.axis_index("blk")
    me = reader * blks + blk
    total = list_tiles(coords_ref, counts_ref, list_ref, reader * blks, 1, blks, cap, 0, blk)
    block, width = own_ref.shape
    head = width // HEADS
    queries = dot(own_ref[...], wq_ref[...]).astype(jnp.bfloat16) * jnp.bfloat16(head**-0.5)
    pairs = [slice(2 * head * p, 2 * head * (p + 1)) for p in range(HEADS // 2)]
    query_stacks = [pair_stack(queries[:, pair]) for pair in pairs]
    cot_stacks = [pair_stack(cot_ref[:, pair]) for pair in pairs]
    acc_ref[...] = jnp.zeros(acc_ref.shape, jnp.float32)

    def tile(slot, other, pattern):
        rows = buf_ref[slot]
        keys = dot(rows, wk_ref[...]).astype(jnp.bfloat16)
        keys_t = dot(wkt_ref[...], rows, NT).astype(jnp.bfloat16)
        values = dot(rows, wv_ref[...]).astype(jnp.bfloat16)
        bias_ref[...] = tile_bias(mask_ref, pattern, other == me)
        for p, pair in enumerate(pairs):
            scores = dot(keys[:, pair], query_stacks[p], NT)
            d_probs = dot(values[:, pair], cot_stacks[p], NT)
            _, d_scores = tile_grads(scores, d_probs, bias_ref[...], stats_ref, block, p)
            for e in range(2):
                at = slice(head * (2 * p + e), head * (2 * p + e + 1))
                acc_ref[at] += dot(keys_t[at], d_scores[e])

    stream_tiles(total, list_ref, [all_ref], [buf_ref], sems, tile)
    grad = (acc_ref[...].T * (head**-0.5)).astype(jnp.bfloat16)
    out_ref[...] = dot(grad, wq_ref[...], NT)


def key_grad_kernel(
    sizes, coords_ref, counts_ref, own_ref, wq_ref, wk_ref, wv_ref, mask_ref, part_ref, all_ref, cots_ref, stats_all_ref,
    out_ref, list_ref, buf_ref, cot_buf_ref, stats_buf_ref, bias_ref, key_acc_ref, value_acc_ref, sems,
):
    readers, blks, cap = sizes
    reader, blk = lax.axis_index("reader"), lax.axis_index("blk")
    me = reader * blks + blk
    total = list_tiles(coords_ref, counts_ref, list_ref, blk, blks, readers, cap, 1, reader)
    block, width = own_ref.shape
    head = width // HEADS
    pairs = [slice(2 * head * p, 2 * head * (p + 1)) for p in range(HEADS // 2)]
    keys = dot(own_ref[...], wk_ref[...]).astype(jnp.bfloat16)
    values = dot(own_ref[...], wv_ref[...]).astype(jnp.bfloat16)
    key_acc_ref[...] = jnp.zeros(key_acc_ref.shape, jnp.float32)
    value_acc_ref[...] = jnp.zeros(value_acc_ref.shape, jnp.float32)

    def tile(slot, other, pattern):
        queries = dot(buf_ref[slot], wq_ref[...]).astype(jnp.bfloat16) * jnp.bfloat16(head**-0.5)
        cot = cot_buf_ref[slot]
        stats = stats_buf_ref[slot]
        bias_ref[...] = tile_bias(mask_ref, pattern, other == me)
        for p, pair in enumerate(pairs):
            query_stack = pair_stack(queries[:, pair])
            cot_stack = pair_stack(cot[:, pair])
            scores = dot(keys[:, pair], query_stack, NT)
            d_probs = dot(values[:, pair], cot_stack, NT)
            probs, d_scores = tile_grads(scores, d_probs, bias_ref[...], stats, block, p)
            value_acc_ref[:, pair] += dot(jnp.concatenate(probs, 1), cot_stack)
            key_acc_ref[:, pair] += dot(jnp.concatenate(d_scores, 1), query_stack)

    stream_tiles(
        total, list_ref, [all_ref, cots_ref, stats_all_ref], [buf_ref, cot_buf_ref, stats_buf_ref], sems, tile
    )
    grad = part_ref[...] + dot(key_acc_ref[...].astype(jnp.bfloat16), wk_ref[...], NT)
    grad = grad + dot(value_acc_ref[...].astype(jnp.bfloat16), wv_ref[...], NT)
    out_ref[...] = grad.astype(out_ref.dtype)


VMEM = pl.BlockSpec(memory_space=pltpu.VMEM)
SMEM = pl.BlockSpec(memory_space=pltpu.SMEM)
ANY = pl.BlockSpec(memory_space=pl.ANY)


def local(features, cotangent, w_query, w_key, w_value, tile_coords, tile_count, mask_table):
    block, width = features.shape
    assert block == mask_table.shape[1]
    readers, blks, cap = lax.axis_size("reader"), lax.axis_size("blk"), tile_coords.shape[2]
    devices = readers * blks
    sizes = (readers, blks, cap)
    f32, bf16, i32 = jnp.float32, jnp.bfloat16, jnp.int32
    masks = mask_table.transpose(0, 2, 1)
    axes = ("reader", "blk")

    listing = jnp.concatenate([tile_coords.reshape(-1), tile_count.reshape(-1)]).astype(bf16)
    listing = jnp.pad(listing, (0, EXTRA * width - listing.shape[0])).reshape(EXTRA, width)
    packed = jnp.concatenate([features, listing], 0)
    rows_all = lax.all_gather(packed[None], axes, axis=0, tiled=True)
    cots_all = lax.all_gather(cotangent[None], axes, axis=0, tiled=True)
    numbers = rows_all[:, block, : 3 * cap + 1].astype(i32)
    coords = numbers[:, : 3 * cap].reshape(-1)
    counts = numbers[:, 3 * cap]

    params = pltpu.CompilerParams(vmem_limit_bytes=VMEM_LIMIT)
    list_space = pltpu.SMEM((2 * (devices * cap + 1),), i32)
    buffer = pltpu.VMEM((2, block, width), bf16)
    bias = pltpu.VMEM((block, block), f32)

    def cost(tiles):
        return pl.CostEstimate(flops=tiles * 200_000_000, bytes_accessed=4_000_000, transcendentals=tiles * 131072)

    attn_out, stats = pl.pallas_call(
        functools.partial(forward_kernel, sizes),
        out_shape=(
            jax.ShapeDtypeStruct((block, width), bf16),
            jax.ShapeDtypeStruct((3 * HEADS, block), f32),
        ),
        in_specs=[SMEM, SMEM, VMEM, VMEM, VMEM, VMEM, VMEM, VMEM, ANY],
        out_specs=(VMEM, VMEM),
        scratch_shapes=[
            list_space, buffer, bias,
            pltpu.VMEM((HEADS, block), f32), pltpu.VMEM((HEADS, block), f32), pltpu.VMEM((width, block), f32),
            pltpu.SemaphoreType.DMA((2, 1)),
        ],
        compiler_params=params,
        cost_estimate=cost(5),
        name="forward",
    )(coords, counts, features, cotangent, w_query, w_key, w_value.T, masks, rows_all)

    stats_all = lax.all_gather(stats[None], axes, axis=0, tiled=True)

    query_part = pl.pallas_call(
        functools.partial(query_grad_kernel, sizes),
        out_shape=jax.ShapeDtypeStruct((block, width), f32),
        in_specs=[SMEM, SMEM] + [VMEM] * 8 + [ANY],
        out_specs=VMEM,
        scratch_shapes=[
            list_space, buffer, bias, pltpu.VMEM((width, block), f32), pltpu.SemaphoreType.DMA((2, 1)),
        ],
        compiler_params=params,
        cost_estimate=cost(5),
        name="query_grad",
    )(coords, counts, features, cotangent, w_query, w_key, w_key.T, w_value, masks, stats, rows_all)

    grad_features = pl.pallas_call(
        functools.partial(key_grad_kernel, sizes),
        out_shape=jax.ShapeDtypeStruct((block, width), bf16),
        in_specs=[SMEM, SMEM] + [VMEM] * 6 + [ANY] * 3,
        out_specs=VMEM,
        scratch_shapes=[
            list_space, buffer, buffer, pltpu.VMEM((2, 3 * HEADS, block), f32), bias,
            pltpu.VMEM((block, width), f32), pltpu.VMEM((block, width), f32), pltpu.SemaphoreType.DMA((2, 3)),
        ],
        compiler_params=params,
        cost_estimate=cost(5),
        name="key_grad",
    )(coords, counts, features, w_query, w_key, w_value, masks, query_part, rows_all, cots_all, stats_all)
    return attn_out, grad_features


def solution(mesh):
    return jax.shard_map(
        local,
        mesh=mesh,
        in_specs=(
            P(("reader", "blk"), None),
            P(("reader", "blk"), None),
            P(),
            P(),
            P(),
            P("reader", "blk", None, None),
            P("reader", "blk"),
            P(),
        ),
        out_specs=(P(("reader", "blk"), None), P(("reader", "blk"), None)),
        check_vma=False,
    )
```

time: 346 us -> 157 us (0.45)
  local copies, waits for them, and re-layouts: 75.2 us -> 7.93 us
  waiting for transfers between devices: 114 us -> 66.7 us
  matrix products: 38.1 us -> 0 us
  blocking collectives: 74.7 us -> 45.7 us
  other arithmetic: 27.3 us -> 3.2 us
  Pallas kernels: 0 us -> 16.3 us
    reduce_scatter x3 -> x0, waiting for transfers between devices: 86.1 us -> none  [the longest x1 29.5 us: local(): lax.psum_scatter(grad_value.reshape(key_count * block_size, model_width),...]
    all_gather x2, waiting for transfers between devices: 0.04 us -> 66 us  [the longest x1 63.7 us: local(): rows_all = lax.all_gather(packed[None], axes, axis=0, tiled=True)]
    gather x17 -> x0, local copies, waits for them, and re-layouts: 38.6 us -> none  [the longest x4 14.3 us: tile_scores(): query_tiles[query_blk]]
    dot_general x14 -> x0, matrix products: 38.1 us -> none  [the longest x3 12.6 us: tile_scores(): jnp.einsum('gqhd,gkhd->ghqk', query_tiles[query_blk], key_tiles[key_blk],...]
    psum x1 -> x0, waiting for transfers between devices: 27.1 us -> none  [local(): weighted_all, totals_all = lax.psum((weighted, totals), 'blk')]
    psum x1 -> x0, blocking collectives: 26.5 us -> none  [local(): weighted_all, totals_all = lax.psum((weighted, totals), 'blk')]
    pmax x1 -> x0, blocking collectives: 26 us -> none  [local(): row_max = lax.pmax(local_max, 'blk')]
    all_gather x2 -> x1, blocking collectives: 22.1 us -> 45.7 us  [local(): stats_all = lax.all_gather(stats[None], axes, axis=0, tiled=True)]
  transfers between devices with their start and end apart: 6 -> 2, of which waited for: 4 -> 2; matrix products, arithmetic and copies ran while one was open for 19% -> 2% of each run, Pallas kernels for 0% -> 6%
where the time goes in v1:
time: 157 us; the launch traced here: 155 us
  waiting for transfers between devices  66.7 us (42%)
  blocking collectives  45.7 us (29%)
  Pallas kernels  16.3 us (10%)
  between operations  14.8 us (9%)
  local copies, waits for them, and re-layouts  7.93 us (5%)
  other arithmetic  3.2 us (2%)
    all_gather x1, waiting for transfers between devices, local(): rows_all = lax.all_gather(packed[None], axes, axis=0, tiled=True)  63.7 us
    all_gather x1, blocking collectives, local(): stats_all = lax.all_gather(stats[None], axes, axis=0, tiled=True)  45.7 us
    unnamed x22, local copies, waits for them, and re-layouts  7.46 us
    pallas_call x1, Pallas kernels, local(): pl.pallas_call(functools.partial(key_grad_kernel, sizes), out_shape=jax.S...  6.31 us
    pallas_call x1, Pallas kernels, local(): pl.pallas_call(functools.partial(forward_kernel, sizes), out_shape=(jax.S...  5.21 us
    pallas_call x1, Pallas kernels, local(): pl.pallas_call(functools.partial(query_grad_kernel, sizes), out_shape=jax...  4.8 us
  transfers between devices with their start and end apart: 2, of which 2 were waited for; matrix products, arithmetic and copies ran while one was open for 2% of the time, Pallas kernels for 6%

profile of v1, /device:TPU:0, one launch (start us, length us, event | category | flops | bytes accessed | tf_op | source)
XLA Modules:
  0.0 154.8 jit_solution(4930941737140695164)
XLA Ops:
  7.2 0.0 all-gather.6.cloned.1.call-start
  7.9 0.7 convert.9
  8.5 0.1 copy.13
  8.6 0.1 reshape.20
  8.7 0.1 fusion.2
  8.8 1.6 %pad_maximum_fusion = bf16[144,512]{1,0:T(8,128)(2,1)} fusion(bf16[16,512]{1,0:T(8,128)(2,1)S(1)} %reshape.22, bf16[128,512]{1,0:T(8,128)(2,1)} %own_ref.5), kind=kLoop, calls=%fused_computation | loop fusion | flops 294912 | bytes 294912 | tf_op jit(solution)/shard_map/concatenate | solution.py:237
  10.4 0.0 copy-start.4
  10.4 0.0 copy-start.6
  10.4 0.0 all-gather.6.cloned.1.call-update
  10.5 0.0 all-gather.8.cloned.1.call-start
  10.5 0.7 all-gather.8.cloned.1.call-update
  11.2 1.3 copy.14
  12.5 1.3 copy.15
  13.7 63.7 %all-gather.6.cloned.1.call-done = bf16[4608,512]{1,0:T(8,128)(2,1)} async-done(((bf16[144,512]{1,0:T(8,128)(2,1)}), bf16[4608,512]{1,0:T(8,128)(2,1)}) %all-gather.6.cloned.1.call-update) | async-done | bytes 4718608 | tf_op jit(solution)/shard_map/all_gather | solution.py:238
  77.4 0.9 slice_convert_fusion
  78.3 0.1 reshape.23.coords_ref
  78.4 0.2 slice_reduce_fusion.counts_ref
  78.5 0.0 copy-start
  78.5 1.0 copy-done
  79.6 0.0 copy-start.2
  79.6 1.0 copy-done.2
  80.6 0.0 copy-start.5
  80.6 1.0 copy-done.5
  81.7 0.0 copy-start.7
  81.7 0.9 copy-done.7
  82.6 0.0 copy-start.9
  82.6 0.9 copy-done.9
  83.5 5.2 %forward.1 = (bf16[128,512]{1,0:T(8,128)(2,1)}, f32[24,128]{1,0:T(8,128)S(1)}) custom-call(s32[768]{0:T(1024)S(1)} %reshape.23.coords_ref, s32[32]{0:T(128)S(1)} %slice_reduce_fusion.counts_ref, bf16[128,512]{1,0:T(8,128)(2,1)S(1)} %copy-done.7, bf16[128,512]{1,0:T(8,128)(2,1)S(1)} %copy-done.9, bf16[512,512]{1,0:T(8,128)(2,1)S(1)} %copy-done.2, ...), custom_call_target="tpu_custom_call" | custom-call | flops 1000000000 | bytes 4000000 | tf_op jit(solution)/shard_map/forward/pallas_call | solution.py:252
  88.7 0.0 copy-start.1
  88.7 0.0 copy-start.3
  88.7 0.0 copy-start.8
  88.7 0.0 copy-done.4
  88.7 0.0 copy-done.6
  88.7 4.8 %query_grad.1.part_ref = f32[128,512]{1,0:T(8,128)S(1)} custom-call(s32[768]{0:T(1024)S(1)} %reshape.23.coords_ref, s32[32]{0:T(128)S(1)} %slice_reduce_fusion.counts_ref, bf16[128,512]{1,0:T(8,128)(2,1)S(1)} %copy-done.7, bf16[128,512]{1,0:T(8,128)(2,1)S(1)} %copy-done.9, bf16[512,512]{1,0:T(8,128)(2,1)S(1)} %copy-done.2, bf16[512,512]{1,0:T(8,128)(2,1)S(1)} %copy-done, ...), custom_call_target="tpu_custom_call" | custom-call | flops 1000000000 | bytes 4000000 | tf_op jit(solution)/shard_map/query_grad/pallas_call | solution.py:272
  93.6 45.7 %all-gather.2 = f32[768,128]{1,0:T(8,128)S(1)} all-gather(f32[24,128]{1,0:T(8,128)S(1)} %get-tuple-element.5.stats_ref), channel_id=4, replica_groups=mesh['reader'=4,'blk'=8] {'reader','blk'}, dimensions={0}, use_global_device_ids=true | all-gather | bytes 405504 | tf_op jit(solution)/shard_map/all_gather | solution.py:270
  139.3 2.3 %all-gather.8.cloned.1.call-done = bf16[4096,512]{1,0:T(8,128)(2,1)} async-done(((bf16[128,512]{1,0:T(8,128)(2,1)}), bf16[4096,512]{1,0:T(8,128)(2,1)}) %all-gather.8.cloned.1.call-update) | async-done | bytes 4194320 | tf_op jit(solution)/shard_map/all_gather | solution.py:239
  141.6 0.0 copy-done.1
  141.6 0.0 copy-done.3
  141.6 0.0 copy-done.8
  141.6 6.3 %key_grad.1 = bf16[128,512]{1,0:T(8,128)(2,1)} custom-call(s32[768]{0:T(1024)S(1)} %reshape.23.coords_ref, s32[32]{0:T(128)S(1)} %slice_reduce_fusion.counts_ref, bf16[128,512]{1,0:T(8,128)(2,1)S(1)} %copy-done.8, bf16[512,512]{1,0:T(8,128)(2,1)S(1)} %copy-done.3, bf16[512,512]{1,0:T(8,128)(2,1)S(1)} %copy-done.1, bf16[512,512]{1,0:T(8,128)(2,1)S(1)} %copy-done.4, ...), custom_call_target="tpu_custom_call" | custom-call | flops 1000000000 | bytes 4000000 | tf_op jit(solution)/shard_map/key_grad/pallas_call | solution.py:285
  (1 shorter events, 0.0 us)
Async XLA Ops:
  7.2 70.3 %all-gather.6.cloned.1.call-start = ((), (), s32[]{:S(2)}) async-start(), calls=%async_computation | async-start | bytes 4866048 | tf_op jit(solution)/shard_map/all_gather | solution.py:238
  10.4 78.3 %copy-start.4 = (bf16[512,512]{1,0:T(8,128)(2,1)S(1)}, bf16[512,512]{1,0:T(8,128)(2,1)}, u32[]{:S(2)}) copy-start(bf16[512,512]{1,0:T(8,128)(2,1)} %wv_ref.3) | copy-start | bytes 1572868
  10.4 78.3 %copy-start.6 = (s32[240,128,4]{1,2,0:T(4,128)S(1)}, s32[240,128,4]{1,2,0:T(4,128)}, u32[]{:S(2)}) copy-start(s32[240,128,4]{1,2,0:T(4,128)} %param.15) | copy-start | bytes 1474564
  10.5 131.1 %all-gather.8.cloned.1.call-start = ((), (), s32[]{:S(2)}) async-start(), calls=%async_computation.1 | async-start | bytes 4325376 | tf_op jit(solution)/shard_map/all_gather | solution.py:239
  78.5 1.0 copy-start
  79.6 1.0 copy-start.2
  80.6 1.0 copy-start.5
  81.7 0.9 copy-start.7
  82.6 0.9 copy-start.9
  88.7 52.9 %copy-start.1 = (bf16[512,512]{1,0:T(8,128)(2,1)S(1)}, bf16[512,512]{1,0:T(8,128)(2,1)}, u32[]{:S(2)}) copy-start(bf16[512,512]{1,0:T(8,128)(2,1)} %wk_ref.5) | copy-start | bytes 1572868
  88.7 52.9 %copy-start.3 = (bf16[512,512]{1,0:T(8,128)(2,1)S(1)}, bf16[512,512]{1,0:T(8,128)(2,1)}, u32[]{:S(2)}) copy-start(bf16[512,512]{1,0:T(8,128)(2,1)} %wq_ref.5) | copy-start | bytes 1572868
  88.7 52.9 %copy-start.8 = (bf16[128,512]{1,0:T(8,128)(2,1)S(1)}, bf16[128,512]{1,0:T(8,128)(2,1)}, u32[]{:S(2)}) copy-start(bf16[128,512]{1,0:T(8,128)(2,1)} %own_ref.5) | copy-start | bytes 393220
Sparse Core Ops, SparseCore 0:
  11.0 66.3 all-gather.5
  80.4 61.1 all-gather.7

commit v2 on v1

--- a/solution.py
+++ b/solution.py
@@ -11,7 +11,6 @@
 NEG_FILL = -1e30
 NT = (((1,), (1,)), ((), ()))
 NN = (((1,), (0,)), ((), ()))
-EXTRA = 16
 VMEM_LIMIT = 48 * 1024 * 1024
 
 
@@ -39,60 +38,113 @@
     return jnp.where((bits == 1) | same, 0.0, NEG_FILL)
 
 
-def list_tiles(coords_ref, counts_ref, list_ref, first, step, lists, cap, column, own):
+def list_tiles(lists_ref, list_ref, count, own_list, column, own, block_of):
+    cap = (lists_ref.shape[1] - 1) // 3
+
     def one_list(index, found):
-        owner = first + step * index
-
         def one_slot(slot, found):
-            base = (owner * cap + slot) * 3
-            other = coords_ref[base + 1 - column]
-            list_ref[found * 2] = other * lists + index if column == 0 else index * step + other
-            list_ref[found * 2 + 1] = coords_ref[base + 2]
-            return found + jnp.where(coords_ref[base + column] == own, 1, 0)
-
-        return lax.fori_loop(0, counts_ref[owner], one_slot, found)
-
-    return lax.fori_loop(0, lists, one_list, 0)
-
-
-def stream_tiles(total, list_ref, sources, buffers, sems, body):
-    def copies(index):
+            list_ref[found * 2] = block_of(jnp.bitwise_xor(index, own_list), lists_ref[index, 3 * slot + 1 - column])
+            list_ref[found * 2 + 1] = lists_ref[index, 3 * slot + 2]
+            return found + jnp.where(lists_ref[index, 3 * slot + column] == own, 1, 0)
+
+        return lax.fori_loop(0, lists_ref[index, 3 * cap], one_slot, found)
+
+    return lax.fori_loop(0, count, one_list, 0)
+
+
+def stream_tiles(total, list_ref, sources, sems, body):
+    def copy_of(which, ref, where, slot):
+        _, _, buf, rows = sources[which]
+        return pltpu.make_async_copy(ref.at[where], buf.at[slot, rows], sems.at[slot, which])
+
+    def start(index):
         block = list_ref[index * 2]
         slot = lax.rem(index, 2)
-        return [
-            pltpu.make_async_copy(
-                src.at[block, pl.ds(0, buf.shape[1])], buf.at[slot], sems.at[slot, which]
-            )
-            for which, (src, buf) in enumerate(zip(sources, buffers))
-        ]
+        for which, (refs, place, _, _) in enumerate(sources):
+            group, where = place(block)
+            for g, ref in enumerate(refs):
+
+                @pl.when(group == g)
+                def _():
+                    copy_of(which, ref, where, slot).start()
 
     @pl.when(total > 0)
     def _():
-        for copy in copies(0):
-            copy.start()
+        start(0)
 
     def step(index, carry):
         @pl.when(index + 1 < total)
         def _():
-            for copy in copies(index + 1):
-                copy.start()
-
-        for copy in copies(index):
-            copy.wait()
-        body(lax.rem(index, 2), list_ref[index * 2], list_ref[index * 2 + 1])
+            start(index + 1)
+
+        slot = lax.rem(index, 2)
+        for which, (refs, _, _, _) in enumerate(sources):
+            copy_of(which, refs[0], 0, slot).wait()
+        body(slot, list_ref[index * 2], list_ref[index * 2 + 1])
         return carry
 
     lax.fori_loop(0, total, step, 0)
 
 
+def bits_of(size):
+    return size.bit_length() - 1
+
+
+def swap(block, mask):
+    axes = ("reader", "blk")
+    count = lax.axis_size("reader") * lax.axis_size("blk")
+    return lax.ppermute(block, axes, [(i, i ^ mask) for i in range(count)])
+
+
+def gather_line(block):
+    return jnp.concatenate([block] + [swap(block, 2 * k) for k in range(1, lax.axis_size("blk") // 2)], 0)
+
+
+def gather_plane(chunk, order):
+    blks = lax.axis_size("blk")
+    for bit in order[:-1]:
+        chunk = jnp.concatenate([chunk, swap(chunk, blks << bit)], 0)
+    return [chunk, swap(chunk, blks << order[-1])]
+
+
+def other_core(groups):
+    return groups + [swap(group, 1) for group in groups]
+
+
+def place_in(order, blks, me):
+    def place(block):
+        apart = jnp.bitwise_xor(block, me)
+        reader, blk = apart // blks, lax.rem(apart, blks)
+        where = blk // 2
+        for at, bit in enumerate(order[:-1]):
+            where = where + (jnp.right_shift(reader, bit) & 1) * ((blks // 2) << at)
+        return (jnp.right_shift(reader, order[-1]) & 1) + 2 * (blk & 1), where
+
+    return place
+
+
+def orders(readers):
+    rising = tuple(range(bits_of(readers)))
+    return rising, rising[::-1]
+
+
+def halves(groups, sizes, me, buffer):
+    readers, blks, _ = sizes
+    rows = buffer.shape[1] // 2
+    return [
+        (refs, place_in(order, blks, me), buffer, pl.ds(rows * k, rows))
+        for k, (refs, order) in enumerate(zip((groups[:4], groups[4:]), orders(readers)))
+    ]
+
+
 def forward_kernel(
-    sizes, coords_ref, counts_ref, own_ref, cot_ref, wq_ref, wk_ref, wvt_ref, mask_ref, all_ref,
-    out_ref, stats_ref, list_ref, buf_ref, bias_ref, max_ref, sum_ref, acc_ref, sems,
+    sizes, lists_ref, own_ref, cot_ref, wq_ref, wk_ref, wvt_ref, mask_ref, *refs,
 ):
+    groups, (out_ref, stats_ref, list_ref, buf_ref, bias_ref, max_ref, sum_ref, acc_ref, sems) = refs[:8], refs[8:]
     readers, blks, cap = sizes
     reader, blk = lax.axis_index("reader"), lax.axis_index("blk")
     me = reader * blks + blk
-    total = list_tiles(coords_ref, counts_ref, list_ref, reader * blks, 1, blks, cap, 0, blk)
+    total = list_tiles(lists_ref, list_ref, blks, blk, 0, blk, lambda b, k: k * blks + b)
     block, width = own_ref.shape
     head = width // HEADS
     queries = dot(own_ref[...], wq_ref[...]).astype(jnp.bfloat16) * jnp.bfloat16(head**-0.5)
@@ -120,7 +172,7 @@
                 at = slice(head * h, head * (h + 1))
                 acc_ref[at] = acc_ref[at] * fade + dot(values[at], expo.astype(jnp.bfloat16))
 
-    stream_tiles(total, list_ref, [all_ref], [buf_ref], sems, tile)
+    stream_tiles(total, list_ref, halves(groups, sizes, me, buf_ref), sems, tile)
     inverse = 1.0 / sum_ref[...]
     cot = cot_ref[...].astype(jnp.float32).T
     stats_ref[0:HEADS] = max_ref[...]
@@ -145,13 +197,13 @@
 
 
 def query_grad_kernel(
-    sizes, coords_ref, counts_ref, own_ref, cot_ref, wq_ref, wk_ref, wkt_ref, wv_ref, mask_ref, stats_ref, all_ref,
-    out_ref, list_ref, buf_ref, bias_ref, acc_ref, sems,
+    sizes, lists_ref, own_ref, cot_ref, wq_ref, wk_ref, wkt_ref, wv_ref, mask_ref, stats_ref, *refs,
 ):
+    groups, (out_ref, list_ref, buf_ref, bias_ref, acc_ref, sems) = refs[:8], refs[8:]
     readers, blks, cap = sizes
     reader, blk = lax.axis_index("reader"), lax.axis_index("blk")
     me = reader * blks + blk
-    total = list_tiles(coords_ref, counts_ref, list_ref, reader * blks, 1, blks, cap, 0, blk)
+    total = list_tiles(lists_ref, list_ref, blks, blk, 0, blk, lambda b, k: k * blks + b)
     block, width = own_ref.shape
     head = width // HEADS
     queries = dot(own_ref[...], wq_ref[...]).astype(jnp.bfloat16) * jnp.bfloat16(head**-0.5)
@@ -174,19 +226,20 @@
                 at = slice(head * (2 * p + e), head * (2 * p + e + 1))
                 acc_ref[at] += dot(keys_t[at], d_scores[e])
 
-    stream_tiles(total, list_ref, [all_ref], [buf_ref], sems, tile)
+    stream_tiles(total, list_ref, halves(groups, sizes, me, buf_ref), sems, tile)
     grad = (acc_ref[...].T * (head**-0.5)).astype(jnp.bfloat16)
     out_ref[...] = dot(grad, wq_ref[...], NT)
 
 
 def key_grad_kernel(
-    sizes, coords_ref, counts_ref, own_ref, wq_ref, wk_ref, wv_ref, mask_ref, part_ref, all_ref, cots_ref, stats_all_ref,
-    out_ref, list_ref, buf_ref, cot_buf_ref, stats_buf_ref, bias_ref, key_acc_ref, value_acc_ref, sems,
+    sizes, lists_ref, own_ref, wq_ref, wk_ref, wv_ref, mask_ref, part_ref, stats_all_ref, *refs,
 ):
+    groups, cot_groups, refs = refs[:8], refs[8:16], refs[16:]
+    out_ref, list_ref, buf_ref, cot_buf_ref, bias_ref, key_acc_ref, value_acc_ref, sems = refs
     readers, blks, cap = sizes
     reader, blk = lax.axis_index("reader"), lax.axis_index("blk")
     me = reader * blks + blk
-    total = list_tiles(coords_ref, counts_ref, list_ref, blk, blks, readers, cap, 1, reader)
+    total = list_tiles(lists_ref, list_ref, readers, reader, 1, reader, lambda r, q: r * blks + q)
     block, width = own_ref.shape
     head = width // HEADS
     pairs = [slice(2 * head * p, 2 * head * (p + 1)) for p in range(HEADS // 2)]
@@ -198,7 +251,8 @@
     def tile(slot, other, pattern):
         queries = dot(buf_ref[slot], wq_ref[...]).astype(jnp.bfloat16) * jnp.bfloat16(head**-0.5)
         cot = cot_buf_ref[slot]
-        stats = stats_buf_ref[slot]
+        apart = jnp.bitwise_xor(other, me)
+        stats = stats_all_ref.at[apart // blks * blks + lax.rem(apart, blks)]
         bias_ref[...] = tile_bias(mask_ref, pattern, other == me)
         for p, pair in enumerate(pairs):
             query_stack = pair_stack(queries[:, pair])
@@ -209,9 +263,8 @@
             value_acc_ref[:, pair] += dot(jnp.concatenate(probs, 1), cot_stack)
             key_acc_ref[:, pair] += dot(jnp.concatenate(d_scores, 1), query_stack)
 
-    stream_tiles(
-        total, list_ref, [all_ref, cots_ref, stats_all_ref], [buf_ref, cot_buf_ref, stats_buf_ref], sems, tile
-    )
+    sources = halves(groups, sizes, me, buf_ref) + halves(cot_groups, sizes, me, cot_buf_ref)
+    stream_tiles(total, list_ref, sources, sems, tile)
     grad = part_ref[...] + dot(key_acc_ref[...].astype(jnp.bfloat16), wk_ref[...], NT)
     grad = grad + dot(value_acc_ref[...].astype(jnp.bfloat16), wv_ref[...], NT)
     out_ref[...] = grad.astype(out_ref.dtype)
@@ -220,31 +273,39 @@
 VMEM = pl.BlockSpec(memory_space=pltpu.VMEM)
 SMEM = pl.BlockSpec(memory_space=pltpu.SMEM)
 ANY = pl.BlockSpec(memory_space=pl.ANY)
+
+
+def after(value, *others):
+    return lax.optimization_barrier((value, *others))[0]
 
 
 def local(features, cotangent, w_query, w_key, w_value, tile_coords, tile_count, mask_table):
     block, width = features.shape
     assert block == mask_table.shape[1]
     readers, blks, cap = lax.axis_size("reader"), lax.axis_size("blk"), tile_coords.shape[2]
-    devices = readers * blks
     sizes = (readers, blks, cap)
     f32, bf16, i32 = jnp.float32, jnp.bfloat16, jnp.int32
     masks = mask_table.transpose(0, 2, 1)
-    axes = ("reader", "blk")
-
-    listing = jnp.concatenate([tile_coords.reshape(-1), tile_count.reshape(-1)]).astype(bf16)
-    listing = jnp.pad(listing, (0, EXTRA * width - listing.shape[0])).reshape(EXTRA, width)
-    packed = jnp.concatenate([features, listing], 0)
-    rows_all = lax.all_gather(packed[None], axes, axis=0, tiled=True)
-    cots_all = lax.all_gather(cotangent[None], axes, axis=0, tiled=True)
-    numbers = rows_all[:, block, : 3 * cap + 1].astype(i32)
-    coords = numbers[:, : 3 * cap].reshape(-1)
-    counts = numbers[:, 3 * cap]
+
+    listing = jnp.concatenate([tile_coords.reshape(1, -1), tile_count.reshape(1, 1)], 1)
+    row_lists = jnp.concatenate([listing] + [swap(listing, k) for k in range(1, blks)], 0)
+    column_lists = jnp.concatenate([listing] + [swap(listing, blks * k) for k in range(1, readers)], 0)
+
+    half = block // 2
+    pair = lambda array: (array[None, :half], array[None, half:])
+    lines = [gather_line(part) for part in pair(features)]
+    planes = [gather_plane(part, order) for part, order in zip(lines, orders(readers))]
+    rows_all = [other_core(groups) for groups in planes]
+    cot_pair = after(pair(cotangent), lines)
+    cot_lines = after([gather_line(part) for part in cot_pair], planes)
+    cots_all = [other_core(gather_plane(part, order)) for part, order in zip(cot_lines, orders(readers))]
 
     params = pltpu.CompilerParams(vmem_limit_bytes=VMEM_LIMIT)
-    list_space = pltpu.SMEM((2 * (devices * cap + 1),), i32)
     buffer = pltpu.VMEM((2, block, width), bf16)
     bias = pltpu.VMEM((block, block), f32)
+
+    def list_space(lists):
+        return pltpu.SMEM((2 * (lists * cap + 1),), i32)
 
     def cost(tiles):
         return pl.CostEstimate(flops=tiles * 200_000_000, bytes_accessed=4_000_000, transcendentals=tiles * 131072)
@@ -255,46 +316,50 @@
             jax.ShapeDtypeStruct((block, width), bf16),
             jax.ShapeDtypeStruct((3 * HEADS, block), f32),
         ),
-        in_specs=[SMEM, SMEM, VMEM, VMEM, VMEM, VMEM, VMEM, VMEM, ANY],
+        in_specs=[SMEM] + [VMEM] * 6 + [ANY] * 8,
         out_specs=(VMEM, VMEM),
         scratch_shapes=[
-            list_space, buffer, bias,
+            list_space(blks), buffer, bias,
             pltpu.VMEM((HEADS, block), f32), pltpu.VMEM((HEADS, block), f32), pltpu.VMEM((width, block), f32),
-            pltpu.SemaphoreType.DMA((2, 1)),
+            pltpu.SemaphoreType.DMA((2, 2)),
         ],
         compiler_params=params,
         cost_estimate=cost(5),
         name="forward",
-    )(coords, counts, features, cotangent, w_query, w_key, w_value.T, masks, rows_all)
-
-    stats_all = lax.all_gather(stats[None], axes, axis=0, tiled=True)
+    )(row_lists, features, cotangent, w_query, w_key, w_value.T, masks, *rows_all[0], *rows_all[1])
+
+    stats_row = jnp.concatenate([stats[None]] + [swap(stats[None], k) for k in range(1, blks)], 0)
+    stats_all = jnp.concatenate([stats_row] + [swap(stats_row, blks * k) for k in range(1, readers)], 0)
 
     query_part = pl.pallas_call(
         functools.partial(query_grad_kernel, sizes),
         out_shape=jax.ShapeDtypeStruct((block, width), f32),
-        in_specs=[SMEM, SMEM] + [VMEM] * 8 + [ANY],
+        in_specs=[SMEM] + [VMEM] * 8 + [ANY] * 8,
         out_specs=VMEM,
         scratch_shapes=[
-            list_space, buffer, bias, pltpu.VMEM((width, block), f32), pltpu.SemaphoreType.DMA((2, 1)),
+            list_space(blks), buffer, bias, pltpu.VMEM((width, block), f32), pltpu.SemaphoreType.DMA((2, 2)),
         ],
         compiler_params=params,
         cost_estimate=cost(5),
         name="query_grad",
-    )(coords, counts, features, cotangent, w_query, w_key, w_key.T, w_value, masks, stats, rows_all)
+    )(row_lists, features, cotangent, w_query, w_key, w_key.T, w_value, masks, stats, *rows_all[0], *rows_all[1])
 
     grad_features = pl.pallas_call(
         functools.partial(key_grad_kernel, sizes),
         out_shape=jax.ShapeDtypeStruct((block, width), bf16),
-        in_specs=[SMEM, SMEM] + [VMEM] * 6 + [ANY] * 3,
+        in_specs=[SMEM] + [VMEM] * 7 + [ANY] * 16,
         out_specs=VMEM,
         scratch_shapes=[
-            list_space, buffer, buffer, pltpu.VMEM((2, 3 * HEADS, block), f32), bias,
-            pltpu.VMEM((block, width), f32), pltpu.VMEM((block, width), f32), pltpu.SemaphoreType.DMA((2, 3)),
+            list_space(readers), buffer, buffer, bias,
+            pltpu.VMEM((block, width), f32), pltpu.VMEM((block, width), f32), pltpu.SemaphoreType.DMA((2, 4)),
         ],
         compiler_params=params,
         cost_estimate=cost(5),
         name="key_grad",
-    )(coords, counts, features, w_query, w_key, w_value, masks, query_part, rows_all, cots_all, stats_all)
+    )(
+        column_lists, features, w_query, w_key, w_value, masks, query_part, stats_all,
+        *rows_all[0], *rows_all[1], *cots_all[0], *cots_all[1],
+    )
     return attn_out, grad_features
 
 

time: 157 us -> 139 us (0.89)
  starting transfers between devices: 0.08 us -> 57.9 us
  blocking collectives: 45.7 us -> 0 us
  between operations: 14.8 us -> 1.75 us
  waiting for transfers between devices: 66.7 us -> 55.6 us
  Pallas kernels: 16.3 us -> 13.2 us
    all_gather x2 -> x0, waiting for transfers between devices: 66 us -> none  [the longest x1 63.7 us: local(): rows_all = lax.all_gather(packed[None], axes, axis=0, tiled=True)]
    ppermute x0 -> x48, starting transfers between devices: none -> 57.9 us  [swap(): return lax.ppermute(block, axes, [(i, i ^ mask) for i in range(count)])]
    ppermute x0 -> x48, waiting for transfers between devices: none -> 55.6 us  [swap(): return lax.ppermute(block, axes, [(i, i ^ mask) for i in range(count)])]
    all_gather x1 -> x0, blocking collectives: 45.7 us -> none  [local(): stats_all = lax.all_gather(stats[None], axes, axis=0, tiled=True)]
    unnamed x22 -> x61, local copies, waits for them, and re-layouts: 7.46 us -> 5.17 us
    pallas_call x1, Pallas kernels: 4.8 us -> 2.94 us  [local(): pl.pallas_call(functools.partial(query_grad_kernel, sizes), out_shape=jax...]
    pallas_call x1, Pallas kernels: 5.21 us -> 3.45 us  [local(): pl.pallas_call(functools.partial(forward_kernel, sizes), out_shape=(jax.S...]
  transfers between devices with their start and end apart: 2 -> 48, of which waited for: 2 -> 21; matrix products, arithmetic and copies ran while one was open for 2% -> 4% of each run, Pallas kernels for 6% -> 5%
where the time goes in v2:
time: 139 us; the launch traced here: 138 us
  starting transfers between devices  57.9 us (42%)
  waiting for transfers between devices  55.6 us (40%)
  Pallas kernels  13.2 us (9%)
  local copies, waits for them, and re-layouts  7.34 us (5%)
  between operations  1.75 us (1%)
  other arithmetic  1.7 us (1%)
    ppermute x48, starting transfers between devices, swap(): return lax.ppermute(block, axes, [(i, i ^ mask) for i in range(count)])  57.9 us
    ppermute x48, waiting for transfers between devices, swap(): return lax.ppermute(block, axes, [(i, i ^ mask) for i in range(count)])  55.6 us
    pallas_call x1, Pallas kernels, local(): pl.pallas_call(functools.partial(key_grad_kernel, sizes), out_shape=jax.S...  6.83 us
    unnamed x61, local copies, waits for them, and re-layouts  5.17 us
    pallas_call x1, Pallas kernels, local(): pl.pallas_call(functools.partial(forward_kernel, sizes), out_shape=(jax.S...  3.45 us
    pallas_call x1, Pallas kernels, local(): pl.pallas_call(functools.partial(query_grad_kernel, sizes), out_shape=jax...  2.94 us
  transfers between devices with their start and end apart: 48, of which 21 were waited for; matrix products, arithmetic and copies ran while one was open for 4% of the time, Pallas kernels for 5%

profile of v2, /device:TPU:0, one launch (start us, length us, event | category | flops | bytes accessed | tf_op | source)
XLA Modules:
  0.0 137.5 jit_solution(7593294353300892037)
XLA Ops:
  0.6 0.9 slice_bitcast_fusion.2
  1.6 3.1 %collective-permute-start.7 = (bf16[1,64,512]{2,1,0:T(8,128)(2,1)S(1)}, bf16[1,64,512]{2,1,0:T(8,128)(2,1)S(1)}, u32[]{:S(2)}, u32[]{:S(2)}) collective-permute-start(bf16[1,64,512]{2,1,0:T(8,128)(2,1)S(1)} %get-tuple-element.17), channel_id=1, source_target_pairs={{0,2},{1,3},{2,0},{3,1},{4,6},{5,7},{6,4},{7,5},{8,10},{9,11},{10,... | collective-permute-start | bytes 196616 | tf_op jit(solution)/shard_map/ppermute | solution.py:96
  4.6 2.6 %collective-permute-start.8 = (bf16[1,64,512]{2,1,0:T(8,128)(2,1)S(1)}, bf16[1,64,512]{2,1,0:T(8,128)(2,1)S(1)}, u32[]{:S(2)}, u32[]{:S(2)}) collective-permute-start(bf16[1,64,512]{2,1,0:T(8,128)(2,1)S(1)} %get-tuple-element.17), channel_id=1, source_target_pairs={{0,4},{1,5},{2,6},{3,7},{4,0},{5,1},{6,2},{7,3},{8,12},{9,13},{10,... | collective-permute-start | bytes 196616 | tf_op jit(solution)/shard_map/ppermute | solution.py:96
  7.2 0.9 collective-permute-start.14
  8.1 3.5 %collective-permute-start.15 = (bf16[1,64,512]{2,1,0:T(8,128)(2,1)S(1)}, bf16[1,64,512]{2,1,0:T(8,128)(2,1)S(1)}, u32[]{:S(2)}, u32[]{:S(2)}) collective-permute-start(bf16[1,64,512]{2,1,0:T(8,128)(2,1)S(1)} %get-tuple-element.16), channel_id=1, source_target_pairs={{0,4},{1,5},{2,6},{3,7},{4,0},{5,1},{6,2},{7,3},{8,12},{9,13},{10,... | collective-permute-start | bytes 196616 | tf_op jit(solution)/shard_map/ppermute | solution.py:96
  12.0 1.8 %collective-permute-done.9 = bf16[1,64,512]{2,1,0:T(8,128)(2,1)S(1)} collective-permute-done((bf16[1,64,512]{2,1,0:T(8,128)(2,1)S(1)}, bf16[1,64,512]{2,1,0:T(8,128)(2,1)S(1)}, u32[]{:S(2)}, u32[]{:S(2)}) %collective-permute-start.9) | collective-permute-done | bytes 65568 | tf_op jit(solution)/shard_map/ppermute | solution.py:96
  13.9 1.6 %collective-permute-start.10 = (bf16[4,64,512]{2,1,0:T(8,128)(2,1)S(1)}, bf16[4,64,512]{2,1,0:T(8,128)(2,1)S(1)}, u32[]{:S(2)}, u32[]{:S(2)}) collective-permute-start(bf16[4,64,512]{2,1,0:T(8,128)(2,1)S(1)} %pad_maximum_fusion), channel_id=1, source_target_pairs={{0,8},{1,9},{2,10},{3,11},{4,12},{5,13},{6,14},{7,15},{8,0},{9,1},... | collective-permute-start | bytes 786440 | tf_op jit(solution)/shard_map/ppermute | solution.py:96
  15.4 2.8 %collective-permute-done.15 = bf16[1,64,512]{2,1,0:T(8,128)(2,1)S(1)} collective-permute-done((bf16[1,64,512]{2,1,0:T(8,128)(2,1)S(1)}, bf16[1,64,512]{2,1,0:T(8,128)(2,1)S(1)}, u32[]{:S(2)}, u32[]{:S(2)}) %collective-permute-start.15) | collective-permute-done | bytes 65568 | tf_op jit(solution)/shard_map/ppermute | solution.py:96
  18.3 1.6 %collective-permute-start.17 = (bf16[4,64,512]{2,1,0:T(8,128)(2,1)S(1)}, bf16[4,64,512]{2,1,0:T(8,128)(2,1)S(1)}, u32[]{:S(2)}, u32[]{:S(2)}) collective-permute-start(bf16[4,64,512]{2,1,0:T(8,128)(2,1)S(1)} %pad_maximum_fusion.1), channel_id=1, source_target_pairs={{0,16},{1,17},{2,18},{3,19},{4,20},{5,21},{6,22},{7,23},{8,24},{9,... | collective-permute-start | bytes 786440 | tf_op jit(solution)/shard_map/ppermute | solution.py:96
  20.3 1.6 %collective-permute-start.11 = (bf16[8,64,512]{2,1,0:T(8,128)(2,1)S(1)}, bf16[8,64,512]{2,1,0:T(8,128)(2,1)S(1)}, u32[]{:S(2)}, u32[]{:S(2)}) collective-permute-start(bf16[8,64,512]{2,1,0:T(8,128)(2,1)S(1)} %constant_dynamic-update-slice_fusion.refs_0_), channel_id=1, source_target_pairs={{0,16},{1,17},{2,18},{3,19},{4,20},{5,21},{6,22},{7,23},{8,24},{9,... | collective-permute-start | bytes 1572872 | tf_op jit(solution)/shard_map/ppermute | solution.py:96
  21.9 5.7 %collective-permute-done.17 = bf16[4,64,512]{2,1,0:T(8,128)(2,1)S(1)} collective-permute-done((bf16[4,64,512]{2,1,0:T(8,128)(2,1)S(1)}, bf16[4,64,512]{2,1,0:T(8,128)(2,1)S(1)}, u32[]{:S(2)}, u32[]{:S(2)}) %collective-permute-start.17) | collective-permute-done | bytes 262176 | tf_op jit(solution)/shard_map/ppermute | solution.py:96
  27.6 1.6 %collective-permute-start.18 = (bf16[8,64,512]{2,1,0:T(8,128)(2,1)S(1)}, bf16[8,64,512]{2,1,0:T(8,128)(2,1)S(1)}, u32[]{:S(2)}, u32[]{:S(2)}) collective-permute-start(bf16[8,64,512]{2,1,0:T(8,128)(2,1)S(1)} %constant_dynamic-update-slice_fusion.5.refs_4_), channel_id=1, source_target_pairs={{0,8},{1,9},{2,10},{3,11},{4,12},{5,13},{6,14},{7,15},{8,0},{9,1},... | collective-permute-start | bytes 1572872 | tf_op jit(solution)/shard_map/ppermute | solution.py:96
  29.2 2.5 %collective-permute-start.36 = (bf16[1,64,512]{2,1,0:T(8,128)(2,1)S(1)}, bf16[1,64,512]{2,1,0:T(8,128)(2,1)S(1)}, u32[]{:S(2)}, u32[]{:S(2)}) collective-permute-start(bf16[1,64,512]{2,1,0:T(8,128)(2,1)S(1)} %get-tuple-element.10), channel_id=1, source_target_pairs={{0,6},{1,7},{2,4},{3,5},{4,2},{5,3},{6,0},{7,1},{8,14},{9,15},{10,... | collective-permute-start | bytes 196616 | tf_op jit(solution)/shard_map/ppermute | solution.py:96
  32.0 1.7 %collective-permute-start.34 = (bf16[1,64,512]{2,1,0:T(8,128)(2,1)S(1)}, bf16[1,64,512]{2,1,0:T(8,128)(2,1)S(1)}, u32[]{:S(2)}, u32[]{:S(2)}) collective-permute-start(bf16[1,64,512]{2,1,0:T(8,128)(2,1)S(1)} %get-tuple-element.10), channel_id=1, source_target_pairs={{0,2},{1,3},{2,0},{3,1},{4,6},{5,7},{6,4},{7,5},{8,10},{9,11},{10,... | collective-permute-start | bytes 196616 | tf_op jit(solution)/shard_map/ppermute | solution.py:96
  33.6 2.3 %collective-permute-done.36 = bf16[1,64,512]{2,1,0:T(8,128)(2,1)S(1)} collective-permute-done((bf16[1,64,512]{2,1,0:T(8,128)(2,1)S(1)}, bf16[1,64,512]{2,1,0:T(8,128)(2,1)S(1)}, u32[]{:S(2)}, u32[]{:S(2)}) %collective-permute-start.36) | collective-permute-done | bytes 65568 | tf_op jit(solution)/shard_map/ppermute | solution.py:96
  35.9 2.1 %collective-permute-start.39 = (bf16[1,64,512]{2,1,0:T(8,128)(2,1)S(1)}, bf16[1,64,512]{2,1,0:T(8,128)(2,1)S(1)}, u32[]{:S(2)}, u32[]{:S(2)}) collective-permute-start(bf16[1,64,512]{2,1,0:T(8,128)(2,1)S(1)} %get-tuple-element.11), channel_id=1, source_target_pairs={{0,6},{1,7},{2,4},{3,5},{4,2},{5,3},{6,0},{7,1},{8,14},{9,15},{10,... | collective-permute-start | bytes 196616 | tf_op jit(solution)/shard_map/ppermute | solution.py:96
  38.1 1.0 collective-permute-start.38
  39.0 1.3 collective-permute-start.37
  40.3 0.7 pad_maximum_fusion.2
  41.1 0.9 collective-permute-done.39
  42.0 2.0 %collective-permute-done.38 = bf16[1,64,512]{2,1,0:T(8,128)(2,1)S(1)} collective-permute-done((bf16[1,64,512]{2,1,0:T(8,128)(2,1)S(1)}, bf16[1,64,512]{2,1,0:T(8,128)(2,1)S(1)}, u32[]{:S(2)}, u32[]{:S(2)}) %collective-permute-start.38) | collective-permute-done | bytes 65568 | tf_op jit(solution)/shard_map/ppermute | solution.py:96
  44.0 0.7 pad_maximum_fusion.3
  44.8 0.6 collective-permute-start.40
  46.3 0.7 collective-permute-start.1
  46.9 1.2 collective-permute-start.2
  48.1 1.3 collective-permute-start.3
  49.4 1.3 collective-permute-start.4
  50.7 1.7 %collective-permute-start.5 = (s32[1,25]{1,0:T(1,128)S(1)}, s32[1,25]{1,0:T(1,128)S(1)}, u32[]{:S(2)}, u32[]{:S(2)}) collective-permute-start(s32[1,25]{1,0:T(1,128)S(1)} %pad_add_fusion.1), channel_id=1, source_target_pairs={{0,6},{1,7},{2,4},{3,5},{4,2},{5,3},{6,0},{7,1},{8,14},{9,15},{10,... | collective-permute-start | bytes 308 | tf_op jit(solution)/shard_map/ppermute | solution.py:96
  52.4 1.9 %collective-permute-start.6 = (s32[1,25]{1,0:T(1,128)S(1)}, s32[1,25]{1,0:T(1,128)S(1)}, u32[]{:S(2)}, u32[]{:S(2)}) collective-permute-start(s32[1,25]{1,0:T(1,128)S(1)} %pad_add_fusion.1), channel_id=1, source_target_pairs={{0,7},{1,6},{2,5},{3,4},{4,3},{5,2},{6,1},{7,0},{8,15},{9,14},{10,... | collective-permute-start | bytes 308 | tf_op jit(solution)/shard_map/ppermute | solution.py:96
  54.9 1.2 collective-permute-done.5
  56.1 1.1 collective-permute-done.6
  57.4 1.0 copy.14
  58.4 1.0 copy.15
  59.4 1.6 %collective-permute-start.44 = (bf16[4,64,512]{2,1,0:T(8,128)(2,1)}, bf16[4,64,512]{2,1,0:T(8,128)(2,1)S(1)}, u32[]{:S(2)}, u32[]{:S(2)}) collective-permute-start(bf16[4,64,512]{2,1,0:T(8,128)(2,1)} %pad_maximum_fusion.3), channel_id=1, source_target_pairs={{0,16},{1,17},{2,18},{3,19},{4,20},{5,21},{6,22},{7,23},{8,24},{9,... | collective-permute-start | bytes 786440 | tf_op jit(solution)/shard_map/ppermute | solution.py:96
  61.0 1.0 constant_dynamic-update-slice_fusion.30
  62.1 1.1 constant_dynamic-update-slice_fusion.29.refs_8_
  63.2 5.1 %collective-permute-done.44 = bf16[4,64,512]{2,1,0:T(8,128)(2,1)S(1)} collective-permute-done((bf16[4,64,512]{2,1,0:T(8,128)(2,1)}, bf16[4,64,512]{2,1,0:T(8,128)(2,1)S(1)}, u32[]{:S(2)}, u32[]{:S(2)}) %collective-permute-start.44) | collective-permute-done | bytes 262176 | tf_op jit(solution)/shard_map/ppermute | solution.py:96
  68.3 2.4 %collective-permute-start.23 = (s32[1,25]{1,0:T(1,128)S(1)}, s32[1,25]{1,0:T(1,128)S(1)}, u32[]{:S(2)}, u32[]{:S(2)}) collective-permute-start(s32[1,25]{1,0:T(1,128)S(1)} %pad_add_fusion.1), channel_id=1, source_target_pairs={{0,24},{1,25},{2,26},{3,27},{4,28},{5,29},{6,30},{7,31},{8,16},{9,... | collective-permute-start | bytes 308 | tf_op jit(solution)/shard_map/ppermute | solution.py:96
  70.8 0.6 collective-permute-start.22
  71.3 1.5 %collective-permute-start.41 = (bf16[8,64,512]{2,1,0:T(8,128)(2,1)S(1)}, bf16[8,64,512]{2,1,0:T(8,128)(2,1)S(1)}, u32[]{:S(2)}, u32[]{:S(2)}) collective-permute-start(bf16[8,64,512]{2,1,0:T(8,128)(2,1)S(1)} %constant_dynamic-update-slice_fusion.29.refs_8_), channel_id=1, source_target_pairs={{0,16},{1,17},{2,18},{3,19},{4,20},{5,21},{6,22},{7,23},{8,24},{9,... | collective-permute-start | bytes 1572872 | tf_op jit(solution)/shard_map/ppermute | solution.py:96
  72.9 0.5 collective-permute-start.45
  73.4 3.4 %forward.1 = (bf16[128,512]{1,0:T(8,128)(2,1)}, f32[24,128]{1,0:T(8,128)S(1)}) custom-call(s32[8,25]{1,0:T(8,128)S(1)} %concatenate.43.lists_ref, bf16[128,512]{1,0:T(8,128)(2,1)S(1)} %copy-done.6, bf16[128,512]{1,0:T(8,128)(2,1)S(1)} %copy-done.9, bf16[512,512]{1,0:T(8,128)(2,1)S(1)} %copy-done.2, bf16[512,512]{1,0:T(8,128)(2,1)S(1)} %copy-done, ...), custom_call_target="tpu_custom_call" | custom-call | flops 1000000000 | bytes 4000000 | tf_op jit(solution)/shard_map/forward/pallas_call | solution.py:313
  77.0 1.2 collective-permute-done.24
  78.1 3.7 %collective-permute-done.25 = f32[1,24,128]{2,1,0:T(8,128)S(1)} collective-permute-done((f32[1,24,128]{2,1,0:T(8,128)S(1)}, f32[1,24,128]{2,1,0:T(8,128)S(1)}, u32[]{:S(2)}, u32[]{:S(2)}) %collective-permute-start.25) | collective-permute-done | bytes 12320 | tf_op jit(solution)/shard_map/ppermute | solution.py:96
  81.8 3.1 %collective-permute-done.26 = f32[1,24,128]{2,1,0:T(8,128)S(1)} collective-permute-done((f32[1,24,128]{2,1,0:T(8,128)S(1)}, f32[1,24,128]{2,1,0:T(8,128)S(1)}, u32[]{:S(2)}, u32[]{:S(2)}) %collective-permute-start.26) | collective-permute-done | bytes 12320 | tf_op jit(solution)/shard_map/ppermute | solution.py:96
  85.0 1.4 %collective-permute-start.27 = (f32[1,24,128]{2,1,0:T(8,128)S(1)}, f32[1,24,128]{2,1,0:T(8,128)S(1)}, u32[]{:S(2)}, u32[]{:S(2)}) collective-permute-start(f32[1,24,128]{2,1,0:T(8,128)S(1)} %bitcast.28), channel_id=1, source_target_pairs={{0,4},{1,5},{2,6},{3,7},{4,0},{5,1},{6,2},{7,3},{8,12},{9,13},{10,... | collective-permute-start | bytes 36872 | tf_op jit(solution)/shard_map/ppermute | solution.py:96
  86.3 3.2 %collective-permute-done.27 = f32[1,24,128]{2,1,0:T(8,128)S(1)} collective-permute-done((f32[1,24,128]{2,1,0:T(8,128)S(1)}, f32[1,24,128]{2,1,0:T(8,128)S(1)}, u32[]{:S(2)}, u32[]{:S(2)}) %collective-permute-start.27) | collective-permute-done | bytes 12320 | tf_op jit(solution)/shard_map/ppermute | solution.py:96
  89.6 4.0 %collective-permute-done.28 = f32[1,24,128]{2,1,0:T(8,128)S(1)} collective-permute-done((f32[1,24,128]{2,1,0:T(8,128)S(1)}, f32[1,24,128]{2,1,0:T(8,128)S(1)}, u32[]{:S(2)}, u32[]{:S(2)}) %collective-permute-start.28) | collective-permute-done | bytes 12320 | tf_op jit(solution)/shard_map/ppermute | solution.py:96
  93.6 2.1 %collective-permute-start.29 = (f32[1,24,128]{2,1,0:T(8,128)S(1)}, f32[1,24,128]{2,1,0:T(8,128)S(1)}, u32[]{:S(2)}, u32[]{:S(2)}) collective-permute-start(f32[1,24,128]{2,1,0:T(8,128)S(1)} %bitcast.30), channel_id=1, source_target_pairs={{0,6},{1,7},{2,4},{3,5},{4,2},{5,3},{6,0},{7,1},{8,14},{9,15},{10,... | collective-permute-start | bytes 36872 | tf_op jit(solution)/shard_map/ppermute | solution.py:96
  95.7 3.4 %collective-permute-done.29 = f32[1,24,128]{2,1,0:T(8,128)S(1)} collective-permute-done((f32[1,24,128]{2,1,0:T(8,128)S(1)}, f32[1,24,128]{2,1,0:T(8,128)S(1)}, u32[]{:S(2)}, u32[]{:S(2)}) %collective-permute-start.29) | collective-permute-done | bytes 12320 | tf_op jit(solution)/shard_map/ppermute | solution.py:96
  99.1 4.9 %collective-permute-done.30 = f32[1,24,128]{2,1,0:T(8,128)S(1)} collective-permute-done((f32[1,24,128]{2,1,0:T(8,128)S(1)}, f32[1,24,128]{2,1,0:T(8,128)S(1)}, u32[]{:S(2)}, u32[]{:S(2)}) %collective-permute-start.30) | collective-permute-done | bytes 12320 | tf_op jit(solution)/shard_map/ppermute | solution.py:96
  104.0 4.2 %collective-permute-start.21 = (s32[1,25]{1,0:T(1,128)S(1)}, s32[1,25]{1,0:T(1,128)S(1)}, u32[]{:S(2)}, u32[]{:S(2)}) collective-permute-start(s32[1,25]{1,0:T(1,128)S(1)} %pad_add_fusion.1), channel_id=1, source_target_pairs={{0,8},{1,9},{2,10},{3,11},{4,12},{5,13},{6,14},{7,15},{8,0},{9,1},... | collective-permute-start | bytes 308 | tf_op jit(solution)/shard_map/ppermute | solution.py:96
  108.3 0.5 collective-permute-start.46
  108.7 0.9 collective-permute-done.21
  109.7 2.0 %collective-permute-start.31 = (f32[8,24,128]{2,1,0:T(8,128)S(1)}, f32[8,24,128]{2,1,0:T(8,128)S(1)}, u32[]{:S(2)}, u32[]{:S(2)}) collective-permute-start(f32[8,24,128]{2,1,0:T(8,128)S(1)} %get-tuple-element.20), channel_id=1, source_target_pairs={{0,8},{1,9},{2,10},{3,11},{4,12},{5,13},{6,14},{7,15},{8,0},{9,1},... | collective-permute-start | bytes 294920 | tf_op jit(solution)/shard_map/ppermute | solution.py:96
  111.7 0.5 collective-permute-start.47
  112.3 2.9 %query_grad.1.part_ref = f32[128,512]{1,0:T(8,128)S(1)} custom-call(s32[8,25]{1,0:T(8,128)S(1)} %concatenate.43.lists_ref, bf16[128,512]{1,0:T(8,128)(2,1)S(1)} %copy-done.6, bf16[128,512]{1,0:T(8,128)(2,1)S(1)} %copy-done.9, bf16[512,512]{1,0:T(8,128)(2,1)S(1)} %copy-done.2, bf16[512,512]{1,0:T(8,128)(2,1)S(1)} %copy-done, bf16[512,512]{1,0:T(8,128)(2,1)S(1)} %bitcast.23, ...), custom_call_target="tpu_custom_call" | custom-call | flops 1000000000 | bytes 4000000 | tf_op jit(solution)/shard_map/query_grad/pallas_call | solution.py:334
  115.3 4.3 %collective-permute-start.32 = (f32[8,24,128]{2,1,0:T(8,128)S(1)}, f32[8,24,128]{2,1,0:T(8,128)S(1)}, u32[]{:S(2)}, u32[]{:S(2)}) collective-permute-start(f32[8,24,128]{2,1,0:T(8,128)S(1)} %get-tuple-element.20), channel_id=1, source_target_pairs={{0,16},{1,17},{2,18},{3,19},{4,20},{5,21},{6,22},{7,23},{8,24},{9,... | collective-permute-start | bytes 294920 | tf_op jit(solution)/shard_map/ppermute | solution.py:96
  119.6 2.8 %collective-permute-done.32 = f32[8,24,128]{2,1,0:T(8,128)S(1)} collective-permute-done((f32[8,24,128]{2,1,0:T(8,128)S(1)}, f32[8,24,128]{2,1,0:T(8,128)S(1)}, u32[]{:S(2)}, u32[]{:S(2)}) %collective-permute-start.32) | collective-permute-done | bytes 98336 | tf_op jit(solution)/shard_map/ppermute | solution.py:96
  122.5 1.4 %collective-permute-start.33 = (f32[8,24,128]{2,1,0:T(8,128)S(1)}, f32[8,24,128]{2,1,0:T(8,128)S(1)}, u32[]{:S(2)}, u32[]{:S(2)}) collective-permute-start(f32[8,24,128]{2,1,0:T(8,128)S(1)} %get-tuple-element.20), channel_id=1, source_target_pairs={{0,24},{1,25},{2,26},{3,27},{4,28},{5,29},{6,30},{7,31},{8,16},{9,... | collective-permute-start | bytes 294920 | tf_op jit(solution)/shard_map/ppermute | solution.py:96
  123.9 4.8 %collective-permute-done.33 = f32[8,24,128]{2,1,0:T(8,128)S(1)} collective-permute-done((f32[8,24,128]{2,1,0:T(8,128)S(1)}, f32[8,24,128]{2,1,0:T(8,128)S(1)}, u32[]{:S(2)}, u32[]{:S(2)}) %collective-permute-start.33) | collective-permute-done | bytes 98336 | tf_op jit(solution)/shard_map/ppermute | solution.py:96
  128.8 0.7 copy-done.15
  129.9 0.8 copy-done.18
  130.7 6.8 %key_grad.1 = bf16[128,512]{1,0:T(8,128)(2,1)} custom-call(s32[4,25]{1,0:T(4,128)S(1)} %pad_add_fusion.lists_ref, bf16[128,512]{1,0:T(8,128)(2,1)S(1)} %copy-done.6, bf16[512,512]{1,0:T(8,128)(2,1)S(1)} %copy-done.2, bf16[512,512]{1,0:T(8,128)(2,1)S(1)} %copy-done, bf16[512,512]{1,0:T(8,128)(2,1)S(1)} %copy-done.1, s32[240,4,128]{2,1,0:T(4,128)S(1)} %bitcast.22, ...), custom_call_target="tpu_custom_call" | custom-call | flops 1000000000 | bytes 4000000 | tf_op jit(solution)/shard_map/key_grad/pallas_call | solution.py:347
  (112 shorter events, 3.0 us)
Async XLA Ops:
  0.6 11.0 %copy-start.6 = (bf16[128,512]{1,0:T(8,128)(2,1)S(1)}, bf16[128,512]{1,0:T(8,128)(2,1)}, u32[]{:S(2)}) copy-start(bf16[128,512]{1,0:T(8,128)(2,1)} %own_ref.5) | copy-start | bytes 393220
  1.6 10.1 %collective-permute-start.7 = (bf16[1,64,512]{2,1,0:T(8,128)(2,1)S(1)}, bf16[1,64,512]{2,1,0:T(8,128)(2,1)S(1)}, u32[]{:S(2)}, u32[]{:S(2)}) collective-permute-start(bf16[1,64,512]{2,1,0:T(8,128)(2,1)S(1)} %get-tuple-element.17), channel_id=1, source_target_pairs={{0,2},{1,3},{2,0},{3,1},{4,6},{5,7},{6,4},{7,5},{8,10},{9,11},{10,... | collective-permute-start | bytes 196616 | tf_op jit(solution)/shard_map/ppermute | solution.py:96
  4.6 7.4 %collective-permute-start.8 = (bf16[1,64,512]{2,1,0:T(8,128)(2,1)S(1)}, bf16[1,64,512]{2,1,0:T(8,128)(2,1)S(1)}, u32[]{:S(2)}, u32[]{:S(2)}) collective-permute-start(bf16[1,64,512]{2,1,0:T(8,128)(2,1)S(1)} %get-tuple-element.17), channel_id=1, source_target_pairs={{0,4},{1,5},{2,6},{3,7},{4,0},{5,1},{6,2},{7,3},{8,12},{9,13},{10,... | collective-permute-start | bytes 196616 | tf_op jit(solution)/shard_map/ppermute | solution.py:96
  7.2 6.6 %collective-permute-start.9 = (bf16[1,64,512]{2,1,0:T(8,128)(2,1)S(1)}, bf16[1,64,512]{2,1,0:T(8,128)(2,1)S(1)}, u32[]{:S(2)}, u32[]{:S(2)}) collective-permute-start(bf16[1,64,512]{2,1,0:T(8,128)(2,1)S(1)} %get-tuple-element.17), channel_id=1, source_target_pairs={{0,6},{1,7},{2,4},{3,5},{4,2},{5,3},{6,0},{7,1},{8,14},{9,15},{10,... | collective-permute-start | bytes 196616 | tf_op jit(solution)/shard_map/ppermute | solution.py:96
  7.2 8.2 %collective-permute-start.14 = (bf16[1,64,512]{2,1,0:T(8,128)(2,1)S(1)}, bf16[1,64,512]{2,1,0:T(8,128)(2,1)S(1)}, u32[]{:S(2)}, u32[]{:S(2)}) collective-permute-start(bf16[1,64,512]{2,1,0:T(8,128)(2,1)S(1)} %get-tuple-element.16), channel_id=1, source_target_pairs={{0,2},{1,3},{2,0},{3,1},{4,6},{5,7},{6,4},{7,5},{8,10},{9,11},{10,... | collective-permute-start | bytes 196616 | tf_op jit(solution)/shard_map/ppermute | solution.py:96
  8.1 10.1 %collective-permute-start.15 = (bf16[1,64,512]{2,1,0:T(8,128)(2,1)S(1)}, bf16[1,64,512]{2,1,0:T(8,128)(2,1)S(1)}, u32[]{:S(2)}, u32[]{:S(2)}) collective-permute-start(bf16[1,64,512]{2,1,0:T(8,128)(2,1)S(1)} %get-tuple-element.16), channel_id=1, source_target_pairs={{0,4},{1,5},{2,6},{3,7},{4,0},{5,1},{6,2},{7,3},{8,12},{9,13},{10,... | collective-permute-start | bytes 196616 | tf_op jit(solution)/shard_map/ppermute | solution.py:96
  11.7 6.6 %collective-permute-start.16 = (bf16[1,64,512]{2,1,0:T(8,128)(2,1)S(1)}, bf16[1,64,512]{2,1,0:T(8,128)(2,1)S(1)}, u32[]{:S(2)}, u32[]{:S(2)}) collective-permute-start(bf16[1,64,512]{2,1,0:T(8,128)(2,1)S(1)} %get-tuple-element.16), channel_id=1, source_target_pairs={{0,6},{1,7},{2,4},{3,5},{4,2},{5,3},{6,0},{7,1},{8,14},{9,15},{10,... | collective-permute-start | bytes 196616 | tf_op jit(solution)/shard_map/ppermute | solution.py:96
  13.9 6.4 %collective-permute-start.10 = (bf16[4,64,512]{2,1,0:T(8,128)(2,1)S(1)}, bf16[4,64,512]{2,1,0:T(8,128)(2,1)S(1)}, u32[]{:S(2)}, u32[]{:S(2)}) collective-permute-start(bf16[4,64,512]{2,1,0:T(8,128)(2,1)S(1)} %pad_maximum_fusion), channel_id=1, source_target_pairs={{0,8},{1,9},{2,10},{3,11},{4,12},{5,13},{6,14},{7,15},{8,0},{9,1},... | collective-permute-start | bytes 786440 | tf_op jit(solution)/shard_map/ppermute | solution.py:96
  18.3 9.3 %collective-permute-start.17 = (bf16[4,64,512]{2,1,0:T(8,128)(2,1)S(1)}, bf16[4,64,512]{2,1,0:T(8,128)(2,1)S(1)}, u32[]{:S(2)}, u32[]{:S(2)}) collective-permute-start(bf16[4,64,512]{2,1,0:T(8,128)(2,1)S(1)} %pad_maximum_fusion.1), channel_id=1, source_target_pairs={{0,16},{1,17},{2,18},{3,19},{4,20},{5,21},{6,22},{7,23},{8,24},{9,... | collective-permute-start | bytes 786440 | tf_op jit(solution)/shard_map/ppermute | solution.py:96
  20.3 8.9 %copy-start.9 = (bf16[128,512]{1,0:T(8,128)(2,1)S(1)}, bf16[128,512]{1,0:T(8,128)(2,1)}, u32[]{:S(2)}) copy-start(bf16[128,512]{1,0:T(8,128)(2,1)} %cot_ref.3) | copy-start | bytes 393220
  20.3 24.4 %collective-permute-start.11 = (bf16[8,64,512]{2,1,0:T(8,128)(2,1)S(1)}, bf16[8,64,512]{2,1,0:T(8,128)(2,1)S(1)}, u32[]{:S(2)}, u32[]{:S(2)}) collective-permute-start(bf16[8,64,512]{2,1,0:T(8,128)(2,1)S(1)} %constant_dynamic-update-slice_fusion.refs_0_), channel_id=1, source_target_pairs={{0,16},{1,17},{2,18},{3,19},{4,20},{5,21},{6,22},{7,23},{8,24},{9,... | collective-permute-start | bytes 1572872 | tf_op jit(solution)/shard_map/ppermute | solution.py:96
  27.6 17.1 %collective-permute-start.18 = (bf16[8,64,512]{2,1,0:T(8,128)(2,1)S(1)}, bf16[8,64,512]{2,1,0:T(8,128)(2,1)S(1)}, u32[]{:S(2)}, u32[]{:S(2)}) collective-permute-start(bf16[8,64,512]{2,1,0:T(8,128)(2,1)S(1)} %constant_dynamic-update-slice_fusion.5.refs_4_), channel_id=1, source_target_pairs={{0,8},{1,9},{2,10},{3,11},{4,12},{5,13},{6,14},{7,15},{8,0},{9,1},... | collective-permute-start | bytes 1572872 | tf_op jit(solution)/shard_map/ppermute | solution.py:96
  29.2 28.2 %copy-start.1 = (bf16[512,512]{1,0:T(8,128)(2,1)S(1)}, bf16[512,512]{1,0:T(8,128)(2,1)}, u32[]{:S(2)}) copy-start(bf16[512,512]{1,0:T(8,128)(2,1)} %wv_ref.3) | copy-start | bytes 1572868
  29.2 6.7 %collective-permute-start.36 = (bf16[1,64,512]{2,1,0:T(8,128)(2,1)S(1)}, bf16[1,64,512]{2,1,0:T(8,128)(2,1)S(1)}, u32[]{:S(2)}, u32[]{:S(2)}) collective-permute-start(bf16[1,64,512]{2,1,0:T(8,128)(2,1)S(1)} %get-tuple-element.10), channel_id=1, source_target_pairs={{0,6},{1,7},{2,4},{3,5},{4,2},{5,3},{6,0},{7,1},{8,14},{9,15},{10,... | collective-permute-start | bytes 196616 | tf_op jit(solution)/shard_map/ppermute | solution.py:96
  31.7 6.3 %collective-permute-start.35 = (bf16[1,64,512]{2,1,0:T(8,128)(2,1)S(1)}, bf16[1,64,512]{2,1,0:T(8,128)(2,1)S(1)}, u32[]{:S(2)}, u32[]{:S(2)}) collective-permute-start(bf16[1,64,512]{2,1,0:T(8,128)(2,1)S(1)} %get-tuple-element.10), channel_id=1, source_target_pairs={{0,4},{1,5},{2,6},{3,7},{4,0},{5,1},{6,2},{7,3},{8,12},{9,13},{10,... | collective-permute-start | bytes 196616 | tf_op jit(solution)/shard_map/ppermute | solution.py:96
  32.0 7.0 %collective-permute-start.34 = (bf16[1,64,512]{2,1,0:T(8,128)(2,1)S(1)}, bf16[1,64,512]{2,1,0:T(8,128)(2,1)S(1)}, u32[]{:S(2)}, u32[]{:S(2)}) collective-permute-start(bf16[1,64,512]{2,1,0:T(8,128)(2,1)S(1)} %get-tuple-element.10), channel_id=1, source_target_pairs={{0,2},{1,3},{2,0},{3,1},{4,6},{5,7},{6,4},{7,5},{8,10},{9,11},{10,... | collective-permute-start | bytes 196616 | tf_op jit(solution)/shard_map/ppermute | solution.py:96
  35.9 6.1 %collective-permute-start.39 = (bf16[1,64,512]{2,1,0:T(8,128)(2,1)S(1)}, bf16[1,64,512]{2,1,0:T(8,128)(2,1)S(1)}, u32[]{:S(2)}, u32[]{:S(2)}) collective-permute-start(bf16[1,64,512]{2,1,0:T(8,128)(2,1)S(1)} %get-tuple-element.11), channel_id=1, source_target_pairs={{0,6},{1,7},{2,4},{3,5},{4,2},{5,3},{6,0},{7,1},{8,14},{9,15},{10,... | collective-permute-start | bytes 196616 | tf_op jit(solution)/shard_map/ppermute | solution.py:96
  38.1 5.9 %collective-permute-start.38 = (bf16[1,64,512]{2,1,0:T(8,128)(2,1)S(1)}, bf16[1,64,512]{2,1,0:T(8,128)(2,1)S(1)}, u32[]{:S(2)}, u32[]{:S(2)}) collective-permute-start(bf16[1,64,512]{2,1,0:T(8,128)(2,1)S(1)} %get-tuple-element.11), channel_id=1, source_target_pairs={{0,4},{1,5},{2,6},{3,7},{4,0},{5,1},{6,2},{7,3},{8,12},{9,13},{10,... | collective-permute-start | bytes 196616 | tf_op jit(solution)/shard_map/ppermute | solution.py:96
  39.0 5.0 %collective-permute-start.37 = (bf16[1,64,512]{2,1,0:T(8,128)(2,1)S(1)}, bf16[1,64,512]{2,1,0:T(8,128)(2,1)S(1)}, u32[]{:S(2)}, u32[]{:S(2)}) collective-permute-start(bf16[1,64,512]{2,1,0:T(8,128)(2,1)S(1)} %get-tuple-element.11), channel_id=1, source_target_pairs={{0,2},{1,3},{2,0},{3,1},{4,6},{5,7},{6,4},{7,5},{8,10},{9,11},{10,... | collective-permute-start | bytes 196616 | tf_op jit(solution)/shard_map/ppermute | solution.py:96
  44.7 1.3 copy-start.19
  44.7 28.7 %copy-start.3 = (bf16[8,64,512]{2,1,0:T(8,128)(2,1)}, bf16[8,64,512]{2,1,0:T(8,128)(2,1)S(1)}, u32[]{:S(2)}) copy-start(bf16[8,64,512]{2,1,0:T(8,128)(2,1)S(1)} %collective-permute-done.18.refs_5_) | copy-start | bytes 1572868
  44.8 14.7 %collective-permute-start.40 = (bf16[4,64,512]{2,1,0:T(8,128)(2,1)}, bf16[4,64,512]{2,1,0:T(8,128)(2,1)}, u32[]{:S(2)}, u32[]{:S(2)}) collective-permute-start(bf16[4,64,512]{2,1,0:T(8,128)(2,1)} %pad_maximum_fusion.2), channel_id=1, source_target_pairs={{0,8},{1,9},{2,10},{3,11},{4,12},{5,13},{6,14},{7,15},{8,0},{9,1},... | collective-permute-start | bytes 786440 | tf_op jit(solution)/shard_map/ppermute | solution.py:96
  46.3 12.1 %copy-start = (bf16[512,512]{1,0:T(8,128)(2,1)S(1)}, bf16[512,512]{1,0:T(8,128)(2,1)}, u32[]{:S(2)}) copy-start(bf16[512,512]{1,0:T(8,128)(2,1)} %wk_ref.5) | copy-start | bytes 1572868
  46.3 3.1 %collective-permute-start = (s32[1,25]{1,0:T(1,128)S(1)}, s32[1,25]{1,0:T(1,128)S(1)}, u32[]{:S(2)}, u32[]{:S(2)}) collective-permute-start(s32[1,25]{1,0:T(1,128)S(1)} %pad_add_fusion.1), channel_id=1, source_target_pairs={{0,1},{1,0},{2,3},{3,2},{4,5},{5,4},{6,7},{7,6},{8,9},{9,8},{10,11... | collective-permute-start | bytes 308 | tf_op jit(solution)/shard_map/ppermute | solution.py:96
  46.3 4.5 %collective-permute-start.1 = (s32[1,25]{1,0:T(1,128)S(1)}, s32[1,25]{1,0:T(1,128)S(1)}, u32[]{:S(2)}, u32[]{:S(2)}) collective-permute-start(s32[1,25]{1,0:T(1,128)S(1)} %pad_add_fusion.1), channel_id=1, source_target_pairs={{0,2},{1,3},{2,0},{3,1},{4,6},{5,7},{6,4},{7,5},{8,10},{9,11},{10,... | collective-permute-start | bytes 308 | tf_op jit(solution)/shard_map/ppermute | solution.py:96
  46.9 5.5 %collective-permute-start.2 = (s32[1,25]{1,0:T(1,128)S(1)}, s32[1,25]{1,0:T(1,128)S(1)}, u32[]{:S(2)}, u32[]{:S(2)}) collective-permute-start(s32[1,25]{1,0:T(1,128)S(1)} %pad_add_fusion.1), channel_id=1, source_target_pairs={{0,3},{1,2},{2,1},{3,0},{4,7},{5,6},{6,5},{7,4},{8,11},{9,10},{10,... | collective-permute-start | bytes 308 | tf_op jit(solution)/shard_map/ppermute | solution.py:96
  48.1 6.2 %collective-permute-start.3 = (s32[1,25]{1,0:T(1,128)S(1)}, s32[1,25]{1,0:T(1,128)S(1)}, u32[]{:S(2)}, u32[]{:S(2)}) collective-permute-start(s32[1,25]{1,0:T(1,128)S(1)} %pad_add_fusion.1), channel_id=1, source_target_pairs={{0,4},{1,5},{2,6},{3,7},{4,0},{5,1},{6,2},{7,3},{8,12},{9,13},{10,... | collective-permute-start | bytes 308 | tf_op jit(solution)/shard_map/ppermute | solution.py:96
  49.4 5.3 %collective-permute-start.4 = (s32[1,25]{1,0:T(1,128)S(1)}, s32[1,25]{1,0:T(1,128)S(1)}, u32[]{:S(2)}, u32[]{:S(2)}) collective-permute-start(s32[1,25]{1,0:T(1,128)S(1)} %pad_add_fusion.1), channel_id=1, source_target_pairs={{0,5},{1,4},{2,7},{3,6},{4,1},{5,0},{6,3},{7,2},{8,13},{9,12},{10,... | collective-permute-start | bytes 308 | tf_op jit(solution)/shard_map/ppermute | solution.py:96
  50.7 5.3 %collective-permute-start.5 = (s32[1,25]{1,0:T(1,128)S(1)}, s32[1,25]{1,0:T(1,128)S(1)}, u32[]{:S(2)}, u32[]{:S(2)}) collective-permute-start(s32[1,25]{1,0:T(1,128)S(1)} %pad_add_fusion.1), channel_id=1, source_target_pairs={{0,6},{1,7},{2,4},{3,5},{4,2},{5,3},{6,0},{7,1},{8,14},{9,15},{10,... | collective-permute-start | bytes 308 | tf_op jit(solution)/shard_map/ppermute | solution.py:96
  52.4 4.8 %collective-permute-start.6 = (s32[1,25]{1,0:T(1,128)S(1)}, s32[1,25]{1,0:T(1,128)S(1)}, u32[]{:S(2)}, u32[]{:S(2)}) collective-permute-start(s32[1,25]{1,0:T(1,128)S(1)} %pad_add_fusion.1), channel_id=1, source_target_pairs={{0,7},{1,6},{2,5},{3,4},{4,3},{5,2},{6,1},{7,0},{8,15},{9,14},{10,... | collective-permute-start | bytes 308 | tf_op jit(solution)/shard_map/ppermute | solution.py:96
  54.3 16.4 %collective-permute-start.12 = (bf16[8,64,512]{2,1,0:T(8,128)(2,1)S(1)}, bf16[8,64,512]{2,1,0:T(8,128)(2,1)}, u32[]{:S(2)}, u32[]{:S(2)}) collective-permute-start(bf16[8,64,512]{2,1,0:T(8,128)(2,1)S(1)} %constant_dynamic-update-slice_fusion.refs_0_), channel_id=1, source_target_pairs={{0,1},{1,0},{2,3},{3,2},{4,5},{5,4},{6,7},{7,6},{8,9},{9,8},{10,11... | collective-permute-start | bytes 1572872 | tf_op jit(solution)/shard_map/ppermute | solution.py:96
  54.7 16.6 %collective-permute-start.19 = (bf16[8,64,512]{2,1,0:T(8,128)(2,1)S(1)}, bf16[8,64,512]{2,1,0:T(8,128)(2,1)}, u32[]{:S(2)}, u32[]{:S(2)}) collective-permute-start(bf16[8,64,512]{2,1,0:T(8,128)(2,1)S(1)} %constant_dynamic-update-slice_fusion.5.refs_4_), channel_id=1, source_target_pairs={{0,1},{1,0},{2,3},{3,2},{4,5},{5,4},{6,7},{7,6},{8,9},{9,8},{10,11... | collective-permute-start | bytes 1572872 | tf_op jit(solution)/shard_map/ppermute | solution.py:96
  56.1 16.8 %collective-permute-start.13 = (bf16[8,64,512]{2,1,0:T(8,128)(2,1)S(1)}, bf16[8,64,512]{2,1,0:T(8,128)(2,1)}, u32[]{:S(2)}, u32[]{:S(2)}) collective-permute-start(bf16[8,64,512]{2,1,0:T(8,128)(2,1)S(1)} %collective-permute-done.11.refs_1_), channel_id=1, source_target_pairs={{0,1},{1,0},{2,3},{3,2},{4,5},{5,4},{6,7},{7,6},{8,9},{9,8},{10,11... | collective-permute-start | bytes 1572872 | tf_op jit(solution)/shard_map/ppermute | solution.py:96
  57.2 16.2 %collective-permute-start.20 = (bf16[8,64,512]{2,1,0:T(8,128)(2,1)S(1)}, bf16[8,64,512]{2,1,0:T(8,128)(2,1)}, u32[]{:S(2)}, u32[]{:S(2)}) collective-permute-start(bf16[8,64,512]{2,1,0:T(8,128)(2,1)S(1)} %collective-permute-done.18.refs_5_), channel_id=1, source_target_pairs={{0,1},{1,0},{2,3},{3,2},{4,5},{5,4},{6,7},{7,6},{8,9},{9,8},{10,11... | collective-permute-start | bytes 1572872 | tf_op jit(solution)/shard_map/ppermute | solution.py:96
  59.4 2.6 %copy-start.12 = (bf16[4,64,512]{2,1,0:T(8,128)(2,1)S(1)}, bf16[4,64,512]{2,1,0:T(8,128)(2,1)}, u32[]{:S(2)}) copy-start(bf16[4,64,512]{2,1,0:T(8,128)(2,1)} %pad_maximum_fusion.3) | copy-start | bytes 786436
  59.4 8.8 %collective-permute-start.44 = (bf16[4,64,512]{2,1,0:T(8,128)(2,1)}, bf16[4,64,512]{2,1,0:T(8,128)(2,1)S(1)}, u32[]{:S(2)}, u32[]{:S(2)}) collective-permute-start(bf16[4,64,512]{2,1,0:T(8,128)(2,1)} %pad_maximum_fusion.3), channel_id=1, source_target_pairs={{0,16},{1,17},{2,18},{3,19},{4,20},{5,21},{6,22},{7,23},{8,24},{9,... | collective-permute-start | bytes 786440 | tf_op jit(solution)/shard_map/ppermute | solution.py:96
  62.0 11.4 %copy-start.8 = (bf16[512,512]{0,1:T(8,128)(2,1)S(1)}, bf16[512,512]{0,1:T(8,128)(2,1)}, u32[]{:S(2)}) copy-start(bf16[512,512]{0,1:T(8,128)(2,1)} %copy.14) | copy-start | bytes 1572868
  62.0 11.4 %copy-start.2 = (bf16[512,512]{1,0:T(8,128)(2,1)S(1)}, bf16[512,512]{1,0:T(8,128)(2,1)}, u32[]{:S(2)}) copy-start(bf16[512,512]{1,0:T(8,128)(2,1)} %wq_ref.5) | copy-start | bytes 1572868
  62.1 11.4 %copy-start.5 = (s32[240,128,4]{1,2,0:T(4,128)S(1)}, s32[240,128,4]{1,2,0:T(4,128)}, u32[]{:S(2)}) copy-start(s32[240,128,4]{1,2,0:T(4,128)} %param.15) | copy-start | bytes 1474564
  63.1 45.0 %copy-start.11 = (bf16[8,64,512]{2,1,0:T(8,128)(2,1)}, bf16[8,64,512]{2,1,0:T(8,128)(2,1)S(1)}, u32[]{:S(2)}) copy-start(bf16[8,64,512]{2,1,0:T(8,128)(2,1)S(1)} %constant_dynamic-update-slice_fusion.29.refs_8_) | copy-start | bytes 1572868
  68.3 39.9 %collective-permute-start.23 = (s32[1,25]{1,0:T(1,128)S(1)}, s32[1,25]{1,0:T(1,128)S(1)}, u32[]{:S(2)}, u32[]{:S(2)}) collective-permute-start(s32[1,25]{1,0:T(1,128)S(1)} %pad_add_fusion.1), channel_id=1, source_target_pairs={{0,24},{1,25},{2,26},{3,27},{4,28},{5,29},{6,30},{7,31},{8,16},{9,... | collective-permute-start | bytes 308 | tf_op jit(solution)/shard_map/ppermute | solution.py:96
  70.7 37.5 %copy-start.10 = (bf16[8,64,512]{2,1,0:T(8,128)(2,1)}, bf16[8,64,512]{2,1,0:T(8,128)(2,1)S(1)}, u32[]{:S(2)}) copy-start(bf16[8,64,512]{2,1,0:T(8,128)(2,1)S(1)} %constant_dynamic-update-slice_fusion.31.refs_12_) | copy-start | bytes 1572868
  70.8 37.5 %collective-permute-start.22 = (s32[1,25]{1,0:T(1,128)S(1)}, s32[1,25]{1,0:T(1,128)S(1)}, u32[]{:S(2)}, u32[]{:S(2)}) collective-permute-start(s32[1,25]{1,0:T(1,128)S(1)} %pad_add_fusion.1), channel_id=1, source_target_pairs={{0,16},{1,17},{2,18},{3,19},{4,20},{5,21},{6,22},{7,23},{8,24},{9,... | collective-permute-start | bytes 308 | tf_op jit(solution)/shard_map/ppermute | solution.py:96
  71.3 40.4 %collective-permute-start.41 = (bf16[8,64,512]{2,1,0:T(8,128)(2,1)S(1)}, bf16[8,64,512]{2,1,0:T(8,128)(2,1)S(1)}, u32[]{:S(2)}, u32[]{:S(2)}) collective-permute-start(bf16[8,64,512]{2,1,0:T(8,128)(2,1)S(1)} %constant_dynamic-update-slice_fusion.29.refs_8_), channel_id=1, source_target_pairs={{0,16},{1,17},{2,18},{3,19},{4,20},{5,21},{6,22},{7,23},{8,24},{9,... | collective-permute-start | bytes 1572872 | tf_op jit(solution)/shard_map/ppermute | solution.py:96
  72.9 38.9 %collective-permute-start.45 = (bf16[8,64,512]{2,1,0:T(8,128)(2,1)S(1)}, bf16[8,64,512]{2,1,0:T(8,128)(2,1)S(1)}, u32[]{:S(2)}, u32[]{:S(2)}) collective-permute-start(bf16[8,64,512]{2,1,0:T(8,128)(2,1)S(1)} %constant_dynamic-update-slice_fusion.31.refs_12_), channel_id=1, source_target_pairs={{0,8},{1,9},{2,10},{3,11},{4,12},{5,13},{6,14},{7,15},{8,0},{9,1},... | collective-permute-start | bytes 1572872 | tf_op jit(solution)/shard_map/ppermute | solution.py:96
  73.4 38.9 %copy-start.7 = (bf16[512,512]{0,1:T(8,128)(2,1)S(1)}, bf16[512,512]{0,1:T(8,128)(2,1)}, u32[]{:S(2)}) copy-start(bf16[512,512]{0,1:T(8,128)(2,1)} %copy.15) | copy-start | bytes 1572868
  76.9 1.2 collective-permute-start.24
  78.1 3.7 %collective-permute-start.25 = (f32[1,24,128]{2,1,0:T(8,128)S(1)}, f32[1,24,128]{2,1,0:T(8,128)S(1)}, u32[]{:S(2)}, u32[]{:S(2)}) collective-permute-start(f32[1,24,128]{2,1,0:T(8,128)S(1)} %bitcast.26), channel_id=1, source_target_pairs={{0,2},{1,3},{2,0},{3,1},{4,6},{5,7},{6,4},{7,5},{8,10},{9,11},{10,... | collective-permute-start | bytes 36872 | tf_op jit(solution)/shard_map/ppermute | solution.py:96
  81.8 3.1 %collective-permute-start.26 = (f32[1,24,128]{2,1,0:T(8,128)S(1)}, f32[1,24,128]{2,1,0:T(8,128)S(1)}, u32[]{:S(2)}, u32[]{:S(2)}) collective-permute-start(f32[1,24,128]{2,1,0:T(8,128)S(1)} %bitcast.27), channel_id=1, source_target_pairs={{0,3},{1,2},{2,1},{3,0},{4,7},{5,6},{6,5},{7,4},{8,11},{9,10},{10,... | collective-permute-start | bytes 36872 | tf_op jit(solution)/shard_map/ppermute | solution.py:96
  85.0 4.6 %collective-permute-start.27 = (f32[1,24,128]{2,1,0:T(8,128)S(1)}, f32[1,24,128]{2,1,0:T(8,128)S(1)}, u32[]{:S(2)}, u32[]{:S(2)}) collective-permute-start(f32[1,24,128]{2,1,0:T(8,128)S(1)} %bitcast.28), channel_id=1, source_target_pairs={{0,4},{1,5},{2,6},{3,7},{4,0},{5,1},{6,2},{7,3},{8,12},{9,13},{10,... | collective-permute-start | bytes 36872 | tf_op jit(solution)/shard_map/ppermute | solution.py:96
  89.5 4.0 %collective-permute-start.28 = (f32[1,24,128]{2,1,0:T(8,128)S(1)}, f32[1,24,128]{2,1,0:T(8,128)S(1)}, u32[]{:S(2)}, u32[]{:S(2)}) collective-permute-start(f32[1,24,128]{2,1,0:T(8,128)S(1)} %bitcast.29), channel_id=1, source_target_pairs={{0,5},{1,4},{2,7},{3,6},{4,1},{5,0},{6,3},{7,2},{8,13},{9,12},{10,... | collective-permute-start | bytes 36872 | tf_op jit(solution)/shard_map/ppermute | solution.py:96
  93.6 5.5 %collective-permute-start.29 = (f32[1,24,128]{2,1,0:T(8,128)S(1)}, f32[1,24,128]{2,1,0:T(8,128)S(1)}, u32[]{:S(2)}, u32[]{:S(2)}) collective-permute-start(f32[1,24,128]{2,1,0:T(8,128)S(1)} %bitcast.30), channel_id=1, source_target_pairs={{0,6},{1,7},{2,4},{3,5},{4,2},{5,3},{6,0},{7,1},{8,14},{9,15},{10,... | collective-permute-start | bytes 36872 | tf_op jit(solution)/shard_map/ppermute | solution.py:96
  99.1 4.9 %collective-permute-start.30 = (f32[1,24,128]{2,1,0:T(8,128)S(1)}, f32[1,24,128]{2,1,0:T(8,128)S(1)}, u32[]{:S(2)}, u32[]{:S(2)}) collective-permute-start(f32[1,24,128]{2,1,0:T(8,128)S(1)} %bitcast.31), channel_id=1, source_target_pairs={{0,7},{1,6},{2,5},{3,4},{4,3},{5,2},{6,1},{7,0},{8,15},{9,14},{10,... | collective-permute-start | bytes 36872 | tf_op jit(solution)/shard_map/ppermute | solution.py:96
  104.0 5.7 %collective-permute-start.21 = (s32[1,25]{1,0:T(1,128)S(1)}, s32[1,25]{1,0:T(1,128)S(1)}, u32[]{:S(2)}, u32[]{:S(2)}) collective-permute-start(s32[1,25]{1,0:T(1,128)S(1)} %pad_add_fusion.1), channel_id=1, source_target_pairs={{0,8},{1,9},{2,10},{3,11},{4,12},{5,13},{6,14},{7,15},{8,0},{9,1},... | collective-permute-start | bytes 308 | tf_op jit(solution)/shard_map/ppermute | solution.py:96
  108.2 20.5 %collective-permute-start.42 = (bf16[8,64,512]{2,1,0:T(8,128)(2,1)S(1)}, bf16[8,64,512]{2,1,0:T(8,128)(2,1)S(1)}, u32[]{:S(2)}, u32[]{:S(2)}) collective-permute-start(bf16[8,64,512]{2,1,0:T(8,128)(2,1)S(1)} %constant_dynamic-update-slice_fusion.29.refs_8_), channel_id=1, source_target_pairs={{0,1},{1,0},{2,3},{3,2},{4,5},{5,4},{6,7},{7,6},{8,9},{9,8},{10,11... | collective-permute-start | bytes 1572872 | tf_op jit(solution)/shard_map/ppermute | solution.py:96
  108.3 20.5 %collective-permute-start.46 = (bf16[8,64,512]{2,1,0:T(8,128)(2,1)S(1)}, bf16[8,64,512]{2,1,0:T(8,128)(2,1)S(1)}, u32[]{:S(2)}, u32[]{:S(2)}) collective-permute-start(bf16[8,64,512]{2,1,0:T(8,128)(2,1)S(1)} %constant_dynamic-update-slice_fusion.31.refs_12_), channel_id=1, source_target_pairs={{0,1},{1,0},{2,3},{3,2},{4,5},{5,4},{6,7},{7,6},{8,9},{9,8},{10,11... | collective-permute-start | bytes 1572872 | tf_op jit(solution)/shard_map/ppermute | solution.py:96
  109.7 5.6 %collective-permute-start.31 = (f32[8,24,128]{2,1,0:T(8,128)S(1)}, f32[8,24,128]{2,1,0:T(8,128)S(1)}, u32[]{:S(2)}, u32[]{:S(2)}) collective-permute-start(f32[8,24,128]{2,1,0:T(8,128)S(1)} %get-tuple-element.20), channel_id=1, source_target_pairs={{0,8},{1,9},{2,10},{3,11},{4,12},{5,13},{6,14},{7,15},{8,0},{9,1},... | collective-permute-start | bytes 294920 | tf_op jit(solution)/shard_map/ppermute | solution.py:96
  111.7 3.5 %copy-start.13 = (bf16[8,64,512]{2,1,0:T(8,128)(2,1)}, bf16[8,64,512]{2,1,0:T(8,128)(2,1)S(1)}, u32[]{:S(2)}) copy-start(bf16[8,64,512]{2,1,0:T(8,128)(2,1)S(1)} %collective-permute-done.41.refs_9_) | copy-start | bytes 1572868
  111.7 17.0 %collective-permute-start.43 = (bf16[8,64,512]{2,1,0:T(8,128)(2,1)S(1)}, bf16[8,64,512]{2,1,0:T(8,128)(2,1)S(1)}, u32[]{:S(2)}, u32[]{:S(2)}) collective-permute-start(bf16[8,64,512]{2,1,0:T(8,128)(2,1)S(1)} %collective-permute-done.41.refs_9_), channel_id=1, source_target_pairs={{0,1},{1,0},{2,3},{3,2},{4,5},{5,4},{6,7},{7,6},{8,9},{9,8},{10,11... | collective-permute-start | bytes 1572872 | tf_op jit(solution)/shard_map/ppermute | solution.py:96
  111.7 3.5 %copy-start.14 = (bf16[8,64,512]{2,1,0:T(8,128)(2,1)}, bf16[8,64,512]{2,1,0:T(8,128)(2,1)S(1)}, u32[]{:S(2)}) copy-start(bf16[8,64,512]{2,1,0:T(8,128)(2,1)S(1)} %collective-permute-done.45.refs_13_) | copy-start | bytes 1572868
  111.7 17.0 %collective-permute-start.47 = (bf16[8,64,512]{2,1,0:T(8,128)(2,1)S(1)}, bf16[8,64,512]{2,1,0:T(8,128)(2,1)S(1)}, u32[]{:S(2)}, u32[]{:S(2)}) collective-permute-start(bf16[8,64,512]{2,1,0:T(8,128)(2,1)S(1)} %collective-permute-done.45.refs_13_), channel_id=1, source_target_pairs={{0,1},{1,0},{2,3},{3,2},{4,5},{5,4},{6,7},{7,6},{8,9},{9,8},{10,11... | collective-permute-start | bytes 1572872 | tf_op jit(solution)/shard_map/ppermute | solution.py:96
  115.3 15.4 %copy-start.4 = (bf16[8,64,512]{2,1,0:T(8,128)(2,1)S(1)}, bf16[8,64,512]{2,1,0:T(8,128)(2,1)}, u32[]{:S(2)}) copy-start(bf16[8,64,512]{2,1,0:T(8,128)(2,1)} %copy-done.3) | copy-start | bytes 1572868
  115.3 7.2 %collective-permute-start.32 = (f32[8,24,128]{2,1,0:T(8,128)S(1)}, f32[8,24,128]{2,1,0:T(8,128)S(1)}, u32[]{:S(2)}, u32[]{:S(2)}) collective-permute-start(f32[8,24,128]{2,1,0:T(8,128)S(1)} %get-tuple-element.20), channel_id=1, source_target_pairs={{0,16},{1,17},{2,18},{3,19},{4,20},{5,21},{6,22},{7,23},{8,24},{9,... | collective-permute-start | bytes 294920 | tf_op jit(solution)/shard_map/ppermute | solution.py:96
  122.5 6.2 %collective-permute-start.33 = (f32[8,24,128]{2,1,0:T(8,128)S(1)}, f32[8,24,128]{2,1,0:T(8,128)S(1)}, u32[]{:S(2)}, u32[]{:S(2)}) collective-permute-start(f32[8,24,128]{2,1,0:T(8,128)S(1)} %get-tuple-element.20), channel_id=1, source_target_pairs={{0,24},{1,25},{2,26},{3,27},{4,28},{5,29},{6,30},{7,31},{8,16},{9,... | collective-permute-start | bytes 294920 | tf_op jit(solution)/shard_map/ppermute | solution.py:96
  (4 other events, 3.7 us)

commit v3 on v1

v3 whole, which is shorter than its diff:
```python
import functools

import jax
import jax.numpy as jnp
from jax import lax
from jax.experimental import pallas as pl
from jax.experimental.pallas import tpu as pltpu
from jax.sharding import PartitionSpec as P

HEADS = 8
NEG_FILL = -1e30
NT = (((1,), (1,)), ((), ()))
NN = (((1,), (0,)), ((), ()))
LIST_ROWS = 16
TILES = 2
KEPT = 4
VMEM_LIMIT = 40 * 1024 * 1024


def dot(a, b, dims=NN):
    return lax.dot_general(a, b, dims, preferred_element_type=jnp.float32)


def pair_stack(rows):
    lane = lax.broadcasted_iota(jnp.int32, rows.shape, 1)
    half = rows.shape[1] // 2
    zero = jnp.zeros_like(rows)
    return jnp.concatenate([jnp.where(lane < half, rows, zero), jnp.where(lane >= half, rows, zero)], 0)


def tile_bias(words, pattern, diag):
    count, size = words.shape
    keys = lax.broadcasted_iota(jnp.int32, (size, size), 0)
    queries = lax.broadcasted_iota(jnp.int32, (size, size), 1)
    spread = jnp.concatenate(
        [jnp.broadcast_to(words[g : g + 1], (size // count, size)) for g in range(count)], 0
    )
    bits = jnp.right_shift(spread, keys & 31) & 1
    same = keys - queries == jnp.where(diag, 0, 2 * size)
    return jnp.where((bits == 1) | same, jnp.where(pattern < 0, NEG_FILL, 0.0), NEG_FILL)


class Layout:
    def __init__(self, readers, blks, cap):
        self.readers, self.blks, self.cap = readers, blks, cap
        self.reader, self.blk = lax.axis_index("reader"), lax.axis_index("blk")
        self.me = self.reader * blks + self.blk

    def apart(self, device):
        far = jnp.bitwise_xor(device, self.me)
        reader, blk = far // self.blks, lax.rem(far, self.blks)
        return reader, blk // 2, blk & 1

    def row_place(self, order, device):
        reader, line, core = self.apart(device)
        for at, bit in enumerate(order[:-1]):
            line = line + (jnp.right_shift(reader, bit) & 1) * ((self.blks // 2) << at)
        return (jnp.right_shift(reader, order[-1]) & 1) + 2 * core, line

    def orders(self):
        return orders(self.readers)

    def half_place(self, bit, device):
        reader, line, core = self.apart(device)
        first = jnp.right_shift(reader, bit) & 1
        low = reader & ((1 << bit) - 1)
        rest = low + (jnp.right_shift(reader, bit + 1) << bit)
        return rest + self.readers // 2 * core, 2 * line + first


def orders(readers):
    rising = tuple(range((readers - 1).bit_length()))
    return rising, rising[::-1]


def start_copy(place, refs, make):
    group, where = place
    for g, ref in enumerate(refs):

        @pl.when(group == g)
        def _():
            make(ref.at[where]).start()


def pack_kernel(own_ref, coords_hbm, count_hbm, out_ref, coords_ref, count_ref, sems):
    block = own_ref.shape[0]
    cap = coords_ref.shape[3]
    copies = [
        pltpu.make_async_copy(coords_hbm, coords_ref, sems.at[0]),
        pltpu.make_async_copy(count_hbm, count_ref, sems.at[1]),
        pltpu.make_async_copy(own_ref, out_ref.at[0, pl.ds(0, block)], sems.at[2]),
    ]
    for copy in copies:
        copy.start()
    copies[0].wait()
    copies[1].wait()
    lane = lax.broadcasted_iota(jnp.int32, (LIST_ROWS, out_ref.shape[2]), 1)
    row = jnp.zeros(lane.shape, jnp.int32)
    for column in range(3):
        for slot in range(cap):
            row = jnp.where(lane == column * cap + slot, coords_ref[0, column, 0, slot], row)
    row = jnp.where(lane == 3 * cap, count_ref[0, 0], row)
    out_ref[0, block:] = row.astype(jnp.float32).astype(jnp.bfloat16)
    copies[2].wait()


def load_lists(refs, half, low_ref, wide_ref, lists_ref, sems):
    copies = []
    for ref, indices in refs:
        for index in indices:
            src = ref.at[index, pl.ds(half, LIST_ROWS), pl.ds(0, 128)]
            copies.append(pltpu.make_async_copy(src, low_ref.at[len(copies)], sems.at[len(copies)]))
    for copy in copies:
        copy.start()
    for copy in copies:
        copy.wait()
    for k in range(low_ref.shape[0]):
        wide_ref[8 * k : 8 * k + 8] = low_ref[k].astype(jnp.float32).astype(jnp.int32)[0:8]
    move = pltpu.make_async_copy(wide_ref, lists_ref, sems.at[0])
    move.start()
    return move


def scan_list(lists_ref, cap, row, column, wanted, found, out_ref, block_of):
    def one_slot(slot, found):
        out_ref[2 * found + 1] = block_of(lists_ref[8 * row, (1 - column) * cap + slot])
        out_ref[2 * found + 2] = lists_ref[8 * row, 2 * cap + slot]
        return found + jnp.where(lists_ref[8 * row, column * cap + slot] == wanted, 1, 0)

    return lax.fori_loop(0, lists_ref[8 * row, 3 * cap], one_slot, found)


def close_work(found, out_ref):
    out_ref[2 * found + 1] = out_ref[2 * found - 1]
    out_ref[2 * found + 2] = -1
    out_ref[0] = (found + 1) // 2


def prepare_kernel(
    sizes, own_ref, cot_ref, wq_ref, wk_ref, wv_ref, line_ref, line_other_ref,
    work_ref, query_stack_ref, cot_stack_ref, key_ref, value_ref, wkt_ref, wvt_ref,
    low_ref, wide_ref, lists_ref, sems,
):
    readers, blks, cap = sizes
    layout = Layout(*sizes)
    block, width = own_ref.shape
    head = width // HEADS
    lines = blks // 2
    refs = [(line_ref, range(lines)), (line_other_ref, range(lines))]
    move = load_lists(refs, block // 2, low_ref, wide_ref, lists_ref, sems)
    queries = dot(own_ref[...], wq_ref[...]).astype(jnp.bfloat16) * jnp.bfloat16(head**-0.5)
    for p in range(HEADS // 2):
        pair = slice(2 * head * p, 2 * head * (p + 1))
        query_stack_ref[p] = pair_stack(queries[:, pair])
        cot_stack_ref[p] = pair_stack(cot_ref[:, pair])
    key_ref[...] = dot(own_ref[...], wk_ref[...]).astype(jnp.bfloat16)
    value_ref[...] = dot(own_ref[...], wv_ref[...]).astype(jnp.bfloat16)
    wkt_ref[...] = wk_ref[...].T
    wvt_ref[...] = wv_ref[...].T
    move.wait()

    def query_side(k, found):
        blk = jnp.bitwise_xor(k, layout.blk)
        row = k // 2 + (k & 1) * lines
        return scan_list(lists_ref, cap, row, 0, layout.blk, found, work_ref, lambda other: other * blks + blk)

    close_work(lax.fori_loop(0, blks, query_side, 0), work_ref)


def key_list_kernel(sizes, here_ref, there_ref, work_ref, low_ref, wide_ref, lists_ref, sems):
    readers, blks, cap = sizes
    layout = Layout(*sizes)
    lines = blks // 2
    starts = range(0, lines * readers // 2, lines)
    half = here_ref.shape[1] - LIST_ROWS
    load_lists([(here_ref, starts), (there_ref, starts)], half, low_ref, wide_ref, lists_ref, sems).wait()
    order = layout.orders()[1]

    def key_side(k, found):
        reader = jnp.bitwise_xor(k, layout.reader)
        row = sum((jnp.right_shift(k, bit) & 1) << at for at, bit in enumerate(order))
        return scan_list(lists_ref, cap, row, 1, layout.reader, found, work_ref, lambda other: reader * blks + other)

    close_work(lax.fori_loop(0, readers, key_side, 0), work_ref)


def step_entry(work_ref, index):
    at = 1 + 2 * TILES * index
    return [work_ref[at + 2 * t] for t in range(TILES)], [work_ref[at + 2 * t + 1] for t in range(TILES)]


def run_steps(work_ref, start, wait, body):
    total = work_ref[0]

    def step(index, carry):
        @pl.when(index + 1 < total)
        def _():
            start(lax.rem(index + 1, 2), *step_entry(work_ref, index + 1))

        slot = lax.rem(index, 2)
        wait(slot)
        body(slot, *step_entry(work_ref, index), index)
        return carry

    lax.fori_loop(0, total, step, 0)


def first_step(work_ref, start):
    start(0, *step_entry(work_ref, 0))


class Rows:
    def __init__(self, layout, groups, mask_ref, buf, words, sems, block):
        self.layout, self.halves, self.mask_ref = layout, (groups[:4], groups[4:]), mask_ref
        self.buf, self.words, self.sems, self.block = buf, words, sems, block

    def rows(self, slot, t, k):
        half = self.block // 2
        into = self.buf.at[slot, pl.ds(t * self.block + k * half, half)]
        return lambda src: pltpu.make_async_copy(src.at[pl.ds(0, half)], into, self.sems.at[slot, t, k])

    def mask(self, slot, t, pattern):
        return pltpu.make_async_copy(self.mask_ref.at[pattern], self.words.at[slot, t], self.sems.at[slot, t, 2])

    def start(self, slot, blocks, patterns):
        for t in range(TILES):
            for k, order in enumerate(self.layout.orders()):
                start_copy(self.layout.row_place(order, blocks[t]), self.halves[k], self.rows(slot, t, k))
            self.mask(slot, t, jnp.maximum(patterns[t], 0)).start()

    def wait(self, slot):
        for t in range(TILES):
            for k in range(2):
                self.rows(slot, t, k)(self.halves[k][0].at[0]).wait()
            self.mask(slot, t, 0).wait()

    def bias(self, slot, blocks, patterns):
        parts = [
            tile_bias(self.words[slot, t], patterns[t], blocks[t] == self.layout.me) for t in range(TILES)
        ]
        return jnp.concatenate(parts, 0)


def query_kernel(
    sizes, work_ref, stack_ref, cot_stack_ref, cot_ref, wq_ref, wk_hbm, wkt_hbm, wv_hbm, wvt_hbm, mask_ref, *refs
):
    groups, refs = refs[:8], refs[8:]
    out_ref, stats_ref, part_ref, wk_ref, wkt_ref, wv_ref, wvt_ref = refs[:7]
    buf, words, bias_ref, max_ref, sum_ref, acc_ref, score_ref, d_prob_ref, key_ref, sems, w_sems = refs[7:]
    layout = Layout(*sizes)
    block, width = cot_ref.shape
    head = width // HEADS
    rows_in = Rows(layout, groups, mask_ref, buf, words, sems, block)
    kept = score_ref.shape[0] - 1
    first_step(work_ref, rows_in.start)
    loads = [
        pltpu.make_async_copy(src, into, w_sems.at[k])
        for k, (src, into) in enumerate(
            ((wk_hbm, wk_ref), (wvt_hbm, wvt_ref), (wv_hbm, wv_ref), (wkt_hbm, wkt_ref))
        )
    ]
    for load in loads:
        load.start()
    max_ref[...] = jnp.full(max_ref.shape, NEG_FILL, jnp.float32)
    sum_ref[...] = jnp.zeros(sum_ref.shape, jnp.float32)
    acc_ref[...] = jnp.zeros(acc_ref.shape, jnp.float32)
    for load in loads:
        load.wait()

    def meet(slot, place, blocks, patterns):
        rows = buf[slot]
        keys = dot(rows, wk_ref[...]).astype(jnp.bfloat16)
        values = dot(rows, wv_ref[...]).astype(jnp.bfloat16)
        key_ref[place] = dot(wkt_ref[...], rows, NT).astype(jnp.bfloat16)
        bias_ref[...] = rows_in.bias(slot, blocks, patterns)
        for p in range(HEADS // 2):
            pair = slice(2 * head * p, 2 * head * (p + 1))
            scores = dot(keys[:, pair], stack_ref[p], NT)
            d_probs = dot(values[:, pair], cot_stack_ref[p], NT)
            for e in range(2):
                of = slice(block * e, block * (e + 1))
                score_ref[place, 2 * p + e] = scores[:, of] + bias_ref[...]
                d_prob_ref[place, 2 * p + e] = d_probs[:, of]

    def soften(slot, blocks, patterns, index):
        place = jnp.minimum(index, kept)
        meet(slot, place, blocks, patterns)
        values = dot(wvt_ref[...], buf[slot], NT).astype(jnp.bfloat16)
        for h in range(HEADS):
            s = score_ref[place, h]
            old = max_ref[h : h + 1]
            new = jnp.maximum(old, jnp.max(s, axis=0, keepdims=True))
            fade = jnp.exp(old - new)
            expo = jnp.exp(s - new)
            max_ref[h : h + 1] = new
            sum_ref[h : h + 1] = sum_ref[h : h + 1] * fade + jnp.sum(expo, axis=0, keepdims=True)
            at = slice(head * h, head * (h + 1))
            acc_ref[at] = acc_ref[at] * fade + dot(values[at], expo.astype(jnp.bfloat16))

    run_steps(work_ref, rows_in.start, rows_in.wait, soften)
    inverse = 1.0 / sum_ref[...]
    cot = cot_ref[...].astype(jnp.float32).T
    stats_ref[0:HEADS] = max_ref[...] + jnp.log(sum_ref[...])
    for h in range(HEADS):
        at = slice(head * h, head * (h + 1))
        outputs = acc_ref[at] * inverse[h : h + 1]
        acc_ref[at] = outputs
        stats_ref[HEADS + h : HEADS + h + 1] = jnp.sum(outputs * cot[at], axis=0, keepdims=True)
    out_ref[...] = acc_ref[...].T.astype(out_ref.dtype)
    acc_ref[...] = jnp.zeros(acc_ref.shape, jnp.float32)

    def slope(index, carry):
        place = jnp.minimum(index, kept)

        @pl.when(index >= kept)
        def _():
            blocks, patterns = step_entry(work_ref, index)
            rows_in.start(0, blocks, patterns)
            rows_in.wait(0)
            meet(0, place, blocks, patterns)

        for h in range(HEADS):
            _, d_scores = tile_grads(
                score_ref[place, h], d_prob_ref[place, h], stats_ref[h : h + 1], stats_ref[HEADS + h : HEADS + h + 1]
            )
            at = slice(head * h, head * (h + 1))
            acc_ref[at] += dot(key_ref[place, at], d_scores)
        return carry

    lax.fori_loop(0, work_ref[0], slope, 0)
    grad = (acc_ref[...].T * (head**-0.5)).astype(jnp.bfloat16)
    part_ref[...] = dot(grad, wq_ref[...], NT)


def tile_grads(scores, d_probs, lse, delta):
    prob = jnp.exp(scores - lse)
    return prob.astype(jnp.bfloat16), (prob * (d_probs - delta)).astype(jnp.bfloat16)


def key_grad_kernel(
    sizes, bits, work_ref, key_ref, value_ref, wq_hbm, wk_hbm, wv_hbm, part_ref, mask_ref, stats_all_ref, *refs
):
    readers = sizes[0]
    groups, refs = refs[:8], refs[8:]
    halves, refs = (refs[:readers], refs[readers : 2 * readers]), refs[2 * readers :]
    out_ref, wq_ref, wk_ref, wv_ref, buf, words, cot_buf, stats, bias_ref = refs[:9]
    key_acc, value_acc, sems, c_sems, w_sems = refs[9:]
    layout = Layout(*sizes)
    block, width = out_ref.shape
    head = width // HEADS
    rows_in = Rows(layout, groups, mask_ref, buf, words, sems, block)

    def half_copy(slot, t, k):
        into = cot_buf.at[slot, pl.ds(t * block + block // 2 * k, block // 2)]
        return lambda src: pltpu.make_async_copy(src, into, c_sems.at[slot, t, k])

    def stats_copy(slot, t, query):
        return pltpu.make_async_copy(stats_all_ref.at[query], stats.at[slot, t], c_sems.at[slot, t, 2])

    def start(slot, blocks, patterns):
        rows_in.start(slot, blocks, patterns)
        for t in range(TILES):
            stats_copy(slot, t, blocks[t]).start()
            for k in range(2):
                start_copy(layout.half_place(bits[k], blocks[t]), halves[k], half_copy(slot, t, k))

    def wait(slot):
        rows_in.wait(slot)
        for t in range(TILES):
            stats_copy(slot, t, 0).wait()
            for k in range(2):
                half_copy(slot, t, k)(halves[k][0].at[0]).wait()

    first_step(work_ref, start)
    loads = [
        pltpu.make_async_copy(src, into, w_sems.at[k])
        for k, (src, into) in enumerate(((wq_hbm, wq_ref), (wk_hbm, wk_ref), (wv_hbm, wv_ref)))
    ]
    for load in loads:
        load.start()
    key_acc[...] = jnp.zeros(key_acc.shape, jnp.float32)
    value_acc[...] = jnp.zeros(value_acc.shape, jnp.float32)
    loads[0].wait()

    def tiles(slot, blocks, patterns, index):
        queries = dot(buf[slot], wq_ref[...]).astype(jnp.bfloat16) * jnp.bfloat16(head**-0.5)
        bias_ref[...] = rows_in.bias(slot, blocks, patterns)
        cots = cot_buf[slot]
        for p in range(HEADS // 2):
            pair = slice(2 * head * p, 2 * head * (p + 1))
            of_tile = [slice(block * t, block * (t + 1)) for t in range(TILES)]
            query_stack = jnp.concatenate([pair_stack(queries[of, pair]) for of in of_tile], 0)
            cot_stack = jnp.concatenate([pair_stack(cots[of, pair]) for of in of_tile], 0)
            scores = dot(key_ref[:, pair], query_stack, NT)
            d_probs = dot(value_ref[:, pair], cot_stack, NT)
            probs, d_scores = [], []
            for t in range(TILES):
                for e in range(2):
                    h = 2 * p + e
                    of = slice(block * (2 * t + e), block * (2 * t + e + 1))
                    prob, d_score = tile_grads(
                        scores[:, of] + bias_ref[of_tile[t]], d_probs[:, of], stats[slot, t, h : h + 1],
                        stats[slot, t, HEADS + h : HEADS + h + 1],
                    )
                    probs.append(prob)
                    d_scores.append(d_score)
            value_acc[:, pair] += dot(jnp.concatenate(probs, 1), cot_stack)
            key_acc[:, pair] += dot(jnp.concatenate(d_scores, 1), query_stack)

    run_steps(work_ref, start, wait, tiles)
    loads[1].wait()
    loads[2].wait()
    grad = part_ref[...] + dot(key_acc[...].astype(jnp.bfloat16), wk_ref[...], NT)
    grad = grad + dot(value_acc[...].astype(jnp.bfloat16), wv_ref[...], NT)
    out_ref[...] = grad.astype(out_ref.dtype)


VMEM = pl.BlockSpec(memory_space=pltpu.VMEM)
SMEM = pl.BlockSpec(memory_space=pltpu.SMEM)
HBM = pl.BlockSpec(memory_space=pltpu.HBM)


def swap(block, mask):
    axes = ("reader", "blk")
    count = lax.axis_size("reader") * lax.axis_size("blk")
    return lax.ppermute(block, axes, [(i, i ^ mask) for i in range(count)])


def after(value, *others):
    return lax.optimization_barrier((value, *others))[0]


def over_readers(chunk, order, blks):
    for bit in order[:-1]:
        chunk = jnp.concatenate([chunk, swap(chunk, blks << bit)], 0)
    return [chunk, swap(chunk, blks << order[-1])]


def other_core(groups):
    return groups + [swap(group, 1) for group in groups]


def local(features, cotangent, w_query, w_key, w_value, tile_coords, tile_count, mask_table):
    block, width = features.shape
    readers, blks, cap = lax.axis_size("reader"), lax.axis_size("blk"), tile_coords.shape[2]
    assert block == mask_table.shape[1] and 3 * cap < 128
    sizes = (readers, blks, cap)
    devices, lines = readers * blks, blks // 2
    f32, bf16, i32 = jnp.float32, jnp.bfloat16, jnp.int32
    shape = jax.ShapeDtypeStruct
    masks = mask_table.transpose(0, 2, 1)
    words = masks.shape[1]
    head = width // HEADS
    half = block // 2
    params = pltpu.CompilerParams(vmem_limit_bytes=VMEM_LIMIT)
    masks_off = [2 * k for k in range(1, lines)]

    packed = pl.pallas_call(
        pack_kernel,
        out_shape=shape((1, block + LIST_ROWS, width), bf16),
        in_specs=[HBM, HBM, HBM],
        out_specs=VMEM,
        scratch_shapes=[
            pltpu.SMEM((1, 3, 1, cap), i32), pltpu.SMEM((1, 1), i32), pltpu.SemaphoreType.DMA((3,)),
        ],
        compiler_params=params,
        name="pack",
    )(features, tile_coords.transpose(0, 3, 1, 2), tile_count)

    lined = [packed] + [swap(packed, m) for m in masks_off]
    chunks = [
        jnp.concatenate([entry[:, :half] for entry in lined], 0),
        jnp.concatenate([entry[:, half:] for entry in lined], 0),
    ]
    here = [over_readers(chunk, order, blks) for chunk, order in zip(chunks, orders(readers))]
    rows_all = [group for groups in here for group in other_core(groups)]

    bits = (0, (readers - 1).bit_length() - 1)
    pairs = []
    for k in range(2):
        part = cotangent[None, half * k : half * (k + 1)]
        pairs += [part, swap(part, blks << bits[k])]
    both = jnp.concatenate(pairs, 0)
    cot_line = [both] + [swap(after(both, *chunks), m) for m in masks_off]
    cots_all = []
    for k in range(2):
        part = jnp.concatenate([entry[2 * k : 2 * k + 2] for entry in cot_line], 0)
        masks_left = [m for m in range(1, readers) if not m >> bits[k] & 1]
        cot_here = [part] + [swap(after(part, here), blks * m) for m in masks_left]
        cots_all += other_core(cot_here)

    def list_scratch(count):
        return [
            pltpu.VMEM((count, LIST_ROWS, 128), bf16), pltpu.VMEM((8 * count, 128), i32),
            pltpu.SMEM((8 * count, 128), i32), pltpu.SemaphoreType.DMA((count,)),
        ]

    def cost(tiles):
        return pl.CostEstimate(flops=tiles * 200_000_000, bytes_accessed=4_000_000, transcendentals=tiles * 131072)

    stacks = shape((HEADS // 2, 2 * block, 2 * head), bf16)
    own = shape((block, width), bf16)
    square = shape((width, width), bf16)
    query_work, query_stack, cot_stack, keys, values, w_key_t, w_value_t = pl.pallas_call(
        functools.partial(prepare_kernel, sizes),
        out_shape=(shape((2 * blks * cap + 5,), i32), stacks, stacks, own, own, square, square),
        in_specs=[VMEM] * 5 + [HBM] * 2,
        out_specs=(SMEM,) + (VMEM,) * 6,
        scratch_shapes=list_scratch(blks),
        compiler_params=params,
        cost_estimate=cost(2),
        name="prepare",
    )(features, cotangent, w_query, w_key, w_value, rows_all[4], rows_all[6])

    key_work = pl.pallas_call(
        functools.partial(key_list_kernel, sizes),
        out_shape=shape((2 * readers * cap + 5,), i32),
        in_specs=[HBM] * 2,
        out_specs=SMEM,
        scratch_shapes=list_scratch(readers),
        compiler_params=params,
        cost_estimate=cost(1),
        name="key_list",
    )(rows_all[4], rows_all[5])

    weight = pltpu.VMEM((width, width), bf16)
    buffer = pltpu.VMEM((2, TILES * block, width), bf16)
    word_buffer = pltpu.VMEM((2, TILES, words, block), i32)
    bias = pltpu.VMEM((TILES * block, block), f32)
    turned = pltpu.VMEM((width, block), f32)
    per_head = pltpu.VMEM((HEADS, block), f32)
    met = pltpu.VMEM((KEPT + 1, HEADS, TILES * block, block), f32)
    row_sems = pltpu.SemaphoreType.DMA((2, TILES, 3))

    attn_out, stats, query_part = pl.pallas_call(
        functools.partial(query_kernel, sizes),
        out_shape=(own, shape((2 * HEADS, block), f32), shape((block, width), f32)),
        in_specs=[SMEM, VMEM, VMEM, VMEM, VMEM] + [HBM] * 13,
        out_specs=(VMEM, VMEM, VMEM),
        scratch_shapes=[
            weight, weight, weight, weight, buffer, word_buffer, bias, per_head, per_head, turned, met, met,
            pltpu.VMEM((KEPT + 1, width, TILES * block), bf16), row_sems, pltpu.SemaphoreType.DMA((4,)),
        ],
        compiler_params=params,
        cost_estimate=cost(10),
        name="query_side",
    )(query_work, query_stack, cot_stack, cotangent, w_query, w_key, w_key_t, w_value, w_value_t, masks, *rows_all)

    sent = jnp.broadcast_to(stats[None], (devices, *stats.shape))
    stats_all = lax.all_to_all(sent, ("reader", "blk"), 0, 0, tiled=True)

    grad_features = pl.pallas_call(
        functools.partial(key_grad_kernel, sizes, bits),
        out_shape=own,
        in_specs=[SMEM, VMEM, VMEM, HBM, HBM, HBM, VMEM, HBM, HBM] + [HBM] * (8 + 2 * readers),
        out_specs=VMEM,
        scratch_shapes=[
            weight, weight, weight, buffer, word_buffer, buffer, pltpu.VMEM((2, TILES, 2 * HEADS, block), f32),
            bias, pltpu.VMEM((block, width), f32), pltpu.VMEM((block, width), f32),
            row_sems, pltpu.SemaphoreType.DMA((2, TILES, 3)), pltpu.SemaphoreType.DMA((3,)),
        ],
        compiler_params=params,
        cost_estimate=cost(5),
        name="key_grad",
    )(key_work, keys, values, w_query, w_key, w_value, query_part, masks, stats_all, *rows_all, *cots_all)
    return attn_out, grad_features


def solution(mesh):
    return jax.shard_map(
        local,
        mesh=mesh,
        in_specs=(
            P(("reader", "blk"), None),
            P(("reader", "blk"), None),
            P(),
            P(),
            P(),
            P("reader", "blk", None, None),
            P("reader", "blk"),
            P(),
        ),
        out_specs=(P(("reader", "blk"), None), P(("reader", "blk"), None)),
        check_vma=False,
    )
```

time: 157 us -> 108 us (0.69)
  blocking collectives: 45.7 us -> 0 us
  starting transfers between devices: 0.08 us -> 30.3 us
  waiting for transfers between devices: 66.7 us -> 45.2 us
  between operations: 14.8 us -> 1.64 us
  local copies, waits for them, and re-layouts: 7.93 us -> 15.7 us
  other arithmetic: 3.2 us -> 0.12 us
  Pallas kernels: 16.3 us -> 13.3 us
    all_gather x2 -> x0, waiting for transfers between devices: 66 us -> none  [the longest x1 63.7 us: local(): rows_all = lax.all_gather(packed[None], axes, axis=0, tiled=True)]
    all_gather x1 -> x0, blocking collectives: 45.7 us -> none  [local(): stats_all = lax.all_gather(stats[None], axes, axis=0, tiled=True)]
    ppermute x0 -> x22, waiting for transfers between devices: none -> 36.6 us  [swap(): return lax.ppermute(block, axes, [(i, i ^ mask) for i in range(count)])]
    ppermute x0 -> x22, starting transfers between devices: none -> 20.8 us  [swap(): return lax.ppermute(block, axes, [(i, i ^ mask) for i in range(count)])]
    all_to_all x0 -> x1, starting transfers between devices: none -> 9.54 us  [local(): stats_all = lax.all_to_all(sent, ('reader', 'blk'), 0, 0, tiled=True)]
    all_to_all x0 -> x1, waiting for transfers between devices: none -> 8.65 us  [local(): stats_all = lax.all_to_all(sent, ('reader', 'blk'), 0, 0, tiled=True)]
    unnamed x22 -> x53, local copies, waits for them, and re-layouts: 7.46 us -> 14.1 us
    pallas_call x3 -> x5, Pallas kernels: 16.3 us -> 13.3 us  [the longest x1 4.6 us: local(): pl.pallas_call(functools.partial(key_grad_kernel, sizes, bits), out_shape...]
  transfers between devices with their start and end apart: 2 -> 23, of which waited for: 2 -> 9; matrix products, arithmetic and copies ran while one was open for 2% -> 5% of each run, Pallas kernels for 6% -> 8%
where the time goes in v3:
time: 108 us; the launch traced here: 106 us
  waiting for transfers between devices  45.2 us (42%)
  starting transfers between devices  30.3 us (28%)
  local copies, waits for them, and re-layouts  15.7 us (15%)
  Pallas kernels  13.3 us (12%)
  between operations  1.64 us (2%)
    ppermute x22, waiting for transfers between devices, swap(): return lax.ppermute(block, axes, [(i, i ^ mask) for i in range(count)])  36.6 us
    ppermute x22, starting transfers between devices, swap(): return lax.ppermute(block, axes, [(i, i ^ mask) for i in range(count)])  20.8 us
    unnamed x53, local copies, waits for them, and re-layouts  14.1 us
    all_to_all x1, starting transfers between devices, local(): stats_all = lax.all_to_all(sent, ('reader', 'blk'), 0, 0, tiled=True)  9.54 us
    all_to_all x1, waiting for transfers between devices, local(): stats_all = lax.all_to_all(sent, ('reader', 'blk'), 0, 0, tiled=True)  8.65 us
    pallas_call x1, Pallas kernels, local(): pl.pallas_call(functools.partial(key_grad_kernel, sizes, bits), out_shape...  4.6 us
    pallas_call x1, Pallas kernels, local(): pl.pallas_call(functools.partial(query_kernel, sizes), out_shape=(own, sh...  3.85 us
    pallas_call x1, Pallas kernels, local(): pl.pallas_call(functools.partial(prepare_kernel, sizes), out_shape=(shape...  2.58 us
  transfers between devices with their start and end apart: 23, of which 9 were waited for; matrix products, arithmetic and copies ran while one was open for 5% of the time, Pallas kernels for 8%

profile of v3, /device:TPU:0, one launch (start us, length us, event | category | flops | bytes accessed | tf_op | source)
XLA Modules:
  0.0 106.3 jit_solution(1718802045423951346)
XLA Ops:
  1.3 0.0 copy-done.23
  1.3 0.9 copy-done.16
  2.2 0.6 pack.1
  2.8 5.1 %collective-permute-start.2 = (bf16[1,144,512]{2,1,0:T(8,128)(2,1)S(1)}, bf16[1,144,512]{2,1,0:T(8,128)(2,1)S(1)}, u32[]{:S(2)}, u32[]{:S(2)}) collective-permute-start(bf16[1,144,512]{2,1,0:T(8,128)(2,1)S(1)} %pack.1), channel_id=1, source_target_pairs={{0,6},{1,7},{2,4},{3,5},{4,2},{5,3},{6,0},{7,1},{8,14},{9,15},{10,... | collective-permute-start | bytes 442376 | tf_op jit(solution)/shard_map/ppermute | solution.py:426
  8.0 0.0 collective-permute-start.1
  8.0 0.6 collective-permute-start
  8.6 1.7 %collective-permute-start.12 = (bf16[1,64,512]{2,1,0:T(8,128)(2,1)S(1)}, bf16[1,64,512]{2,1,0:T(8,128)(2,1)S(1)}, u32[]{:S(2)}, u32[]{:S(2)}) collective-permute-start(bf16[1,64,512]{2,1,0:T(8,128)(2,1)S(1)} %get-tuple-element.52), channel_id=1, source_target_pairs={{0,16},{1,17},{2,18},{3,19},{4,20},{5,21},{6,22},{7,23},{8,24},{9,... | collective-permute-start | bytes 196616 | tf_op jit(solution)/shard_map/ppermute | solution.py:426
  10.3 1.5 %collective-permute-start.11 = (bf16[1,64,512]{2,1,0:T(8,128)(2,1)S(1)}, bf16[1,64,512]{2,1,0:T(8,128)(2,1)S(1)}, u32[]{:S(2)}, u32[]{:S(2)}) collective-permute-start(bf16[1,64,512]{2,1,0:T(8,128)(2,1)S(1)} %get-tuple-element.53), channel_id=1, source_target_pairs={{0,8},{1,9},{2,10},{3,11},{4,12},{5,13},{6,14},{7,15},{8,0},{9,1},... | collective-permute-start | bytes 196616 | tf_op jit(solution)/shard_map/ppermute | solution.py:426
  11.9 0.7 constant_dynamic-update-slice_fusion.13
  12.5 0.4 collective-permute-done.12
  12.9 1.7 %collective-permute-done.11 = bf16[1,64,512]{2,1,0:T(8,128)(2,1)S(1)} collective-permute-done((bf16[1,64,512]{2,1,0:T(8,128)(2,1)S(1)}, bf16[1,64,512]{2,1,0:T(8,128)(2,1)S(1)}, u32[]{:S(2)}, u32[]{:S(2)}) %collective-permute-start.11) | collective-permute-done | bytes 65568 | tf_op jit(solution)/shard_map/ppermute | solution.py:426
  14.6 2.8 %collective-permute-done = bf16[1,144,512]{2,1,0:T(8,128)(2,1)S(1)} collective-permute-done((bf16[1,144,512]{2,1,0:T(8,128)(2,1)S(1)}, bf16[1,144,512]{2,1,0:T(8,128)(2,1)S(1)}, u32[]{:S(2)}, u32[]{:S(2)}) %collective-permute-start) | collective-permute-done | bytes 147488 | tf_op jit(solution)/shard_map/ppermute | solution.py:426
  17.5 2.9 %collective-permute-done.1 = bf16[1,144,512]{2,1,0:T(8,128)(2,1)S(1)} collective-permute-done((bf16[1,144,512]{2,1,0:T(8,128)(2,1)S(1)}, bf16[1,144,512]{2,1,0:T(8,128)(2,1)S(1)}, u32[]{:S(2)}, u32[]{:S(2)}) %collective-permute-start.1) | collective-permute-done | bytes 147488 | tf_op jit(solution)/shard_map/ppermute | solution.py:426
  20.4 0.0 collective-permute-done.2
  20.5 1.6 %collective-permute-start.3 = (bf16[4,80,512]{2,1,0:T(8,128)(2,1)S(1)}, bf16[4,80,512]{2,1,0:T(8,128)(2,1)S(1)}, u32[]{:S(2)}, u32[]{:S(2)}) collective-permute-start(bf16[4,80,512]{2,1,0:T(8,128)(2,1)S(1)} %pad_maximum_fusion), channel_id=1, source_target_pairs={{0,16},{1,17},{2,18},{3,19},{4,20},{5,21},{6,22},{7,23},{8,24},{9,... | collective-permute-start | bytes 983048 | tf_op jit(solution)/shard_map/ppermute | solution.py:426
  22.2 1.6 %collective-permute-start.5 = (bf16[4,64,512]{2,1,0:T(8,128)(2,1)S(1)}, bf16[4,64,512]{2,1,0:T(8,128)(2,1)S(1)}, u32[]{:S(2)}, u32[]{:S(2)}) collective-permute-start(bf16[4,64,512]{2,1,0:T(8,128)(2,1)S(1)} %pad_maximum_fusion.1), channel_id=1, source_target_pairs={{0,8},{1,9},{2,10},{3,11},{4,12},{5,13},{6,14},{7,15},{8,0},{9,1},... | collective-permute-start | bytes 786440 | tf_op jit(solution)/shard_map/ppermute | solution.py:426
  23.8 0.6 constant_dynamic-update-slice_fusion.12
  24.4 0.0 collective-permute-start.13
  24.4 5.0 %collective-permute-done.3 = bf16[4,80,512]{2,1,0:T(8,128)(2,1)S(1)} collective-permute-done((bf16[4,80,512]{2,1,0:T(8,128)(2,1)S(1)}, bf16[4,80,512]{2,1,0:T(8,128)(2,1)S(1)}, u32[]{:S(2)}, u32[]{:S(2)}) %collective-permute-start.3) | collective-permute-done | bytes 327712 | tf_op jit(solution)/shard_map/ppermute | solution.py:426
  29.4 1.6 %collective-permute-start.9 = (bf16[8,80,512]{2,1,0:T(8,128)(2,1)S(1)}, bf16[8,80,512]{2,1,0:T(8,128)(2,1)S(1)}, u32[]{:S(2)}, u32[]{:S(2)}) collective-permute-start(bf16[8,80,512]{2,1,0:T(8,128)(2,1)S(1)} %constant_dynamic-update-slice_fusion.line_ref.refs_4_.here_ref), channel_id=1, source_target_pairs={{0,8},{1,9},{2,10},{3,11},{4,12},{5,13},{6,14},{7,15},{8,0},{9,1},... | collective-permute-start | bytes 1966088 | tf_op jit(solution)/shard_map/ppermute | solution.py:426
  30.9 0.6 constant_dynamic-update-slice_fusion.10
  31.6 0.0 collective-permute-start.14
  31.6 2.3 %collective-permute-start.15 = (bf16[4,64,512]{2,1,0:T(8,128)(2,1)S(1)}, bf16[4,64,512]{2,1,0:T(8,128)(2,1)S(1)}, u32[]{:S(2)}, u32[]{:S(2)}) collective-permute-start(bf16[4,64,512]{2,1,0:T(8,128)(2,1)S(1)} %pad_maximum_fusion.2), channel_id=1, source_target_pairs={{0,6},{1,7},{2,4},{3,5},{4,2},{5,3},{6,0},{7,1},{8,14},{9,15},{10,... | collective-permute-start | bytes 786440 | tf_op jit(solution)/shard_map/ppermute | solution.py:426
  33.9 0.0 collective-permute-done.5
  33.9 1.6 %collective-permute-start.6 = (bf16[8,64,512]{2,1,0:T(8,128)(2,1)S(1)}, bf16[8,64,512]{2,1,0:T(8,128)(2,1)S(1)}, u32[]{:S(2)}, u32[]{:S(2)}) collective-permute-start(bf16[8,64,512]{2,1,0:T(8,128)(2,1)S(1)} %constant_dynamic-update-slice_fusion.5.refs_0_), channel_id=1, source_target_pairs={{0,16},{1,17},{2,18},{3,19},{4,20},{5,21},{6,22},{7,23},{8,24},{9,... | collective-permute-start | bytes 1572872 | tf_op jit(solution)/shard_map/ppermute | solution.py:426
  35.5 0.0 collective-permute-done.13
  35.5 0.7 slice_dynamic-update-slice_fusion.2
  36.3 13.2 %collective-permute-done.14 = bf16[4,64,512]{2,1,0:T(8,128)(2,1)S(1)} collective-permute-done((bf16[4,64,512]{2,1,0:T(8,128)(2,1)S(1)}, bf16[4,64,512]{2,1,0:T(8,128)(2,1)S(1)}, u32[]{:S(2)}, u32[]{:S(2)}) %collective-permute-start.14) | collective-permute-done | bytes 262176 | tf_op jit(solution)/shard_map/ppermute | solution.py:426
  49.5 0.0 collective-permute-start.7
  49.5 0.7 slice_dynamic-update-slice_fusion.1
  50.2 0.5 collective-permute-start.10
  50.7 0.0 collective-permute-done.15
  50.7 0.7 slice_dynamic-update-slice_fusion
  51.4 0.0 collective-permute-start.8
  51.5 1.6 %collective-permute-start.16 = (bf16[8,64,512]{2,1,0:T(8,128)(2,1)}, bf16[8,64,512]{2,1,0:T(8,128)(2,1)}, u32[]{:S(2)}, u32[]{:S(2)}) collective-permute-start(bf16[8,64,512]{2,1,0:T(8,128)(2,1)} %get-tuple-element.26.refs_8_), channel_id=1, source_target_pairs={{0,16},{1,17},{2,18},{3,19},{4,20},{5,21},{6,22},{7,23},{8,24},{9,... | collective-permute-start | bytes 1572872 | tf_op jit(solution)/shard_map/ppermute | solution.py:426
  53.0 0.5 collective-permute-start.19
  53.6 2.6 %prepare.1 = (s32[133]{0:T(256)S(1)}, bf16[4,256,128]{2,1,0:T(8,128)(2,1)S(1)}, bf16[4,256,128]{2,1,0:T(8,128)(2,1)S(1)}, bf16[128,512]{1,0:T(8,128)(2,1)S(1)}, ...) custom-call(bf16[128,512]{1,0:T(8,128)(2,1)S(1)} %copy-done.16, ...), custom_call_target="tpu_custom_call" | custom-call | flops 400000000 | bytes 4000000 | tf_op jit(solution)/shard_map/prepare/pallas_call | solution.py:504
  56.2 0.0 copy-start.19
  56.2 0.0 collective-permute-done.7.refs_2_
  56.2 0.1 collective-permute-start.17
  56.3 0.5 collective-permute-start.20
  56.8 9.3 %collective-permute-done.16.refs_9_ = bf16[8,64,512]{2,1,0:T(8,128)(2,1)} collective-permute-done((bf16[8,64,512]{2,1,0:T(8,128)(2,1)}, bf16[8,64,512]{2,1,0:T(8,128)(2,1)}, u32[]{:S(2)}, u32[]{:S(2)}) %collective-permute-start.16) | collective-permute-done | bytes 524320 | tf_op jit(solution)/shard_map/ppermute | solution.py:426
  66.1 1.2 %collective-permute-done.19.refs_13_ = bf16[8,64,512]{2,1,0:T(8,128)(2,1)} collective-permute-done((bf16[8,64,512]{2,1,0:T(8,128)(2,1)}, bf16[8,64,512]{2,1,0:T(8,128)(2,1)}, u32[]{:S(2)}, u32[]{:S(2)}) %collective-permute-start.19) | collective-permute-done | bytes 524320 | tf_op jit(solution)/shard_map/ppermute | solution.py:426
  67.3 0.0 collective-permute-start.21
  67.4 0.0 collective-permute-done.10.refs_7_
  67.4 3.9 %query_side.1 = (bf16[128,512]{1,0:T(8,128)(2,1)}, f32[16,128]{1,0:T(8,128)S(1)}, f32[128,512]{1,0:T(8,128)S(1)}) custom-call(s32[133]{0:T(256)S(1)} %get-tuple-element.15.work_ref, bf16[4,256,128]{2,1,0:T(8,128)(2,1)S(1)} %get-tuple-element.16.stack_ref, bf16[4,256,128]{2,1,0:T(8,128)(2,1)S(1)} %get-tuple-element.17.cot_stack_ref, ...), custom_call_target="tpu_custom_call" | custom-call | flops 2000000000 | bytes 4000000 | tf_op jit(solution)/shard_map/query_side/pallas_call | solution.py:535
  71.3 0.7 copy-done.17
  72.1 0.7 broadcast_in_dim.12
  72.8 9.5 %all-to-all-start = ((f32[32,16,128]{2,1,0:T(8,128)}), f32[32,16,128]{2,1,0:T(8,128)}, u32[]{:S(2)}, u32[]{:S(2)}) async-start(f32[32,16,128]{2,1,0:T(8,128)} %broadcast_in_dim.12), calls=%async_computation | async-start | bytes 524288 | tf_op jit(solution)/shard_map/all_to_all | solution.py:550
  82.3 1.7 %key_list.1.work_ref = s32[69]{0:T(128)S(1)} custom-call(bf16[8,80,512]{2,1,0:T(8,128)(2,1)S(1)} %constant_dynamic-update-slice_fusion.line_ref.refs_4_.here_ref, bf16[8,80,512]{2,1,0:T(8,128)(2,1)S(1)} %collective-permute-done.9.refs_5_.there_ref), custom_call_target="tpu_custom_call" | custom-call | flops 200000000 | bytes 4000000 | tf_op jit(solution)/shard_map/key_list/pallas_call | solution.py:515
  84.0 0.0 collective-permute-done.17.refs_10_
  84.0 0.0 collective-permute-done.18.refs_11_
  84.0 0.0 collective-permute-done.21.refs_15_
  84.1 8.6 %all-to-all-done.stats_all_ref = f32[32,16,128]{2,1,0:T(8,128)} async-done(((f32[32,16,128]{2,1,0:T(8,128)}), f32[32,16,128]{2,1,0:T(8,128)}, u32[]{:S(2)}, u32[]{:S(2)}) %all-to-all-start) | async-done | bytes 262176 | tf_op jit(solution)/shard_map/all_to_all | solution.py:550
  92.7 1.1 %copy-done.4 = bf16[8,80,512]{2,1,0:T(8,128)(2,1)S(1)} copy-done((bf16[8,80,512]{2,1,0:T(8,128)(2,1)S(1)}, bf16[8,80,512]{2,1,0:T(8,128)(2,1)}, u32[]{:S(2)}) %copy-start.4) | copy-done | bytes 655384
  93.8 1.0 copy-done.6
  94.8 1.0 copy-done.9
  95.9 1.0 copy-done.11
  96.9 1.0 copy-done.13
  98.0 1.0 copy-done.15
  99.0 0.9 copy-done.18
  99.9 0.9 copy-done.20
  100.8 0.9 copy-done.22
  101.7 4.6 %key_grad.1 = bf16[128,512]{1,0:T(8,128)(2,1)} custom-call(s32[69]{0:T(128)S(1)} %key_list.1.work_ref, bf16[128,512]{1,0:T(8,128)(2,1)S(1)} %copy-done.20, bf16[128,512]{1,0:T(8,128)(2,1)S(1)} %copy-done.22, bf16[512,512]{1,0:T(8,128)(2,1)S(1)} %copy-done, bf16[512,512]{1,0:T(8,128)(2,1)S(1)} %copy-done.1, bf16[512,512]{1,0:T(8,128)(2,1)S(1)} %copy-done.2, ...), custom_call_target="tpu_custom_call" | custom-call | flops 1000000000 | bytes 4000000 | tf_op jit(solution)/shard_map/key_grad/pallas_call | solution.py:552
  (56 shorter events, 0.3 us)
Async XLA Ops:
  0.6 0.7 copy-start.23
  1.3 0.9 copy-start.16
  2.2 6.4 %copy-start.7 = (bf16[128,512]{1,0:T(8,128)(2,1)S(1)}, bf16[128,512]{1,0:T(8,128)(2,1)}, u32[]{:S(2)}) copy-start(bf16[128,512]{1,0:T(8,128)(2,1)} %cot_ref.3) | copy-start | bytes 393220
  2.8 17.6 %collective-permute-start.2 = (bf16[1,144,512]{2,1,0:T(8,128)(2,1)S(1)}, bf16[1,144,512]{2,1,0:T(8,128)(2,1)S(1)}, u32[]{:S(2)}, u32[]{:S(2)}) collective-permute-start(bf16[1,144,512]{2,1,0:T(8,128)(2,1)S(1)} %pack.1), channel_id=1, source_target_pairs={{0,6},{1,7},{2,4},{3,5},{4,2},{5,3},{6,0},{7,1},{8,14},{9,15},{10,... | collective-permute-start | bytes 442376 | tf_op jit(solution)/shard_map/ppermute | solution.py:426
  8.0 12.5 %collective-permute-start.1 = (bf16[1,144,512]{2,1,0:T(8,128)(2,1)S(1)}, bf16[1,144,512]{2,1,0:T(8,128)(2,1)S(1)}, u32[]{:S(2)}, u32[]{:S(2)}) collective-permute-start(bf16[1,144,512]{2,1,0:T(8,128)(2,1)S(1)} %pack.1), channel_id=1, source_target_pairs={{0,4},{1,5},{2,6},{3,7},{4,0},{5,1},{6,2},{7,3},{8,12},{9,13},{10,... | collective-permute-start | bytes 442376 | tf_op jit(solution)/shard_map/ppermute | solution.py:426
  8.0 9.5 %collective-permute-start = (bf16[1,144,512]{2,1,0:T(8,128)(2,1)S(1)}, bf16[1,144,512]{2,1,0:T(8,128)(2,1)S(1)}, u32[]{:S(2)}, u32[]{:S(2)}) collective-permute-start(bf16[1,144,512]{2,1,0:T(8,128)(2,1)S(1)} %pack.1), channel_id=1, source_target_pairs={{0,2},{1,3},{2,0},{3,1},{4,6},{5,7},{6,4},{7,5},{8,10},{9,11},{10,... | collective-permute-start | bytes 442376 | tf_op jit(solution)/shard_map/ppermute | solution.py:426
  8.6 4.3 %collective-permute-start.12 = (bf16[1,64,512]{2,1,0:T(8,128)(2,1)S(1)}, bf16[1,64,512]{2,1,0:T(8,128)(2,1)S(1)}, u32[]{:S(2)}, u32[]{:S(2)}) collective-permute-start(bf16[1,64,512]{2,1,0:T(8,128)(2,1)S(1)} %get-tuple-element.52), channel_id=1, source_target_pairs={{0,16},{1,17},{2,18},{3,19},{4,20},{5,21},{6,22},{7,23},{8,24},{9,... | collective-permute-start | bytes 196616 | tf_op jit(solution)/shard_map/ppermute | solution.py:426
  10.3 4.3 %collective-permute-start.11 = (bf16[1,64,512]{2,1,0:T(8,128)(2,1)S(1)}, bf16[1,64,512]{2,1,0:T(8,128)(2,1)S(1)}, u32[]{:S(2)}, u32[]{:S(2)}) collective-permute-start(bf16[1,64,512]{2,1,0:T(8,128)(2,1)S(1)} %get-tuple-element.53), channel_id=1, source_target_pairs={{0,8},{1,9},{2,10},{3,11},{4,12},{5,13},{6,14},{7,15},{8,0},{9,1},... | collective-permute-start | bytes 196616 | tf_op jit(solution)/shard_map/ppermute | solution.py:426
  20.5 8.8 %collective-permute-start.3 = (bf16[4,80,512]{2,1,0:T(8,128)(2,1)S(1)}, bf16[4,80,512]{2,1,0:T(8,128)(2,1)S(1)}, u32[]{:S(2)}, u32[]{:S(2)}) collective-permute-start(bf16[4,80,512]{2,1,0:T(8,128)(2,1)S(1)} %pad_maximum_fusion), channel_id=1, source_target_pairs={{0,16},{1,17},{2,18},{3,19},{4,20},{5,21},{6,22},{7,23},{8,24},{9,... | collective-permute-start | bytes 983048 | tf_op jit(solution)/shard_map/ppermute | solution.py:426
  22.2 11.7 %collective-permute-start.5 = (bf16[4,64,512]{2,1,0:T(8,128)(2,1)S(1)}, bf16[4,64,512]{2,1,0:T(8,128)(2,1)S(1)}, u32[]{:S(2)}, u32[]{:S(2)}) collective-permute-start(bf16[4,64,512]{2,1,0:T(8,128)(2,1)S(1)} %pad_maximum_fusion.1), channel_id=1, source_target_pairs={{0,8},{1,9},{2,10},{3,11},{4,12},{5,13},{6,14},{7,15},{8,0},{9,1},... | collective-permute-start | bytes 786440 | tf_op jit(solution)/shard_map/ppermute | solution.py:426
  24.4 11.1 %collective-permute-start.13 = (bf16[4,64,512]{2,1,0:T(8,128)(2,1)S(1)}, bf16[4,64,512]{2,1,0:T(8,128)(2,1)S(1)}, u32[]{:S(2)}, u32[]{:S(2)}) collective-permute-start(bf16[4,64,512]{2,1,0:T(8,128)(2,1)S(1)} %pad_maximum_fusion.2), channel_id=1, source_target_pairs={{0,2},{1,3},{2,0},{3,1},{4,6},{5,7},{6,4},{7,5},{8,10},{9,11},{10,... | collective-permute-start | bytes 786440 | tf_op jit(solution)/shard_map/ppermute | solution.py:426
  29.4 20.8 %collective-permute-start.9 = (bf16[8,80,512]{2,1,0:T(8,128)(2,1)S(1)}, bf16[8,80,512]{2,1,0:T(8,128)(2,1)S(1)}, u32[]{:S(2)}, u32[]{:S(2)}) collective-permute-start(bf16[8,80,512]{2,1,0:T(8,128)(2,1)S(1)} %constant_dynamic-update-slice_fusion.line_ref.refs_4_.here_ref), channel_id=1, source_target_pairs={{0,8},{1,9},{2,10},{3,11},{4,12},{5,13},{6,14},{7,15},{8,0},{9,1},... | collective-permute-start | bytes 1966088 | tf_op jit(solution)/shard_map/ppermute | solution.py:426
  31.6 17.9 %collective-permute-start.14 = (bf16[4,64,512]{2,1,0:T(8,128)(2,1)S(1)}, bf16[4,64,512]{2,1,0:T(8,128)(2,1)S(1)}, u32[]{:S(2)}, u32[]{:S(2)}) collective-permute-start(bf16[4,64,512]{2,1,0:T(8,128)(2,1)S(1)} %pad_maximum_fusion.2), channel_id=1, source_target_pairs={{0,4},{1,5},{2,6},{3,7},{4,0},{5,1},{6,2},{7,3},{8,12},{9,13},{10,... | collective-permute-start | bytes 786440 | tf_op jit(solution)/shard_map/ppermute | solution.py:426
  31.6 19.1 %collective-permute-start.15 = (bf16[4,64,512]{2,1,0:T(8,128)(2,1)S(1)}, bf16[4,64,512]{2,1,0:T(8,128)(2,1)S(1)}, u32[]{:S(2)}, u32[]{:S(2)}) collective-permute-start(bf16[4,64,512]{2,1,0:T(8,128)(2,1)S(1)} %pad_maximum_fusion.2), channel_id=1, source_target_pairs={{0,6},{1,7},{2,4},{3,5},{4,2},{5,3},{6,0},{7,1},{8,14},{9,15},{10,... | collective-permute-start | bytes 786440 | tf_op jit(solution)/shard_map/ppermute | solution.py:426
  33.9 33.4 %copy-start.5 = (bf16[8,64,512]{2,1,0:T(8,128)(2,1)}, bf16[8,64,512]{2,1,0:T(8,128)(2,1)S(1)}, u32[]{:S(2)}) copy-start(bf16[8,64,512]{2,1,0:T(8,128)(2,1)S(1)} %constant_dynamic-update-slice_fusion.5.refs_0_) | copy-start | bytes 1572868
  33.9 17.5 %collective-permute-start.6 = (bf16[8,64,512]{2,1,0:T(8,128)(2,1)S(1)}, bf16[8,64,512]{2,1,0:T(8,128)(2,1)S(1)}, u32[]{:S(2)}, u32[]{:S(2)}) collective-permute-start(bf16[8,64,512]{2,1,0:T(8,128)(2,1)S(1)} %constant_dynamic-update-slice_fusion.5.refs_0_), channel_id=1, source_target_pairs={{0,16},{1,17},{2,18},{3,19},{4,20},{5,21},{6,22},{7,23},{8,24},{9,... | collective-permute-start | bytes 1572872 | tf_op jit(solution)/shard_map/ppermute | solution.py:426
  35.5 17.5 %collective-permute-start.4 = (bf16[8,80,512]{2,1,0:T(8,128)(2,1)S(1)}, bf16[8,80,512]{2,1,0:T(8,128)(2,1)S(1)}, u32[]{:S(2)}, u32[]{:S(2)}) collective-permute-start(bf16[8,80,512]{2,1,0:T(8,128)(2,1)S(1)} %constant_dynamic-update-slice_fusion.line_ref.refs_4_.here_ref), channel_id=1, source_target_pairs={{0,1},{1,0},{2,3},{3,2},{4,5},{5,4},{6,7},{7,6},{8,9},{9,8},{10,11... | collective-permute-start | bytes 1966088 | tf_op jit(solution)/shard_map/ppermute | solution.py:426
  35.5 18.0 %copy-start.2 = (bf16[512,512]{1,0:T(8,128)(2,1)S(1)}, bf16[512,512]{1,0:T(8,128)(2,1)}, u32[]{:S(2)}) copy-start(bf16[512,512]{1,0:T(8,128)(2,1)} %wv_hbm.3) | copy-start | bytes 1572868
  49.5 6.7 %collective-permute-start.7 = (bf16[8,64,512]{2,1,0:T(8,128)(2,1)S(1)}, bf16[8,64,512]{2,1,0:T(8,128)(2,1)S(1)}, u32[]{:S(2)}, u32[]{:S(2)}) collective-permute-start(bf16[8,64,512]{2,1,0:T(8,128)(2,1)S(1)} %constant_dynamic-update-slice_fusion.5.refs_0_), channel_id=1, source_target_pairs={{0,1},{1,0},{2,3},{3,2},{4,5},{5,4},{6,7},{7,6},{8,9},{9,8},{10,11... | collective-permute-start | bytes 1572872 | tf_op jit(solution)/shard_map/ppermute | solution.py:426
  49.5 4.1 %copy-start = (bf16[512,512]{1,0:T(8,128)(2,1)S(1)}, bf16[512,512]{1,0:T(8,128)(2,1)}, u32[]{:S(2)}) copy-start(bf16[512,512]{1,0:T(8,128)(2,1)} %wq_hbm.1) | copy-start | bytes 1572868
  49.5 4.1 %copy-start.1 = (bf16[512,512]{1,0:T(8,128)(2,1)S(1)}, bf16[512,512]{1,0:T(8,128)(2,1)}, u32[]{:S(2)}) copy-start(bf16[512,512]{1,0:T(8,128)(2,1)} %wk_hbm.3) | copy-start | bytes 1572868
  50.2 17.1 %collective-permute-start.10 = (bf16[8,80,512]{2,1,0:T(8,128)(2,1)S(1)}, bf16[8,80,512]{2,1,0:T(8,128)(2,1)S(1)}, u32[]{:S(2)}, u32[]{:S(2)}) collective-permute-start(bf16[8,80,512]{2,1,0:T(8,128)(2,1)S(1)} %collective-permute-done.9.refs_5_.there_ref), channel_id=1, source_target_pairs={{0,1},{1,0},{2,3},{3,2},{4,5},{5,4},{6,7},{7,6},{8,9},{9,8},{10,11... | collective-permute-start | bytes 1966088 | tf_op jit(solution)/shard_map/ppermute | solution.py:426
  51.4 15.9 %copy-start.8 = (bf16[8,64,512]{2,1,0:T(8,128)(2,1)}, bf16[8,64,512]{2,1,0:T(8,128)(2,1)S(1)}, u32[]{:S(2)}) copy-start(bf16[8,64,512]{2,1,0:T(8,128)(2,1)S(1)} %collective-permute-done.6.refs_1_) | copy-start | bytes 1572868
  51.4 4.9 %collective-permute-start.8 = (bf16[8,64,512]{2,1,0:T(8,128)(2,1)S(1)}, bf16[8,64,512]{2,1,0:T(8,128)(2,1)S(1)}, u32[]{:S(2)}, u32[]{:S(2)}) collective-permute-start(bf16[8,64,512]{2,1,0:T(8,128)(2,1)S(1)} %collective-permute-done.6.refs_1_), channel_id=1, source_target_pairs={{0,1},{1,0},{2,3},{3,2},{4,5},{5,4},{6,7},{7,6},{8,9},{9,8},{10,11... | collective-permute-start | bytes 1572872 | tf_op jit(solution)/shard_map/ppermute | solution.py:426
  51.5 14.6 %collective-permute-start.16 = (bf16[8,64,512]{2,1,0:T(8,128)(2,1)}, bf16[8,64,512]{2,1,0:T(8,128)(2,1)}, u32[]{:S(2)}, u32[]{:S(2)}) collective-permute-start(bf16[8,64,512]{2,1,0:T(8,128)(2,1)} %get-tuple-element.26.refs_8_), channel_id=1, source_target_pairs={{0,16},{1,17},{2,18},{3,19},{4,20},{5,21},{6,22},{7,23},{8,24},{9,... | collective-permute-start | bytes 1572872 | tf_op jit(solution)/shard_map/ppermute | solution.py:426
  53.0 14.3 %copy-start.14 = (s32[240,128,4]{1,2,0:T(4,128)S(1)}, s32[240,128,4]{1,2,0:T(4,128)}, u32[]{:S(2)}) copy-start(s32[240,128,4]{1,2,0:T(4,128)} %param.15) | copy-start | bytes 1474564
  53.0 14.3 %collective-permute-start.19 = (bf16[8,64,512]{2,1,0:T(8,128)(2,1)}, bf16[8,64,512]{2,1,0:T(8,128)(2,1)}, u32[]{:S(2)}, u32[]{:S(2)}) collective-permute-start(bf16[8,64,512]{2,1,0:T(8,128)(2,1)} %get-tuple-element.27.refs_12_), channel_id=1, source_target_pairs={{0,8},{1,9},{2,10},{3,11},{4,12},{5,13},{6,14},{7,15},{8,0},{9,1},... | collective-permute-start | bytes 1572872 | tf_op jit(solution)/shard_map/ppermute | solution.py:426
  56.2 15.1 %copy-start.19 = (bf16[128,512]{1,0:T(8,128)(2,1)}, bf16[128,512]{1,0:T(8,128)(2,1)S(1)}, u32[]{:S(2)}) copy-start(bf16[128,512]{1,0:T(8,128)(2,1)S(1)} %get-tuple-element.21.key_ref) | copy-start | bytes 393220
  56.2 15.1 %copy-start.21 = (bf16[128,512]{1,0:T(8,128)(2,1)}, bf16[128,512]{1,0:T(8,128)(2,1)S(1)}, u32[]{:S(2)}) copy-start(bf16[128,512]{1,0:T(8,128)(2,1)S(1)} %get-tuple-element.22.value_ref) | copy-start | bytes 393220
  56.2 15.1 %copy-start.10 = (bf16[8,64,512]{2,1,0:T(8,128)(2,1)}, bf16[8,64,512]{2,1,0:T(8,128)(2,1)S(1)}, u32[]{:S(2)}) copy-start(bf16[8,64,512]{2,1,0:T(8,128)(2,1)S(1)} %collective-permute-done.7.refs_2_) | copy-start | bytes 1572868
  56.2 27.8 %collective-permute-start.17 = (bf16[8,64,512]{2,1,0:T(8,128)(2,1)}, bf16[8,64,512]{2,1,0:T(8,128)(2,1)}, u32[]{:S(2)}, u32[]{:S(2)}) collective-permute-start(bf16[8,64,512]{2,1,0:T(8,128)(2,1)} %get-tuple-element.26.refs_8_), channel_id=1, source_target_pairs={{0,1},{1,0},{2,3},{3,2},{4,5},{5,4},{6,7},{7,6},{8,9},{9,8},{10,11... | collective-permute-start | bytes 1572872 | tf_op jit(solution)/shard_map/ppermute | solution.py:426
  56.3 15.0 %copy-start.12 = (bf16[8,64,512]{2,1,0:T(8,128)(2,1)}, bf16[8,64,512]{2,1,0:T(8,128)(2,1)S(1)}, u32[]{:S(2)}) copy-start(bf16[8,64,512]{2,1,0:T(8,128)(2,1)S(1)} %collective-permute-done.8.refs_3_) | copy-start | bytes 1572868
  56.3 27.7 %collective-permute-start.20 = (bf16[8,64,512]{2,1,0:T(8,128)(2,1)}, bf16[8,64,512]{2,1,0:T(8,128)(2,1)}, u32[]{:S(2)}, u32[]{:S(2)}) collective-permute-start(bf16[8,64,512]{2,1,0:T(8,128)(2,1)} %get-tuple-element.27.refs_12_), channel_id=1, source_target_pairs={{0,1},{1,0},{2,3},{3,2},{4,5},{5,4},{6,7},{7,6},{8,9},{9,8},{10,11... | collective-permute-start | bytes 1572872 | tf_op jit(solution)/shard_map/ppermute | solution.py:426
  66.1 17.9 %collective-permute-start.18 = (bf16[8,64,512]{2,1,0:T(8,128)(2,1)}, bf16[8,64,512]{2,1,0:T(8,128)(2,1)}, u32[]{:S(2)}, u32[]{:S(2)}) collective-permute-start(bf16[8,64,512]{2,1,0:T(8,128)(2,1)} %collective-permute-done.16.refs_9_), channel_id=1, source_target_pairs={{0,1},{1,0},{2,3},{3,2},{4,5},{5,4},{6,7},{7,6},{8,9},{9,8},{10,11... | collective-permute-start | bytes 1572872 | tf_op jit(solution)/shard_map/ppermute | solution.py:426
  67.3 16.7 %collective-permute-start.21 = (bf16[8,64,512]{2,1,0:T(8,128)(2,1)}, bf16[8,64,512]{2,1,0:T(8,128)(2,1)}, u32[]{:S(2)}, u32[]{:S(2)}) collective-permute-start(bf16[8,64,512]{2,1,0:T(8,128)(2,1)} %collective-permute-done.19.refs_13_), channel_id=1, source_target_pairs={{0,1},{1,0},{2,3},{3,2},{4,5},{5,4},{6,7},{7,6},{8,9},{9,8},{10,11... | collective-permute-start | bytes 1572872 | tf_op jit(solution)/shard_map/ppermute | solution.py:426
  67.4 3.9 %copy-start.3 = (bf16[8,80,512]{2,1,0:T(8,128)(2,1)}, bf16[8,80,512]{2,1,0:T(8,128)(2,1)S(1)}, u32[]{:S(2)}) copy-start(bf16[8,80,512]{2,1,0:T(8,128)(2,1)S(1)} %collective-permute-done.10.refs_7_) | copy-start | bytes 1966084
  71.3 0.8 copy-start.17
  72.8 19.9 %all-to-all-start = ((f32[32,16,128]{2,1,0:T(8,128)}), f32[32,16,128]{2,1,0:T(8,128)}, u32[]{:S(2)}, u32[]{:S(2)}) async-start(f32[32,16,128]{2,1,0:T(8,128)} %broadcast_in_dim.12), calls=%async_computation | async-start | bytes 524288 | tf_op jit(solution)/shard_map/all_to_all | solution.py:550
  92.7 1.1 %copy-start.4 = (bf16[8,80,512]{2,1,0:T(8,128)(2,1)S(1)}, bf16[8,80,512]{2,1,0:T(8,128)(2,1)}, u32[]{:S(2)}) copy-start(bf16[8,80,512]{2,1,0:T(8,128)(2,1)} %copy-done.3) | copy-start | bytes 1966084
  93.8 1.0 copy-start.6
  94.8 1.0 copy-start.9
  95.9 1.0 copy-start.11
  96.9 1.0 copy-start.13
  98.0 1.0 copy-start.15
  99.0 0.9 copy-start.18
  99.9 0.9 copy-start.20
  100.8 0.9 copy-start.22

commit v4 on v3

--- a/solution.py
+++ b/solution.py
@@ -14,7 +14,7 @@
 LIST_ROWS = 16
 TILES = 2
 KEPT = 4
-VMEM_LIMIT = 40 * 1024 * 1024
+VMEM_LIMIT = 58 * 1024 * 1024
 
 
 def dot(a, b, dims=NN):
@@ -63,6 +63,8 @@
     def half_place(self, bit, device):
         reader, line, core = self.apart(device)
         first = jnp.right_shift(reader, bit) & 1
+        top = (self.blks // 2 - 1).bit_length() - 1
+        line = sum((jnp.right_shift(line, top - at) & 1) << at for at in range(top + 1))
         low = reader & ((1 << bit) - 1)
         rest = low + (jnp.right_shift(reader, bit + 1) << bit)
         return rest + self.readers // 2 * core, 2 * line + first
@@ -242,11 +244,11 @@
 
 
 def query_kernel(
-    sizes, work_ref, stack_ref, cot_stack_ref, cot_ref, wq_ref, wk_hbm, wkt_hbm, wv_hbm, wvt_hbm, mask_ref, *refs
+    sizes, work_ref, stack_hbm, cot_stack_hbm, cot_hbm, wq_hbm, wk_hbm, wkt_hbm, wv_hbm, wvt_hbm, mask_ref, *refs
 ):
     groups, refs = refs[:8], refs[8:]
-    out_ref, stats_ref, part_ref, wk_ref, wkt_ref, wv_ref, wvt_ref = refs[:7]
-    buf, words, bias_ref, max_ref, sum_ref, acc_ref, score_ref, d_prob_ref, key_ref, sems, w_sems = refs[7:]
+    out_ref, sent_ref, part_ref, stack_ref, cot_stack_ref, cot_ref, wq_ref, wk_ref, wkt_ref, wv_ref, wvt_ref = refs[:11]
+    stats_ref, buf, words, bias_ref, max_ref, sum_ref, acc_ref, score_ref, d_prob_ref, key_ref, sems, w_sems = refs[11:]
     layout = Layout(*sizes)
     block, width = cot_ref.shape
     head = width // HEADS
@@ -255,16 +257,17 @@
     first_step(work_ref, rows_in.start)
     loads = [
         pltpu.make_async_copy(src, into, w_sems.at[k])
-        for k, (src, into) in enumerate(
-            ((wk_hbm, wk_ref), (wvt_hbm, wvt_ref), (wv_hbm, wv_ref), (wkt_hbm, wkt_ref))
-        )
+        for k, (src, into) in enumerate((
+            (wk_hbm, wk_ref), (stack_hbm, stack_ref), (wv_hbm, wv_ref), (cot_stack_hbm, cot_stack_ref),
+            (wkt_hbm, wkt_ref), (wvt_hbm, wvt_ref), (cot_hbm, cot_ref), (wq_hbm, wq_ref),
+        ))
     ]
     for load in loads:
         load.start()
     max_ref[...] = jnp.full(max_ref.shape, NEG_FILL, jnp.float32)
     sum_ref[...] = jnp.zeros(sum_ref.shape, jnp.float32)
     acc_ref[...] = jnp.zeros(acc_ref.shape, jnp.float32)
-    for load in loads:
+    for load in loads[:6]:
         load.wait()
 
     def meet(slot, place, blocks, patterns):
@@ -298,6 +301,8 @@
             acc_ref[at] = acc_ref[at] * fade + dot(values[at], expo.astype(jnp.bfloat16))
 
     run_steps(work_ref, rows_in.start, rows_in.wait, soften)
+    for load in loads[6:]:
+        load.wait()
     inverse = 1.0 / sum_ref[...]
     cot = cot_ref[...].astype(jnp.float32).T
     stats_ref[0:HEADS] = max_ref[...] + jnp.log(sum_ref[...])
@@ -306,6 +311,7 @@
         outputs = acc_ref[at] * inverse[h : h + 1]
         acc_ref[at] = outputs
         stats_ref[HEADS + h : HEADS + h + 1] = jnp.sum(outputs * cot[at], axis=0, keepdims=True)
+    sent_ref[...] = jnp.broadcast_to(stats_ref[...], sent_ref.shape)
     out_ref[...] = acc_ref[...].T.astype(out_ref.dtype)
     acc_ref[...] = jnp.zeros(acc_ref.shape, jnp.float32)
 
@@ -338,13 +344,13 @@
 
 
 def key_grad_kernel(
-    sizes, bits, work_ref, key_ref, value_ref, wq_hbm, wk_hbm, wv_hbm, part_ref, mask_ref, stats_all_ref, *refs
+    sizes, bits, work_ref, key_hbm, value_hbm, wq_hbm, wk_hbm, wv_hbm, part_hbm, mask_ref, stats_all_ref, *refs
 ):
     readers = sizes[0]
     groups, refs = refs[:8], refs[8:]
     halves, refs = (refs[:readers], refs[readers : 2 * readers]), refs[2 * readers :]
-    out_ref, wq_ref, wk_ref, wv_ref, buf, words, cot_buf, stats, bias_ref = refs[:9]
-    key_acc, value_acc, sems, c_sems, w_sems = refs[9:]
+    out_ref, key_ref, value_ref, part_ref, wq_ref, wk_ref, wv_ref, buf, words, cot_buf, stats, bias_ref = refs[:12]
+    key_acc, value_acc, sems, c_sems, w_sems = refs[12:]
     layout = Layout(*sizes)
     block, width = out_ref.shape
     head = width // HEADS
@@ -374,13 +380,17 @@
     first_step(work_ref, start)
     loads = [
         pltpu.make_async_copy(src, into, w_sems.at[k])
-        for k, (src, into) in enumerate(((wq_hbm, wq_ref), (wk_hbm, wk_ref), (wv_hbm, wv_ref)))
+        for k, (src, into) in enumerate((
+            (wq_hbm, wq_ref), (key_hbm, key_ref), (value_hbm, value_ref),
+            (wk_hbm, wk_ref), (wv_hbm, wv_ref), (part_hbm, part_ref),
+        ))
     ]
     for load in loads:
         load.start()
     key_acc[...] = jnp.zeros(key_acc.shape, jnp.float32)
     value_acc[...] = jnp.zeros(value_acc.shape, jnp.float32)
-    loads[0].wait()
+    for load in loads[:3]:
+        load.wait()
 
     def tiles(slot, blocks, patterns, index):
         queries = dot(buf[slot], wq_ref[...]).astype(jnp.bfloat16) * jnp.bfloat16(head**-0.5)
@@ -408,8 +418,8 @@
             key_acc[:, pair] += dot(jnp.concatenate(d_scores, 1), query_stack)
 
     run_steps(work_ref, start, wait, tiles)
-    loads[1].wait()
-    loads[2].wait()
+    for load in loads[3:]:
+        load.wait()
     grad = part_ref[...] + dot(key_acc[...].astype(jnp.bfloat16), wk_ref[...], NT)
     grad = grad + dot(value_acc[...].astype(jnp.bfloat16), wv_ref[...], NT)
     out_ref[...] = grad.astype(out_ref.dtype)
@@ -481,13 +491,16 @@
         part = cotangent[None, half * k : half * (k + 1)]
         pairs += [part, swap(part, blks << bits[k])]
     both = jnp.concatenate(pairs, 0)
-    cot_line = [both] + [swap(after(both, *chunks), m) for m in masks_off]
-    cots_all = []
+    cot_line = after(both, *chunks)[None]
+    mask = blks // 2
+    while mask > 1:
+        cot_line = jnp.concatenate([cot_line, swap(cot_line, mask)], 0)
+        mask //= 2
+    cots_here, cots_all = [], []
     for k in range(2):
-        part = jnp.concatenate([entry[2 * k : 2 * k + 2] for entry in cot_line], 0)
+        part = cot_line[:, 2 * k : 2 * k + 2].reshape(2 * lines, half, width)
         masks_left = [m for m in range(1, readers) if not m >> bits[k] & 1]
-        cot_here = [part] + [swap(after(part, here), blks * m) for m in masks_left]
-        cots_all += other_core(cot_here)
+        cots_here.append([part] + [swap(after(part, here), blks * m) for m in masks_left])
 
     def list_scratch(count):
         return [
@@ -524,6 +537,8 @@
     )(rows_all[4], rows_all[5])
 
     weight = pltpu.VMEM((width, width), bf16)
+    stack_space = pltpu.VMEM(stacks.shape, bf16)
+    rows_low, rows_wide = pltpu.VMEM((block, width), bf16), pltpu.VMEM((block, width), f32)
     buffer = pltpu.VMEM((2, TILES * block, width), bf16)
     word_buffer = pltpu.VMEM((2, TILES, words, block), i32)
     bias = pltpu.VMEM((TILES * block, block), f32)
@@ -534,30 +549,32 @@
 
     attn_out, stats, query_part = pl.pallas_call(
         functools.partial(query_kernel, sizes),
-        out_shape=(own, shape((2 * HEADS, block), f32), shape((block, width), f32)),
-        in_specs=[SMEM, VMEM, VMEM, VMEM, VMEM] + [HBM] * 13,
+        out_shape=(own, shape((devices, 2 * HEADS, block), f32), shape((block, width), f32)),
+        in_specs=[SMEM] + [HBM] * 17,
         out_specs=(VMEM, VMEM, VMEM),
         scratch_shapes=[
-            weight, weight, weight, weight, buffer, word_buffer, bias, per_head, per_head, turned, met, met,
-            pltpu.VMEM((KEPT + 1, width, TILES * block), bf16), row_sems, pltpu.SemaphoreType.DMA((4,)),
+            stack_space, stack_space, rows_low, weight, weight, weight, weight, weight, pltpu.VMEM((2 * HEADS, block), f32),
+            buffer, word_buffer, bias, per_head, per_head, turned, met, met,
+            pltpu.VMEM((KEPT + 1, width, TILES * block), bf16), row_sems, pltpu.SemaphoreType.DMA((8,)),
         ],
         compiler_params=params,
         cost_estimate=cost(10),
         name="query_side",
     )(query_work, query_stack, cot_stack, cotangent, w_query, w_key, w_key_t, w_value, w_value_t, masks, *rows_all)
 
-    sent = jnp.broadcast_to(stats[None], (devices, *stats.shape))
-    stats_all = lax.all_to_all(sent, ("reader", "blk"), 0, 0, tiled=True)
+    for first, *rest in cots_here:
+        cots_all += [first, *rest, swap(after(first, rows_all), 1)] + [swap(after(part, stats), 1) for part in rest]
+    stats_all = lax.all_to_all(stats, ("reader", "blk"), 0, 0, tiled=True)
 
     grad_features = pl.pallas_call(
         functools.partial(key_grad_kernel, sizes, bits),
         out_shape=own,
-        in_specs=[SMEM, VMEM, VMEM, HBM, HBM, HBM, VMEM, HBM, HBM] + [HBM] * (8 + 2 * readers),
+        in_specs=[SMEM] + [HBM] * (16 + 2 * readers),
         out_specs=VMEM,
         scratch_shapes=[
-            weight, weight, weight, buffer, word_buffer, buffer, pltpu.VMEM((2, TILES, 2 * HEADS, block), f32),
-            bias, pltpu.VMEM((block, width), f32), pltpu.VMEM((block, width), f32),
-            row_sems, pltpu.SemaphoreType.DMA((2, TILES, 3)), pltpu.SemaphoreType.DMA((3,)),
+            rows_low, rows_low, rows_wide, weight, weight, weight,
+            buffer, word_buffer, buffer, pltpu.VMEM((2, TILES, 2 * HEADS, block), f32), bias, rows_wide, rows_wide,
+            row_sems, pltpu.SemaphoreType.DMA((2, TILES, 3)), pltpu.SemaphoreType.DMA((6,)),
         ],
         compiler_params=params,
         cost_estimate=cost(5),

time: 108 us -> 89.4 us (0.83)
  local copies, waits for them, and re-layouts: 15.7 us -> 3.77 us
  starting transfers between devices: 30.3 us -> 21.7 us
  Pallas kernels: 13.3 us -> 21.2 us
  waiting for transfers between devices: 45.2 us -> 39.9 us
    unnamed x53 -> x30, local copies, waits for them, and re-layouts: 14.1 us -> 2.58 us
    all_to_all x1, starting transfers between devices: 9.54 us -> 3.98 us  [local(): stats_all = lax.all_to_all(stats, ('reader', 'blk'), 0, 0, tiled=True)]
    ppermute x22 -> x21, waiting for transfers between devices: 36.6 us -> 31.8 us  [swap(): return lax.ppermute(block, axes, [(i, i ^ mask) for i in range(count)])]
    pallas_call x1, Pallas kernels: 3.85 us -> 7.07 us  [local(): pl.pallas_call(functools.partial(query_kernel, sizes), out_shape=(own, sh...]
    ppermute x22 -> x21, starting transfers between devices: 20.8 us -> 17.7 us  [swap(): return lax.ppermute(block, axes, [(i, i ^ mask) for i in range(count)])]
    pallas_call x1, Pallas kernels: 2.58 us -> 5.43 us  [local(): pl.pallas_call(functools.partial(prepare_kernel, sizes), out_shape=(shape...]
  transfers between devices with their start and end apart: 23 -> 22, of which waited for: 9 -> 8; matrix products, arithmetic and copies ran while one was open for 5% -> 2% of each run, Pallas kernels for 8% -> 17%
where the time goes in v4:
time: 89.4 us; the launch traced here: 88.5 us
  waiting for transfers between devices  39.9 us (45%)
  starting transfers between devices  21.7 us (24%)
  Pallas kernels  21.2 us (24%)
  local copies, waits for them, and re-layouts  3.77 us (4%)
  between operations  1.63 us (2%)
    ppermute x21, waiting for transfers between devices, swap(): return lax.ppermute(block, axes, [(i, i ^ mask) for i in range(count)])  31.8 us
    ppermute x21, starting transfers between devices, swap(): return lax.ppermute(block, axes, [(i, i ^ mask) for i in range(count)])  17.7 us
    all_to_all x1, waiting for transfers between devices, local(): stats_all = lax.all_to_all(stats, ('reader', 'blk'), 0, 0, tiled=True)  8.09 us
    pallas_call x1, Pallas kernels, local(): pl.pallas_call(functools.partial(query_kernel, sizes), out_shape=(own, sh...  7.07 us
    pallas_call x1, Pallas kernels, local(): pl.pallas_call(functools.partial(prepare_kernel, sizes), out_shape=(shape...  5.43 us
    pallas_call x1, Pallas kernels, local(): pl.pallas_call(functools.partial(key_grad_kernel, sizes, bits), out_shape...  4.84 us
    all_to_all x1, starting transfers between devices, local(): stats_all = lax.all_to_all(stats, ('reader', 'blk'), 0, 0, tiled=True)  3.98 us
    unnamed x30, local copies, waits for them, and re-layouts  2.58 us
  transfers between devices with their start and end apart: 22, of which 8 were waited for; matrix products, arithmetic and copies ran while one was open for 2% of the time, Pallas kernels for 17%

profile of v4, /device:TPU:0, one launch (start us, length us, event | category | flops | bytes accessed | tf_op | source)
XLA Modules:
  0.0 88.5 jit_solution(2006992989457472602)
XLA Ops:
  1.3 0.0 copy-start.8
  1.3 1.6 %pack.1 = bf16[1,144,512]{2,1,0:T(8,128)(2,1)} custom-call(bf16[128,512]{1,0:T(8,128)(2,1)} %own_ref.3, s32[1,3,1,8]{3,2,1,0:T(1,128)} %bitcast.14, s32[1,1]{1,0:T(1,128)S(6)} %copy.18.count_hbm), custom_call_target="tpu_custom_call" | custom-call | tf_op jit(solution)/shard_map/pack/pallas_call | solution.py:468
  2.9 0.0 copy-start.10
  2.9 5.1 %collective-permute-start.2 = (bf16[1,144,512]{2,1,0:T(8,128)(2,1)}, bf16[1,144,512]{2,1,0:T(8,128)(2,1)S(1)}, u32[]{:S(2)}, u32[]{:S(2)}) collective-permute-start(bf16[1,144,512]{2,1,0:T(8,128)(2,1)} %pack.1), channel_id=1, source_target_pairs={{0,6},{1,7},{2,4},{3,5},{4,2},{5,3},{6,0},{7,1},{8,14},{9,15},{10,... | collective-permute-start | bytes 442376 | tf_op jit(solution)/shard_map/ppermute | solution.py:436
  8.0 0.0 collective-permute-start.1
  8.0 0.6 collective-permute-start
  8.7 0.0 copy-done.8
  8.7 1.7 %collective-permute-start.12 = (bf16[1,64,512]{2,1,0:T(8,128)(2,1)S(1)}, bf16[1,64,512]{2,1,0:T(8,128)(2,1)S(1)}, u32[]{:S(2)}, u32[]{:S(2)}) collective-permute-start(bf16[1,64,512]{2,1,0:T(8,128)(2,1)S(1)} %get-tuple-element.55), channel_id=1, source_target_pairs={{0,16},{1,17},{2,18},{3,19},{4,20},{5,21},{6,22},{7,23},{8,24},{9,... | collective-permute-start | bytes 196616 | tf_op jit(solution)/shard_map/ppermute | solution.py:436
  10.4 1.5 %collective-permute-start.11 = (bf16[1,64,512]{2,1,0:T(8,128)(2,1)S(1)}, bf16[1,64,512]{2,1,0:T(8,128)(2,1)S(1)}, u32[]{:S(2)}, u32[]{:S(2)}) collective-permute-start(bf16[1,64,512]{2,1,0:T(8,128)(2,1)S(1)} %get-tuple-element.54), channel_id=1, source_target_pairs={{0,8},{1,9},{2,10},{3,11},{4,12},{5,13},{6,14},{7,15},{8,0},{9,1},... | collective-permute-start | bytes 196616 | tf_op jit(solution)/shard_map/ppermute | solution.py:436
  12.0 5.9 %collective-permute-done = bf16[1,144,512]{2,1,0:T(8,128)(2,1)S(1)} collective-permute-done((bf16[1,144,512]{2,1,0:T(8,128)(2,1)}, bf16[1,144,512]{2,1,0:T(8,128)(2,1)S(1)}, u32[]{:S(2)}, u32[]{:S(2)}) %collective-permute-start) | collective-permute-done | bytes 147488 | tf_op jit(solution)/shard_map/ppermute | solution.py:436
  17.9 2.8 %collective-permute-done.1 = bf16[1,144,512]{2,1,0:T(8,128)(2,1)S(1)} collective-permute-done((bf16[1,144,512]{2,1,0:T(8,128)(2,1)}, bf16[1,144,512]{2,1,0:T(8,128)(2,1)S(1)}, u32[]{:S(2)}, u32[]{:S(2)}) %collective-permute-start.1) | collective-permute-done | bytes 147488 | tf_op jit(solution)/shard_map/ppermute | solution.py:436
  20.7 0.0 collective-permute-done.2
  20.8 1.6 %collective-permute-start.3 = (bf16[4,80,512]{2,1,0:T(8,128)(2,1)S(1)}, bf16[4,80,512]{2,1,0:T(8,128)(2,1)S(1)}, u32[]{:S(2)}, u32[]{:S(2)}) collective-permute-start(bf16[4,80,512]{2,1,0:T(8,128)(2,1)S(1)} %pad_maximum_fusion.2), channel_id=1, source_target_pairs={{0,16},{1,17},{2,18},{3,19},{4,20},{5,21},{6,22},{7,23},{8,24},{9,... | collective-permute-start | bytes 983048 | tf_op jit(solution)/shard_map/ppermute | solution.py:436
  22.5 1.6 %collective-permute-start.5 = (bf16[4,64,512]{2,1,0:T(8,128)(2,1)S(1)}, bf16[4,64,512]{2,1,0:T(8,128)(2,1)S(1)}, u32[]{:S(2)}, u32[]{:S(2)}) collective-permute-start(bf16[4,64,512]{2,1,0:T(8,128)(2,1)S(1)} %pad_maximum_fusion.3), channel_id=1, source_target_pairs={{0,8},{1,9},{2,10},{3,11},{4,12},{5,13},{6,14},{7,15},{8,0},{9,1},... | collective-permute-start | bytes 786440 | tf_op jit(solution)/shard_map/ppermute | solution.py:436
  24.1 0.0 collective-permute-done.12
  24.1 0.0 collective-permute-done.11
  24.1 0.1 collective-permute-start.13
  24.2 5.5 %collective-permute-done.3 = bf16[4,80,512]{2,1,0:T(8,128)(2,1)S(1)} collective-permute-done((bf16[4,80,512]{2,1,0:T(8,128)(2,1)S(1)}, bf16[4,80,512]{2,1,0:T(8,128)(2,1)S(1)}, u32[]{:S(2)}, u32[]{:S(2)}) %collective-permute-start.3) | collective-permute-done | bytes 327712 | tf_op jit(solution)/shard_map/ppermute | solution.py:436
  29.7 1.6 %collective-permute-start.9 = (bf16[8,80,512]{2,1,0:T(8,128)(2,1)S(1)}, bf16[8,80,512]{2,1,0:T(8,128)(2,1)S(1)}, u32[]{:S(2)}, u32[]{:S(2)}) collective-permute-start(bf16[8,80,512]{2,1,0:T(8,128)(2,1)S(1)} %constant_dynamic-update-slice_fusion.line_ref.refs_4_.here_ref), channel_id=1, source_target_pairs={{0,8},{1,9},{2,10},{3,11},{4,12},{5,13},{6,14},{7,15},{8,0},{9,1},... | collective-permute-start | bytes 1966088 | tf_op jit(solution)/shard_map/ppermute | solution.py:436
  31.3 0.0 collective-permute-done.5
  31.3 0.0 copy-start.4
  31.3 1.6 %collective-permute-start.6 = (bf16[8,64,512]{2,1,0:T(8,128)(2,1)S(1)}, bf16[8,64,512]{2,1,0:T(8,128)(2,1)S(1)}, u32[]{:S(2)}, u32[]{:S(2)}) collective-permute-start(bf16[8,64,512]{2,1,0:T(8,128)(2,1)S(1)} %constant_dynamic-update-slice_fusion.5.refs_0_), channel_id=1, source_target_pairs={{0,16},{1,17},{2,18},{3,19},{4,20},{5,21},{6,22},{7,23},{8,24},{9,... | collective-permute-start | bytes 1572872 | tf_op jit(solution)/shard_map/ppermute | solution.py:436
  32.9 4.3 %collective-permute-done.13 = bf16[1,4,64,512]{3,2,1,0:T(8,128)(2,1)S(1)} collective-permute-done((bf16[1,4,64,512]{3,2,1,0:T(8,128)(2,1)S(1)}, bf16[1,4,64,512]{3,2,1,0:T(8,128)(2,1)S(1)}, u32[]{:S(2)}, u32[]{:S(2)}) %collective-permute-start.13) | collective-permute-done | bytes 262176 | tf_op jit(solution)/shard_map/ppermute | solution.py:436
  37.2 0.1 pad_maximum_fusion.1
  37.2 0.1 collective-permute-start.14
  37.3 0.1 collective-permute-start.4
  37.4 0.5 collective-permute-start.7
  37.9 5.2 %collective-permute-done.6.refs_1_ = bf16[8,64,512]{2,1,0:T(8,128)(2,1)S(1)} collective-permute-done((bf16[8,64,512]{2,1,0:T(8,128)(2,1)S(1)}, bf16[8,64,512]{2,1,0:T(8,128)(2,1)S(1)}, u32[]{:S(2)}, u32[]{:S(2)}) %collective-permute-start.6) | collective-permute-done | bytes 524320 | tf_op jit(solution)/shard_map/ppermute | solution.py:436
  43.1 0.0 collective-permute-start.8
  43.1 1.5 %collective-permute-done.9.refs_5_.there_ref = bf16[8,80,512]{2,1,0:T(8,128)(2,1)S(1)} collective-permute-done((bf16[8,80,512]{2,1,0:T(8,128)(2,1)S(1)}, bf16[8,80,512]{2,1,0:T(8,128)(2,1)S(1)}, u32[]{:S(2)}, u32[]{:S(2)}) %collective-permute-start.9) | collective-permute-done | bytes 655392 | tf_op jit(solution)/shard_map/ppermute | solution.py:436
  44.6 0.0 collective-permute-start.10
  44.6 6.5 %collective-permute-done.14 = bf16[2,4,64,512]{3,2,1,0:T(8,128)(2,1)S(1)} collective-permute-done((bf16[2,4,64,512]{3,2,1,0:T(8,128)(2,1)S(1)}, bf16[2,4,64,512]{3,2,1,0:T(8,128)(2,1)S(1)}, u32[]{:S(2)}, u32[]{:S(2)}) %collective-permute-start.14) | collective-permute-done | bytes 524320 | tf_op jit(solution)/shard_map/ppermute | solution.py:436
  51.1 0.1 pad_maximum_fusion
  51.3 1.0 %fusion = (bf16[4,2,64,512]{3,2,1,0:T(8,128)(2,1)}, bf16[4,2,64,512]{3,2,1,0:T(8,128)(2,1)}) fusion(bf16[4,4,64,512]{3,2,1,0:T(8,128)(2,1)S(1)} %pad_maximum_fusion), kind=kLoop, calls=%fused_computation.17 | loop fusion | bytes 2097152 | tf_op jit(solution)/shard_map/slice | solution.py:501
  52.3 0.5 collective-permute-start.15
  52.8 0.0 collective-permute-done.4.line_other_ref.refs_6_
  52.8 0.5 collective-permute-start.18
  53.4 0.3 copy-done.2
  53.7 5.4 %prepare.1 = (s32[133]{0:T(256)}, bf16[4,256,128]{2,1,0:T(8,128)(2,1)}, bf16[4,256,128]{2,1,0:T(8,128)(2,1)}, bf16[128,512]{1,0:T(8,128)(2,1)}, bf16[128,512]{1,...) custom-call(bf16[128,512]{1,0:T(8,128)(2,1)} %own_ref.3, bf16[128,512]{1,0:T(8,128)(2,1)} %cot_hbm.1, ...), custom_call_target="tpu_custom_call" | custom-call | flops 400000000 | bytes 4000000 | tf_op jit(solution)/shard_map/prepare/pallas_call | solution.py:517
  59.1 0.0 collective-permute-done.7.refs_2_
  59.2 0.0 collective-permute-done.8.refs_3_
  59.2 0.0 collective-permute-done.10.refs_7_
  59.2 0.0 copy-start.3
  59.2 0.1 collective-permute-start.16
  59.3 0.7 copy-done.6
  60.0 0.2 copy-done.7
  60.2 0.2 copy-done.3
  60.4 7.1 %query_side.1 = (bf16[128,512]{1,0:T(8,128)(2,1)}, f32[32,16,128]{2,1,0:T(8,128)}, f32[128,512]{1,0:T(8,128)}) custom-call(s32[133]{0:T(256)} %get-tuple-element.19.work_ref, bf16[4,256,128]{2,1,0:T(8,128)(2,1)} %get-tuple-element.20.stack_hbm, bf16[4,256,128]{2,1,0:T(8,128)(2,1)} %get-tuple-element.21.cot_stack_hbm, bf16[128,512]{1,0:T(8,128)(2,1)} %cot_hbm.1, ...), custom_call_target="tpu_custom_call" | custom-call | flops 2000000000 | bytes 4000000 | tf_op jit(solution)/shard_map/query_side/pallas_call | solution.py:550
  67.5 0.0 collective-permute-done.15.refs_9_
  67.5 0.1 collective-permute-start.17
  67.6 0.5 collective-permute-start.19
  68.1 0.0 collective-permute-done.18.refs_13_
  68.1 0.1 collective-permute-start.20
  68.2 4.0 %all-to-all-start = ((f32[32,16,128]{2,1,0:T(8,128)}), f32[32,16,128]{2,1,0:T(8,128)S(1)}, u32[]{:S(2)}, u32[]{:S(2)}) async-start(f32[32,16,128]{2,1,0:T(8,128)} %get-tuple-element.28), calls=%async_computation | async-start | bytes 524288 | tf_op jit(solution)/shard_map/all_to_all | solution.py:567
  72.2 2.3 %key_list.1.work_ref = s32[69]{0:T(128)} custom-call(bf16[8,80,512]{2,1,0:T(8,128)(2,1)} %copy-done, bf16[8,80,512]{2,1,0:T(8,128)(2,1)} %copy-done.1), custom_call_target="tpu_custom_call" | custom-call | flops 200000000 | bytes 4000000 | tf_op jit(solution)/shard_map/key_list/pallas_call | solution.py:528
  74.5 8.1 %all-to-all-done.stats_all_ref = f32[32,16,128]{2,1,0:T(8,128)S(1)} async-done(((f32[32,16,128]{2,1,0:T(8,128)}), f32[32,16,128]{2,1,0:T(8,128)S(1)}, u32[]{:S(2)}, u32[]{:S(2)}) %all-to-all-start) | async-done | bytes 262176 | tf_op jit(solution)/shard_map/all_to_all | solution.py:567
  82.5 0.0 collective-permute-done.16.refs_10_
  82.5 0.0 collective-permute-done.17.refs_11_
  82.6 0.0 collective-permute-done.19.refs_14_
  82.6 0.0 collective-permute-done.20.refs_15_
  82.6 0.7 copy-done.9
  83.3 0.2 copy-done.13
  83.5 0.2 copy-done.14
  83.7 4.8 %key_grad.1 = bf16[128,512]{1,0:T(8,128)(2,1)} custom-call(s32[69]{0:T(128)} %key_list.1.work_ref, bf16[128,512]{1,0:T(8,128)(2,1)} %get-tuple-element.25.key_hbm, bf16[128,512]{1,0:T(8,128)(2,1)} %get-tuple-element.26.value_hbm, bf16[512,512]{1,0:T(8,128)(2,1)} %wq_hbm.3, bf16[512,512]{1,0:T(8,128)(2,1)} %wk_hbm.3, bf16[512,512]{1,0:T(8,128)(2,1)} %wv_hbm.3, ...), custom_call_target="tpu_custom_call" | custom-call | flops 1000000000 | bytes 4000000 | tf_op jit(solution)/shard_map/key_grad/pallas_call | solution.py:569
  (32 shorter events, 0.3 us)
Async XLA Ops:
  1.3 7.4 %copy-start.8 = (bf16[128,512]{1,0:T(8,128)(2,1)S(1)}, bf16[128,512]{1,0:T(8,128)(2,1)}, u32[]{:S(2)}) copy-start(bf16[128,512]{1,0:T(8,128)(2,1)} %cot_hbm.1) | copy-start | bytes 393220
  2.9 9.0 %copy-start.10 = (bf16[1,144,512]{2,1,0:T(8,128)(2,1)S(1)}, bf16[1,144,512]{2,1,0:T(8,128)(2,1)}, u32[]{:S(2)}) copy-start(bf16[1,144,512]{2,1,0:T(8,128)(2,1)} %pack.1) | copy-start | bytes 442372
  2.9 17.8 %collective-permute-start.2 = (bf16[1,144,512]{2,1,0:T(8,128)(2,1)}, bf16[1,144,512]{2,1,0:T(8,128)(2,1)S(1)}, u32[]{:S(2)}, u32[]{:S(2)}) collective-permute-start(bf16[1,144,512]{2,1,0:T(8,128)(2,1)} %pack.1), channel_id=1, source_target_pairs={{0,6},{1,7},{2,4},{3,5},{4,2},{5,3},{6,0},{7,1},{8,14},{9,15},{10,... | collective-permute-start | bytes 442376 | tf_op jit(solution)/shard_map/ppermute | solution.py:436
  8.0 12.7 %collective-permute-start.1 = (bf16[1,144,512]{2,1,0:T(8,128)(2,1)}, bf16[1,144,512]{2,1,0:T(8,128)(2,1)S(1)}, u32[]{:S(2)}, u32[]{:S(2)}) collective-permute-start(bf16[1,144,512]{2,1,0:T(8,128)(2,1)} %pack.1), channel_id=1, source_target_pairs={{0,4},{1,5},{2,6},{3,7},{4,0},{5,1},{6,2},{7,3},{8,12},{9,13},{10,... | collective-permute-start | bytes 442376 | tf_op jit(solution)/shard_map/ppermute | solution.py:436
  8.0 9.8 %collective-permute-start = (bf16[1,144,512]{2,1,0:T(8,128)(2,1)}, bf16[1,144,512]{2,1,0:T(8,128)(2,1)S(1)}, u32[]{:S(2)}, u32[]{:S(2)}) collective-permute-start(bf16[1,144,512]{2,1,0:T(8,128)(2,1)} %pack.1), channel_id=1, source_target_pairs={{0,2},{1,3},{2,0},{3,1},{4,6},{5,7},{6,4},{7,5},{8,10},{9,11},{10,... | collective-permute-start | bytes 442376 | tf_op jit(solution)/shard_map/ppermute | solution.py:436
  8.7 15.4 %collective-permute-start.12 = (bf16[1,64,512]{2,1,0:T(8,128)(2,1)S(1)}, bf16[1,64,512]{2,1,0:T(8,128)(2,1)S(1)}, u32[]{:S(2)}, u32[]{:S(2)}) collective-permute-start(bf16[1,64,512]{2,1,0:T(8,128)(2,1)S(1)} %get-tuple-element.55), channel_id=1, source_target_pairs={{0,16},{1,17},{2,18},{3,19},{4,20},{5,21},{6,22},{7,23},{8,24},{9,... | collective-permute-start | bytes 196616 | tf_op jit(solution)/shard_map/ppermute | solution.py:436
  10.4 13.6 %collective-permute-start.11 = (bf16[1,64,512]{2,1,0:T(8,128)(2,1)S(1)}, bf16[1,64,512]{2,1,0:T(8,128)(2,1)S(1)}, u32[]{:S(2)}, u32[]{:S(2)}) collective-permute-start(bf16[1,64,512]{2,1,0:T(8,128)(2,1)S(1)} %get-tuple-element.54), channel_id=1, source_target_pairs={{0,8},{1,9},{2,10},{3,11},{4,12},{5,13},{6,14},{7,15},{8,0},{9,1},... | collective-permute-start | bytes 196616 | tf_op jit(solution)/shard_map/ppermute | solution.py:436
  20.8 8.8 %collective-permute-start.3 = (bf16[4,80,512]{2,1,0:T(8,128)(2,1)S(1)}, bf16[4,80,512]{2,1,0:T(8,128)(2,1)S(1)}, u32[]{:S(2)}, u32[]{:S(2)}) collective-permute-start(bf16[4,80,512]{2,1,0:T(8,128)(2,1)S(1)} %pad_maximum_fusion.2), channel_id=1, source_target_pairs={{0,16},{1,17},{2,18},{3,19},{4,20},{5,21},{6,22},{7,23},{8,24},{9,... | collective-permute-start | bytes 983048 | tf_op jit(solution)/shard_map/ppermute | solution.py:436
  22.5 8.7 %collective-permute-start.5 = (bf16[4,64,512]{2,1,0:T(8,128)(2,1)S(1)}, bf16[4,64,512]{2,1,0:T(8,128)(2,1)S(1)}, u32[]{:S(2)}, u32[]{:S(2)}) collective-permute-start(bf16[4,64,512]{2,1,0:T(8,128)(2,1)S(1)} %pad_maximum_fusion.3), channel_id=1, source_target_pairs={{0,8},{1,9},{2,10},{3,11},{4,12},{5,13},{6,14},{7,15},{8,0},{9,1},... | collective-permute-start | bytes 786440 | tf_op jit(solution)/shard_map/ppermute | solution.py:436
  24.1 13.1 %collective-permute-start.13 = (bf16[1,4,64,512]{3,2,1,0:T(8,128)(2,1)S(1)}, bf16[1,4,64,512]{3,2,1,0:T(8,128)(2,1)S(1)}, u32[]{:S(2)}, u32[]{:S(2)}) collective-permute-start(bf16[1,4,64,512]{3,2,1,0:T(8,128)(2,1)S(1)} %bitcast.9), channel_id=1, source_target_pairs={{0,4},{1,5},{2,6},{3,7},{4,0},{5,1},{6,2},{7,3},{8,12},{9,13},{10,... | collective-permute-start | bytes 786440 | tf_op jit(solution)/shard_map/ppermute | solution.py:436
  29.7 7.6 %copy-start = (bf16[8,80,512]{2,1,0:T(8,128)(2,1)}, bf16[8,80,512]{2,1,0:T(8,128)(2,1)S(1)}, u32[]{:S(2)}) copy-start(bf16[8,80,512]{2,1,0:T(8,128)(2,1)S(1)} %constant_dynamic-update-slice_fusion.line_ref.refs_4_.here_ref) | copy-start | bytes 1966084
  29.7 14.9 %collective-permute-start.9 = (bf16[8,80,512]{2,1,0:T(8,128)(2,1)S(1)}, bf16[8,80,512]{2,1,0:T(8,128)(2,1)S(1)}, u32[]{:S(2)}, u32[]{:S(2)}) collective-permute-start(bf16[8,80,512]{2,1,0:T(8,128)(2,1)S(1)} %constant_dynamic-update-slice_fusion.line_ref.refs_4_.here_ref), channel_id=1, source_target_pairs={{0,8},{1,9},{2,10},{3,11},{4,12},{5,13},{6,14},{7,15},{8,0},{9,1},... | collective-permute-start | bytes 1966088 | tf_op jit(solution)/shard_map/ppermute | solution.py:436
  31.3 20.0 %copy-start.4 = (bf16[8,64,512]{2,1,0:T(8,128)(2,1)}, bf16[8,64,512]{2,1,0:T(8,128)(2,1)S(1)}, u32[]{:S(2)}) copy-start(bf16[8,64,512]{2,1,0:T(8,128)(2,1)S(1)} %constant_dynamic-update-slice_fusion.5.refs_0_) | copy-start | bytes 1572868
  31.3 11.8 %collective-permute-start.6 = (bf16[8,64,512]{2,1,0:T(8,128)(2,1)S(1)}, bf16[8,64,512]{2,1,0:T(8,128)(2,1)S(1)}, u32[]{:S(2)}, u32[]{:S(2)}) collective-permute-start(bf16[8,64,512]{2,1,0:T(8,128)(2,1)S(1)} %constant_dynamic-update-slice_fusion.5.refs_0_), channel_id=1, source_target_pairs={{0,16},{1,17},{2,18},{3,19},{4,20},{5,21},{6,22},{7,23},{8,24},{9,... | collective-permute-start | bytes 1572872 | tf_op jit(solution)/shard_map/ppermute | solution.py:436
  37.2 13.9 %collective-permute-start.14 = (bf16[2,4,64,512]{3,2,1,0:T(8,128)(2,1)S(1)}, bf16[2,4,64,512]{3,2,1,0:T(8,128)(2,1)S(1)}, u32[]{:S(2)}, u32[]{:S(2)}) collective-permute-start(bf16[2,4,64,512]{3,2,1,0:T(8,128)(2,1)S(1)} %pad_maximum_fusion.1), channel_id=1, source_target_pairs={{0,2},{1,3},{2,0},{3,1},{4,6},{5,7},{6,4},{7,5},{8,10},{9,11},{10,... | collective-permute-start | bytes 1572872 | tf_op jit(solution)/shard_map/ppermute | solution.py:436
  37.3 15.5 %collective-permute-start.4 = (bf16[8,80,512]{2,1,0:T(8,128)(2,1)S(1)}, bf16[8,80,512]{2,1,0:T(8,128)(2,1)S(1)}, u32[]{:S(2)}, u32[]{:S(2)}) collective-permute-start(bf16[8,80,512]{2,1,0:T(8,128)(2,1)S(1)} %constant_dynamic-update-slice_fusion.line_ref.refs_4_.here_ref), channel_id=1, source_target_pairs={{0,1},{1,0},{2,3},{3,2},{4,5},{5,4},{6,7},{7,6},{8,9},{9,8},{10,11... | collective-permute-start | bytes 1966088 | tf_op jit(solution)/shard_map/ppermute | solution.py:436
  37.4 21.7 %collective-permute-start.7 = (bf16[8,64,512]{2,1,0:T(8,128)(2,1)S(1)}, bf16[8,64,512]{2,1,0:T(8,128)(2,1)S(1)}, u32[]{:S(2)}, u32[]{:S(2)}) collective-permute-start(bf16[8,64,512]{2,1,0:T(8,128)(2,1)S(1)} %constant_dynamic-update-slice_fusion.5.refs_0_), channel_id=1, source_target_pairs={{0,1},{1,0},{2,3},{3,2},{4,5},{5,4},{6,7},{7,6},{8,9},{9,8},{10,11... | collective-permute-start | bytes 1572872 | tf_op jit(solution)/shard_map/ppermute | solution.py:436
  43.1 8.1 %copy-start.5 = (bf16[8,64,512]{2,1,0:T(8,128)(2,1)}, bf16[8,64,512]{2,1,0:T(8,128)(2,1)S(1)}, u32[]{:S(2)}) copy-start(bf16[8,64,512]{2,1,0:T(8,128)(2,1)S(1)} %collective-permute-done.6.refs_1_) | copy-start | bytes 1572868
  43.1 16.0 %collective-permute-start.8 = (bf16[8,64,512]{2,1,0:T(8,128)(2,1)S(1)}, bf16[8,64,512]{2,1,0:T(8,128)(2,1)S(1)}, u32[]{:S(2)}, u32[]{:S(2)}) collective-permute-start(bf16[8,64,512]{2,1,0:T(8,128)(2,1)S(1)} %collective-permute-done.6.refs_1_), channel_id=1, source_target_pairs={{0,1},{1,0},{2,3},{3,2},{4,5},{5,4},{6,7},{7,6},{8,9},{9,8},{10,11... | collective-permute-start | bytes 1572872 | tf_op jit(solution)/shard_map/ppermute | solution.py:436
  44.6 6.7 %copy-start.1 = (bf16[8,80,512]{2,1,0:T(8,128)(2,1)}, bf16[8,80,512]{2,1,0:T(8,128)(2,1)S(1)}, u32[]{:S(2)}) copy-start(bf16[8,80,512]{2,1,0:T(8,128)(2,1)S(1)} %collective-permute-done.9.refs_5_.there_ref) | copy-start | bytes 1966084
  44.6 14.6 %collective-permute-start.10 = (bf16[8,80,512]{2,1,0:T(8,128)(2,1)S(1)}, bf16[8,80,512]{2,1,0:T(8,128)(2,1)S(1)}, u32[]{:S(2)}, u32[]{:S(2)}) collective-permute-start(bf16[8,80,512]{2,1,0:T(8,128)(2,1)S(1)} %collective-permute-done.9.refs_5_.there_ref), channel_id=1, source_target_pairs={{0,1},{1,0},{2,3},{3,2},{4,5},{5,4},{6,7},{7,6},{8,9},{9,8},{10,11... | collective-permute-start | bytes 1966088 | tf_op jit(solution)/shard_map/ppermute | solution.py:436
  52.3 15.2 %collective-permute-start.15 = (bf16[8,64,512]{2,1,0:T(8,128)(2,1)}, bf16[8,64,512]{2,1,0:T(8,128)(2,1)S(1)}, u32[]{:S(2)}, u32[]{:S(2)}) collective-permute-start(bf16[8,64,512]{2,1,0:T(8,128)(2,1)} %bitcast.5.refs_8_), channel_id=1, source_target_pairs={{0,16},{1,17},{2,18},{3,19},{4,20},{5,21},{6,22},{7,23},{8,24},{9,... | collective-permute-start | bytes 1572872 | tf_op jit(solution)/shard_map/ppermute | solution.py:436
  52.8 0.9 copy-start.2
  52.8 15.2 %collective-permute-start.18 = (bf16[8,64,512]{2,1,0:T(8,128)(2,1)}, bf16[8,64,512]{2,1,0:T(8,128)(2,1)S(1)}, u32[]{:S(2)}, u32[]{:S(2)}) collective-permute-start(bf16[8,64,512]{2,1,0:T(8,128)(2,1)} %bitcast.6.refs_12_), channel_id=1, source_target_pairs={{0,8},{1,9},{2,10},{3,11},{4,12},{5,13},{6,14},{7,15},{8,0},{9,1},... | collective-permute-start | bytes 1572872 | tf_op jit(solution)/shard_map/ppermute | solution.py:436
  59.2 0.8 copy-start.6
  59.2 1.0 %copy-start.7 = (bf16[8,64,512]{2,1,0:T(8,128)(2,1)}, bf16[8,64,512]{2,1,0:T(8,128)(2,1)S(1)}, u32[]{:S(2)}) copy-start(bf16[8,64,512]{2,1,0:T(8,128)(2,1)S(1)} %collective-permute-done.8.refs_3_) | copy-start | bytes 1572868
  59.2 1.2 %copy-start.3 = (bf16[8,80,512]{2,1,0:T(8,128)(2,1)}, bf16[8,80,512]{2,1,0:T(8,128)(2,1)S(1)}, u32[]{:S(2)}) copy-start(bf16[8,80,512]{2,1,0:T(8,128)(2,1)S(1)} %collective-permute-done.10.refs_7_) | copy-start | bytes 1966084
  59.2 23.3 %collective-permute-start.16 = (bf16[8,64,512]{2,1,0:T(8,128)(2,1)}, bf16[8,64,512]{2,1,0:T(8,128)(2,1)S(1)}, u32[]{:S(2)}, u32[]{:S(2)}) collective-permute-start(bf16[8,64,512]{2,1,0:T(8,128)(2,1)} %bitcast.5.refs_8_), channel_id=1, source_target_pairs={{0,1},{1,0},{2,3},{3,2},{4,5},{5,4},{6,7},{7,6},{8,9},{9,8},{10,11... | collective-permute-start | bytes 1572872 | tf_op jit(solution)/shard_map/ppermute | solution.py:436
  67.5 6.9 %copy-start.11 = (bf16[8,64,512]{2,1,0:T(8,128)(2,1)}, bf16[8,64,512]{2,1,0:T(8,128)(2,1)S(1)}, u32[]{:S(2)}) copy-start(bf16[8,64,512]{2,1,0:T(8,128)(2,1)S(1)} %collective-permute-done.15.refs_9_) | copy-start | bytes 1572868
  67.5 15.0 %collective-permute-start.17 = (bf16[8,64,512]{2,1,0:T(8,128)(2,1)S(1)}, bf16[8,64,512]{2,1,0:T(8,128)(2,1)S(1)}, u32[]{:S(2)}, u32[]{:S(2)}) collective-permute-start(bf16[8,64,512]{2,1,0:T(8,128)(2,1)S(1)} %collective-permute-done.15.refs_9_), channel_id=1, source_target_pairs={{0,1},{1,0},{2,3},{3,2},{4,5},{5,4},{6,7},{7,6},{8,9},{9,8},{10,11... | collective-permute-start | bytes 1572872 | tf_op jit(solution)/shard_map/ppermute | solution.py:436
  67.6 15.0 %collective-permute-start.19 = (bf16[8,64,512]{2,1,0:T(8,128)(2,1)}, bf16[8,64,512]{2,1,0:T(8,128)(2,1)}, u32[]{:S(2)}, u32[]{:S(2)}) collective-permute-start(bf16[8,64,512]{2,1,0:T(8,128)(2,1)} %bitcast.6.refs_12_), channel_id=1, source_target_pairs={{0,1},{1,0},{2,3},{3,2},{4,5},{5,4},{6,7},{7,6},{8,9},{9,8},{10,11... | collective-permute-start | bytes 1572872 | tf_op jit(solution)/shard_map/ppermute | solution.py:436
  68.1 6.4 %copy-start.12 = (bf16[8,64,512]{2,1,0:T(8,128)(2,1)}, bf16[8,64,512]{2,1,0:T(8,128)(2,1)S(1)}, u32[]{:S(2)}) copy-start(bf16[8,64,512]{2,1,0:T(8,128)(2,1)S(1)} %collective-permute-done.18.refs_13_) | copy-start | bytes 1572868
  68.1 14.5 %collective-permute-start.20 = (bf16[8,64,512]{2,1,0:T(8,128)(2,1)S(1)}, bf16[8,64,512]{2,1,0:T(8,128)(2,1)}, u32[]{:S(2)}, u32[]{:S(2)}) collective-permute-start(bf16[8,64,512]{2,1,0:T(8,128)(2,1)S(1)} %collective-permute-done.18.refs_13_), channel_id=1, source_target_pairs={{0,1},{1,0},{2,3},{3,2},{4,5},{5,4},{6,7},{7,6},{8,9},{9,8},{10,11... | collective-permute-start | bytes 1572872 | tf_op jit(solution)/shard_map/ppermute | solution.py:436
  68.2 14.4 %all-to-all-start = ((f32[32,16,128]{2,1,0:T(8,128)}), f32[32,16,128]{2,1,0:T(8,128)S(1)}, u32[]{:S(2)}, u32[]{:S(2)}) async-start(f32[32,16,128]{2,1,0:T(8,128)} %get-tuple-element.28), calls=%async_computation | async-start | bytes 524288 | tf_op jit(solution)/shard_map/all_to_all | solution.py:567
  82.5 0.7 copy-start.9
  82.5 0.9 %copy-start.13 = (bf16[8,64,512]{2,1,0:T(8,128)(2,1)}, bf16[8,64,512]{2,1,0:T(8,128)(2,1)S(1)}, u32[]{:S(2)}) copy-start(bf16[8,64,512]{2,1,0:T(8,128)(2,1)S(1)} %collective-permute-done.16.refs_10_) | copy-start | bytes 1572868
  82.6 1.1 %copy-start.14 = (bf16[8,64,512]{2,1,0:T(8,128)(2,1)}, bf16[8,64,512]{2,1,0:T(8,128)(2,1)S(1)}, u32[]{:S(2)}) copy-start(bf16[8,64,512]{2,1,0:T(8,128)(2,1)S(1)} %collective-permute-done.17.refs_11_) | copy-start | bytes 1572868

commit v5 on v4

v5 whole, which is shorter than its diff:
```python
import functools

import jax
import jax.numpy as jnp
from jax import lax
from jax.experimental import pallas as pl
from jax.experimental.pallas import tpu as pltpu
from jax.sharding import PartitionSpec as P

HEADS = 8
NEG_FILL = -1e30
NT = (((1,), (1,)), ((), ()))
NN = (((1,), (0,)), ((), ()))
TILES = 2
VMEM_SOME = 40 * 1024 * 1024
VMEM_MOST = 58 * 1024 * 1024


def dot(a, b, dims=NN):
    return lax.dot_general(a, b, dims, preferred_element_type=jnp.float32)


def pair_stack(rows):
    lane = lax.broadcasted_iota(jnp.int32, rows.shape, 1)
    half = rows.shape[1] // 2
    zero = jnp.zeros_like(rows)
    return jnp.concatenate([jnp.where(lane < half, rows, zero), jnp.where(lane >= half, rows, zero)], 0)


def tile_bias(words, pattern, diag):
    count, size = words.shape
    keys = lax.broadcasted_iota(jnp.int32, (size, size), 0)
    queries = lax.broadcasted_iota(jnp.int32, (size, size), 1)
    spread = jnp.concatenate(
        [jnp.broadcast_to(words[g : g + 1], (size // count, size)) for g in range(count)], 0
    )
    bits = jnp.right_shift(spread, keys & 31) & 1
    same = keys - queries == jnp.where(diag, 0, 2 * size)
    return jnp.where((bits == 1) | same, jnp.where(pattern < 0, NEG_FILL, 0.0), NEG_FILL)


class Layout:
    def __init__(self, readers, blks, cap):
        self.readers, self.blks, self.cap = readers, blks, cap
        self.reader, self.blk = lax.axis_index("reader"), lax.axis_index("blk")
        self.me = self.reader * blks + self.blk

    def apart(self, device):
        far = jnp.bitwise_xor(device, self.me)
        reader, blk = far // self.blks, lax.rem(far, self.blks)
        return reader, blk // 2, blk & 1

    def row_place(self, order, device):
        reader, line, core = self.apart(device)
        for at, bit in enumerate(order[:-1]):
            line = line + (jnp.right_shift(reader, bit) & 1) * ((self.blks // 2) << at)
        return (jnp.right_shift(reader, order[-1]) & 1) + 2 * core, line

    def orders(self):
        return orders(self.readers)

    def half_place(self, bit, device):
        reader, line, core = self.apart(device)
        first = jnp.right_shift(reader, bit) & 1
        top = (self.blks // 2 - 1).bit_length() - 1
        line = sum((jnp.right_shift(line, top - at) & 1) << at for at in range(top + 1))
        low = reader & ((1 << bit) - 1)
        rest = low + (jnp.right_shift(reader, bit + 1) << bit)
        return rest + self.readers // 2 * core, 2 * line + first


def orders(readers):
    rising = tuple(range((readers - 1).bit_length()))
    return rising, rising[::-1]


def start_copy(place, refs, make):
    group, where = place
    for g, ref in enumerate(refs):

        @pl.when(group == g)
        def _():
            make(ref.at[where]).start()


def send_list_kernel(coords_hbm, count_hbm, out_ref, coords_ref, count_ref, sems):
    cap = coords_ref.shape[3]
    copies = [
        pltpu.make_async_copy(coords_hbm, coords_ref, sems.at[0]),
        pltpu.make_async_copy(count_hbm, count_ref, sems.at[1]),
    ]
    for copy in copies:
        copy.start()
    for copy in copies:
        copy.wait()
    lane = lax.broadcasted_iota(jnp.int32, out_ref.shape[1:], 1)
    row = jnp.zeros(lane.shape, jnp.int32)
    for column in range(3):
        for slot in range(cap):
            row = jnp.where(lane == column * cap + slot, coords_ref[0, column, 0, slot], row)
    row = jnp.where(lane == 3 * cap, count_ref[0, 0], row)
    out_ref[...] = jnp.broadcast_to(row[None], out_ref.shape)


def scan_list(lists_ref, cap, row, column, wanted, found, out_ref, block_of):
    def one_slot(slot, found):
        out_ref[2 * found + 1] = block_of(lists_ref[row, (1 - column) * cap + slot])
        out_ref[2 * found + 2] = lists_ref[row, 2 * cap + slot]
        return found + jnp.where(lists_ref[row, column * cap + slot] == wanted, 1, 0)

    return lax.fori_loop(0, lists_ref[row, 3 * cap], one_slot, found)


def close_work(found, out_ref):
    out_ref[2 * found + 1] = out_ref[2 * found - 1]
    out_ref[2 * found + 2] = -1
    out_ref[0] = (found + 1) // 2


def work_kernel(sizes, lists_hbm, query_work_ref, key_work_ref, lists_ref, sem):
    readers, blks, cap = sizes
    layout = Layout(*sizes)
    copy = pltpu.make_async_copy(lists_hbm, lists_ref, sem)
    copy.start()
    copy.wait()

    def query_side(blk, found):
        row = layout.reader * blks + blk
        put = lambda other: other * blks + blk
        return scan_list(lists_ref, cap, row, 0, layout.blk, found, query_work_ref, put)

    close_work(lax.fori_loop(0, blks, query_side, 0), query_work_ref)

    def key_side(reader, found):
        row = reader * blks + layout.blk
        put = lambda other: reader * blks + other
        return scan_list(lists_ref, cap, row, 1, layout.reader, found, key_work_ref, put)

    close_work(lax.fori_loop(0, readers, key_side, 0), key_work_ref)


def prepare_kernel(
    own_ref, cot_ref, wq_ref, wk_ref, wv_ref, query_stack_ref, cot_stack_ref, key_ref, value_ref, wkt_ref, wvt_ref
):
    head = own_ref.shape[1] // HEADS
    queries = dot(own_ref[...], wq_ref[...]).astype(jnp.bfloat16) * jnp.bfloat16(head**-0.5)
    for p in range(HEADS // 2):
        pair = slice(2 * head * p, 2 * head * (p + 1))
        query_stack_ref[p] = pair_stack(queries[:, pair])
        cot_stack_ref[p] = pair_stack(cot_ref[:, pair])
    key_ref[...] = dot(own_ref[...], wk_ref[...]).astype(jnp.bfloat16)
    value_ref[...] = dot(own_ref[...], wv_ref[...]).astype(jnp.bfloat16)
    wkt_ref[...] = wk_ref[...].T
    wvt_ref[...] = wv_ref[...].T


def step_entry(work_ref, index):
    at = 1 + 2 * TILES * index
    return [work_ref[at + 2 * t] for t in range(TILES)], [work_ref[at + 2 * t + 1] for t in range(TILES)]


def run_steps(work_ref, start, wait, body):
    total = work_ref[0]

    def step(index, carry):
        @pl.when(index + 1 < total)
        def _():
            start(lax.rem(index + 1, 2), *step_entry(work_ref, index + 1))

        slot = lax.rem(index, 2)
        wait(slot)
        body(slot, *step_entry(work_ref, index), index)
        return carry

    lax.fori_loop(0, total, step, 0)


def first_step(work_ref, start):
    start(0, *step_entry(work_ref, 0))


class Rows:
    def __init__(self, layout, groups, mask_ref, buf, words, sems, block):
        self.layout, self.halves, self.mask_ref = layout, (groups[:4], groups[4:]), mask_ref
        self.buf, self.words, self.sems, self.block = buf, words, sems, block

    def rows(self, slot, t, k):
        half = self.block // 2
        into = self.buf.at[slot, pl.ds(t * self.block + k * half, half)]
        return lambda src: pltpu.make_async_copy(src.at[pl.ds(0, half)], into, self.sems.at[slot, t, k])

    def mask(self, slot, t, pattern):
        return pltpu.make_async_copy(self.mask_ref.at[pattern], self.words.at[slot, t], self.sems.at[slot, t, 2])

    def start(self, slot, blocks, patterns):
        for t in range(TILES):
            for k, order in enumerate(self.layout.orders()):
                start_copy(self.layout.row_place(order, blocks[t]), self.halves[k], self.rows(slot, t, k))
            self.mask(slot, t, jnp.maximum(patterns[t], 0)).start()

    def wait(self, slot):
        for t in range(TILES):
            for k in range(2):
                self.rows(slot, t, k)(self.halves[k][0].at[0]).wait()
            self.mask(slot, t, 0).wait()

    def bias(self, slot, blocks, patterns):
        parts = [
            tile_bias(self.words[slot, t], patterns[t], blocks[t] == self.layout.me) for t in range(TILES)
        ]
        return jnp.concatenate(parts, 0)


def load(pairs, sems):
    copies = [pltpu.make_async_copy(src, into, sems.at[k]) for k, (src, into) in enumerate(pairs)]
    for copy in copies:
        copy.start()
    return copies


def forward_kernel(sizes, work_ref, stack_ref, cot_ref, wk_ref, wvt_ref, mask_ref, *refs):
    groups, refs = refs[:8], refs[8:]
    out_ref, sent_ref, stats_ref, buf, words, bias_ref, max_ref, sum_ref, acc_ref, score_ref, sems = refs
    layout = Layout(*sizes)
    block, width = cot_ref.shape
    head = width // HEADS
    rows_in = Rows(layout, groups, mask_ref, buf, words, sems, block)
    first_step(work_ref, rows_in.start)
    max_ref[...] = jnp.full(max_ref.shape, NEG_FILL, jnp.float32)
    sum_ref[...] = jnp.zeros(sum_ref.shape, jnp.float32)
    acc_ref[...] = jnp.zeros(acc_ref.shape, jnp.float32)

    def tiles(slot, blocks, patterns, index):
        rows = buf[slot]
        keys = dot(rows, wk_ref[...]).astype(jnp.bfloat16)
        values = dot(wvt_ref[...], rows, NT).astype(jnp.bfloat16)
        bias_ref[...] = rows_in.bias(slot, blocks, patterns)
        for p in range(HEADS // 2):
            scores = dot(keys[:, 2 * head * p : 2 * head * (p + 1)], stack_ref[p], NT)
            for e in range(2):
                score_ref[2 * p + e] = scores[:, block * e : block * (e + 1)] + bias_ref[...]
        for h in range(HEADS):
            s = score_ref[h]
            old = max_ref[h : h + 1]
            new = jnp.maximum(old, jnp.max(s, axis=0, keepdims=True))
            fade = jnp.exp(old - new)
            expo = jnp.exp(s - new)
            max_ref[h : h + 1] = new
            sum_ref[h : h + 1] = sum_ref[h : h + 1] * fade + jnp.sum(expo, axis=0, keepdims=True)
            at = slice(head * h, head * (h + 1))
            acc_ref[at] = acc_ref[at] * fade + dot(values[at], expo.astype(jnp.bfloat16))

    run_steps(work_ref, rows_in.start, rows_in.wait, tiles)
    inverse = 1.0 / sum_ref[...]
    cot = cot_ref[...].astype(jnp.float32).T
    stats_ref[0:HEADS] = max_ref[...] + jnp.log(sum_ref[...])
    for h in range(HEADS):
        at = slice(head * h, head * (h + 1))
        outputs = acc_ref[at] * inverse[h : h + 1]
        acc_ref[at] = outputs
        stats_ref[HEADS + h : HEADS + h + 1] = jnp.sum(outputs * cot[at], axis=0, keepdims=True)
    sent_ref[...] = jnp.broadcast_to(stats_ref[...], sent_ref.shape)
    out_ref[...] = acc_ref[...].T.astype(out_ref.dtype)


def tile_grads(scores, d_probs, lse, delta):
    prob = jnp.exp(scores - lse)
    return prob.astype(jnp.bfloat16), (prob * (d_probs - delta)).astype(jnp.bfloat16)


def query_grad_kernel(
    sizes, work_ref, stack_hbm, cot_stack_hbm, stats_hbm, wq_hbm, wk_hbm, wkt_hbm, wv_hbm, mask_ref, *refs
):
    groups, refs = refs[:8], refs[8:]
    part_ref, stack_ref, cot_stack_ref, stats_ref, wq_ref, wk_ref, wkt_ref, wv_ref = refs[:8]
    buf, words, bias_ref, acc_ref, score_ref, d_prob_ref, sems, w_sems = refs[8:]
    layout = Layout(*sizes)
    block, width = part_ref.shape
    head = width // HEADS
    rows_in = Rows(layout, groups, mask_ref, buf, words, sems, block)
    first_step(work_ref, rows_in.start)
    loads = load((
        (wk_hbm, wk_ref), (stack_hbm, stack_ref), (wv_hbm, wv_ref), (cot_stack_hbm, cot_stack_ref),
        (wkt_hbm, wkt_ref), (stats_hbm.at[0], stats_ref), (wq_hbm, wq_ref),
    ), w_sems)
    acc_ref[...] = jnp.zeros(acc_ref.shape, jnp.float32)
    for copy in loads[:6]:
        copy.wait()

    def tiles(slot, blocks, patterns, index):
        rows = buf[slot]
        keys = dot(rows, wk_ref[...]).astype(jnp.bfloat16)
        values = dot(rows, wv_ref[...]).astype(jnp.bfloat16)
        keys_t = dot(wkt_ref[...], rows, NT).astype(jnp.bfloat16)
        bias_ref[...] = rows_in.bias(slot, blocks, patterns)
        for p in range(HEADS // 2):
            pair = slice(2 * head * p, 2 * head * (p + 1))
            scores = dot(keys[:, pair], stack_ref[p], NT)
            d_probs = dot(values[:, pair], cot_stack_ref[p], NT)
            for e in range(2):
                of = slice(block * e, block * (e + 1))
                score_ref[2 * p + e] = scores[:, of] + bias_ref[...]
                d_prob_ref[2 * p + e] = d_probs[:, of]
        for h in range(HEADS):
            _, d_scores = tile_grads(
                score_ref[h], d_prob_ref[h], stats_ref[h : h + 1], stats_ref[HEADS + h : HEADS + h + 1]
            )
            at = slice(head * h, head * (h + 1))
            acc_ref[at] += dot(keys_t[at], d_scores)

    run_steps(work_ref, rows_in.start, rows_in.wait, tiles)
    loads[6].wait()
    grad = (acc_ref[...].T * (head**-0.5)).astype(jnp.bfloat16)
    part_ref[...] = dot(grad, wq_ref[...], NT)


def key_grad_kernel(
    sizes, bits, work_ref, key_hbm, value_hbm, wq_hbm, wk_hbm, wv_hbm, part_hbm, mask_ref, stats_all_ref, *refs
):
    readers = sizes[0]
    groups, refs = refs[:8], refs[8:]
    halves, refs = (refs[:readers], refs[readers : 2 * readers]), refs[2 * readers :]
    out_ref, key_ref, value_ref, part_ref, wq_ref, wk_ref, wv_ref, buf, words, cot_buf, stats, bias_ref = refs[:12]
    query_stack_ref, cot_stack_ref, score_ref, d_prob_ref, key_acc, value_acc, sems, c_sems, w_sems = refs[12:]
    layout = Layout(*sizes)
    block, width = out_ref.shape
    head = width // HEADS
    rows_in = Rows(layout, groups, mask_ref, buf, words, sems, block)

    def half_copy(slot, t, k):
        into = cot_buf.at[slot, pl.ds(t * block + block // 2 * k, block // 2)]
        return lambda src: pltpu.make_async_copy(src, into, c_sems.at[slot, t, k])

    def stats_copy(slot, t, query):
        return pltpu.make_async_copy(stats_all_ref.at[query], stats.at[slot, t], c_sems.at[slot, t, 2])

    def start(slot, blocks, patterns):
        rows_in.start(slot, blocks, patterns)
        for t in range(TILES):
            stats_copy(slot, t, blocks[t]).start()
            for k in range(2):
                start_copy(layout.half_place(bits[k], blocks[t]), halves[k], half_copy(slot, t, k))

    def wait(slot):
        rows_in.wait(slot)
        for t in range(TILES):
            stats_copy(slot, t, 0).wait()
            for k in range(2):
                half_copy(slot, t, k)(halves[k][0].at[0]).wait()

    first_step(work_ref, start)
    loads = load((
        (wq_hbm, wq_ref), (key_hbm, key_ref), (value_hbm, value_ref),
        (wk_hbm, wk_ref), (wv_hbm, wv_ref), (part_hbm, part_ref),
    ), w_sems)
    key_acc[...] = jnp.zeros(key_acc.shape, jnp.float32)
    value_acc[...] = jnp.zeros(value_acc.shape, jnp.float32)
    for copy in loads[:3]:
        copy.wait()

    def tiles(slot, blocks, patterns, index):
        queries = dot(buf[slot], wq_ref[...]).astype(jnp.bfloat16) * jnp.bfloat16(head**-0.5)
        bias_ref[...] = rows_in.bias(slot, blocks, patterns)
        cots = cot_buf[slot]
        pairs = [slice(2 * head * p, 2 * head * (p + 1)) for p in range(HEADS // 2)]
        of_tile = [slice(block * t, block * (t + 1)) for t in range(TILES)]
        for p, pair in enumerate(pairs):
            query_stack_ref[p] = jnp.concatenate([pair_stack(queries[of, pair]) for of in of_tile], 0)
            cot_stack_ref[p] = jnp.concatenate([pair_stack(cots[of, pair]) for of in of_tile], 0)
            score_ref[p] = dot(key_ref[:, pair], query_stack_ref[p], NT)
            d_prob_ref[p] = dot(value_ref[:, pair], cot_stack_ref[p], NT)
        for p, pair in enumerate(pairs):
            probs, d_scores = [], []
            for t in range(TILES):
                for e in range(2):
                    h = 2 * p + e
                    of = slice(block * (2 * t + e), block * (2 * t + e + 1))
                    prob, d_score = tile_grads(
                        score_ref[p, :, of] + bias_ref[of_tile[t]], d_prob_ref[p, :, of], stats[slot, t, h : h + 1],
                        stats[slot, t, HEADS + h : HEADS + h + 1],
                    )
                    probs.append(prob)
                    d_scores.append(d_score)
            value_acc[:, pair] += dot(jnp.concatenate(probs, 1), cot_stack_ref[p])
            key_acc[:, pair] += dot(jnp.concatenate(d_scores, 1), query_stack_ref[p])

    run_steps(work_ref, start, wait, tiles)
    for copy in loads[3:]:
        copy.wait()
    grad = part_ref[...] + dot(key_acc[...].astype(jnp.bfloat16), wk_ref[...], NT)
    grad = grad + dot(value_acc[...].astype(jnp.bfloat16), wv_ref[...], NT)
    out_ref[...] = grad.astype(out_ref.dtype)


VMEM = pl.BlockSpec(memory_space=pltpu.VMEM)
SMEM = pl.BlockSpec(memory_space=pltpu.SMEM)
HBM = pl.BlockSpec(memory_space=pltpu.HBM)


def swap(block, mask):
    axes = ("reader", "blk")
    count = lax.axis_size("reader") * lax.axis_size("blk")
    return lax.ppermute(block, axes, [(i, i ^ mask) for i in range(count)])


def after(value, *others):
    return lax.optimization_barrier((value, *others))[0]


def over_readers(chunk, order, blks):
    for bit in order[:-1]:
        chunk = jnp.concatenate([chunk, swap(chunk, blks << bit)], 0)
    return [chunk, swap(chunk, blks << order[-1])]


def local(features, cotangent, w_query, w_key, w_value, tile_coords, tile_count, mask_table):
    block, width = features.shape
    readers, blks, cap = lax.axis_size("reader"), lax.axis_size("blk"), tile_coords.shape[2]
    assert block == mask_table.shape[1] and 3 * cap < 128
    sizes = (readers, blks, cap)
    devices, lines = readers * blks, blks // 2
    f32, bf16, i32 = jnp.float32, jnp.bfloat16, jnp.int32
    shape = jax.ShapeDtypeStruct
    masks = mask_table.transpose(0, 2, 1)
    words = masks.shape[1]
    head = width // HEADS
    half = block // 2
    some = pltpu.CompilerParams(vmem_limit_bytes=VMEM_SOME)
    most = pltpu.CompilerParams(vmem_limit_bytes=VMEM_MOST)
    axes = ("reader", "blk")

    def cost(tiles):
        return pl.CostEstimate(flops=tiles * 200_000_000, bytes_accessed=4_000_000, transcendentals=tiles * 131072)

    rows = features[None]
    lined = [rows] + [swap(rows, 2 * k) for k in range(1, lines)]

    bits = (0, (readers - 1).bit_length() - 1)
    cot_parts = [cotangent[None, half * k : half * (k + 1)] for k in range(2)]
    cot_other = [swap(part, blks << bit) for part, bit in zip(cot_parts, bits)]

    sent = pl.pallas_call(
        send_list_kernel,
        out_shape=shape((devices, 8, 128), i32),
        in_specs=[HBM, HBM],
        out_specs=VMEM,
        scratch_shapes=[
            pltpu.SMEM((1, 3, 1, cap), i32), pltpu.SMEM((1, 1), i32), pltpu.SemaphoreType.DMA((2,)),
        ],
        compiler_params=some,
        name="send_list",
    )(tile_coords.transpose(0, 3, 1, 2), tile_count)
    lists = lax.all_to_all(after(sent, *cot_other), axes, 0, 0, tiled=True)[:, 0]
    query_work, key_work = pl.pallas_call(
        functools.partial(work_kernel, sizes),
        out_shape=(shape((2 * blks * cap + 5,), i32), shape((2 * readers * cap + 5,), i32)),
        in_specs=[HBM],
        out_specs=(SMEM, SMEM),
        scratch_shapes=[pltpu.SMEM((devices, 128), i32), pltpu.SemaphoreType.DMA],
        compiler_params=some,
        cost_estimate=cost(2),
        name="work",
    )(lists)

    stacks = shape((HEADS // 2, 2 * block, 2 * head), bf16)
    own = shape((block, width), bf16)
    square = shape((width, width), bf16)
    prepared = pl.pallas_call(
        prepare_kernel,
        out_shape=(stacks, stacks, own, own, square, square),
        in_specs=[VMEM] * 5,
        out_specs=(VMEM,) * 6,
        compiler_params=some,
        cost_estimate=cost(2),
        name="prepare",
    )(features, cotangent, w_query, w_key, w_value)
    query_stack, cot_stack, keys, values, w_key_t, w_value_t = prepared

    lined = after(lined, prepared)
    chunks = [jnp.concatenate([entry[:, half * k : half * (k + 1)] for entry in lined], 0) for k in range(2)]
    here = [over_readers(chunk, order, blks) for chunk, order in zip(chunks, orders(readers))]
    rows_all = []
    for first, last in here:
        rows_all += [first, last, swap(after(first, query_work), 1), swap(last, 1)]

    both = jnp.concatenate([cot_parts[0], cot_other[0], cot_parts[1], cot_other[1]], 0)
    cot_line = after(both, *chunks)[None]
    mask = blks // 2
    while mask > 1:
        cot_line = jnp.concatenate([cot_line, swap(cot_line, mask)], 0)
        mask //= 2

    weight = pltpu.VMEM((width, width), bf16)
    stack_space = pltpu.VMEM(stacks.shape, bf16)
    rows_low, rows_wide = pltpu.VMEM((block, width), bf16), pltpu.VMEM((block, width), f32)
    buffer = pltpu.VMEM((2, TILES * block, width), bf16)
    word_buffer = pltpu.VMEM((2, TILES, words, block), i32)
    bias = pltpu.VMEM((TILES * block, block), f32)
    turned = pltpu.VMEM((width, block), f32)
    per_head = pltpu.VMEM((HEADS, block), f32)
    own_stats = pltpu.VMEM((2 * HEADS, block), f32)
    met = pltpu.VMEM((HEADS, TILES * block, block), f32)
    pair_met = pltpu.VMEM((HEADS // 2, block, 2 * TILES * block), f32)
    pair_rows = pltpu.VMEM((HEADS // 2, 2 * TILES * block, 2 * head), bf16)
    row_sems = pltpu.SemaphoreType.DMA((2, TILES, 3))

    attn_out, stats = pl.pallas_call(
        functools.partial(forward_kernel, sizes),
        out_shape=(own, shape((devices, 2 * HEADS, block), f32)),
        in_specs=[SMEM] + [VMEM] * 4 + [HBM] * 9,
        out_specs=(VMEM, VMEM),
        scratch_shapes=[own_stats, buffer, word_buffer, bias, per_head, per_head, turned, met, row_sems],
        compiler_params=some,
        cost_estimate=cost(5),
        name="forward",
    )(query_work, query_stack, cotangent, w_key, w_value_t, masks, *rows_all)

    cots_here = []
    for k in range(2):
        part = after(cot_line[:, 2 * k : 2 * k + 2].reshape(2 * lines, half, width), stats)
        masks_left = [m for m in range(1, readers) if not m >> bits[k] & 1]
        cots_here.append((part, [swap(part, blks * m) for m in masks_left], swap(part, 1)))
    stats_all = lax.all_to_all(stats, axes, 0, 0, tiled=True)

    query_part = pl.pallas_call(
        functools.partial(query_grad_kernel, sizes),
        out_shape=shape((block, width), f32),
        in_specs=[SMEM] + [HBM] * 16,
        out_specs=VMEM,
        scratch_shapes=[
            stack_space, stack_space, own_stats, weight, weight, weight, weight, buffer, word_buffer, bias, turned,
            met, met, row_sems, pltpu.SemaphoreType.DMA((7,)),
        ],
        compiler_params=most,
        cost_estimate=cost(5),
        name="query_grad",
    )(query_work, query_stack, cot_stack, stats, w_query, w_key, w_key_t, w_value, masks, *rows_all)

    cots_all = []
    for first, rest, other in cots_here:
        cots_all += [first, *rest, other] + [swap(after(part, stats_all, query_part), 1) for part in rest]

    grad_features = pl.pallas_call(
        functools.partial(key_grad_kernel, sizes, bits),
        out_shape=own,
        in_specs=[SMEM] + [HBM] * (16 + 2 * readers),
        out_specs=VMEM,
        scratch_shapes=[
            rows_low, rows_low, rows_wide, weight, weight, weight,
            buffer, word_buffer, buffer, pltpu.VMEM((2, TILES, 2 * HEADS, block), f32), bias,
            pair_rows, pair_rows, pair_met, pair_met, rows_wide, rows_wide,
            row_sems, pltpu.SemaphoreType.DMA((2, TILES, 3)), pltpu.SemaphoreType.DMA((6,)),
        ],
        compiler_params=most,
        cost_estimate=cost(5),
        name="key_grad",
    )(key_work, keys, values, w_query, w_key, w_value, query_part, masks, stats_all, *rows_all, *cots_all)
    return attn_out, grad_features


def solution(mesh):
    return jax.shard_map(
        local,
        mesh=mesh,
        in_specs=(
            P(("reader", "blk"), None),
            P(("reader", "blk"), None),
            P(),
            P(),
            P(),
            P("reader", "blk", None, None),
            P("reader", "blk"),
            P(),
        ),
        out_specs=(P(("reader", "blk"), None), P(("reader", "blk"), None)),
        check_vma=False,
    )
```

time: 89.4 us -> 89.7 us (level)
  waiting for transfers between devices: 39.9 us -> 22.3 us
  blocking collectives: 0 us -> 15.1 us
  local copies, waits for them, and re-layouts: 3.77 us -> 7.79 us
  Pallas kernels: 21.2 us -> 18.8 us
  starting transfers between devices: 21.7 us -> 22.8 us
    ppermute x21, waiting for transfers between devices: 31.8 us -> 15.7 us  [swap(): return lax.ppermute(block, axes, [(i, i ^ mask) for i in range(count)])]
    all_to_all x0 -> x1, blocking collectives: none -> 15.1 us  [local(): lax.all_to_all(after(sent, *cot_other), axes, 0, 0, tiled=True)[:, 0]]
    unnamed x30 -> x64, local copies, waits for them, and re-layouts: 2.58 us -> 6.72 us
    pallas_call x4 -> x5, Pallas kernels: 16.4 us -> 13 us  [the longest x1 5.62 us: local(): pl.pallas_call(functools.partial(query_grad_kernel, sizes), out_shape=sha...]
    ppermute x21, starting transfers between devices: 17.7 us -> 19.7 us  [swap(): return lax.ppermute(block, axes, [(i, i ^ mask) for i in range(count)])]
    all_to_all x1, waiting for transfers between devices: 8.09 us -> 6.58 us  [local(): stats_all = lax.all_to_all(stats, axes, 0, 0, tiled=True)]
    slice x9 -> x6, local copies, waits for them, and re-layouts: 1.14 us -> 0.16 us  [the longest x4 0.08 us: local(): entry[:, half * k:half * (k + 1)]]
    pallas_call x1, Pallas kernels: 4.84 us -> 5.75 us  [local(): pl.pallas_call(functools.partial(key_grad_kernel, sizes, bits), out_shape...]
  transfers between devices with their start and end apart: 22 -> 22, of which waited for: 8 -> 11; matrix products, arithmetic and copies ran while one was open for 2% -> 2% of each run, Pallas kernels for 17% -> 10%
where the time goes in v5:
time: 89.7 us; the launch traced here: 88.8 us
  starting transfers between devices  22.8 us (25%)
  waiting for transfers between devices  22.3 us (25%)
  Pallas kernels  18.8 us (21%)
  blocking collectives  15.1 us (17%)
  local copies, waits for them, and re-layouts  7.79 us (9%)
  between operations  1.7 us (2%)
    ppermute x21, starting transfers between devices, swap(): return lax.ppermute(block, axes, [(i, i ^ mask) for i in range(count)])  19.7 us
    ppermute x21, waiting for transfers between devices, swap(): return lax.ppermute(block, axes, [(i, i ^ mask) for i in range(count)])  15.7 us
    all_to_all x1, blocking collectives, local(): lax.all_to_all(after(sent, *cot_other), axes, 0, 0, tiled=True)[:, 0]  15.1 us
    unnamed x64, local copies, waits for them, and re-layouts  6.72 us
    all_to_all x1, waiting for transfers between devices, local(): stats_all = lax.all_to_all(stats, axes, 0, 0, tiled=True)  6.58 us
    pallas_call x1, Pallas kernels, local(): pl.pallas_call(functools.partial(key_grad_kernel, sizes, bits), out_shape...  5.75 us
    pallas_call x1, Pallas kernels, local(): pl.pallas_call(functools.partial(query_grad_kernel, sizes), out_shape=sha...  5.62 us
    pallas_call x1, Pallas kernels, local(): pl.pallas_call(functools.partial(forward_kernel, sizes), out_shape=(own,...  4.29 us
  transfers between devices with their start and end apart: 22, of which 11 were waited for; matrix products, arithmetic and copies ran while one was open for 2% of the time, Pallas kernels for 10%

profile of v5, /device:TPU:0, one launch (start us, length us, event | category | flops | bytes accessed | tf_op | source)
XLA Modules:
  0.0 88.8 jit_solution(8282238486133281622)
XLA Ops:
  0.6 5.1 %collective-permute-start.4 = (bf16[1,128,512]{2,1,0:T(8,128)(2,1)}, bf16[1,128,512]{2,1,0:T(8,128)(2,1)S(1)}, u32[]{:S(2)}, u32[]{:S(2)}) collective-permute-start(bf16[1,128,512]{2,1,0:T(8,128)(2,1)} %bitcast.16), channel_id=1, source_target_pairs={{0,6},{1,7},{2,4},{3,5},{4,2},{5,3},{6,0},{7,1},{8,14},{9,15},{10,... | collective-permute-start | bytes 393224 | tf_op jit(solution)/shard_map/ppermute | solution.py:403
  5.8 0.0 collective-permute-start.3
  5.8 0.6 collective-permute-start.2
  6.4 0.9 slice_bitcast_fusion
  7.3 1.7 %collective-permute-start.1 = (bf16[1,64,512]{2,1,0:T(8,128)(2,1)S(1)}, bf16[1,64,512]{2,1,0:T(8,128)(2,1)S(1)}, u32[]{:S(2)}, u32[]{:S(2)}) collective-permute-start(bf16[1,64,512]{2,1,0:T(8,128)(2,1)S(1)} %get-tuple-element.64), channel_id=1, source_target_pairs={{0,16},{1,17},{2,18},{3,19},{4,20},{5,21},{6,22},{7,23},{8,24},{9,... | collective-permute-start | bytes 196616 | tf_op jit(solution)/shard_map/ppermute | solution.py:403
  9.0 1.5 %collective-permute-start = (bf16[1,64,512]{2,1,0:T(8,128)(2,1)S(1)}, bf16[1,64,512]{2,1,0:T(8,128)(2,1)S(1)}, u32[]{:S(2)}, u32[]{:S(2)}) collective-permute-start(bf16[1,64,512]{2,1,0:T(8,128)(2,1)S(1)} %get-tuple-element.65), channel_id=1, source_target_pairs={{0,8},{1,9},{2,10},{3,11},{4,12},{5,13},{6,14},{7,15},{8,0},{9,1},... | collective-permute-start | bytes 196616 | tf_op jit(solution)/shard_map/ppermute | solution.py:403
  10.5 1.0 %copy-done = bf16[512,512]{1,0:T(8,128)(2,1)S(1)} copy-done((bf16[512,512]{1,0:T(8,128)(2,1)S(1)}, bf16[512,512]{1,0:T(8,128)(2,1)}, u32[]{:S(2)}) %copy-start) | copy-done | bytes 524312
  11.6 1.0 %copy-done.4 = bf16[512,512]{1,0:T(8,128)(2,1)S(1)} copy-done((bf16[512,512]{1,0:T(8,128)(2,1)S(1)}, bf16[512,512]{1,0:T(8,128)(2,1)}, u32[]{:S(2)}) %copy-start.4) | copy-done | bytes 524312
  12.6 1.0 %copy-done.5 = bf16[512,512]{1,0:T(8,128)(2,1)S(1)} copy-done((bf16[512,512]{1,0:T(8,128)(2,1)S(1)}, bf16[512,512]{1,0:T(8,128)(2,1)}, u32[]{:S(2)}) %copy-start.5) | copy-done | bytes 524312
  13.6 0.4 prepare.1
  14.1 0.8 copy-done.16
  14.9 0.6 copy-done.18
  15.5 0.6 copy-done.19
  16.2 0.0 collective-permute-done.4
  16.2 0.8 collective-permute-done.3
  17.0 0.0 collective-permute-done.2
  17.2 1.6 %collective-permute-start.9 = (bf16[4,64,512]{2,1,0:T(8,128)(2,1)S(1)}, bf16[4,64,512]{2,1,0:T(8,128)(2,1)S(1)}, u32[]{:S(2)}, u32[]{:S(2)}) collective-permute-start(bf16[4,64,512]{2,1,0:T(8,128)(2,1)S(1)} %pad_maximum_fusion.3), channel_id=1, source_target_pairs={{0,16},{1,17},{2,18},{3,19},{4,20},{5,21},{6,22},{7,23},{8,24},{9,... | collective-permute-start | bytes 786440 | tf_op jit(solution)/shard_map/ppermute | solution.py:403
  18.8 1.6 %collective-permute-start.5 = (bf16[4,64,512]{2,1,0:T(8,128)(2,1)S(1)}, bf16[4,64,512]{2,1,0:T(8,128)(2,1)S(1)}, u32[]{:S(2)}, u32[]{:S(2)}) collective-permute-start(bf16[4,64,512]{2,1,0:T(8,128)(2,1)S(1)} %pad_maximum_fusion.2), channel_id=1, source_target_pairs={{0,8},{1,9},{2,10},{3,11},{4,12},{5,13},{6,14},{7,15},{8,0},{9,1},... | collective-permute-start | bytes 786440 | tf_op jit(solution)/shard_map/ppermute | solution.py:403
  20.4 0.0 collective-permute-done.1
  20.4 0.0 collective-permute-done
  20.4 0.1 collective-permute-start.13
  20.5 4.1 %collective-permute-done.9 = bf16[4,64,512]{2,1,0:T(8,128)(2,1)S(1)} collective-permute-done((bf16[4,64,512]{2,1,0:T(8,128)(2,1)S(1)}, bf16[4,64,512]{2,1,0:T(8,128)(2,1)S(1)}, u32[]{:S(2)}, u32[]{:S(2)}) %collective-permute-start.9) | collective-permute-done | bytes 262176 | tf_op jit(solution)/shard_map/ppermute | solution.py:403
  24.7 1.6 %collective-permute-start.10 = (bf16[8,64,512]{2,1,0:T(8,128)(2,1)S(1)}, bf16[8,64,512]{2,1,0:T(8,128)(2,1)S(1)}, u32[]{:S(2)}, u32[]{:S(2)}) collective-permute-start(bf16[8,64,512]{2,1,0:T(8,128)(2,1)S(1)} %constant_dynamic-update-slice_fusion.5.refs_4_), channel_id=1, source_target_pairs={{0,8},{1,9},{2,10},{3,11},{4,12},{5,13},{6,14},{7,15},{8,0},{9,1},... | collective-permute-start | bytes 1572872 | tf_op jit(solution)/shard_map/ppermute | solution.py:403
  26.2 0.1 collective-permute-done.5
  26.4 1.5 %collective-permute-start.6 = (bf16[8,64,512]{2,1,0:T(8,128)(2,1)S(1)}, bf16[8,64,512]{2,1,0:T(8,128)(2,1)S(1)}, u32[]{:S(2)}, u32[]{:S(2)}) collective-permute-start(bf16[8,64,512]{2,1,0:T(8,128)(2,1)S(1)} %constant_dynamic-update-slice_fusion.refs_0_), channel_id=1, source_target_pairs={{0,16},{1,17},{2,18},{3,19},{4,20},{5,21},{6,22},{7,23},{8,24},{9,... | collective-permute-start | bytes 1572872 | tf_op jit(solution)/shard_map/ppermute | solution.py:403
  27.9 5.6 %collective-permute-done.13 = bf16[1,4,64,512]{3,2,1,0:T(8,128)(2,1)S(1)} collective-permute-done((bf16[1,4,64,512]{3,2,1,0:T(8,128)(2,1)S(1)}, bf16[1,4,64,512]{3,2,1,0:T(8,128)(2,1)S(1)}, u32[]{:S(2)}, u32[]{:S(2)}) %collective-permute-start.13) | collective-permute-done | bytes 262176 | tf_op jit(solution)/shard_map/ppermute | solution.py:403
  33.5 0.1 pad_maximum_fusion.1
  33.5 0.0 copy-start.21
  33.5 0.1 collective-permute-start.14
  34.3 0.6 send_list.1
  34.9 15.1 %all_to_all.10 = s32[32,8,128]{2,1,0:T(8,128)S(1)} all-to-all(s32[32,8,128]{2,1,0:T(8,128)S(1)} %send_list.1), channel_id=1, replica_groups=mesh['reader'=4,'blk'=8] {'reader','blk'}, dimensions={0} | all-to-all | bytes 262144 | tf_op jit(solution)/shard_map/all_to_all | solution.py:453
  50.0 2.1 %work.1 = (s32[133]{0:T(256)S(1)}, s32[69]{0:T(128)S(1)}) custom-call(s32[32,128]{1,0:T(8,128)S(1)} %bitcast.20), custom_call_target="tpu_custom_call" | custom-call | flops 400000000 | bytes 4000000 | tf_op jit(solution)/shard_map/work/pallas_call | solution.py:454
  52.1 0.6 copy-done.22
  52.7 0.3 collective-permute-start.11
  53.0 0.2 collective-permute-start.7
  53.2 0.0 collective-permute-done.10.refs_5_
  53.2 0.3 collective-permute-start.12
  53.5 0.0 collective-permute-done.6.refs_1_
  53.5 0.2 collective-permute-start.8
  53.7 0.0 collective-permute-done.14
  53.7 0.1 pad_maximum_fusion
  53.8 0.0 copy-start.1
  53.8 0.0 copy-start.12
  53.8 0.1 fusion
  53.9 0.6 collective-permute-done.11.refs_6_
  54.6 0.7 collective-permute-done.7.refs_2_
  55.3 0.7 collective-permute-done.12.refs_7_
  56.1 0.7 collective-permute-done.8.refs_3_
  56.9 4.3 %forward.1 = (bf16[128,512]{1,0:T(8,128)(2,1)}, f32[32,16,128]{2,1,0:T(8,128)}) custom-call(s32[133]{0:T(256)S(1)} %get-tuple-element.25.work_ref, bf16[4,256,128]{2,1,0:T(8,128)(2,1)S(1)} %get-tuple-element.26.stack_ref.stack_hbm, bf16[128,512]{1,0:T(8,128)(2,1)S(1)} %copy-done.13, bf16[512,512]{1,0:T(8,128)(2,1)S(1)} %copy-done.1, ...), custom_call_target="tpu_custom_call" | custom-call | flops 1000000000 | bytes 4000000 | tf_op jit(solution)/shard_map/forward/pallas_call | solution.py:507
  61.2 2.3 %collective-permute-start.15 = (bf16[8,64,512]{2,1,0:T(8,128)(2,1)S(1)}, bf16[8,64,512]{2,1,0:T(8,128)(2,1)S(1)}, u32[]{:S(2)}, u32[]{:S(2)}) collective-permute-start(bf16[8,64,512]{2,1,0:T(8,128)(2,1)S(1)} %bitcast.28), channel_id=1, source_target_pairs={{0,16},{1,17},{2,18},{3,19},{4,20},{5,21},{6,22},{7,23},{8,24},{9,... | collective-permute-start | bytes 1572872 | tf_op jit(solution)/shard_map/ppermute | solution.py:403
  63.5 0.0 collective-permute-start.18
  63.5 3.2 %all-to-all-start.1 = ((f32[32,16,128]{2,1,0:T(8,128)}), f32[32,16,128]{2,1,0:T(8,128)S(1)}, u32[]{:S(2)}, u32[]{:S(2)}) async-start(f32[32,16,128]{2,1,0:T(8,128)} %get-tuple-element.40.stats_hbm), calls=%async_computation.1 | async-start | bytes 524288 | tf_op jit(solution)/shard_map/all_to_all | solution.py:523
  66.7 0.3 collective-permute-start.16
  67.0 0.3 collective-permute-start.19
  67.2 5.6 %query_grad.1.part_hbm = f32[128,512]{1,0:T(8,128)} custom-call(s32[133]{0:T(256)} %copy-done.20, bf16[4,256,128]{2,1,0:T(8,128)(2,1)} %copy-done.14, bf16[4,256,128]{2,1,0:T(8,128)(2,1)} %copy-done.17, f32[32,16,128]{2,1,0:T(8,128)} %get-tuple-element.40.stats_hbm, bf16[512,512]{1,0:T(8,128)(2,1)} %wq_hbm.3, bf16[512,512]{1,0:T(8,128)(2,1)} %wk_hbm.3, ...), custom_call_target="tpu_custom_call" | custom-call | flops 1000000000 | bytes 4000000 | tf_op jit(solution)/shard_map/query_grad/pallas_call | solution.py:525
  72.9 6.6 %all-to-all-done.1.stats_all_ref = f32[32,16,128]{2,1,0:T(8,128)S(1)} async-done(((f32[32,16,128]{2,1,0:T(8,128)}), f32[32,16,128]{2,1,0:T(8,128)S(1)}, u32[]{:S(2)}, u32[]{:S(2)}) %all-to-all-start.1) | async-done | bytes 262176 | tf_op jit(solution)/shard_map/all_to_all | solution.py:523
  79.4 0.0 collective-permute-done.15.refs_9_
  79.5 0.1 collective-permute-start.17
  79.5 0.5 collective-permute-start.20
  80.0 0.0 collective-permute-done.16.refs_10_
  80.0 1.4 %collective-permute-done.17.refs_11_ = bf16[8,64,512]{2,1,0:T(8,128)(2,1)S(1)} collective-permute-done((bf16[8,64,512]{2,1,0:T(8,128)(2,1)S(1)}, bf16[8,64,512]{2,1,0:T(8,128)(2,1)S(1)}, u32[]{:S(2)}, u32[]{:S(2)}) %collective-permute-start.17) | collective-permute-done | bytes 524320 | tf_op jit(solution)/shard_map/ppermute | solution.py:403
  81.4 0.7 collective-permute-done.20.refs_15_
  82.2 0.8 copy-done.31
  83.0 5.8 %key_grad.1 = bf16[128,512]{1,0:T(8,128)(2,1)} custom-call(s32[69]{0:T(128)} %copy-done.22, bf16[128,512]{1,0:T(8,128)(2,1)} %copy-done.18, bf16[128,512]{1,0:T(8,128)(2,1)} %copy-done.19, bf16[512,512]{1,0:T(8,128)(2,1)} %wq_hbm.3, bf16[512,512]{1,0:T(8,128)(2,1)} %wk_hbm.3, bf16[512,512]{1,0:T(8,128)(2,1)} %wv_hbm.3, f32[128,512]{1,0:T(8,128)} %query_grad.1.part_hbm, ...), custom_call_target="tpu_custom_call" | custom-call | flops 1000000000 | bytes 4000000 | tf_op jit(solution)/shard_map/key_grad/pallas_call | solution.py:543
  (65 shorter events, 0.3 us)
Async XLA Ops:
  0.6 9.9 %copy-start.13 = (bf16[128,512]{1,0:T(8,128)(2,1)S(1)}, bf16[128,512]{1,0:T(8,128)(2,1)}, u32[]{:S(2)}) copy-start(bf16[128,512]{1,0:T(8,128)(2,1)} %cot_ref.3) | copy-start | bytes 393220
  0.6 9.9 %copy-start.15 = (bf16[128,512]{1,0:T(8,128)(2,1)S(1)}, bf16[128,512]{1,0:T(8,128)(2,1)}, u32[]{:S(2)}) copy-start(bf16[128,512]{1,0:T(8,128)(2,1)} %own_ref.1) | copy-start | bytes 393220
  0.6 15.6 %collective-permute-start.4 = (bf16[1,128,512]{2,1,0:T(8,128)(2,1)}, bf16[1,128,512]{2,1,0:T(8,128)(2,1)S(1)}, u32[]{:S(2)}, u32[]{:S(2)}) collective-permute-start(bf16[1,128,512]{2,1,0:T(8,128)(2,1)} %bitcast.16), channel_id=1, source_target_pairs={{0,6},{1,7},{2,4},{3,5},{4,2},{5,3},{6,0},{7,1},{8,14},{9,15},{10,... | collective-permute-start | bytes 393224 | tf_op jit(solution)/shard_map/ppermute | solution.py:403
  5.8 11.3 %collective-permute-start.3 = (bf16[1,128,512]{2,1,0:T(8,128)(2,1)}, bf16[1,128,512]{2,1,0:T(8,128)(2,1)S(1)}, u32[]{:S(2)}, u32[]{:S(2)}) collective-permute-start(bf16[1,128,512]{2,1,0:T(8,128)(2,1)} %bitcast.17), channel_id=1, source_target_pairs={{0,4},{1,5},{2,6},{3,7},{4,0},{5,1},{6,2},{7,3},{8,12},{9,13},{10,... | collective-permute-start | bytes 393224 | tf_op jit(solution)/shard_map/ppermute | solution.py:403
  5.8 11.3 %collective-permute-start.2 = (bf16[1,128,512]{2,1,0:T(8,128)(2,1)}, bf16[1,128,512]{2,1,0:T(8,128)(2,1)S(1)}, u32[]{:S(2)}, u32[]{:S(2)}) collective-permute-start(bf16[1,128,512]{2,1,0:T(8,128)(2,1)} %bitcast.18), channel_id=1, source_target_pairs={{0,2},{1,3},{2,0},{3,1},{4,6},{5,7},{6,4},{7,5},{8,10},{9,11},{10,... | collective-permute-start | bytes 393224 | tf_op jit(solution)/shard_map/ppermute | solution.py:403
  7.3 13.1 %collective-permute-start.1 = (bf16[1,64,512]{2,1,0:T(8,128)(2,1)S(1)}, bf16[1,64,512]{2,1,0:T(8,128)(2,1)S(1)}, u32[]{:S(2)}, u32[]{:S(2)}) collective-permute-start(bf16[1,64,512]{2,1,0:T(8,128)(2,1)S(1)} %get-tuple-element.64), channel_id=1, source_target_pairs={{0,16},{1,17},{2,18},{3,19},{4,20},{5,21},{6,22},{7,23},{8,24},{9,... | collective-permute-start | bytes 196616 | tf_op jit(solution)/shard_map/ppermute | solution.py:403
  9.0 11.4 %collective-permute-start = (bf16[1,64,512]{2,1,0:T(8,128)(2,1)S(1)}, bf16[1,64,512]{2,1,0:T(8,128)(2,1)S(1)}, u32[]{:S(2)}, u32[]{:S(2)}) collective-permute-start(bf16[1,64,512]{2,1,0:T(8,128)(2,1)S(1)} %get-tuple-element.65), channel_id=1, source_target_pairs={{0,8},{1,9},{2,10},{3,11},{4,12},{5,13},{6,14},{7,15},{8,0},{9,1},... | collective-permute-start | bytes 196616 | tf_op jit(solution)/shard_map/ppermute | solution.py:403
  10.5 1.0 %copy-start = (bf16[512,512]{1,0:T(8,128)(2,1)S(1)}, bf16[512,512]{1,0:T(8,128)(2,1)}, u32[]{:S(2)}) copy-start(bf16[512,512]{1,0:T(8,128)(2,1)} %wk_hbm.3) | copy-start | bytes 1572868
  11.6 1.0 %copy-start.4 = (bf16[512,512]{1,0:T(8,128)(2,1)S(1)}, bf16[512,512]{1,0:T(8,128)(2,1)}, u32[]{:S(2)}) copy-start(bf16[512,512]{1,0:T(8,128)(2,1)} %wq_hbm.3) | copy-start | bytes 1572868
  12.6 1.0 %copy-start.5 = (bf16[512,512]{1,0:T(8,128)(2,1)S(1)}, bf16[512,512]{1,0:T(8,128)(2,1)}, u32[]{:S(2)}) copy-start(bf16[512,512]{1,0:T(8,128)(2,1)} %wv_hbm.3) | copy-start | bytes 1572868
  14.1 0.8 copy-start.16
  14.9 0.6 copy-start.18
  15.5 0.7 copy-start.19
  16.2 0.9 %copy-start.17 = (bf16[4,256,128]{2,1,0:T(8,128)(2,1)}, bf16[4,256,128]{2,1,0:T(8,128)(2,1)S(1)}, u32[]{:S(2)}) copy-start(bf16[4,256,128]{2,1,0:T(8,128)(2,1)S(1)} %get-tuple-element.28.cot_stack_hbm) | copy-start | bytes 786436
  16.2 40.6 %copy-start.14 = (bf16[4,256,128]{2,1,0:T(8,128)(2,1)}, bf16[4,256,128]{2,1,0:T(8,128)(2,1)S(1)}, u32[]{:S(2)}) copy-start(bf16[4,256,128]{2,1,0:T(8,128)(2,1)S(1)} %get-tuple-element.26.stack_ref.stack_hbm) | copy-start | bytes 786436
  17.2 7.4 %collective-permute-start.9 = (bf16[4,64,512]{2,1,0:T(8,128)(2,1)S(1)}, bf16[4,64,512]{2,1,0:T(8,128)(2,1)S(1)}, u32[]{:S(2)}, u32[]{:S(2)}) collective-permute-start(bf16[4,64,512]{2,1,0:T(8,128)(2,1)S(1)} %pad_maximum_fusion.3), channel_id=1, source_target_pairs={{0,16},{1,17},{2,18},{3,19},{4,20},{5,21},{6,22},{7,23},{8,24},{9,... | collective-permute-start | bytes 786440 | tf_op jit(solution)/shard_map/ppermute | solution.py:403
  18.8 7.5 %collective-permute-start.5 = (bf16[4,64,512]{2,1,0:T(8,128)(2,1)S(1)}, bf16[4,64,512]{2,1,0:T(8,128)(2,1)S(1)}, u32[]{:S(2)}, u32[]{:S(2)}) collective-permute-start(bf16[4,64,512]{2,1,0:T(8,128)(2,1)S(1)} %pad_maximum_fusion.2), channel_id=1, source_target_pairs={{0,8},{1,9},{2,10},{3,11},{4,12},{5,13},{6,14},{7,15},{8,0},{9,1},... | collective-permute-start | bytes 786440 | tf_op jit(solution)/shard_map/ppermute | solution.py:403
  20.4 13.0 %collective-permute-start.13 = (bf16[1,4,64,512]{3,2,1,0:T(8,128)(2,1)S(1)}, bf16[1,4,64,512]{3,2,1,0:T(8,128)(2,1)S(1)}, u32[]{:S(2)}, u32[]{:S(2)}) collective-permute-start(bf16[1,4,64,512]{3,2,1,0:T(8,128)(2,1)S(1)} %bitcast.22), channel_id=1, source_target_pairs={{0,4},{1,5},{2,6},{3,7},{4,0},{5,1},{6,2},{7,3},{8,12},{9,13},{10,... | collective-permute-start | bytes 786440 | tf_op jit(solution)/shard_map/ppermute | solution.py:403
  24.7 32.2 %copy-start.3 = (bf16[8,64,512]{2,1,0:T(8,128)(2,1)}, bf16[8,64,512]{2,1,0:T(8,128)(2,1)S(1)}, u32[]{:S(2)}) copy-start(bf16[8,64,512]{2,1,0:T(8,128)(2,1)S(1)} %constant_dynamic-update-slice_fusion.5.refs_4_) | copy-start | bytes 1572868
  24.7 28.5 %collective-permute-start.10 = (bf16[8,64,512]{2,1,0:T(8,128)(2,1)S(1)}, bf16[8,64,512]{2,1,0:T(8,128)(2,1)S(1)}, u32[]{:S(2)}, u32[]{:S(2)}) collective-permute-start(bf16[8,64,512]{2,1,0:T(8,128)(2,1)S(1)} %constant_dynamic-update-slice_fusion.5.refs_4_), channel_id=1, source_target_pairs={{0,8},{1,9},{2,10},{3,11},{4,12},{5,13},{6,14},{7,15},{8,0},{9,1},... | collective-permute-start | bytes 1572872 | tf_op jit(solution)/shard_map/ppermute | solution.py:403
  26.4 30.5 %copy-start.2 = (bf16[8,64,512]{2,1,0:T(8,128)(2,1)}, bf16[8,64,512]{2,1,0:T(8,128)(2,1)S(1)}, u32[]{:S(2)}) copy-start(bf16[8,64,512]{2,1,0:T(8,128)(2,1)S(1)} %constant_dynamic-update-slice_fusion.refs_0_) | copy-start | bytes 1572868
  26.4 27.1 %collective-permute-start.6 = (bf16[8,64,512]{2,1,0:T(8,128)(2,1)S(1)}, bf16[8,64,512]{2,1,0:T(8,128)(2,1)S(1)}, u32[]{:S(2)}, u32[]{:S(2)}) collective-permute-start(bf16[8,64,512]{2,1,0:T(8,128)(2,1)S(1)} %constant_dynamic-update-slice_fusion.refs_0_), channel_id=1, source_target_pairs={{0,16},{1,17},{2,18},{3,19},{4,20},{5,21},{6,22},{7,23},{8,24},{9,... | collective-permute-start | bytes 1572872 | tf_op jit(solution)/shard_map/ppermute | solution.py:403
  33.5 0.7 copy-start.21
  33.5 20.2 %collective-permute-start.14 = (bf16[2,4,64,512]{3,2,1,0:T(8,128)(2,1)S(1)}, bf16[2,4,64,512]{3,2,1,0:T(8,128)(2,1)S(1)}, u32[]{:S(2)}, u32[]{:S(2)}) collective-permute-start(bf16[2,4,64,512]{3,2,1,0:T(8,128)(2,1)S(1)} %pad_maximum_fusion.1), channel_id=1, source_target_pairs={{0,2},{1,3},{2,0},{3,1},{4,6},{5,7},{6,4},{7,5},{8,10},{9,11},{10,... | collective-permute-start | bytes 1572872 | tf_op jit(solution)/shard_map/ppermute | solution.py:403
  52.1 0.6 copy-start.22
  52.7 4.2 %copy-start.20 = (s32[133]{0:T(256)}, s32[133]{0:T(256)S(1)}, u32[]{:S(2)}) copy-start(s32[133]{0:T(256)S(1)} %get-tuple-element.25.work_ref) | copy-start | bytes 1600
  52.7 1.9 %collective-permute-start.11 = (bf16[8,64,512]{2,1,0:T(8,128)(2,1)S(1)}, bf16[8,64,512]{2,1,0:T(8,128)(2,1)S(1)}, u32[]{:S(2)}, u32[]{:S(2)}) collective-permute-start(bf16[8,64,512]{2,1,0:T(8,128)(2,1)S(1)} %constant_dynamic-update-slice_fusion.5.refs_4_), channel_id=1, source_target_pairs={{0,1},{1,0},{2,3},{3,2},{4,5},{5,4},{6,7},{7,6},{8,9},{9,8},{10,11... | collective-permute-start | bytes 1572872 | tf_op jit(solution)/shard_map/ppermute | solution.py:403
  53.0 2.3 %collective-permute-start.7 = (bf16[8,64,512]{2,1,0:T(8,128)(2,1)S(1)}, bf16[8,64,512]{2,1,0:T(8,128)(2,1)S(1)}, u32[]{:S(2)}, u32[]{:S(2)}) collective-permute-start(bf16[8,64,512]{2,1,0:T(8,128)(2,1)S(1)} %constant_dynamic-update-slice_fusion.refs_0_), channel_id=1, source_target_pairs={{0,1},{1,0},{2,3},{3,2},{4,5},{5,4},{6,7},{7,6},{8,9},{9,8},{10,11... | collective-permute-start | bytes 1572872 | tf_op jit(solution)/shard_map/ppermute | solution.py:403
  53.2 3.7 %copy-start.6 = (bf16[8,64,512]{2,1,0:T(8,128)(2,1)}, bf16[8,64,512]{2,1,0:T(8,128)(2,1)S(1)}, u32[]{:S(2)}) copy-start(bf16[8,64,512]{2,1,0:T(8,128)(2,1)S(1)} %collective-permute-done.10.refs_5_) | copy-start | bytes 1572868
  53.2 2.9 %collective-permute-start.12 = (bf16[8,64,512]{2,1,0:T(8,128)(2,1)S(1)}, bf16[8,64,512]{2,1,0:T(8,128)(2,1)S(1)}, u32[]{:S(2)}, u32[]{:S(2)}) collective-permute-start(bf16[8,64,512]{2,1,0:T(8,128)(2,1)S(1)} %collective-permute-done.10.refs_5_), channel_id=1, source_target_pairs={{0,1},{1,0},{2,3},{3,2},{4,5},{5,4},{6,7},{7,6},{8,9},{9,8},{10,11... | collective-permute-start | bytes 1572872 | tf_op jit(solution)/shard_map/ppermute | solution.py:403
  53.5 3.3 %copy-start.7 = (bf16[8,64,512]{2,1,0:T(8,128)(2,1)}, bf16[8,64,512]{2,1,0:T(8,128)(2,1)S(1)}, u32[]{:S(2)}) copy-start(bf16[8,64,512]{2,1,0:T(8,128)(2,1)S(1)} %collective-permute-done.6.refs_1_) | copy-start | bytes 1572868
  53.5 3.3 %collective-permute-start.8 = (bf16[8,64,512]{2,1,0:T(8,128)(2,1)S(1)}, bf16[8,64,512]{2,1,0:T(8,128)(2,1)S(1)}, u32[]{:S(2)}, u32[]{:S(2)}) collective-permute-start(bf16[8,64,512]{2,1,0:T(8,128)(2,1)S(1)} %collective-permute-done.6.refs_1_), channel_id=1, source_target_pairs={{0,1},{1,0},{2,3},{3,2},{4,5},{5,4},{6,7},{7,6},{8,9},{9,8},{10,11... | collective-permute-start | bytes 1572872 | tf_op jit(solution)/shard_map/ppermute | solution.py:403
  53.8 3.1 %copy-start.1 = (bf16[512,512]{1,0:T(8,128)(2,1)S(1)}, bf16[512,512]{1,0:T(8,128)(2,1)}, u32[]{:S(2)}) copy-start(bf16[512,512]{1,0:T(8,128)(2,1)} %wk_hbm.3) | copy-start | bytes 1572868
  53.8 3.1 %copy-start.12 = (s32[240,128,4]{1,2,0:T(4,128)S(1)}, s32[240,128,4]{1,2,0:T(4,128)}, u32[]{:S(2)}) copy-start(s32[240,128,4]{1,2,0:T(4,128)} %param.15) | copy-start | bytes 1474564
  53.9 12.7 %copy-start.24 = (bf16[4,2,64,512]{3,2,1,0:T(8,128)(2,1)}, bf16[4,2,64,512]{3,2,1,0:T(8,128)(2,1)S(1)}, u32[]{:S(2)}) copy-start(bf16[4,2,64,512]{3,2,1,0:T(8,128)(2,1)S(1)} %get-tuple-element.47) | copy-start | bytes 1572868
  53.9 13.1 %copy-start.23 = (bf16[4,2,64,512]{3,2,1,0:T(8,128)(2,1)}, bf16[4,2,64,512]{3,2,1,0:T(8,128)(2,1)S(1)}, u32[]{:S(2)}) copy-start(bf16[4,2,64,512]{3,2,1,0:T(8,128)(2,1)S(1)} %get-tuple-element.46) | copy-start | bytes 1572868
  54.6 6.6 %copy-start.8 = (bf16[8,64,512]{2,1,0:T(8,128)(2,1)}, bf16[8,64,512]{2,1,0:T(8,128)(2,1)S(1)}, u32[]{:S(2)}) copy-start(bf16[8,64,512]{2,1,0:T(8,128)(2,1)S(1)} %collective-permute-done.11.refs_6_) | copy-start | bytes 1572868
  55.3 5.9 %copy-start.9 = (bf16[8,64,512]{2,1,0:T(8,128)(2,1)}, bf16[8,64,512]{2,1,0:T(8,128)(2,1)S(1)}, u32[]{:S(2)}) copy-start(bf16[8,64,512]{2,1,0:T(8,128)(2,1)S(1)} %collective-permute-done.7.refs_2_) | copy-start | bytes 1572868
  56.1 5.1 %copy-start.10 = (bf16[8,64,512]{2,1,0:T(8,128)(2,1)}, bf16[8,64,512]{2,1,0:T(8,128)(2,1)S(1)}, u32[]{:S(2)}) copy-start(bf16[8,64,512]{2,1,0:T(8,128)(2,1)S(1)} %collective-permute-done.12.refs_7_) | copy-start | bytes 1572868
  56.8 4.4 %copy-start.11 = (bf16[8,64,512]{2,1,0:T(8,128)(2,1)}, bf16[8,64,512]{2,1,0:T(8,128)(2,1)S(1)}, u32[]{:S(2)}) copy-start(bf16[8,64,512]{2,1,0:T(8,128)(2,1)S(1)} %collective-permute-done.8.refs_3_) | copy-start | bytes 1572868
  61.2 18.2 %collective-permute-start.15 = (bf16[8,64,512]{2,1,0:T(8,128)(2,1)S(1)}, bf16[8,64,512]{2,1,0:T(8,128)(2,1)S(1)}, u32[]{:S(2)}, u32[]{:S(2)}) collective-permute-start(bf16[8,64,512]{2,1,0:T(8,128)(2,1)S(1)} %bitcast.28), channel_id=1, source_target_pairs={{0,16},{1,17},{2,18},{3,19},{4,20},{5,21},{6,22},{7,23},{8,24},{9,... | collective-permute-start | bytes 1572872 | tf_op jit(solution)/shard_map/ppermute | solution.py:403
  63.5 16.0 %collective-permute-start.18 = (bf16[8,64,512]{2,1,0:T(8,128)(2,1)S(1)}, bf16[8,64,512]{2,1,0:T(8,128)(2,1)S(1)}, u32[]{:S(2)}, u32[]{:S(2)}) collective-permute-start(bf16[8,64,512]{2,1,0:T(8,128)(2,1)S(1)} %bitcast.25), channel_id=1, source_target_pairs={{0,8},{1,9},{2,10},{3,11},{4,12},{5,13},{6,14},{7,15},{8,0},{9,1},... | collective-permute-start | bytes 1572872 | tf_op jit(solution)/shard_map/ppermute | solution.py:403
  63.5 16.0 %all-to-all-start.1 = ((f32[32,16,128]{2,1,0:T(8,128)}), f32[32,16,128]{2,1,0:T(8,128)S(1)}, u32[]{:S(2)}, u32[]{:S(2)}) async-start(f32[32,16,128]{2,1,0:T(8,128)} %get-tuple-element.40.stats_hbm), calls=%async_computation.1 | async-start | bytes 524288 | tf_op jit(solution)/shard_map/all_to_all | solution.py:523
  66.7 13.4 %collective-permute-start.16 = (bf16[8,64,512]{2,1,0:T(8,128)(2,1)S(1)}, bf16[8,64,512]{2,1,0:T(8,128)(2,1)S(1)}, u32[]{:S(2)}, u32[]{:S(2)}) collective-permute-start(bf16[8,64,512]{2,1,0:T(8,128)(2,1)S(1)} %bitcast.29), channel_id=1, source_target_pairs={{0,1},{1,0},{2,3},{3,2},{4,5},{5,4},{6,7},{7,6},{8,9},{9,8},{10,11... | collective-permute-start | bytes 1572872 | tf_op jit(solution)/shard_map/ppermute | solution.py:403
  67.0 13.1 %collective-permute-start.19 = (bf16[8,64,512]{2,1,0:T(8,128)(2,1)S(1)}, bf16[8,64,512]{2,1,0:T(8,128)(2,1)S(1)}, u32[]{:S(2)}, u32[]{:S(2)}) collective-permute-start(bf16[8,64,512]{2,1,0:T(8,128)(2,1)S(1)} %bitcast.26), channel_id=1, source_target_pairs={{0,1},{1,0},{2,3},{3,2},{4,5},{5,4},{6,7},{7,6},{8,9},{9,8},{10,11... | collective-permute-start | bytes 1572872 | tf_op jit(solution)/shard_map/ppermute | solution.py:403
  79.4 2.7 %copy-start.25 = (f32[32,16,128]{2,1,0:T(8,128)}, f32[32,16,128]{2,1,0:T(8,128)S(1)}, u32[]{:S(2)}) copy-start(f32[32,16,128]{2,1,0:T(8,128)S(1)} %all-to-all-done.1.stats_all_ref) | copy-start | bytes 786436
  79.4 2.7 %copy-start.26 = (bf16[8,64,512]{2,1,0:T(8,128)(2,1)}, bf16[8,64,512]{2,1,0:T(8,128)(2,1)S(1)}, u32[]{:S(2)}) copy-start(bf16[8,64,512]{2,1,0:T(8,128)(2,1)S(1)} %collective-permute-done.15.refs_9_) | copy-start | bytes 1572868
  79.5 2.0 %collective-permute-start.17 = (bf16[8,64,512]{2,1,0:T(8,128)(2,1)S(1)}, bf16[8,64,512]{2,1,0:T(8,128)(2,1)S(1)}, u32[]{:S(2)}, u32[]{:S(2)}) collective-permute-start(bf16[8,64,512]{2,1,0:T(8,128)(2,1)S(1)} %collective-permute-done.15.refs_9_), channel_id=1, source_target_pairs={{0,1},{1,0},{2,3},{3,2},{4,5},{5,4},{6,7},{7,6},{8,9},{9,8},{10,11... | collective-permute-start | bytes 1572872 | tf_op jit(solution)/shard_map/ppermute | solution.py:403
  79.5 2.6 %copy-start.27 = (bf16[8,64,512]{2,1,0:T(8,128)(2,1)}, bf16[8,64,512]{2,1,0:T(8,128)(2,1)S(1)}, u32[]{:S(2)}) copy-start(bf16[8,64,512]{2,1,0:T(8,128)(2,1)S(1)} %collective-permute-done.18.refs_13_) | copy-start | bytes 1572868
  79.5 2.6 %collective-permute-start.20 = (bf16[8,64,512]{2,1,0:T(8,128)(2,1)S(1)}, bf16[8,64,512]{2,1,0:T(8,128)(2,1)S(1)}, u32[]{:S(2)}, u32[]{:S(2)}) collective-permute-start(bf16[8,64,512]{2,1,0:T(8,128)(2,1)S(1)} %collective-permute-done.18.refs_13_), channel_id=1, source_target_pairs={{0,1},{1,0},{2,3},{3,2},{4,5},{5,4},{6,7},{7,6},{8,9},{9,8},{10,11... | collective-permute-start | bytes 1572872 | tf_op jit(solution)/shard_map/ppermute | solution.py:403
  80.0 2.2 %copy-start.28 = (bf16[8,64,512]{2,1,0:T(8,128)(2,1)}, bf16[8,64,512]{2,1,0:T(8,128)(2,1)S(1)}, u32[]{:S(2)}) copy-start(bf16[8,64,512]{2,1,0:T(8,128)(2,1)S(1)} %collective-permute-done.16.refs_10_) | copy-start | bytes 1572868
  80.0 2.2 %copy-start.29 = (bf16[8,64,512]{2,1,0:T(8,128)(2,1)}, bf16[8,64,512]{2,1,0:T(8,128)(2,1)S(1)}, u32[]{:S(2)}) copy-start(bf16[8,64,512]{2,1,0:T(8,128)(2,1)S(1)} %collective-permute-done.19.refs_14_) | copy-start | bytes 1572868
  81.4 0.8 copy-start.30
  82.2 0.9 copy-start.31

commit v6 on v5

--- a/solution.py
+++ b/solution.py
@@ -99,7 +99,7 @@
         for slot in range(cap):
             row = jnp.where(lane == column * cap + slot, coords_ref[0, column, 0, slot], row)
     row = jnp.where(lane == 3 * cap, count_ref[0, 0], row)
-    out_ref[...] = jnp.broadcast_to(row[None], out_ref.shape)
+    out_ref[0] = row
 
 
 def scan_list(lists_ref, cap, row, column, wanted, found, out_ref, block_of):
@@ -117,39 +117,50 @@
     out_ref[0] = (found + 1) // 2
 
 
-def work_kernel(sizes, lists_hbm, query_work_ref, key_work_ref, lists_ref, sem):
+def query_work_kernel(sizes, lists_hbm, work_ref, lists_ref, sem):
     readers, blks, cap = sizes
     layout = Layout(*sizes)
     copy = pltpu.make_async_copy(lists_hbm, lists_ref, sem)
     copy.start()
     copy.wait()
 
-    def query_side(blk, found):
-        row = layout.reader * blks + blk
+    def one(k, found):
+        blk = jnp.bitwise_xor(k, layout.blk)
+        row = k // 2 + (k & 1) * (blks // 2)
         put = lambda other: other * blks + blk
-        return scan_list(lists_ref, cap, row, 0, layout.blk, found, query_work_ref, put)
-
-    close_work(lax.fori_loop(0, blks, query_side, 0), query_work_ref)
-
-    def key_side(reader, found):
-        row = reader * blks + layout.blk
+        return scan_list(lists_ref, cap, row, 0, layout.blk, found, work_ref, put)
+
+    close_work(lax.fori_loop(0, blks, one, 0), work_ref)
+
+
+def key_work_kernel(sizes, lists_hbm, work_ref, lists_ref, sem):
+    readers, blks, cap = sizes
+    layout = Layout(*sizes)
+    copy = pltpu.make_async_copy(lists_hbm, lists_ref, sem)
+    copy.start()
+    copy.wait()
+
+    def one(k, found):
+        reader = jnp.bitwise_xor(k, layout.reader)
         put = lambda other: reader * blks + other
-        return scan_list(lists_ref, cap, row, 1, layout.reader, found, key_work_ref, put)
-
-    close_work(lax.fori_loop(0, readers, key_side, 0), key_work_ref)
+        return scan_list(lists_ref, cap, k, 1, layout.reader, found, work_ref, put)
+
+    close_work(lax.fori_loop(0, readers, one, 0), work_ref)
 
 
 def prepare_kernel(
-    own_ref, cot_ref, wq_ref, wk_ref, wv_ref, query_stack_ref, cot_stack_ref, key_ref, value_ref, wkt_ref, wvt_ref
+    own_ref, cot_ref, wq_ref, wk_ref, wv_ref,
+    query_stack_ref, cot_stack_ref, key_ref, value_ref, wqt_ref, wkt_ref, wvt_ref,
 ):
     head = own_ref.shape[1] // HEADS
     queries = dot(own_ref[...], wq_ref[...]).astype(jnp.bfloat16) * jnp.bfloat16(head**-0.5)
     for p in range(HEADS // 2):
         pair = slice(2 * head * p, 2 * head * (p + 1))
-        query_stack_ref[p] = pair_stack(queries[:, pair])
-        cot_stack_ref[p] = pair_stack(cot_ref[:, pair])
+        query_stack_ref[p] = pair_stack(queries[:, pair]).T
+        cot_stack_ref[p] = pair_stack(cot_ref[:, pair]).T
     key_ref[...] = dot(own_ref[...], wk_ref[...]).astype(jnp.bfloat16)
     value_ref[...] = dot(own_ref[...], wv_ref[...]).astype(jnp.bfloat16)
+    wqt_ref[...] = wq_ref[...].T
     wkt_ref[...] = wk_ref[...].T
     wvt_ref[...] = wv_ref[...].T
 
@@ -236,7 +247,7 @@
         values = dot(wvt_ref[...], rows, NT).astype(jnp.bfloat16)
         bias_ref[...] = rows_in.bias(slot, blocks, patterns)
         for p in range(HEADS // 2):
-            scores = dot(keys[:, 2 * head * p : 2 * head * (p + 1)], stack_ref[p], NT)
+            scores = dot(keys[:, 2 * head * p : 2 * head * (p + 1)], stack_ref[p])
             for e in range(2):
                 score_ref[2 * p + e] = scores[:, block * e : block * (e + 1)] + bias_ref[...]
         for h in range(HEADS):
@@ -269,10 +280,10 @@
 
 
 def query_grad_kernel(
-    sizes, work_ref, stack_hbm, cot_stack_hbm, stats_hbm, wq_hbm, wk_hbm, wkt_hbm, wv_hbm, mask_ref, *refs
+    sizes, work_ref, stack_hbm, cot_stack_hbm, stats_hbm, wqt_hbm, wk_hbm, wkt_hbm, wv_hbm, mask_ref, *refs
 ):
     groups, refs = refs[:8], refs[8:]
-    part_ref, stack_ref, cot_stack_ref, stats_ref, wq_ref, wk_ref, wkt_ref, wv_ref = refs[:8]
+    part_ref, stack_ref, cot_stack_ref, stats_ref, wqt_ref, wk_ref, wkt_ref, wv_ref = refs[:8]
     buf, words, bias_ref, acc_ref, score_ref, d_prob_ref, sems, w_sems = refs[8:]
     layout = Layout(*sizes)
     block, width = part_ref.shape
@@ -281,7 +292,7 @@
     first_step(work_ref, rows_in.start)
     loads = load((
         (wk_hbm, wk_ref), (stack_hbm, stack_ref), (wv_hbm, wv_ref), (cot_stack_hbm, cot_stack_ref),
-        (wkt_hbm, wkt_ref), (stats_hbm.at[0], stats_ref), (wq_hbm, wq_ref),
+        (wkt_hbm, wkt_ref), (stats_hbm.at[0], stats_ref), (wqt_hbm, wqt_ref),
     ), w_sems)
     acc_ref[...] = jnp.zeros(acc_ref.shape, jnp.float32)
     for copy in loads[:6]:
@@ -295,8 +306,8 @@
         bias_ref[...] = rows_in.bias(slot, blocks, patterns)
         for p in range(HEADS // 2):
             pair = slice(2 * head * p, 2 * head * (p + 1))
-            scores = dot(keys[:, pair], stack_ref[p], NT)
-            d_probs = dot(values[:, pair], cot_stack_ref[p], NT)
+            scores = dot(keys[:, pair], stack_ref[p])
+            d_probs = dot(values[:, pair], cot_stack_ref[p])
             for e in range(2):
                 of = slice(block * e, block * (e + 1))
                 score_ref[2 * p + e] = scores[:, of] + bias_ref[...]
@@ -311,16 +322,16 @@
     run_steps(work_ref, rows_in.start, rows_in.wait, tiles)
     loads[6].wait()
     grad = (acc_ref[...].T * (head**-0.5)).astype(jnp.bfloat16)
-    part_ref[...] = dot(grad, wq_ref[...], NT)
+    part_ref[...] = dot(grad, wqt_ref[...])
 
 
 def key_grad_kernel(
-    sizes, bits, work_ref, key_hbm, value_hbm, wq_hbm, wk_hbm, wv_hbm, part_hbm, mask_ref, stats_all_ref, *refs
+    sizes, bits, work_ref, key_hbm, value_hbm, wq_hbm, wkt_hbm, wvt_hbm, part_hbm, mask_ref, stats_all_ref, *refs
 ):
     readers = sizes[0]
     groups, refs = refs[:8], refs[8:]
     halves, refs = (refs[:readers], refs[readers : 2 * readers]), refs[2 * readers :]
-    out_ref, key_ref, value_ref, part_ref, wq_ref, wk_ref, wv_ref, buf, words, cot_buf, stats, bias_ref = refs[:12]
+    out_ref, key_ref, value_ref, part_ref, wq_ref, wkt_ref, wvt_ref, buf, words, cot_buf, stats, bias_ref = refs[:12]
     query_stack_ref, cot_stack_ref, score_ref, d_prob_ref, key_acc, value_acc, sems, c_sems, w_sems = refs[12:]
     layout = Layout(*sizes)
     block, width = out_ref.shape
@@ -351,7 +362,7 @@
     first_step(work_ref, start)
     loads = load((
         (wq_hbm, wq_ref), (key_hbm, key_ref), (value_hbm, value_ref),
-        (wk_hbm, wk_ref), (wv_hbm, wv_ref), (part_hbm, part_ref),
+        (wkt_hbm, wkt_ref), (wvt_hbm, wvt_ref), (part_hbm, part_ref),
     ), w_sems)
     key_acc[...] = jnp.zeros(key_acc.shape, jnp.float32)
     value_acc[...] = jnp.zeros(value_acc.shape, jnp.float32)
@@ -387,8 +398,8 @@
     run_steps(work_ref, start, wait, tiles)
     for copy in loads[3:]:
         copy.wait()
-    grad = part_ref[...] + dot(key_acc[...].astype(jnp.bfloat16), wk_ref[...], NT)
-    grad = grad + dot(value_acc[...].astype(jnp.bfloat16), wv_ref[...], NT)
+    grad = part_ref[...] + dot(key_acc[...].astype(jnp.bfloat16), wkt_ref[...])
+    grad = grad + dot(value_acc[...].astype(jnp.bfloat16), wvt_ref[...])
     out_ref[...] = grad.astype(out_ref.dtype)
 
 
@@ -407,9 +418,10 @@
     return lax.optimization_barrier((value, *others))[0]
 
 
-def over_readers(chunk, order, blks):
+def over_readers(chunk, order, blks, *others):
     for bit in order[:-1]:
         chunk = jnp.concatenate([chunk, swap(chunk, blks << bit)], 0)
+    chunk = after(chunk, *others)
     return [chunk, swap(chunk, blks << order[-1])]
 
 
@@ -441,7 +453,7 @@
 
     sent = pl.pallas_call(
         send_list_kernel,
-        out_shape=shape((devices, 8, 128), i32),
+        out_shape=shape((1, 8, 128), i32),
         in_specs=[HBM, HBM],
         out_specs=VMEM,
         scratch_shapes=[
@@ -450,38 +462,47 @@
         compiler_params=some,
         name="send_list",
     )(tile_coords.transpose(0, 3, 1, 2), tile_count)
-    lists = lax.all_to_all(after(sent, *cot_other), axes, 0, 0, tiled=True)[:, 0]
-    query_work, key_work = pl.pallas_call(
-        functools.partial(work_kernel, sizes),
-        out_shape=(shape((2 * blks * cap + 5,), i32), shape((2 * readers * cap + 5,), i32)),
-        in_specs=[HBM],
-        out_specs=(SMEM, SMEM),
-        scratch_shapes=[pltpu.SMEM((devices, 128), i32), pltpu.SemaphoreType.DMA],
-        compiler_params=some,
-        cost_estimate=cost(2),
-        name="work",
-    )(lists)
-
-    stacks = shape((HEADS // 2, 2 * block, 2 * head), bf16)
+    sent = after(sent, *cot_other)
+    line_lists = jnp.concatenate([sent] + [swap(sent, 2 * k) for k in range(1, lines)], 0)
+    row_lists = jnp.concatenate([line_lists, swap(line_lists, 1)], 0)
+    sent = after(sent, line_lists)
+    column_lists = jnp.concatenate([sent] + [swap(sent, blks * k) for k in range(1, readers)], 0)
+
+    def work(kernel, lists, count, name):
+        return pl.pallas_call(
+            functools.partial(kernel, sizes),
+            out_shape=shape((2 * count * cap + 5,), i32),
+            in_specs=[HBM],
+            out_specs=SMEM,
+            scratch_shapes=[pltpu.SMEM((count, 128), i32), pltpu.SemaphoreType.DMA],
+            compiler_params=some,
+            cost_estimate=cost(1),
+            name=name,
+        )(lists[:, 0])
+
+    query_work = work(query_work_kernel, row_lists, blks, "query_work")
+    key_work = work(key_work_kernel, column_lists, readers, "key_work")
+
+    stacks = shape((HEADS // 2, 2 * head, 2 * block), bf16)
     own = shape((block, width), bf16)
     square = shape((width, width), bf16)
     prepared = pl.pallas_call(
         prepare_kernel,
-        out_shape=(stacks, stacks, own, own, square, square),
+        out_shape=(stacks, stacks, own, own, square, square, square),
         in_specs=[VMEM] * 5,
-        out_specs=(VMEM,) * 6,
+        out_specs=(VMEM,) * 7,
         compiler_params=some,
         cost_estimate=cost(2),
         name="prepare",
     )(features, cotangent, w_query, w_key, w_value)
-    query_stack, cot_stack, keys, values, w_key_t, w_value_t = prepared
+    query_stack, cot_stack, keys, values, w_query_t, w_key_t, w_value_t = prepared
 
     lined = after(lined, prepared)
     chunks = [jnp.concatenate([entry[:, half * k : half * (k + 1)] for entry in lined], 0) for k in range(2)]
-    here = [over_readers(chunk, order, blks) for chunk, order in zip(chunks, orders(readers))]
+    here = [over_readers(chunk, order, blks, row_lists) for chunk, order in zip(chunks, orders(readers))]
     rows_all = []
     for first, last in here:
-        rows_all += [first, last, swap(after(first, query_work), 1), swap(last, 1)]
+        rows_all += [first, last, swap(after(first, query_work, key_work), 1), swap(last, 1)]
 
     both = jnp.concatenate([cot_parts[0], cot_other[0], cot_parts[1], cot_other[1]], 0)
     cot_line = after(both, *chunks)[None]
@@ -534,7 +555,7 @@
         compiler_params=most,
         cost_estimate=cost(5),
         name="query_grad",
-    )(query_work, query_stack, cot_stack, stats, w_query, w_key, w_key_t, w_value, masks, *rows_all)
+    )(query_work, query_stack, cot_stack, stats, w_query_t, w_key, w_key_t, w_value, masks, *rows_all)
 
     cots_all = []
     for first, rest, other in cots_here:
@@ -554,7 +575,7 @@
         compiler_params=most,
         cost_estimate=cost(5),
         name="key_grad",
-    )(key_work, keys, values, w_query, w_key, w_value, query_part, masks, stats_all, *rows_all, *cots_all)
+    )(key_work, keys, values, w_query, w_key_t, w_value_t, query_part, masks, stats_all, *rows_all, *cots_all)
     return attn_out, grad_features
 
 

time: 89.7 us -> 86.6 us (0.965)
  blocking collectives: 15.1 us -> 0 us
  starting transfers between devices: 22.8 us -> 34.4 us
  Pallas kernels: 18.8 us -> 17.4 us
  waiting for transfers between devices: 22.3 us -> 23.7 us
    all_to_all x1 -> x0, blocking collectives: 15.1 us -> none  [local(): lax.all_to_all(after(sent, *cot_other), axes, 0, 0, tiled=True)[:, 0]]
    ppermute x21 -> x28, starting transfers between devices: 19.7 us -> 31.8 us  [swap(): return lax.ppermute(block, axes, [(i, i ^ mask) for i in range(count)])]
    ppermute x21 -> x28, waiting for transfers between devices: 15.7 us -> 18.3 us  [swap(): return lax.ppermute(block, axes, [(i, i ^ mask) for i in range(count)])]
    pallas_call x1, Pallas kernels: 4.29 us -> 2.93 us  [local(): pl.pallas_call(functools.partial(forward_kernel, sizes), out_shape=(own,...]
    all_to_all x1, waiting for transfers between devices: 6.58 us -> 5.37 us  [local(): stats_all = lax.all_to_all(stats, axes, 0, 0, tiled=True)]
    pallas_call x1, Pallas kernels: 5.62 us -> 4.57 us  [local(): pl.pallas_call(functools.partial(query_grad_kernel, sizes), out_shape=sha...]
    pallas_call x2 -> x3, Pallas kernels: 2.67 us -> 3.6 us  [the longest x2 3 us: work(): pl.pallas_call(functools.partial(kernel, sizes), out_shape=shape((2 * cou...]
    unnamed x64 -> x70, local copies, waits for them, and re-layouts: 6.72 us -> 7.36 us
  transfers between devices with their start and end apart: 22 -> 29, of which waited for: 11 -> 12; matrix products, arithmetic and copies ran while one was open for 2% -> 2% of each run, Pallas kernels for 10% -> 10%
where the time goes in v6:
time: 86.6 us; the launch traced here: 86 us
  starting transfers between devices  34.4 us (40%)
  waiting for transfers between devices  23.7 us (27%)
  Pallas kernels  17.4 us (20%)
  local copies, waits for them, and re-layouts  8.48 us (10%)
  between operations  1.78 us (2%)
    ppermute x28, starting transfers between devices, swap(): return lax.ppermute(block, axes, [(i, i ^ mask) for i in range(count)])  31.8 us
    ppermute x28, waiting for transfers between devices, swap(): return lax.ppermute(block, axes, [(i, i ^ mask) for i in range(count)])  18.3 us
    unnamed x70, local copies, waits for them, and re-layouts  7.36 us
    pallas_call x1, Pallas kernels, local(): pl.pallas_call(functools.partial(key_grad_kernel, sizes, bits), out_shape...  5.58 us
    all_to_all x1, waiting for transfers between devices, local(): stats_all = lax.all_to_all(stats, axes, 0, 0, tiled=True)  5.37 us
    pallas_call x1, Pallas kernels, local(): pl.pallas_call(functools.partial(query_grad_kernel, sizes), out_shape=sha...  4.57 us
    pallas_call x2, Pallas kernels, work(): pl.pallas_call(functools.partial(kernel, sizes), out_shape=shape((2 * cou...  3 us
    pallas_call x1, Pallas kernels, local(): pl.pallas_call(functools.partial(forward_kernel, sizes), out_shape=(own,...  2.93 us
  transfers between devices with their start and end apart: 29, of which 12 were waited for; matrix products, arithmetic and copies ran while one was open for 2% of the time, Pallas kernels for 10%

profile of v6, /device:TPU:0, one launch (start us, length us, event | category | flops | bytes accessed | tf_op | source)
XLA Modules:
  0.0 86.0 jit_solution(15026823158591809511)
XLA Ops:
  0.6 5.1 %collective-permute-start.8 = (bf16[1,128,512]{2,1,0:T(8,128)(2,1)}, bf16[1,128,512]{2,1,0:T(8,128)(2,1)S(1)}, u32[]{:S(2)}, u32[]{:S(2)}) collective-permute-start(bf16[1,128,512]{2,1,0:T(8,128)(2,1)} %bitcast.19), channel_id=1, source_target_pairs={{0,6},{1,7},{2,4},{3,5},{4,2},{5,3},{6,0},{7,1},{8,14},{9,15},{10,... | collective-permute-start | bytes 393224 | tf_op jit(solution)/shard_map/ppermute | solution.py:414
  5.8 0.6 collective-permute-start.6
  6.4 0.9 %slice_bitcast_fusion = (bf16[1,64,512]{2,1,0:T(8,128)(2,1)S(1)}, bf16[1,64,512]{2,1,0:T(8,128)(2,1)S(1)}) fusion(bf16[128,512]{1,0:T(8,128)(2,1)} %cot_ref.3), kind=kLoop, calls=%fused_computation.5 | loop fusion | bytes 262144 | tf_op jit(solution)/shard_map/broadcast_in_dim | solution.py:451
  7.3 1.7 %collective-permute-start.1 = (bf16[1,64,512]{2,1,0:T(8,128)(2,1)S(1)}, bf16[1,64,512]{2,1,0:T(8,128)(2,1)S(1)}, u32[]{:S(2)}, u32[]{:S(2)}) collective-permute-start(bf16[1,64,512]{2,1,0:T(8,128)(2,1)S(1)} %get-tuple-element.68), channel_id=1, source_target_pairs={{0,16},{1,17},{2,18},{3,19},{4,20},{5,21},{6,22},{7,23},{8,24},{9,... | collective-permute-start | bytes 196616 | tf_op jit(solution)/shard_map/ppermute | solution.py:414
  9.0 1.5 %collective-permute-start = (bf16[1,64,512]{2,1,0:T(8,128)(2,1)S(1)}, bf16[1,64,512]{2,1,0:T(8,128)(2,1)S(1)}, u32[]{:S(2)}, u32[]{:S(2)}) collective-permute-start(bf16[1,64,512]{2,1,0:T(8,128)(2,1)S(1)} %get-tuple-element.69), channel_id=1, source_target_pairs={{0,8},{1,9},{2,10},{3,11},{4,12},{5,13},{6,14},{7,15},{8,0},{9,1},... | collective-permute-start | bytes 196616 | tf_op jit(solution)/shard_map/ppermute | solution.py:414
  11.2 0.6 send_list.1
  11.8 0.0 copy-start.2
  11.8 1.0 %copy-done.2 = bf16[512,512]{1,0:T(8,128)(2,1)S(1)} copy-done((bf16[512,512]{1,0:T(8,128)(2,1)S(1)}, bf16[512,512]{1,0:T(8,128)(2,1)}, u32[]{:S(2)}) %copy-start.2) | copy-done | bytes 524312
  12.8 1.0 %copy-done.11 = bf16[512,512]{1,0:T(8,128)(2,1)S(1)} copy-done((bf16[512,512]{1,0:T(8,128)(2,1)S(1)}, bf16[512,512]{1,0:T(8,128)(2,1)}, u32[]{:S(2)}) %copy-start.11) | copy-done | bytes 524312
  13.9 1.0 %copy-done.12 = bf16[512,512]{1,0:T(8,128)(2,1)S(1)} copy-done((bf16[512,512]{1,0:T(8,128)(2,1)S(1)}, bf16[512,512]{1,0:T(8,128)(2,1)}, u32[]{:S(2)}) %copy-start.12) | copy-done | bytes 524312
  14.9 0.7 prepare.1
  15.7 0.8 copy-done.19
  16.5 0.7 copy-done.20
  17.2 0.7 copy-done.21
  17.8 0.6 copy-done.22
  18.5 3.7 %collective-permute-start.4 = (s32[1,8,128]{2,0,1:T(1,128)S(1)}, s32[1,8,128]{2,0,1:T(1,128)S(1)}, u32[]{:S(2)}, u32[]{:S(2)}) collective-permute-start(s32[1,8,128]{2,0,1:T(1,128)S(1)} %bitcast.23), channel_id=1, source_target_pairs={{0,6},{1,7},{2,4},{3,5},{4,2},{5,3},{6,0},{7,1},{8,14},{9,15},{10,... | collective-permute-start | bytes 12296 | tf_op jit(solution)/shard_map/ppermute | solution.py:414
  22.2 0.8 collective-permute-start.2
  23.1 0.6 collective-permute-start.9
  23.8 0.4 collective-permute-start.16
  24.2 2.4 %collective-permute-start.20 = (bf16[1,4,64,512]{3,2,1,0:T(8,128)(2,1)S(1)}, bf16[1,4,64,512]{3,2,1,0:T(8,128)(2,1)S(1)}, u32[]{:S(2)}, u32[]{:S(2)}) collective-permute-start(bf16[1,4,64,512]{3,2,1,0:T(8,128)(2,1)S(1)} %bitcast.33), channel_id=1, source_target_pairs={{0,4},{1,5},{2,6},{3,7},{4,0},{5,1},{6,2},{7,3},{8,12},{9,13},{10,... | collective-permute-start | bytes 786440 | tf_op jit(solution)/shard_map/ppermute | solution.py:414
  26.6 2.4 %collective-permute-done.3 = s32[1,8,128]{2,0,1:T(1,128)S(1)} collective-permute-done((s32[1,8,128]{2,0,1:T(1,128)S(1)}, s32[1,8,128]{2,0,1:T(1,128)S(1)}, u32[]{:S(2)}, u32[]{:S(2)}) %collective-permute-start.3) | collective-permute-done | bytes 4128 | tf_op jit(solution)/shard_map/ppermute | solution.py:414
  29.0 0.1 collective-permute-start.5
  29.1 1.2 %collective-permute-done.5 = s32[4,8,128]{2,0,1:T(4,128)S(1)} collective-permute-done((s32[4,8,128]{2,0,1:T(4,128)S(1)}, s32[4,8,128]{2,0,1:T(4,128)S(1)}, u32[]{:S(2)}, u32[]{:S(2)}) %collective-permute-start.5) | collective-permute-done | bytes 16416 | tf_op jit(solution)/shard_map/ppermute | solution.py:414
  30.4 1.4 %collective-permute-start.17 = (bf16[8,64,512]{2,1,0:T(8,128)(2,1)S(1)}, bf16[8,64,512]{2,1,0:T(8,128)(2,1)S(1)}, u32[]{:S(2)}, u32[]{:S(2)}) collective-permute-start(bf16[8,64,512]{2,1,0:T(8,128)(2,1)S(1)} %constant_dynamic-update-slice_fusion.5.refs_4_), channel_id=1, source_target_pairs={{0,8},{1,9},{2,10},{3,11},{4,12},{5,13},{6,14},{7,15},{8,0},{9,1},... | collective-permute-start | bytes 1572872 | tf_op jit(solution)/shard_map/ppermute | solution.py:414
  31.8 0.5 collective-permute-start.10
  32.3 4.1 %collective-permute-done.20 = bf16[1,4,64,512]{3,2,1,0:T(8,128)(2,1)S(1)} collective-permute-done((bf16[1,4,64,512]{3,2,1,0:T(8,128)(2,1)S(1)}, bf16[1,4,64,512]{3,2,1,0:T(8,128)(2,1)S(1)}, u32[]{:S(2)}, u32[]{:S(2)}) %collective-permute-start.20) | collective-permute-done | bytes 262176 | tf_op jit(solution)/shard_map/ppermute | solution.py:414
  36.4 0.1 pad_maximum_fusion.1
  36.5 0.4 collective-permute-start.21
  36.9 2.4 %collective-permute-start.13 = (s32[1,8,128]{2,0,1:T(1,128)S(1)}, s32[1,8,128]{2,0,1:T(1,128)S(1)}, u32[]{:S(2)}, u32[]{:S(2)}) collective-permute-start(s32[1,8,128]{2,0,1:T(1,128)S(1)} %bitcast.28), channel_id=1, source_target_pairs={{0,24},{1,25},{2,26},{3,27},{4,28},{5,29},{6,30},{7,31},{8,16},{9,... | collective-permute-start | bytes 12296 | tf_op jit(solution)/shard_map/ppermute | solution.py:414
  39.3 0.5 collective-permute-start.12
  39.8 3.4 %collective-permute-done.13 = s32[1,8,128]{2,0,1:T(1,128)S(1)} collective-permute-done((s32[1,8,128]{2,0,1:T(1,128)S(1)}, s32[1,8,128]{2,0,1:T(1,128)S(1)}, u32[]{:S(2)}, u32[]{:S(2)}) %collective-permute-start.13) | collective-permute-done | bytes 4128 | tf_op jit(solution)/shard_map/ppermute | solution.py:414
  43.2 1.5 %collective-permute-start.11 = (s32[1,8,128]{2,0,1:T(1,128)S(1)}, s32[1,8,128]{2,0,1:T(1,128)S(1)}, u32[]{:S(2)}, u32[]{:S(2)}) collective-permute-start(s32[1,8,128]{2,0,1:T(1,128)S(1)} %bitcast.30), channel_id=1, source_target_pairs={{0,8},{1,9},{2,10},{3,11},{4,12},{5,13},{6,14},{7,15},{8,0},{9,1},... | collective-permute-start | bytes 12296 | tf_op jit(solution)/shard_map/ppermute | solution.py:414
  44.7 2.1 %collective-permute-done.11 = s32[1,8,128]{2,0,1:T(1,128)S(1)} collective-permute-done((s32[1,8,128]{2,0,1:T(1,128)S(1)}, s32[1,8,128]{2,0,1:T(1,128)S(1)}, u32[]{:S(2)}, u32[]{:S(2)}) %collective-permute-start.11) | collective-permute-done | bytes 4128 | tf_op jit(solution)/shard_map/ppermute | solution.py:414
  46.8 1.3 %key_work.1.work_ref = s32[69]{0:T(128)S(1)} custom-call(s32[4,128]{1,0:T(4,128)S(1)} %fusion.lists_hbm), custom_call_target="tpu_custom_call" | custom-call | flops 200000000 | bytes 4000000 | tf_op jit(solution)/shard_map/key_work/pallas_call | solution.py:472
  48.2 0.5 copy-done.25
  48.7 1.7 %query_work.1.work_ref = s32[133]{0:T(256)S(1)} custom-call(s32[8,128]{1,0:T(8,128)S(1)} %slice_bitcast_fusion.2.lists_hbm), custom_call_target="tpu_custom_call" | custom-call | flops 200000000 | bytes 4000000 | tf_op jit(solution)/shard_map/query_work/pallas_call | solution.py:472
  50.4 0.0 copy-start.23
  50.4 0.1 collective-permute-start.18
  50.5 0.5 collective-permute-start.14
  51.0 0.1 collective-permute-start.19
  51.1 0.4 collective-permute-start.15
  51.5 0.1 pad_maximum_fusion
  51.6 0.0 copy-start.3
  51.6 0.0 copy-start.10
  51.7 0.1 fusion.1
  51.8 0.6 collective-permute-done.18.refs_6_
  52.4 0.7 collective-permute-done.14.refs_2_
  53.1 0.7 collective-permute-done.19.refs_7_
  53.9 0.7 collective-permute-done.15.refs_3_
  54.7 2.9 %forward.1 = (bf16[128,512]{1,0:T(8,128)(2,1)}, f32[32,16,128]{2,1,0:T(8,128)}) custom-call(s32[133]{0:T(256)S(1)} %query_work.1.work_ref, bf16[4,128,256]{2,1,0:T(8,128)(2,1)S(1)} %get-tuple-element.27.stack_ref.stack_hbm, bf16[128,512]{1,0:T(8,128)(2,1)S(1)} %copy-done.16, bf16[512,512]{1,0:T(8,128)(2,1)S(1)} %copy-done.3, ...), custom_call_target="tpu_custom_call" | custom-call | flops 1000000000 | bytes 4000000 | tf_op jit(solution)/shard_map/forward/pallas_call | solution.py:528
  57.7 2.8 %collective-permute-start.22 = (bf16[8,64,512]{2,1,0:T(8,128)(2,1)S(1)}, bf16[8,64,512]{2,1,0:T(8,128)(2,1)S(1)}, u32[]{:S(2)}, u32[]{:S(2)}) collective-permute-start(bf16[8,64,512]{2,1,0:T(8,128)(2,1)S(1)} %bitcast.39), channel_id=1, source_target_pairs={{0,16},{1,17},{2,18},{3,19},{4,20},{5,21},{6,22},{7,23},{8,24},{9,... | collective-permute-start | bytes 1572872 | tf_op jit(solution)/shard_map/ppermute | solution.py:414
  60.5 3.2 %collective-permute-start.25 = (bf16[8,64,512]{2,1,0:T(8,128)(2,1)S(1)}, bf16[8,64,512]{2,1,0:T(8,128)(2,1)S(1)}, u32[]{:S(2)}, u32[]{:S(2)}) collective-permute-start(bf16[8,64,512]{2,1,0:T(8,128)(2,1)S(1)} %bitcast.36), channel_id=1, source_target_pairs={{0,8},{1,9},{2,10},{3,11},{4,12},{5,13},{6,14},{7,15},{8,0},{9,1},... | collective-permute-start | bytes 1572872 | tf_op jit(solution)/shard_map/ppermute | solution.py:414
  63.7 2.6 %all-to-all-start = ((f32[32,16,128]{2,1,0:T(8,128)}), f32[32,16,128]{2,1,0:T(8,128)S(1)}, u32[]{:S(2)}, u32[]{:S(2)}) async-start(f32[32,16,128]{2,1,0:T(8,128)} %get-tuple-element.44.stats_hbm), calls=%async_computation | async-start | bytes 524288 | tf_op jit(solution)/shard_map/all_to_all | solution.py:544
  66.3 0.2 collective-permute-start.23
  66.5 0.4 collective-permute-start.26
  66.9 4.6 %query_grad.1.part_hbm = f32[128,512]{1,0:T(8,128)} custom-call(s32[133]{0:T(256)} %copy-done.23, bf16[4,128,256]{2,1,0:T(8,128)(2,1)} %copy-done.17, bf16[4,128,256]{2,1,0:T(8,128)(2,1)} %copy-done.20, f32[32,16,128]{2,1,0:T(8,128)} %get-tuple-element.44.stats_hbm, bf16[512,512]{1,0:T(8,128)(2,1)} %copy-done.19, bf16[512,512]{1,0:T(8,128)(2,1)} %wk_hbm.1, ...), custom_call_target="tpu_custom_call" | custom-call | flops 1000000000 | bytes 4000000 | tf_op jit(solution)/shard_map/query_grad/pallas_call | solution.py:546
  71.5 5.4 %all-to-all-done.stats_all_ref = f32[32,16,128]{2,1,0:T(8,128)S(1)} async-done(((f32[32,16,128]{2,1,0:T(8,128)}), f32[32,16,128]{2,1,0:T(8,128)S(1)}, u32[]{:S(2)}, u32[]{:S(2)}) %all-to-all-start) | async-done | bytes 262176 | tf_op jit(solution)/shard_map/all_to_all | solution.py:544
  76.8 0.3 collective-permute-start.24
  77.1 0.3 collective-permute-start.27
  77.4 1.4 %collective-permute-done.24.refs_11_ = bf16[8,64,512]{2,1,0:T(8,128)(2,1)S(1)} collective-permute-done((bf16[8,64,512]{2,1,0:T(8,128)(2,1)S(1)}, bf16[8,64,512]{2,1,0:T(8,128)(2,1)S(1)}, u32[]{:S(2)}, u32[]{:S(2)}) %collective-permute-start.24) | collective-permute-done | bytes 524320 | tf_op jit(solution)/shard_map/ppermute | solution.py:414
  78.8 0.7 collective-permute-done.27.refs_15_
  79.6 0.1 copy-done.33
  79.6 0.8 copy-done.34
  80.4 5.6 %key_grad.1 = bf16[128,512]{1,0:T(8,128)(2,1)} custom-call(s32[69]{0:T(128)} %copy-done.25, bf16[128,512]{1,0:T(8,128)(2,1)} %copy-done.21, bf16[128,512]{1,0:T(8,128)(2,1)} %copy-done.22, bf16[512,512]{1,0:T(8,128)(2,1)} %wq_hbm.1, bf16[512,512]{1,0:T(8,128)(2,1)} %copy-done.13, bf16[512,512]{1,0:T(8,128)(2,1)} %copy-done.14, ...), custom_call_target="tpu_custom_call" | custom-call | flops 1000000000 | bytes 4000000 | tf_op jit(solution)/shard_map/key_grad/pallas_call | solution.py:564
  (88 shorter events, 0.5 us)
Async XLA Ops:
  0.6 11.2 %copy-start.16 = (bf16[128,512]{1,0:T(8,128)(2,1)S(1)}, bf16[128,512]{1,0:T(8,128)(2,1)}, u32[]{:S(2)}) copy-start(bf16[128,512]{1,0:T(8,128)(2,1)} %cot_ref.3) | copy-start | bytes 393220
  0.6 11.2 %copy-start.18 = (bf16[128,512]{1,0:T(8,128)(2,1)S(1)}, bf16[128,512]{1,0:T(8,128)(2,1)}, u32[]{:S(2)}) copy-start(bf16[128,512]{1,0:T(8,128)(2,1)} %own_ref.1) | copy-start | bytes 393220
  0.6 21.5 %collective-permute-start.8 = (bf16[1,128,512]{2,1,0:T(8,128)(2,1)}, bf16[1,128,512]{2,1,0:T(8,128)(2,1)S(1)}, u32[]{:S(2)}, u32[]{:S(2)}) collective-permute-start(bf16[1,128,512]{2,1,0:T(8,128)(2,1)} %bitcast.19), channel_id=1, source_target_pairs={{0,6},{1,7},{2,4},{3,5},{4,2},{5,3},{6,0},{7,1},{8,14},{9,15},{10,... | collective-permute-start | bytes 393224 | tf_op jit(solution)/shard_map/ppermute | solution.py:414
  5.8 17.2 %collective-permute-start.7 = (bf16[1,128,512]{2,1,0:T(8,128)(2,1)}, bf16[1,128,512]{2,1,0:T(8,128)(2,1)S(1)}, u32[]{:S(2)}, u32[]{:S(2)}) collective-permute-start(bf16[1,128,512]{2,1,0:T(8,128)(2,1)} %bitcast.20), channel_id=1, source_target_pairs={{0,4},{1,5},{2,6},{3,7},{4,0},{5,1},{6,2},{7,3},{8,12},{9,13},{10,... | collective-permute-start | bytes 393224 | tf_op jit(solution)/shard_map/ppermute | solution.py:414
  5.8 17.2 %collective-permute-start.6 = (bf16[1,128,512]{2,1,0:T(8,128)(2,1)}, bf16[1,128,512]{2,1,0:T(8,128)(2,1)S(1)}, u32[]{:S(2)}, u32[]{:S(2)}) collective-permute-start(bf16[1,128,512]{2,1,0:T(8,128)(2,1)} %bitcast.21), channel_id=1, source_target_pairs={{0,2},{1,3},{2,0},{3,1},{4,6},{5,7},{6,4},{7,5},{8,10},{9,11},{10,... | collective-permute-start | bytes 393224 | tf_op jit(solution)/shard_map/ppermute | solution.py:414
  7.3 11.2 %collective-permute-start.1 = (bf16[1,64,512]{2,1,0:T(8,128)(2,1)S(1)}, bf16[1,64,512]{2,1,0:T(8,128)(2,1)S(1)}, u32[]{:S(2)}, u32[]{:S(2)}) collective-permute-start(bf16[1,64,512]{2,1,0:T(8,128)(2,1)S(1)} %get-tuple-element.68), channel_id=1, source_target_pairs={{0,16},{1,17},{2,18},{3,19},{4,20},{5,21},{6,22},{7,23},{8,24},{9,... | collective-permute-start | bytes 196616 | tf_op jit(solution)/shard_map/ppermute | solution.py:414
  9.0 2.1 %copy-start.24 = (s32[1,1,8,3]{2,1,3,0:T(1,128)S(1)}, s32[1,1,8,3]{2,1,3,0:T(1,128)}, u32[]{:S(2)}) copy-start(s32[1,1,8,3]{2,1,3,0:T(1,128)} %param.13) | copy-start | bytes 292
  9.0 9.4 %collective-permute-start = (bf16[1,64,512]{2,1,0:T(8,128)(2,1)S(1)}, bf16[1,64,512]{2,1,0:T(8,128)(2,1)S(1)}, u32[]{:S(2)}, u32[]{:S(2)}) collective-permute-start(bf16[1,64,512]{2,1,0:T(8,128)(2,1)S(1)} %get-tuple-element.69), channel_id=1, source_target_pairs={{0,8},{1,9},{2,10},{3,11},{4,12},{5,13},{6,14},{7,15},{8,0},{9,1},... | collective-permute-start | bytes 196616 | tf_op jit(solution)/shard_map/ppermute | solution.py:414
  11.8 1.0 %copy-start.2 = (bf16[512,512]{1,0:T(8,128)(2,1)S(1)}, bf16[512,512]{1,0:T(8,128)(2,1)}, u32[]{:S(2)}) copy-start(bf16[512,512]{1,0:T(8,128)(2,1)} %wk_hbm.1) | copy-start | bytes 1572868
  12.8 1.0 %copy-start.11 = (bf16[512,512]{1,0:T(8,128)(2,1)S(1)}, bf16[512,512]{1,0:T(8,128)(2,1)}, u32[]{:S(2)}) copy-start(bf16[512,512]{1,0:T(8,128)(2,1)} %wv_hbm.1) | copy-start | bytes 1572868
  13.9 1.0 %copy-start.12 = (bf16[512,512]{1,0:T(8,128)(2,1)S(1)}, bf16[512,512]{1,0:T(8,128)(2,1)}, u32[]{:S(2)}) copy-start(bf16[512,512]{1,0:T(8,128)(2,1)} %wq_hbm.1) | copy-start | bytes 1572868
  15.7 0.8 copy-start.19
  16.5 0.7 copy-start.20
  17.2 0.7 copy-start.21
  17.8 0.6 copy-start.22
  18.5 4.6 %copy-start.13 = (bf16[512,512]{1,0:T(8,128)(2,1)}, bf16[512,512]{1,0:T(8,128)(2,1)S(1)}, u32[]{:S(2)}) copy-start(bf16[512,512]{1,0:T(8,128)(2,1)S(1)} %get-tuple-element.33.wkt_hbm) | copy-start | bytes 1572868
  18.5 4.6 %copy-start.14 = (bf16[512,512]{1,0:T(8,128)(2,1)}, bf16[512,512]{1,0:T(8,128)(2,1)S(1)}, u32[]{:S(2)}) copy-start(bf16[512,512]{1,0:T(8,128)(2,1)S(1)} %get-tuple-element.28.wvt_ref.wvt_hbm) | copy-start | bytes 1572868
  18.5 36.2 %copy-start.17 = (bf16[4,128,256]{2,1,0:T(8,128)(2,1)}, bf16[4,128,256]{2,1,0:T(8,128)(2,1)S(1)}, u32[]{:S(2)}) copy-start(bf16[4,128,256]{2,1,0:T(8,128)(2,1)S(1)} %get-tuple-element.27.stack_ref.stack_hbm) | copy-start | bytes 786436
  18.5 5.7 %collective-permute-start.4 = (s32[1,8,128]{2,0,1:T(1,128)S(1)}, s32[1,8,128]{2,0,1:T(1,128)S(1)}, u32[]{:S(2)}, u32[]{:S(2)}) collective-permute-start(s32[1,8,128]{2,0,1:T(1,128)S(1)} %bitcast.23), channel_id=1, source_target_pairs={{0,6},{1,7},{2,4},{3,5},{4,2},{5,3},{6,0},{7,1},{8,14},{9,15},{10,... | collective-permute-start | bytes 12296 | tf_op jit(solution)/shard_map/ppermute | solution.py:414
  22.1 6.8 %collective-permute-start.3 = (s32[1,8,128]{2,0,1:T(1,128)S(1)}, s32[1,8,128]{2,0,1:T(1,128)S(1)}, u32[]{:S(2)}, u32[]{:S(2)}) collective-permute-start(s32[1,8,128]{2,0,1:T(1,128)S(1)} %bitcast.24), channel_id=1, source_target_pairs={{0,4},{1,5},{2,6},{3,7},{4,0},{5,1},{6,2},{7,3},{8,12},{9,13},{10,... | collective-permute-start | bytes 12296 | tf_op jit(solution)/shard_map/ppermute | solution.py:414
  22.2 6.8 %collective-permute-start.2 = (s32[1,8,128]{2,0,1:T(1,128)S(1)}, s32[1,8,128]{2,0,1:T(1,128)S(1)}, u32[]{:S(2)}, u32[]{:S(2)}) collective-permute-start(s32[1,8,128]{2,0,1:T(1,128)S(1)} %bitcast.25), channel_id=1, source_target_pairs={{0,2},{1,3},{2,0},{3,1},{4,6},{5,7},{6,4},{7,5},{8,10},{9,11},{10,... | collective-permute-start | bytes 12296 | tf_op jit(solution)/shard_map/ppermute | solution.py:414
  23.1 7.2 %collective-permute-start.9 = (bf16[4,64,512]{2,1,0:T(8,128)(2,1)S(1)}, bf16[4,64,512]{2,1,0:T(8,128)(2,1)S(1)}, u32[]{:S(2)}, u32[]{:S(2)}) collective-permute-start(bf16[4,64,512]{2,1,0:T(8,128)(2,1)S(1)} %pad_maximum_fusion.2), channel_id=1, source_target_pairs={{0,8},{1,9},{2,10},{3,11},{4,12},{5,13},{6,14},{7,15},{8,0},{9,1},... | collective-permute-start | bytes 786440 | tf_op jit(solution)/shard_map/ppermute | solution.py:414
  23.8 6.6 %collective-permute-start.16 = (bf16[4,64,512]{2,1,0:T(8,128)(2,1)S(1)}, bf16[4,64,512]{2,1,0:T(8,128)(2,1)S(1)}, u32[]{:S(2)}, u32[]{:S(2)}) collective-permute-start(bf16[4,64,512]{2,1,0:T(8,128)(2,1)S(1)} %pad_maximum_fusion.3), channel_id=1, source_target_pairs={{0,16},{1,17},{2,18},{3,19},{4,20},{5,21},{6,22},{7,23},{8,24},{9,... | collective-permute-start | bytes 786440 | tf_op jit(solution)/shard_map/ppermute | solution.py:414
  24.2 12.2 %collective-permute-start.20 = (bf16[1,4,64,512]{3,2,1,0:T(8,128)(2,1)S(1)}, bf16[1,4,64,512]{3,2,1,0:T(8,128)(2,1)S(1)}, u32[]{:S(2)}, u32[]{:S(2)}) collective-permute-start(bf16[1,4,64,512]{3,2,1,0:T(8,128)(2,1)S(1)} %bitcast.33), channel_id=1, source_target_pairs={{0,4},{1,5},{2,6},{3,7},{4,0},{5,1},{6,2},{7,3},{8,12},{9,13},{10,... | collective-permute-start | bytes 786440 | tf_op jit(solution)/shard_map/ppermute | solution.py:414
  29.0 1.2 %collective-permute-start.5 = (s32[4,8,128]{2,0,1:T(4,128)S(1)}, s32[4,8,128]{2,0,1:T(4,128)S(1)}, u32[]{:S(2)}, u32[]{:S(2)}) collective-permute-start(s32[4,8,128]{2,0,1:T(4,128)S(1)} %pad_add_fusion), channel_id=1, source_target_pairs={{0,1},{1,0},{2,3},{3,2},{4,5},{5,4},{6,7},{7,6},{8,9},{9,8},{10,11... | collective-permute-start | bytes 49160 | tf_op jit(solution)/shard_map/ppermute | solution.py:414
  30.3 24.3 %copy-start = (bf16[8,64,512]{2,1,0:T(8,128)(2,1)}, bf16[8,64,512]{2,1,0:T(8,128)(2,1)S(1)}, u32[]{:S(2)}) copy-start(bf16[8,64,512]{2,1,0:T(8,128)(2,1)S(1)} %constant_dynamic-update-slice_fusion.refs_0_) | copy-start | bytes 1572868
  30.4 24.3 %copy-start.1 = (bf16[8,64,512]{2,1,0:T(8,128)(2,1)}, bf16[8,64,512]{2,1,0:T(8,128)(2,1)S(1)}, u32[]{:S(2)}) copy-start(bf16[8,64,512]{2,1,0:T(8,128)(2,1)S(1)} %constant_dynamic-update-slice_fusion.5.refs_4_) | copy-start | bytes 1572868
  30.4 20.6 %collective-permute-start.17 = (bf16[8,64,512]{2,1,0:T(8,128)(2,1)S(1)}, bf16[8,64,512]{2,1,0:T(8,128)(2,1)S(1)}, u32[]{:S(2)}, u32[]{:S(2)}) collective-permute-start(bf16[8,64,512]{2,1,0:T(8,128)(2,1)S(1)} %constant_dynamic-update-slice_fusion.5.refs_4_), channel_id=1, source_target_pairs={{0,8},{1,9},{2,10},{3,11},{4,12},{5,13},{6,14},{7,15},{8,0},{9,1},... | collective-permute-start | bytes 1572872 | tf_op jit(solution)/shard_map/ppermute | solution.py:414
  31.8 19.3 %collective-permute-start.10 = (bf16[8,64,512]{2,1,0:T(8,128)(2,1)S(1)}, bf16[8,64,512]{2,1,0:T(8,128)(2,1)S(1)}, u32[]{:S(2)}, u32[]{:S(2)}) collective-permute-start(bf16[8,64,512]{2,1,0:T(8,128)(2,1)S(1)} %constant_dynamic-update-slice_fusion.refs_0_), channel_id=1, source_target_pairs={{0,16},{1,17},{2,18},{3,19},{4,20},{5,21},{6,22},{7,23},{8,24},{9,... | collective-permute-start | bytes 1572872 | tf_op jit(solution)/shard_map/ppermute | solution.py:414
  36.5 15.0 %collective-permute-start.21 = (bf16[2,4,64,512]{3,2,1,0:T(8,128)(2,1)S(1)}, bf16[2,4,64,512]{3,2,1,0:T(8,128)(2,1)S(1)}, u32[]{:S(2)}, u32[]{:S(2)}) collective-permute-start(bf16[2,4,64,512]{3,2,1,0:T(8,128)(2,1)S(1)} %pad_maximum_fusion.1), channel_id=1, source_target_pairs={{0,2},{1,3},{2,0},{3,1},{4,6},{5,7},{6,4},{7,5},{8,10},{9,11},{10,... | collective-permute-start | bytes 1572872 | tf_op jit(solution)/shard_map/ppermute | solution.py:414
  36.9 6.3 %collective-permute-start.13 = (s32[1,8,128]{2,0,1:T(1,128)S(1)}, s32[1,8,128]{2,0,1:T(1,128)S(1)}, u32[]{:S(2)}, u32[]{:S(2)}) collective-permute-start(s32[1,8,128]{2,0,1:T(1,128)S(1)} %bitcast.28), channel_id=1, source_target_pairs={{0,24},{1,25},{2,26},{3,27},{4,28},{5,29},{6,30},{7,31},{8,16},{9,... | collective-permute-start | bytes 12296 | tf_op jit(solution)/shard_map/ppermute | solution.py:414
  39.3 5.4 %collective-permute-start.12 = (s32[1,8,128]{2,0,1:T(1,128)S(1)}, s32[1,8,128]{2,0,1:T(1,128)S(1)}, u32[]{:S(2)}, u32[]{:S(2)}) collective-permute-start(s32[1,8,128]{2,0,1:T(1,128)S(1)} %bitcast.29), channel_id=1, source_target_pairs={{0,16},{1,17},{2,18},{3,19},{4,20},{5,21},{6,22},{7,23},{8,24},{9,... | collective-permute-start | bytes 12296 | tf_op jit(solution)/shard_map/ppermute | solution.py:414
  43.2 3.6 %collective-permute-start.11 = (s32[1,8,128]{2,0,1:T(1,128)S(1)}, s32[1,8,128]{2,0,1:T(1,128)S(1)}, u32[]{:S(2)}, u32[]{:S(2)}) collective-permute-start(s32[1,8,128]{2,0,1:T(1,128)S(1)} %bitcast.30), channel_id=1, source_target_pairs={{0,8},{1,9},{2,10},{3,11},{4,12},{5,13},{6,14},{7,15},{8,0},{9,1},... | collective-permute-start | bytes 12296 | tf_op jit(solution)/shard_map/ppermute | solution.py:414
  48.2 0.5 copy-start.25
  50.4 4.3 %copy-start.23 = (s32[133]{0:T(256)}, s32[133]{0:T(256)S(1)}, u32[]{:S(2)}) copy-start(s32[133]{0:T(256)S(1)} %query_work.1.work_ref) | copy-start | bytes 1600
  50.4 2.0 %collective-permute-start.18 = (bf16[8,64,512]{2,1,0:T(8,128)(2,1)S(1)}, bf16[8,64,512]{2,1,0:T(8,128)(2,1)S(1)}, u32[]{:S(2)}, u32[]{:S(2)}) collective-permute-start(bf16[8,64,512]{2,1,0:T(8,128)(2,1)S(1)} %constant_dynamic-update-slice_fusion.5.refs_4_), channel_id=1, source_target_pairs={{0,1},{1,0},{2,3},{3,2},{4,5},{5,4},{6,7},{7,6},{8,9},{9,8},{10,11... | collective-permute-start | bytes 1572872 | tf_op jit(solution)/shard_map/ppermute | solution.py:414
  50.5 2.6 %collective-permute-start.14 = (bf16[8,64,512]{2,1,0:T(8,128)(2,1)S(1)}, bf16[8,64,512]{2,1,0:T(8,128)(2,1)S(1)}, u32[]{:S(2)}, u32[]{:S(2)}) collective-permute-start(bf16[8,64,512]{2,1,0:T(8,128)(2,1)S(1)} %constant_dynamic-update-slice_fusion.refs_0_), channel_id=1, source_target_pairs={{0,1},{1,0},{2,3},{3,2},{4,5},{5,4},{6,7},{7,6},{8,9},{9,8},{10,11... | collective-permute-start | bytes 1572872 | tf_op jit(solution)/shard_map/ppermute | solution.py:414
  51.0 3.7 %copy-start.4 = (bf16[8,64,512]{2,1,0:T(8,128)(2,1)}, bf16[8,64,512]{2,1,0:T(8,128)(2,1)S(1)}, u32[]{:S(2)}) copy-start(bf16[8,64,512]{2,1,0:T(8,128)(2,1)S(1)} %collective-permute-done.17.refs_5_) | copy-start | bytes 1572868
  51.0 2.9 %collective-permute-start.19 = (bf16[8,64,512]{2,1,0:T(8,128)(2,1)S(1)}, bf16[8,64,512]{2,1,0:T(8,128)(2,1)S(1)}, u32[]{:S(2)}, u32[]{:S(2)}) collective-permute-start(bf16[8,64,512]{2,1,0:T(8,128)(2,1)S(1)} %collective-permute-done.17.refs_5_), channel_id=1, source_target_pairs={{0,1},{1,0},{2,3},{3,2},{4,5},{5,4},{6,7},{7,6},{8,9},{9,8},{10,11... | collective-permute-start | bytes 1572872 | tf_op jit(solution)/shard_map/ppermute | solution.py:414
  51.1 3.6 %copy-start.5 = (bf16[8,64,512]{2,1,0:T(8,128)(2,1)}, bf16[8,64,512]{2,1,0:T(8,128)(2,1)S(1)}, u32[]{:S(2)}) copy-start(bf16[8,64,512]{2,1,0:T(8,128)(2,1)S(1)} %collective-permute-done.10.refs_1_) | copy-start | bytes 1572868
  51.1 3.6 %collective-permute-start.15 = (bf16[8,64,512]{2,1,0:T(8,128)(2,1)S(1)}, bf16[8,64,512]{2,1,0:T(8,128)(2,1)S(1)}, u32[]{:S(2)}, u32[]{:S(2)}) collective-permute-start(bf16[8,64,512]{2,1,0:T(8,128)(2,1)S(1)} %collective-permute-done.10.refs_1_), channel_id=1, source_target_pairs={{0,1},{1,0},{2,3},{3,2},{4,5},{5,4},{6,7},{7,6},{8,9},{9,8},{10,11... | collective-permute-start | bytes 1572872 | tf_op jit(solution)/shard_map/ppermute | solution.py:414
  51.6 3.1 %copy-start.3 = (bf16[512,512]{1,0:T(8,128)(2,1)S(1)}, bf16[512,512]{1,0:T(8,128)(2,1)}, u32[]{:S(2)}) copy-start(bf16[512,512]{1,0:T(8,128)(2,1)} %wk_hbm.1) | copy-start | bytes 1572868
  51.6 3.1 %copy-start.10 = (s32[240,128,4]{1,2,0:T(4,128)S(1)}, s32[240,128,4]{1,2,0:T(4,128)}, u32[]{:S(2)}) copy-start(s32[240,128,4]{1,2,0:T(4,128)} %param.15) | copy-start | bytes 1474564
  51.6 3.1 %copy-start.15 = (bf16[512,512]{1,0:T(8,128)(2,1)S(1)}, bf16[512,512]{1,0:T(8,128)(2,1)}, u32[]{:S(2)}) copy-start(bf16[512,512]{1,0:T(8,128)(2,1)} %copy-done.14) | copy-start | bytes 1572868
  51.7 14.6 %copy-start.27 = (bf16[4,2,64,512]{3,2,1,0:T(8,128)(2,1)}, bf16[4,2,64,512]{3,2,1,0:T(8,128)(2,1)S(1)}, u32[]{:S(2)}) copy-start(bf16[4,2,64,512]{3,2,1,0:T(8,128)(2,1)S(1)} %get-tuple-element.51) | copy-start | bytes 1572868
  51.7 14.7 %copy-start.26 = (bf16[4,2,64,512]{3,2,1,0:T(8,128)(2,1)}, bf16[4,2,64,512]{3,2,1,0:T(8,128)(2,1)S(1)}, u32[]{:S(2)}) copy-start(bf16[4,2,64,512]{3,2,1,0:T(8,128)(2,1)S(1)} %get-tuple-element.50) | copy-start | bytes 1572868
  52.4 5.3 %copy-start.6 = (bf16[8,64,512]{2,1,0:T(8,128)(2,1)}, bf16[8,64,512]{2,1,0:T(8,128)(2,1)S(1)}, u32[]{:S(2)}) copy-start(bf16[8,64,512]{2,1,0:T(8,128)(2,1)S(1)} %collective-permute-done.18.refs_6_) | copy-start | bytes 1572868
  53.1 4.5 %copy-start.7 = (bf16[8,64,512]{2,1,0:T(8,128)(2,1)}, bf16[8,64,512]{2,1,0:T(8,128)(2,1)S(1)}, u32[]{:S(2)}) copy-start(bf16[8,64,512]{2,1,0:T(8,128)(2,1)S(1)} %collective-permute-done.14.refs_2_) | copy-start | bytes 1572868
  53.9 3.8 %copy-start.8 = (bf16[8,64,512]{2,1,0:T(8,128)(2,1)}, bf16[8,64,512]{2,1,0:T(8,128)(2,1)S(1)}, u32[]{:S(2)}) copy-start(bf16[8,64,512]{2,1,0:T(8,128)(2,1)S(1)} %collective-permute-done.19.refs_7_) | copy-start | bytes 1572868
  54.6 3.0 %copy-start.9 = (bf16[8,64,512]{2,1,0:T(8,128)(2,1)}, bf16[8,64,512]{2,1,0:T(8,128)(2,1)S(1)}, u32[]{:S(2)}) copy-start(bf16[8,64,512]{2,1,0:T(8,128)(2,1)S(1)} %collective-permute-done.15.refs_3_) | copy-start | bytes 1572868
  57.7 19.1 %collective-permute-start.22 = (bf16[8,64,512]{2,1,0:T(8,128)(2,1)S(1)}, bf16[8,64,512]{2,1,0:T(8,128)(2,1)S(1)}, u32[]{:S(2)}, u32[]{:S(2)}) collective-permute-start(bf16[8,64,512]{2,1,0:T(8,128)(2,1)S(1)} %bitcast.39), channel_id=1, source_target_pairs={{0,16},{1,17},{2,18},{3,19},{4,20},{5,21},{6,22},{7,23},{8,24},{9,... | collective-permute-start | bytes 1572872 | tf_op jit(solution)/shard_map/ppermute | solution.py:414
  60.5 16.6 %collective-permute-start.25 = (bf16[8,64,512]{2,1,0:T(8,128)(2,1)S(1)}, bf16[8,64,512]{2,1,0:T(8,128)(2,1)S(1)}, u32[]{:S(2)}, u32[]{:S(2)}) collective-permute-start(bf16[8,64,512]{2,1,0:T(8,128)(2,1)S(1)} %bitcast.36), channel_id=1, source_target_pairs={{0,8},{1,9},{2,10},{3,11},{4,12},{5,13},{6,14},{7,15},{8,0},{9,1},... | collective-permute-start | bytes 1572872 | tf_op jit(solution)/shard_map/ppermute | solution.py:414
  63.7 13.1 %all-to-all-start = ((f32[32,16,128]{2,1,0:T(8,128)}), f32[32,16,128]{2,1,0:T(8,128)S(1)}, u32[]{:S(2)}, u32[]{:S(2)}) async-start(f32[32,16,128]{2,1,0:T(8,128)} %get-tuple-element.44.stats_hbm), calls=%async_computation | async-start | bytes 524288 | tf_op jit(solution)/shard_map/all_to_all | solution.py:544
  66.3 11.1 %collective-permute-start.23 = (bf16[8,64,512]{2,1,0:T(8,128)(2,1)S(1)}, bf16[8,64,512]{2,1,0:T(8,128)(2,1)S(1)}, u32[]{:S(2)}, u32[]{:S(2)}) collective-permute-start(bf16[8,64,512]{2,1,0:T(8,128)(2,1)S(1)} %bitcast.40), channel_id=1, source_target_pairs={{0,1},{1,0},{2,3},{3,2},{4,5},{5,4},{6,7},{7,6},{8,9},{9,8},{10,11... | collective-permute-start | bytes 1572872 | tf_op jit(solution)/shard_map/ppermute | solution.py:414
  66.5 10.9 %collective-permute-start.26 = (bf16[8,64,512]{2,1,0:T(8,128)(2,1)S(1)}, bf16[8,64,512]{2,1,0:T(8,128)(2,1)S(1)}, u32[]{:S(2)}, u32[]{:S(2)}) collective-permute-start(bf16[8,64,512]{2,1,0:T(8,128)(2,1)S(1)} %bitcast.37), channel_id=1, source_target_pairs={{0,1},{1,0},{2,3},{3,2},{4,5},{5,4},{6,7},{7,6},{8,9},{9,8},{10,11... | collective-permute-start | bytes 1572872 | tf_op jit(solution)/shard_map/ppermute | solution.py:414
  76.8 2.7 %copy-start.28 = (f32[32,16,128]{2,1,0:T(8,128)}, f32[32,16,128]{2,1,0:T(8,128)S(1)}, u32[]{:S(2)}) copy-start(f32[32,16,128]{2,1,0:T(8,128)S(1)} %all-to-all-done.stats_all_ref) | copy-start | bytes 786436
  76.8 2.7 %copy-start.29 = (bf16[8,64,512]{2,1,0:T(8,128)(2,1)}, bf16[8,64,512]{2,1,0:T(8,128)(2,1)S(1)}, u32[]{:S(2)}) copy-start(bf16[8,64,512]{2,1,0:T(8,128)(2,1)S(1)} %collective-permute-done.22.refs_9_) | copy-start | bytes 1572868
  76.8 2.0 %collective-permute-start.24 = (bf16[8,64,512]{2,1,0:T(8,128)(2,1)S(1)}, bf16[8,64,512]{2,1,0:T(8,128)(2,1)S(1)}, u32[]{:S(2)}, u32[]{:S(2)}) collective-permute-start(bf16[8,64,512]{2,1,0:T(8,128)(2,1)S(1)} %collective-permute-done.22.refs_9_), channel_id=1, source_target_pairs={{0,1},{1,0},{2,3},{3,2},{4,5},{5,4},{6,7},{7,6},{8,9},{9,8},{10,11... | collective-permute-start | bytes 1572872 | tf_op jit(solution)/shard_map/ppermute | solution.py:414
  77.1 2.4 %copy-start.30 = (bf16[8,64,512]{2,1,0:T(8,128)(2,1)}, bf16[8,64,512]{2,1,0:T(8,128)(2,1)S(1)}, u32[]{:S(2)}) copy-start(bf16[8,64,512]{2,1,0:T(8,128)(2,1)S(1)} %collective-permute-done.25.refs_13_) | copy-start | bytes 1572868
  77.1 2.4 %collective-permute-start.27 = (bf16[8,64,512]{2,1,0:T(8,128)(2,1)S(1)}, bf16[8,64,512]{2,1,0:T(8,128)(2,1)S(1)}, u32[]{:S(2)}, u32[]{:S(2)}) collective-permute-start(bf16[8,64,512]{2,1,0:T(8,128)(2,1)S(1)} %collective-permute-done.25.refs_13_), channel_id=1, source_target_pairs={{0,1},{1,0},{2,3},{3,2},{4,5},{5,4},{6,7},{7,6},{8,9},{9,8},{10,11... | collective-permute-start | bytes 1572872 | tf_op jit(solution)/shard_map/ppermute | solution.py:414
  77.4 2.2 %copy-start.31 = (bf16[8,64,512]{2,1,0:T(8,128)(2,1)}, bf16[8,64,512]{2,1,0:T(8,128)(2,1)S(1)}, u32[]{:S(2)}) copy-start(bf16[8,64,512]{2,1,0:T(8,128)(2,1)S(1)} %collective-permute-done.23.refs_10_) | copy-start | bytes 1572868
  77.4 2.2 %copy-start.32 = (bf16[8,64,512]{2,1,0:T(8,128)(2,1)}, bf16[8,64,512]{2,1,0:T(8,128)(2,1)S(1)}, u32[]{:S(2)}) copy-start(bf16[8,64,512]{2,1,0:T(8,128)(2,1)S(1)} %collective-permute-done.26.refs_14_) | copy-start | bytes 1572868
  78.8 0.8 copy-start.33
  79.6 0.8 copy-start.34

commit v7 on v6

--- a/solution.py
+++ b/solution.py
@@ -99,7 +99,7 @@
         for slot in range(cap):
             row = jnp.where(lane == column * cap + slot, coords_ref[0, column, 0, slot], row)
     row = jnp.where(lane == 3 * cap, count_ref[0, 0], row)
-    out_ref[0] = row
+    out_ref[...] = jnp.broadcast_to(row[None], out_ref.shape)
 
 
 def scan_list(lists_ref, cap, row, column, wanted, found, out_ref, block_of):
@@ -125,10 +125,8 @@
     copy.wait()
 
     def one(k, found):
-        blk = jnp.bitwise_xor(k, layout.blk)
-        row = k // 2 + (k & 1) * (blks // 2)
-        put = lambda other: other * blks + blk
-        return scan_list(lists_ref, cap, row, 0, layout.blk, found, work_ref, put)
+        put = lambda other: other * blks + k
+        return scan_list(lists_ref, cap, k, 0, layout.blk, found, work_ref, put)
 
     close_work(lax.fori_loop(0, blks, one, 0), work_ref)
 
@@ -141,17 +139,29 @@
     copy.wait()
 
     def one(k, found):
-        reader = jnp.bitwise_xor(k, layout.reader)
-        put = lambda other: reader * blks + other
+        put = lambda other: k * blks + other
         return scan_list(lists_ref, cap, k, 1, layout.reader, found, work_ref, put)
 
     close_work(lax.fori_loop(0, readers, one, 0), work_ref)
 
 
+def load(pairs, sems):
+    copies = [pltpu.make_async_copy(src, into, sems.at[k]) for k, (src, into) in enumerate(pairs)]
+    for copy in copies:
+        copy.start()
+    return copies
+
+
 def prepare_kernel(
-    own_ref, cot_ref, wq_ref, wk_ref, wv_ref,
+    own_hbm, cot_hbm, wq_hbm, wk_hbm, wv_hbm,
     query_stack_ref, cot_stack_ref, key_ref, value_ref, wqt_ref, wkt_ref, wvt_ref,
+    own_ref, cot_ref, wq_ref, wk_ref, wv_ref, sems,
 ):
+    loads = load((
+        (own_hbm, own_ref), (wq_hbm, wq_ref), (wk_hbm, wk_ref), (wv_hbm, wv_ref), (cot_hbm, cot_ref),
+    ), sems)
+    for copy in loads:
+        copy.wait()
     head = own_ref.shape[1] // HEADS
     queries = dot(own_ref[...], wq_ref[...]).astype(jnp.bfloat16) * jnp.bfloat16(head**-0.5)
     for p in range(HEADS // 2):
@@ -220,13 +230,6 @@
             tile_bias(self.words[slot, t], patterns[t], blocks[t] == self.layout.me) for t in range(TILES)
         ]
         return jnp.concatenate(parts, 0)
-
-
-def load(pairs, sems):
-    copies = [pltpu.make_async_copy(src, into, sems.at[k]) for k, (src, into) in enumerate(pairs)]
-    for copy in copies:
-        copy.start()
-    return copies
 
 
 def forward_kernel(sizes, work_ref, stack_ref, cot_ref, wk_ref, wvt_ref, mask_ref, *refs):
@@ -418,10 +421,9 @@
     return lax.optimization_barrier((value, *others))[0]
 
 
-def over_readers(chunk, order, blks, *others):
+def over_readers(chunk, order, blks):
     for bit in order[:-1]:
         chunk = jnp.concatenate([chunk, swap(chunk, blks << bit)], 0)
-    chunk = after(chunk, *others)
     return [chunk, swap(chunk, blks << order[-1])]
 
 
@@ -453,7 +455,7 @@
 
     sent = pl.pallas_call(
         send_list_kernel,
-        out_shape=shape((1, 8, 128), i32),
+        out_shape=shape((blks, 8, 128), i32),
         in_specs=[HBM, HBM],
         out_specs=VMEM,
         scratch_shapes=[
@@ -462,11 +464,7 @@
         compiler_params=some,
         name="send_list",
     )(tile_coords.transpose(0, 3, 1, 2), tile_count)
-    sent = after(sent, *cot_other)
-    line_lists = jnp.concatenate([sent] + [swap(sent, 2 * k) for k in range(1, lines)], 0)
-    row_lists = jnp.concatenate([line_lists, swap(line_lists, 1)], 0)
-    sent = after(sent, line_lists)
-    column_lists = jnp.concatenate([sent] + [swap(sent, blks * k) for k in range(1, readers)], 0)
+    row_lists = lax.all_to_all(after(sent, *lined), "blk", 0, 0, tiled=True)
 
     def work(kernel, lists, count, name):
         return pl.pallas_call(
@@ -481,17 +479,19 @@
         )(lists[:, 0])
 
     query_work = work(query_work_kernel, row_lists, blks, "query_work")
-    key_work = work(key_work_kernel, column_lists, readers, "key_work")
 
     stacks = shape((HEADS // 2, 2 * head, 2 * block), bf16)
     own = shape((block, width), bf16)
     square = shape((width, width), bf16)
+    weight = pltpu.VMEM((width, width), bf16)
+    rows_low, rows_wide = pltpu.VMEM((block, width), bf16), pltpu.VMEM((block, width), f32)
     prepared = pl.pallas_call(
         prepare_kernel,
         out_shape=(stacks, stacks, own, own, square, square, square),
-        in_specs=[VMEM] * 5,
+        in_specs=[HBM] * 5,
         out_specs=(VMEM,) * 7,
-        compiler_params=some,
+        scratch_shapes=[rows_low, rows_low, weight, weight, weight, pltpu.SemaphoreType.DMA((5,))],
+        compiler_params=most,
         cost_estimate=cost(2),
         name="prepare",
     )(features, cotangent, w_query, w_key, w_value)
@@ -499,21 +499,19 @@
 
     lined = after(lined, prepared)
     chunks = [jnp.concatenate([entry[:, half * k : half * (k + 1)] for entry in lined], 0) for k in range(2)]
-    here = [over_readers(chunk, order, blks, row_lists) for chunk, order in zip(chunks, orders(readers))]
+    here = [over_readers(chunk, order, blks) for chunk, order in zip(chunks, orders(readers))]
     rows_all = []
     for first, last in here:
-        rows_all += [first, last, swap(after(first, query_work, key_work), 1), swap(last, 1)]
+        rows_all += [first, last, swap(first, 1), swap(last, 1)]
 
     both = jnp.concatenate([cot_parts[0], cot_other[0], cot_parts[1], cot_other[1]], 0)
     cot_line = after(both, *chunks)[None]
     mask = blks // 2
     while mask > 1:
-        cot_line = jnp.concatenate([cot_line, swap(cot_line, mask)], 0)
+        cot_line = after(jnp.concatenate([cot_line, swap(cot_line, mask)], 0), query_work)
         mask //= 2
 
-    weight = pltpu.VMEM((width, width), bf16)
     stack_space = pltpu.VMEM(stacks.shape, bf16)
-    rows_low, rows_wide = pltpu.VMEM((block, width), bf16), pltpu.VMEM((block, width), f32)
     buffer = pltpu.VMEM((2, TILES * block, width), bf16)
     word_buffer = pltpu.VMEM((2, TILES, words, block), i32)
     bias = pltpu.VMEM((TILES * block, block), f32)
@@ -542,6 +540,9 @@
         masks_left = [m for m in range(1, readers) if not m >> bits[k] & 1]
         cots_here.append((part, [swap(part, blks * m) for m in masks_left], swap(part, 1)))
     stats_all = lax.all_to_all(stats, axes, 0, 0, tiled=True)
+
+    column_lists = lax.all_to_all(after(sent, stats)[:readers], "reader", 0, 0, tiled=True)
+    key_work = work(key_work_kernel, column_lists, readers, "key_work")
 
     query_part = pl.pallas_call(
         functools.partial(query_grad_kernel, sizes),
@@ -559,7 +560,7 @@
 
     cots_all = []
     for first, rest, other in cots_here:
-        cots_all += [first, *rest, other] + [swap(after(part, stats_all, query_part), 1) for part in rest]
+        cots_all += [first, *rest, other] + [swap(after(part, stats_all, query_part, key_work), 1) for part in rest]
 
     grad_features = pl.pallas_call(
         functools.partial(key_grad_kernel, sizes, bits),

time: 86.6 us -> 99.3 us (1.15)
  blocking collectives: 0 us -> 9.9 us
  Pallas kernels: 17.4 us -> 23 us
  local copies, waits for them, and re-layouts: 8.48 us -> 5.5 us
    all_to_all x0 -> x1, blocking collectives: none -> 9.9 us  [local(): lax.all_to_all(after(sent, stats)[:readers], 'reader', 0, 0, tiled=True)]
    ppermute x28 -> x21, starting transfers between devices: 31.8 us -> 22.4 us  [swap(): return lax.ppermute(block, axes, [(i, i ^ mask) for i in range(count)])]
    all_to_all x1, starting transfers between devices: 2.58 us -> 8.07 us  [local(): stats_all = lax.all_to_all(stats, axes, 0, 0, tiled=True)]
    ppermute x28 -> x21, waiting for transfers between devices: 18.3 us -> 22.1 us  [swap(): return lax.ppermute(block, axes, [(i, i ^ mask) for i in range(count)])]
    all_to_all x0 -> x1, starting transfers between devices: none -> 3.75 us  [local(): row_lists = lax.all_to_all(after(sent, *lined), 'blk', 0, 0, tiled=True)]
    unnamed x70 -> x50, local copies, waits for them, and re-layouts: 7.36 us -> 3.71 us
    all_to_all x1, waiting for transfers between devices: 5.37 us -> 2.31 us  [local(): stats_all = lax.all_to_all(stats, axes, 0, 0, tiled=True)]
    pallas_call x1, Pallas kernels: 0.73 us -> 3.34 us  [local(): pl.pallas_call(prepare_kernel, out_shape=(stacks, stacks, own, own, squar...]
  transfers between devices with their start and end apart: 29 -> 23, of which waited for: 12 -> 9; matrix products, arithmetic and copies ran while one was open for 2% -> 2% of each run, Pallas kernels for 10% -> 13%
where the time goes in v7:
time: 99.3 us; the launch traced here: 99 us
  starting transfers between devices  34.2 us (34%)
  waiting for transfers between devices  24.4 us (25%)
  Pallas kernels  23 us (23%)
  blocking collectives  9.9 us (10%)
  local copies, waits for them, and re-layouts  5.5 us (6%)
  between operations  1.71 us (2%)
    ppermute x21, starting transfers between devices, swap(): return lax.ppermute(block, axes, [(i, i ^ mask) for i in range(count)])  22.4 us
    ppermute x21, waiting for transfers between devices, swap(): return lax.ppermute(block, axes, [(i, i ^ mask) for i in range(count)])  22.1 us
    all_to_all x1, blocking collectives, local(): lax.all_to_all(after(sent, stats)[:readers], 'reader', 0, 0, tiled=True)  9.9 us
    all_to_all x1, starting transfers between devices, local(): stats_all = lax.all_to_all(stats, axes, 0, 0, tiled=True)  8.07 us
    pallas_call x1, Pallas kernels, local(): pl.pallas_call(functools.partial(query_grad_kernel, sizes), out_shape=sha...  5.6 us
    pallas_call x1, Pallas kernels, local(): pl.pallas_call(functools.partial(key_grad_kernel, sizes, bits), out_shape...  5.59 us
    pallas_call x1, Pallas kernels, local(): pl.pallas_call(functools.partial(forward_kernel, sizes), out_shape=(own,...  4.28 us
    all_to_all x1, starting transfers between devices, local(): row_lists = lax.all_to_all(after(sent, *lined), 'blk', 0, 0, tiled=True)  3.75 us
  transfers between devices with their start and end apart: 23, of which 9 were waited for; matrix products, arithmetic and copies ran while one was open for 2% of the time, Pallas kernels for 13%

profile of v7, /device:TPU:0, one launch (start us, length us, event | category | flops | bytes accessed | tf_op | source)
XLA Modules:
  0.0 99.0 jit_solution(1214779633109339689)
XLA Ops:
  0.6 5.1 %collective-permute-start.2 = (bf16[1,128,512]{2,1,0:T(8,128)(2,1)}, bf16[1,128,512]{2,1,0:T(8,128)(2,1)S(1)}, u32[]{:S(2)}, u32[]{:S(2)}) collective-permute-start(bf16[1,128,512]{2,1,0:T(8,128)(2,1)} %bitcast.30), channel_id=1, source_target_pairs={{0,6},{1,7},{2,4},{3,5},{4,2},{5,3},{6,0},{7,1},{8,14},{9,15},{10,... | collective-permute-start | bytes 393224 | tf_op jit(solution)/shard_map/ppermute | solution.py:417
  5.7 0.0 collective-permute-start.1
  5.7 0.6 collective-permute-start
  6.4 0.9 slice_bitcast_fusion.1
  7.3 1.7 %collective-permute-start.11 = (bf16[1,64,512]{2,1,0:T(8,128)(2,1)S(1)}, bf16[1,64,512]{2,1,0:T(8,128)(2,1)S(1)}, u32[]{:S(2)}, u32[]{:S(2)}) collective-permute-start(bf16[1,64,512]{2,1,0:T(8,128)(2,1)S(1)} %get-tuple-element.48), channel_id=1, source_target_pairs={{0,8},{1,9},{2,10},{3,11},{4,12},{5,13},{6,14},{7,15},{8,0},{9,1},... | collective-permute-start | bytes 196616 | tf_op jit(solution)/shard_map/ppermute | solution.py:417
  9.0 1.5 %collective-permute-start.12 = (bf16[1,64,512]{2,1,0:T(8,128)(2,1)S(1)}, bf16[1,64,512]{2,1,0:T(8,128)(2,1)S(1)}, u32[]{:S(2)}, u32[]{:S(2)}) collective-permute-start(bf16[1,64,512]{2,1,0:T(8,128)(2,1)S(1)} %get-tuple-element.49), channel_id=1, source_target_pairs={{0,16},{1,17},{2,18},{3,19},{4,20},{5,21},{6,22},{7,23},{8,24},{9,... | collective-permute-start | bytes 196616 | tf_op jit(solution)/shard_map/ppermute | solution.py:417
  11.2 1.2 %send_list.1 = s32[8,8,128]{2,1,0:T(8,128)} custom-call(s32[1,3,1,8]{3,2,1,0:T(1,128)S(1)} %bitcast.21, s32[1,1]{1,0:T(1,128)S(6)} %copy.24.count_hbm), custom_call_target="tpu_custom_call" | custom-call | tf_op jit(solution)/shard_map/send_list/pallas_call | solution.py:456
  12.4 0.0 copy-start.19
  12.4 3.3 %prepare.1 = (bf16[4,128,256]{2,1,0:T(8,128)(2,1)}, bf16[4,128,256]{2,1,0:T(8,128)(2,1)}, bf16[128,512]{1,0:T(8,128)(2,1)}, bf16[128,512]{1,0:T(8,128)(2,1)}, bf...) custom-call(bf16[128,512]{1,0:T(8,128)(2,1)} %own_hbm.1, bf16[128,512]{1,0:T(8,128)(2,1)} %cot_ref.1, ...), custom_call_target="tpu_custom_call" | custom-call | flops 400000000 | bytes 4000000 | tf_op jit(solution)/shard_map/prepare/pallas_call | solution.py:488
  15.7 0.0 collective-permute-done.2
  15.8 1.3 %collective-permute-done.1 = bf16[1,128,512]{2,1,0:T(8,128)(2,1)S(1)} collective-permute-done((bf16[1,128,512]{2,1,0:T(8,128)(2,1)}, bf16[1,128,512]{2,1,0:T(8,128)(2,1)S(1)}, u32[]{:S(2)}, u32[]{:S(2)}) %collective-permute-start.1) | collective-permute-done | bytes 131104 | tf_op jit(solution)/shard_map/ppermute | solution.py:417
  17.0 0.0 collective-permute-done
  17.0 3.8 %all-to-all-start = ((s32[8,8,128]{2,1,0:T(8,128)}), s32[8,8,128]{2,1,0:T(8,128)S(1)}, u32[]{:S(2)}, u32[]{:S(2)}) async-start(s32[8,8,128]{2,1,0:T(8,128)} %send_list.1), calls=%async_computation | async-start | bytes 65536 | tf_op jit(solution)/shard_map/all_to_all | solution.py:467
  20.9 1.6 %collective-permute-start.7 = (bf16[4,64,512]{2,1,0:T(8,128)(2,1)S(1)}, bf16[4,64,512]{2,1,0:T(8,128)(2,1)S(1)}, u32[]{:S(2)}, u32[]{:S(2)}) collective-permute-start(bf16[4,64,512]{2,1,0:T(8,128)(2,1)S(1)} %pad_maximum_fusion.3), channel_id=1, source_target_pairs={{0,16},{1,17},{2,18},{3,19},{4,20},{5,21},{6,22},{7,23},{8,24},{9,... | collective-permute-start | bytes 786440 | tf_op jit(solution)/shard_map/ppermute | solution.py:417
  22.6 1.6 %collective-permute-start.3 = (bf16[4,64,512]{2,1,0:T(8,128)(2,1)S(1)}, bf16[4,64,512]{2,1,0:T(8,128)(2,1)S(1)}, u32[]{:S(2)}, u32[]{:S(2)}) collective-permute-start(bf16[4,64,512]{2,1,0:T(8,128)(2,1)S(1)} %pad_maximum_fusion.2), channel_id=1, source_target_pairs={{0,8},{1,9},{2,10},{3,11},{4,12},{5,13},{6,14},{7,15},{8,0},{9,1},... | collective-permute-start | bytes 786440 | tf_op jit(solution)/shard_map/ppermute | solution.py:417
  24.1 0.0 collective-permute-done.11
  24.1 0.0 collective-permute-done.12
  24.2 3.0 %collective-permute-start.13 = (bf16[1,4,64,512]{3,2,1,0:T(8,128)(2,1)S(1)}, bf16[1,4,64,512]{3,2,1,0:T(8,128)(2,1)S(1)}, u32[]{:S(2)}, u32[]{:S(2)}) collective-permute-start(bf16[1,4,64,512]{3,2,1,0:T(8,128)(2,1)S(1)} %bitcast.28), channel_id=1, source_target_pairs={{0,4},{1,5},{2,6},{3,7},{4,0},{5,1},{6,2},{7,3},{8,12},{9,13},{10,... | collective-permute-start | bytes 786440 | tf_op jit(solution)/shard_map/ppermute | solution.py:417
  27.2 0.0 all-to-all-done
  27.2 1.6 %query_work.1.work_ref = s32[133]{0:T(256)S(1)} custom-call(s32[8,128]{1,0:T(8,128)S(1)} %bitcast.19), custom_call_target="tpu_custom_call" | custom-call | flops 200000000 | bytes 4000000 | tf_op jit(solution)/shard_map/query_work/pallas_call | solution.py:470
  28.8 0.9 collective-permute-done.7
  29.8 1.6 %collective-permute-start.8 = (bf16[8,64,512]{2,1,0:T(8,128)(2,1)S(1)}, bf16[8,64,512]{2,1,0:T(8,128)(2,1)S(1)}, u32[]{:S(2)}, u32[]{:S(2)}) collective-permute-start(bf16[8,64,512]{2,1,0:T(8,128)(2,1)S(1)} %constant_dynamic-update-slice_fusion.5.refs_4_), channel_id=1, source_target_pairs={{0,8},{1,9},{2,10},{3,11},{4,12},{5,13},{6,14},{7,15},{8,0},{9,1},... | collective-permute-start | bytes 1572872 | tf_op jit(solution)/shard_map/ppermute | solution.py:417
  31.3 1.6 %collective-permute-start.4 = (bf16[8,64,512]{2,1,0:T(8,128)(2,1)S(1)}, bf16[8,64,512]{2,1,0:T(8,128)(2,1)S(1)}, u32[]{:S(2)}, u32[]{:S(2)}) collective-permute-start(bf16[8,64,512]{2,1,0:T(8,128)(2,1)S(1)} %constant_dynamic-update-slice_fusion.refs_0_), channel_id=1, source_target_pairs={{0,16},{1,17},{2,18},{3,19},{4,20},{5,21},{6,22},{7,23},{8,24},{9,... | collective-permute-start | bytes 1572872 | tf_op jit(solution)/shard_map/ppermute | solution.py:417
  32.9 6.0 %collective-permute-done.13 = bf16[1,4,64,512]{3,2,1,0:T(8,128)(2,1)S(1)} collective-permute-done((bf16[1,4,64,512]{3,2,1,0:T(8,128)(2,1)S(1)}, bf16[1,4,64,512]{3,2,1,0:T(8,128)(2,1)S(1)}, u32[]{:S(2)}, u32[]{:S(2)}) %collective-permute-start.13) | collective-permute-done | bytes 262176 | tf_op jit(solution)/shard_map/ppermute | solution.py:417
  38.9 0.1 pad_maximum_fusion.1
  39.0 0.7 collective-permute-start.14
  39.7 0.0 collective-permute-start.9
  39.7 0.5 collective-permute-start.5
  40.2 3.2 %collective-permute-done.8.refs_5_ = bf16[8,64,512]{2,1,0:T(8,128)(2,1)S(1)} collective-permute-done((bf16[8,64,512]{2,1,0:T(8,128)(2,1)S(1)}, bf16[8,64,512]{2,1,0:T(8,128)(2,1)S(1)}, u32[]{:S(2)}, u32[]{:S(2)}) %collective-permute-start.8) | collective-permute-done | bytes 524320 | tf_op jit(solution)/shard_map/ppermute | solution.py:417
  43.4 1.3 %collective-permute-done.4.refs_1_ = bf16[8,64,512]{2,1,0:T(8,128)(2,1)S(1)} collective-permute-done((bf16[8,64,512]{2,1,0:T(8,128)(2,1)S(1)}, bf16[8,64,512]{2,1,0:T(8,128)(2,1)S(1)}, u32[]{:S(2)}, u32[]{:S(2)}) %collective-permute-start.4) | collective-permute-done | bytes 524320 | tf_op jit(solution)/shard_map/ppermute | solution.py:417
  44.7 7.3 %collective-permute-done.14 = bf16[2,4,64,512]{3,2,1,0:T(8,128)(2,1)S(1)} collective-permute-done((bf16[2,4,64,512]{3,2,1,0:T(8,128)(2,1)S(1)}, bf16[2,4,64,512]{3,2,1,0:T(8,128)(2,1)S(1)}, u32[]{:S(2)}, u32[]{:S(2)}) %collective-permute-start.14) | collective-permute-done | bytes 524320 | tf_op jit(solution)/shard_map/ppermute | solution.py:417
  51.9 0.1 pad_maximum_fusion
  52.0 0.0 copy-start.2
  52.0 0.0 copy-start.9
  52.1 0.0 copy-start.11
  52.1 0.1 fusion
  52.2 0.0 collective-permute-done.9.refs_6_
  52.2 0.0 collective-permute-done.5.refs_2_
  52.3 0.8 copy-done.2
  53.1 0.5 copy-done.9
  53.6 0.6 copy-done.10
  54.2 0.1 copy-done.11
  54.3 0.3 copy-done.12
  54.6 4.3 %forward.1 = (bf16[128,512]{1,0:T(8,128)(2,1)}, f32[32,16,128]{2,1,0:T(8,128)}) custom-call(s32[133]{0:T(256)S(1)} %query_work.1.work_ref, bf16[4,128,256]{2,1,0:T(8,128)(2,1)S(1)} %copy-done.12, bf16[128,512]{1,0:T(8,128)(2,1)S(1)} %copy-done.11, bf16[512,512]{1,0:T(8,128)(2,1)S(1)} %copy-done.2, bf16[512,512]{1,0:T(8,128)(2,1)S(1)} %copy-done.10, ...), custom_call_target="tpu_custom_call" | custom-call | flops 1000000000 | bytes 4000000 | tf_op jit(solution)/shard_map/forward/pallas_call | solution.py:526
  58.9 0.6 collective-permute-start.18
  59.5 1.2 %collective-permute-start.15 = (bf16[8,64,512]{2,1,0:T(8,128)(2,1)S(1)}, bf16[8,64,512]{2,1,0:T(8,128)(2,1)S(1)}, u32[]{:S(2)}, u32[]{:S(2)}) collective-permute-start(bf16[8,64,512]{2,1,0:T(8,128)(2,1)S(1)} %bitcast.25), channel_id=1, source_target_pairs={{0,16},{1,17},{2,18},{3,19},{4,20},{5,21},{6,22},{7,23},{8,24},{9,... | collective-permute-start | bytes 1572872 | tf_op jit(solution)/shard_map/ppermute | solution.py:417
  60.7 0.7 slice.54
  61.4 9.9 %all_to_all.15 = s32[4,8,128]{2,1,0:T(8,128)S(1)} all-to-all(s32[4,8,128]{2,1,0:T(8,128)S(1)} %slice.54), channel_id=1, replica_groups=mesh['reader'=4,'blk'=8] {'reader'}, dimensions={0} | all-to-all | bytes 32768 | tf_op jit(solution)/shard_map/all_to_all | solution.py:544
  71.3 8.1 %all-to-all-start.2 = ((f32[32,16,128]{2,1,0:T(8,128)}), f32[32,16,128]{2,1,0:T(8,128)S(1)}, u32[]{:S(2)}, u32[]{:S(2)}) async-start(f32[32,16,128]{2,1,0:T(8,128)} %get-tuple-element.37.stats_hbm), calls=%async_computation.2 | async-start | bytes 524288 | tf_op jit(solution)/shard_map/all_to_all | solution.py:542
  79.4 0.3 collective-permute-start.19
  79.7 0.3 collective-permute-start.16
  80.0 5.6 %query_grad.1.part_hbm = f32[128,512]{1,0:T(8,128)} custom-call(s32[133]{0:T(256)} %copy-done.13, bf16[4,128,256]{2,1,0:T(8,128)(2,1)} %get-tuple-element.25.stack_ref.stack_hbm, bf16[4,128,256]{2,1,0:T(8,128)(2,1)} %get-tuple-element.27.cot_stack_hbm, f32[32,16,128]{2,1,0:T(8,128)} %get-tuple-element.37.stats_hbm, ...), custom_call_target="tpu_custom_call" | custom-call | flops 1000000000 | bytes 4000000 | tf_op jit(solution)/shard_map/query_grad/pallas_call | solution.py:547
  85.6 1.3 %key_work.1.work_ref = s32[69]{0:T(128)S(1)} custom-call(s32[4,128]{1,0:T(4,128)S(1)} %bitcast.20), custom_call_target="tpu_custom_call" | custom-call | flops 200000000 | bytes 4000000 | tf_op jit(solution)/shard_map/key_work/pallas_call | solution.py:470
  87.0 0.5 copy-done.15
  87.5 2.3 %all-to-all-done.2.stats_all_ref = f32[32,16,128]{2,1,0:T(8,128)S(1)} async-done(((f32[32,16,128]{2,1,0:T(8,128)}), f32[32,16,128]{2,1,0:T(8,128)S(1)}, u32[]{:S(2)}, u32[]{:S(2)}) %all-to-all-start.2) | async-done | bytes 262176 | tf_op jit(solution)/shard_map/all_to_all | solution.py:542
  89.8 0.4 collective-permute-start.20
  90.2 0.1 collective-permute-start.17
  90.4 0.0 collective-permute-done.19.refs_14_
  90.4 0.0 collective-permute-done.16.refs_10_
  90.4 1.4 %collective-permute-done.20.refs_15_ = bf16[8,64,512]{2,1,0:T(8,128)(2,1)S(1)} collective-permute-done((bf16[8,64,512]{2,1,0:T(8,128)(2,1)S(1)}, bf16[8,64,512]{2,1,0:T(8,128)(2,1)S(1)}, u32[]{:S(2)}, u32[]{:S(2)}) %collective-permute-start.20) | collective-permute-done | bytes 524320 | tf_op jit(solution)/shard_map/ppermute | solution.py:417
  91.8 0.7 collective-permute-done.17.refs_11_
  92.5 0.0 copy-done.23
  92.6 0.8 copy-done.24
  93.4 5.6 %key_grad.1 = bf16[128,512]{1,0:T(8,128)(2,1)} custom-call(s32[69]{0:T(128)} %copy-done.15, bf16[128,512]{1,0:T(8,128)(2,1)} %get-tuple-element.28.key_hbm, bf16[128,512]{1,0:T(8,128)(2,1)} %get-tuple-element.29.value_hbm, bf16[512,512]{1,0:T(8,128)(2,1)} %wq_hbm.3, bf16[512,512]{1,0:T(8,128)(2,1)} %get-tuple-element.31.wkt_hbm, ...), custom_call_target="tpu_custom_call" | custom-call | flops 1000000000 | bytes 4000000 | tf_op jit(solution)/shard_map/key_grad/pallas_call | solution.py:565
  (56 shorter events, 0.3 us)
Async XLA Ops:
  0.6 15.1 %collective-permute-start.2 = (bf16[1,128,512]{2,1,0:T(8,128)(2,1)}, bf16[1,128,512]{2,1,0:T(8,128)(2,1)S(1)}, u32[]{:S(2)}, u32[]{:S(2)}) collective-permute-start(bf16[1,128,512]{2,1,0:T(8,128)(2,1)} %bitcast.30), channel_id=1, source_target_pairs={{0,6},{1,7},{2,4},{3,5},{4,2},{5,3},{6,0},{7,1},{8,14},{9,15},{10,... | collective-permute-start | bytes 393224 | tf_op jit(solution)/shard_map/ppermute | solution.py:417
  5.7 11.3 %collective-permute-start.1 = (bf16[1,128,512]{2,1,0:T(8,128)(2,1)}, bf16[1,128,512]{2,1,0:T(8,128)(2,1)S(1)}, u32[]{:S(2)}, u32[]{:S(2)}) collective-permute-start(bf16[1,128,512]{2,1,0:T(8,128)(2,1)} %bitcast.31), channel_id=1, source_target_pairs={{0,4},{1,5},{2,6},{3,7},{4,0},{5,1},{6,2},{7,3},{8,12},{9,13},{10,... | collective-permute-start | bytes 393224 | tf_op jit(solution)/shard_map/ppermute | solution.py:417
  5.7 11.3 %collective-permute-start = (bf16[1,128,512]{2,1,0:T(8,128)(2,1)}, bf16[1,128,512]{2,1,0:T(8,128)(2,1)S(1)}, u32[]{:S(2)}, u32[]{:S(2)}) collective-permute-start(bf16[1,128,512]{2,1,0:T(8,128)(2,1)} %bitcast.32), channel_id=1, source_target_pairs={{0,2},{1,3},{2,0},{3,1},{4,6},{5,7},{6,4},{7,5},{8,10},{9,11},{10,... | collective-permute-start | bytes 393224 | tf_op jit(solution)/shard_map/ppermute | solution.py:417
  7.3 16.9 %collective-permute-start.11 = (bf16[1,64,512]{2,1,0:T(8,128)(2,1)S(1)}, bf16[1,64,512]{2,1,0:T(8,128)(2,1)S(1)}, u32[]{:S(2)}, u32[]{:S(2)}) collective-permute-start(bf16[1,64,512]{2,1,0:T(8,128)(2,1)S(1)} %get-tuple-element.48), channel_id=1, source_target_pairs={{0,8},{1,9},{2,10},{3,11},{4,12},{5,13},{6,14},{7,15},{8,0},{9,1},... | collective-permute-start | bytes 196616 | tf_op jit(solution)/shard_map/ppermute | solution.py:417
  9.0 2.2 %copy-start.14 = (s32[1,1,8,3]{2,1,3,0:T(1,128)S(1)}, s32[1,1,8,3]{2,1,3,0:T(1,128)}, u32[]{:S(2)}) copy-start(s32[1,1,8,3]{2,1,3,0:T(1,128)} %param.13) | copy-start | bytes 292
  9.0 15.2 %collective-permute-start.12 = (bf16[1,64,512]{2,1,0:T(8,128)(2,1)S(1)}, bf16[1,64,512]{2,1,0:T(8,128)(2,1)S(1)}, u32[]{:S(2)}, u32[]{:S(2)}) collective-permute-start(bf16[1,64,512]{2,1,0:T(8,128)(2,1)S(1)} %get-tuple-element.49), channel_id=1, source_target_pairs={{0,16},{1,17},{2,18},{3,19},{4,20},{5,21},{6,22},{7,23},{8,24},{9,... | collective-permute-start | bytes 196616 | tf_op jit(solution)/shard_map/ppermute | solution.py:417
  12.4 8.4 %copy-start.19 = (bf16[128,512]{1,0:T(8,128)(2,1)S(1)}, bf16[128,512]{1,0:T(8,128)(2,1)}, u32[]{:S(2)}) copy-start(bf16[128,512]{1,0:T(8,128)(2,1)} %own_hbm.1) | copy-start | bytes 393220
  17.0 10.1 %all-to-all-start = ((s32[8,8,128]{2,1,0:T(8,128)}), s32[8,8,128]{2,1,0:T(8,128)S(1)}, u32[]{:S(2)}, u32[]{:S(2)}) async-start(s32[8,8,128]{2,1,0:T(8,128)} %send_list.1), calls=%async_computation | async-start | bytes 65536 | tf_op jit(solution)/shard_map/all_to_all | solution.py:467
  20.9 8.8 %collective-permute-start.7 = (bf16[4,64,512]{2,1,0:T(8,128)(2,1)S(1)}, bf16[4,64,512]{2,1,0:T(8,128)(2,1)S(1)}, u32[]{:S(2)}, u32[]{:S(2)}) collective-permute-start(bf16[4,64,512]{2,1,0:T(8,128)(2,1)S(1)} %pad_maximum_fusion.3), channel_id=1, source_target_pairs={{0,16},{1,17},{2,18},{3,19},{4,20},{5,21},{6,22},{7,23},{8,24},{9,... | collective-permute-start | bytes 786440 | tf_op jit(solution)/shard_map/ppermute | solution.py:417
  22.6 8.7 %collective-permute-start.3 = (bf16[4,64,512]{2,1,0:T(8,128)(2,1)S(1)}, bf16[4,64,512]{2,1,0:T(8,128)(2,1)S(1)}, u32[]{:S(2)}, u32[]{:S(2)}) collective-permute-start(bf16[4,64,512]{2,1,0:T(8,128)(2,1)S(1)} %pad_maximum_fusion.2), channel_id=1, source_target_pairs={{0,8},{1,9},{2,10},{3,11},{4,12},{5,13},{6,14},{7,15},{8,0},{9,1},... | collective-permute-start | bytes 786440 | tf_op jit(solution)/shard_map/ppermute | solution.py:417
  24.2 14.7 %collective-permute-start.13 = (bf16[1,4,64,512]{3,2,1,0:T(8,128)(2,1)S(1)}, bf16[1,4,64,512]{3,2,1,0:T(8,128)(2,1)S(1)}, u32[]{:S(2)}, u32[]{:S(2)}) collective-permute-start(bf16[1,4,64,512]{3,2,1,0:T(8,128)(2,1)S(1)} %bitcast.28), channel_id=1, source_target_pairs={{0,4},{1,5},{2,6},{3,7},{4,0},{5,1},{6,2},{7,3},{8,12},{9,13},{10,... | collective-permute-start | bytes 786440 | tf_op jit(solution)/shard_map/ppermute | solution.py:417
  28.8 23.5 %copy-start.13 = (s32[133]{0:T(256)}, s32[133]{0:T(256)S(1)}, u32[]{:S(2)}) copy-start(s32[133]{0:T(256)S(1)} %query_work.1.work_ref) | copy-start | bytes 1600
  29.7 22.5 %copy-start.1 = (bf16[8,64,512]{2,1,0:T(8,128)(2,1)}, bf16[8,64,512]{2,1,0:T(8,128)(2,1)S(1)}, u32[]{:S(2)}) copy-start(bf16[8,64,512]{2,1,0:T(8,128)(2,1)S(1)} %constant_dynamic-update-slice_fusion.5.refs_4_) | copy-start | bytes 1572868
  29.8 13.6 %collective-permute-start.8 = (bf16[8,64,512]{2,1,0:T(8,128)(2,1)S(1)}, bf16[8,64,512]{2,1,0:T(8,128)(2,1)S(1)}, u32[]{:S(2)}, u32[]{:S(2)}) collective-permute-start(bf16[8,64,512]{2,1,0:T(8,128)(2,1)S(1)} %constant_dynamic-update-slice_fusion.5.refs_4_), channel_id=1, source_target_pairs={{0,8},{1,9},{2,10},{3,11},{4,12},{5,13},{6,14},{7,15},{8,0},{9,1},... | collective-permute-start | bytes 1572872 | tf_op jit(solution)/shard_map/ppermute | solution.py:417
  31.3 21.0 %copy-start = (bf16[8,64,512]{2,1,0:T(8,128)(2,1)}, bf16[8,64,512]{2,1,0:T(8,128)(2,1)S(1)}, u32[]{:S(2)}) copy-start(bf16[8,64,512]{2,1,0:T(8,128)(2,1)S(1)} %constant_dynamic-update-slice_fusion.refs_0_) | copy-start | bytes 1572868
  31.3 13.3 %collective-permute-start.4 = (bf16[8,64,512]{2,1,0:T(8,128)(2,1)S(1)}, bf16[8,64,512]{2,1,0:T(8,128)(2,1)S(1)}, u32[]{:S(2)}, u32[]{:S(2)}) collective-permute-start(bf16[8,64,512]{2,1,0:T(8,128)(2,1)S(1)} %constant_dynamic-update-slice_fusion.refs_0_), channel_id=1, source_target_pairs={{0,16},{1,17},{2,18},{3,19},{4,20},{5,21},{6,22},{7,23},{8,24},{9,... | collective-permute-start | bytes 1572872 | tf_op jit(solution)/shard_map/ppermute | solution.py:417
  39.0 13.0 %collective-permute-start.14 = (bf16[2,4,64,512]{3,2,1,0:T(8,128)(2,1)S(1)}, bf16[2,4,64,512]{3,2,1,0:T(8,128)(2,1)S(1)}, u32[]{:S(2)}, u32[]{:S(2)}) collective-permute-start(bf16[2,4,64,512]{3,2,1,0:T(8,128)(2,1)S(1)} %pad_maximum_fusion.1), channel_id=1, source_target_pairs={{0,2},{1,3},{2,0},{3,1},{4,6},{5,7},{6,4},{7,5},{8,10},{9,11},{10,... | collective-permute-start | bytes 1572872 | tf_op jit(solution)/shard_map/ppermute | solution.py:417
  39.7 12.5 %collective-permute-start.9 = (bf16[8,64,512]{2,1,0:T(8,128)(2,1)S(1)}, bf16[8,64,512]{2,1,0:T(8,128)(2,1)S(1)}, u32[]{:S(2)}, u32[]{:S(2)}) collective-permute-start(bf16[8,64,512]{2,1,0:T(8,128)(2,1)S(1)} %constant_dynamic-update-slice_fusion.5.refs_4_), channel_id=1, source_target_pairs={{0,1},{1,0},{2,3},{3,2},{4,5},{5,4},{6,7},{7,6},{8,9},{9,8},{10,11... | collective-permute-start | bytes 1572872 | tf_op jit(solution)/shard_map/ppermute | solution.py:417
  39.7 12.5 %collective-permute-start.5 = (bf16[8,64,512]{2,1,0:T(8,128)(2,1)S(1)}, bf16[8,64,512]{2,1,0:T(8,128)(2,1)S(1)}, u32[]{:S(2)}, u32[]{:S(2)}) collective-permute-start(bf16[8,64,512]{2,1,0:T(8,128)(2,1)S(1)} %constant_dynamic-update-slice_fusion.refs_0_), channel_id=1, source_target_pairs={{0,1},{1,0},{2,3},{3,2},{4,5},{5,4},{6,7},{7,6},{8,9},{9,8},{10,11... | collective-permute-start | bytes 1572872 | tf_op jit(solution)/shard_map/ppermute | solution.py:417
  43.4 8.9 %copy-start.3 = (bf16[8,64,512]{2,1,0:T(8,128)(2,1)}, bf16[8,64,512]{2,1,0:T(8,128)(2,1)S(1)}, u32[]{:S(2)}) copy-start(bf16[8,64,512]{2,1,0:T(8,128)(2,1)S(1)} %collective-permute-done.8.refs_5_) | copy-start | bytes 1572868
  43.4 8.9 %collective-permute-start.10 = (bf16[8,64,512]{2,1,0:T(8,128)(2,1)S(1)}, bf16[8,64,512]{2,1,0:T(8,128)(2,1)S(1)}, u32[]{:S(2)}, u32[]{:S(2)}) collective-permute-start(bf16[8,64,512]{2,1,0:T(8,128)(2,1)S(1)} %collective-permute-done.8.refs_5_), channel_id=1, source_target_pairs={{0,1},{1,0},{2,3},{3,2},{4,5},{5,4},{6,7},{7,6},{8,9},{9,8},{10,11... | collective-permute-start | bytes 1572872 | tf_op jit(solution)/shard_map/ppermute | solution.py:417
  44.7 7.6 %copy-start.4 = (bf16[8,64,512]{2,1,0:T(8,128)(2,1)}, bf16[8,64,512]{2,1,0:T(8,128)(2,1)S(1)}, u32[]{:S(2)}) copy-start(bf16[8,64,512]{2,1,0:T(8,128)(2,1)S(1)} %collective-permute-done.4.refs_1_) | copy-start | bytes 1572868
  44.7 7.6 %collective-permute-start.6 = (bf16[8,64,512]{2,1,0:T(8,128)(2,1)S(1)}, bf16[8,64,512]{2,1,0:T(8,128)(2,1)S(1)}, u32[]{:S(2)}, u32[]{:S(2)}) collective-permute-start(bf16[8,64,512]{2,1,0:T(8,128)(2,1)S(1)} %collective-permute-done.4.refs_1_), channel_id=1, source_target_pairs={{0,1},{1,0},{2,3},{3,2},{4,5},{5,4},{6,7},{7,6},{8,9},{9,8},{10,11... | collective-permute-start | bytes 1572872 | tf_op jit(solution)/shard_map/ppermute | solution.py:417
  52.0 1.1 %copy-start.2 = (bf16[512,512]{1,0:T(8,128)(2,1)S(1)}, bf16[512,512]{1,0:T(8,128)(2,1)}, u32[]{:S(2)}) copy-start(bf16[512,512]{1,0:T(8,128)(2,1)} %wk_hbm.3) | copy-start | bytes 1572868
  52.0 1.6 %copy-start.9 = (s32[240,128,4]{1,2,0:T(4,128)S(1)}, s32[240,128,4]{1,2,0:T(4,128)}, u32[]{:S(2)}) copy-start(s32[240,128,4]{1,2,0:T(4,128)} %param.15) | copy-start | bytes 1474564
  52.1 2.1 %copy-start.10 = (bf16[512,512]{1,0:T(8,128)(2,1)S(1)}, bf16[512,512]{1,0:T(8,128)(2,1)}, u32[]{:S(2)}) copy-start(bf16[512,512]{1,0:T(8,128)(2,1)} %get-tuple-element.26.wvt_ref.wvt_hbm) | copy-start | bytes 1572868
  52.1 2.2 %copy-start.11 = (bf16[128,512]{1,0:T(8,128)(2,1)S(1)}, bf16[128,512]{1,0:T(8,128)(2,1)}, u32[]{:S(2)}) copy-start(bf16[128,512]{1,0:T(8,128)(2,1)} %cot_ref.1) | copy-start | bytes 393220
  52.1 2.5 %copy-start.12 = (bf16[4,128,256]{2,1,0:T(8,128)(2,1)S(1)}, bf16[4,128,256]{2,1,0:T(8,128)(2,1)}, u32[]{:S(2)}) copy-start(bf16[4,128,256]{2,1,0:T(8,128)(2,1)} %get-tuple-element.25.stack_ref.stack_hbm) | copy-start | bytes 786436
  52.2 27.2 %copy-start.16 = (bf16[4,2,64,512]{3,2,1,0:T(8,128)(2,1)}, bf16[4,2,64,512]{3,2,1,0:T(8,128)(2,1)S(1)}, u32[]{:S(2)}) copy-start(bf16[4,2,64,512]{3,2,1,0:T(8,128)(2,1)S(1)} %get-tuple-element.46) | copy-start | bytes 1572868
  52.2 27.5 %copy-start.17 = (bf16[4,2,64,512]{3,2,1,0:T(8,128)(2,1)}, bf16[4,2,64,512]{3,2,1,0:T(8,128)(2,1)S(1)}, u32[]{:S(2)}) copy-start(bf16[4,2,64,512]{3,2,1,0:T(8,128)(2,1)S(1)} %get-tuple-element.47) | copy-start | bytes 1572868
  52.2 6.7 %copy-start.5 = (bf16[8,64,512]{2,1,0:T(8,128)(2,1)}, bf16[8,64,512]{2,1,0:T(8,128)(2,1)S(1)}, u32[]{:S(2)}) copy-start(bf16[8,64,512]{2,1,0:T(8,128)(2,1)S(1)} %collective-permute-done.9.refs_6_) | copy-start | bytes 1572868
  52.2 6.6 %copy-start.6 = (bf16[8,64,512]{2,1,0:T(8,128)(2,1)}, bf16[8,64,512]{2,1,0:T(8,128)(2,1)S(1)}, u32[]{:S(2)}) copy-start(bf16[8,64,512]{2,1,0:T(8,128)(2,1)S(1)} %collective-permute-done.5.refs_2_) | copy-start | bytes 1572868
  52.2 6.6 %copy-start.7 = (bf16[8,64,512]{2,1,0:T(8,128)(2,1)}, bf16[8,64,512]{2,1,0:T(8,128)(2,1)S(1)}, u32[]{:S(2)}) copy-start(bf16[8,64,512]{2,1,0:T(8,128)(2,1)S(1)} %collective-permute-done.10.refs_7_) | copy-start | bytes 1572868
  52.3 6.6 %copy-start.8 = (bf16[8,64,512]{2,1,0:T(8,128)(2,1)}, bf16[8,64,512]{2,1,0:T(8,128)(2,1)S(1)}, u32[]{:S(2)}) copy-start(bf16[8,64,512]{2,1,0:T(8,128)(2,1)S(1)} %collective-permute-done.6.refs_3_) | copy-start | bytes 1572868
  58.9 30.9 %collective-permute-start.18 = (bf16[8,64,512]{2,1,0:T(8,128)(2,1)S(1)}, bf16[8,64,512]{2,1,0:T(8,128)(2,1)S(1)}, u32[]{:S(2)}, u32[]{:S(2)}) collective-permute-start(bf16[8,64,512]{2,1,0:T(8,128)(2,1)S(1)} %bitcast.22), channel_id=1, source_target_pairs={{0,8},{1,9},{2,10},{3,11},{4,12},{5,13},{6,14},{7,15},{8,0},{9,1},... | collective-permute-start | bytes 1572872 | tf_op jit(solution)/shard_map/ppermute | solution.py:417
  59.5 30.7 %collective-permute-start.15 = (bf16[8,64,512]{2,1,0:T(8,128)(2,1)S(1)}, bf16[8,64,512]{2,1,0:T(8,128)(2,1)S(1)}, u32[]{:S(2)}, u32[]{:S(2)}) collective-permute-start(bf16[8,64,512]{2,1,0:T(8,128)(2,1)S(1)} %bitcast.25), channel_id=1, source_target_pairs={{0,16},{1,17},{2,18},{3,19},{4,20},{5,21},{6,22},{7,23},{8,24},{9,... | collective-permute-start | bytes 1572872 | tf_op jit(solution)/shard_map/ppermute | solution.py:417
  71.3 18.5 %all-to-all-start.2 = ((f32[32,16,128]{2,1,0:T(8,128)}), f32[32,16,128]{2,1,0:T(8,128)S(1)}, u32[]{:S(2)}, u32[]{:S(2)}) async-start(f32[32,16,128]{2,1,0:T(8,128)} %get-tuple-element.37.stats_hbm), calls=%async_computation.2 | async-start | bytes 524288 | tf_op jit(solution)/shard_map/all_to_all | solution.py:542
  79.4 11.0 %collective-permute-start.19 = (bf16[8,64,512]{2,1,0:T(8,128)(2,1)S(1)}, bf16[8,64,512]{2,1,0:T(8,128)(2,1)S(1)}, u32[]{:S(2)}, u32[]{:S(2)}) collective-permute-start(bf16[8,64,512]{2,1,0:T(8,128)(2,1)S(1)} %bitcast.23), channel_id=1, source_target_pairs={{0,1},{1,0},{2,3},{3,2},{4,5},{5,4},{6,7},{7,6},{8,9},{9,8},{10,11... | collective-permute-start | bytes 1572872 | tf_op jit(solution)/shard_map/ppermute | solution.py:417
  79.7 10.6 %collective-permute-start.16 = (bf16[8,64,512]{2,1,0:T(8,128)(2,1)S(1)}, bf16[8,64,512]{2,1,0:T(8,128)(2,1)}, u32[]{:S(2)}, u32[]{:S(2)}) collective-permute-start(bf16[8,64,512]{2,1,0:T(8,128)(2,1)S(1)} %bitcast.26), channel_id=1, source_target_pairs={{0,1},{1,0},{2,3},{3,2},{4,5},{5,4},{6,7},{7,6},{8,9},{9,8},{10,11... | collective-permute-start | bytes 1572872 | tf_op jit(solution)/shard_map/ppermute | solution.py:417
  86.9 0.5 copy-start.15
  89.8 2.7 %copy-start.18 = (f32[32,16,128]{2,1,0:T(8,128)}, f32[32,16,128]{2,1,0:T(8,128)S(1)}, u32[]{:S(2)}) copy-start(f32[32,16,128]{2,1,0:T(8,128)S(1)} %all-to-all-done.2.stats_all_ref) | copy-start | bytes 786436
  89.8 2.7 %copy-start.20 = (bf16[8,64,512]{2,1,0:T(8,128)(2,1)}, bf16[8,64,512]{2,1,0:T(8,128)(2,1)S(1)}, u32[]{:S(2)}) copy-start(bf16[8,64,512]{2,1,0:T(8,128)(2,1)S(1)} %collective-permute-done.18.refs_13_) | copy-start | bytes 1572868
  89.8 2.0 %collective-permute-start.20 = (bf16[8,64,512]{2,1,0:T(8,128)(2,1)S(1)}, bf16[8,64,512]{2,1,0:T(8,128)(2,1)S(1)}, u32[]{:S(2)}, u32[]{:S(2)}) collective-permute-start(bf16[8,64,512]{2,1,0:T(8,128)(2,1)S(1)} %collective-permute-done.18.refs_13_), channel_id=1, source_target_pairs={{0,1},{1,0},{2,3},{3,2},{4,5},{5,4},{6,7},{7,6},{8,9},{9,8},{10,11... | collective-permute-start | bytes 1572872 | tf_op jit(solution)/shard_map/ppermute | solution.py:417
  90.2 2.3 %copy-start.21 = (bf16[8,64,512]{2,1,0:T(8,128)(2,1)}, bf16[8,64,512]{2,1,0:T(8,128)(2,1)S(1)}, u32[]{:S(2)}) copy-start(bf16[8,64,512]{2,1,0:T(8,128)(2,1)S(1)} %collective-permute-done.15.refs_9_) | copy-start | bytes 1572868
  90.2 2.3 %collective-permute-start.17 = (bf16[8,64,512]{2,1,0:T(8,128)(2,1)S(1)}, bf16[8,64,512]{2,1,0:T(8,128)(2,1)S(1)}, u32[]{:S(2)}, u32[]{:S(2)}) collective-permute-start(bf16[8,64,512]{2,1,0:T(8,128)(2,1)S(1)} %collective-permute-done.15.refs_9_), channel_id=1, source_target_pairs={{0,1},{1,0},{2,3},{3,2},{4,5},{5,4},{6,7},{7,6},{8,9},{9,8},{10,11... | collective-permute-start | bytes 1572872 | tf_op jit(solution)/shard_map/ppermute | solution.py:417
  90.4 2.2 %copy-start.22 = (bf16[8,64,512]{2,1,0:T(8,128)(2,1)}, bf16[8,64,512]{2,1,0:T(8,128)(2,1)S(1)}, u32[]{:S(2)}) copy-start(bf16[8,64,512]{2,1,0:T(8,128)(2,1)S(1)} %collective-permute-done.19.refs_14_) | copy-start | bytes 1572868
  91.8 0.8 copy-start.23
  92.6 0.9 copy-start.24
